TPU v7x, 32 devices: a whole 2x2x4 slice. The times are simulated.
32 devices in a mesh: row: 4 (over y, core), col: 8 (over z, x).
Axes of the slice: x: 2, y: 2, z: 4, core: 2. Of those that a mesh axis runs over, the one named last changes fastest.
Arguments:
- density: bfloat16 [32, 15, 128, 128], P(('row', 'col')), may hold values from -0.5 to 0.5
- pattern: int32 [32, 15], P(('row', 'col')), may hold values 0 or 1
- filter_mask: int32 [32, 29], P(('row', 'col')), may hold values 0 or 1
Outputs:
- purified: bfloat16 [32, 29, 128, 128], P(('row', 'col'))
All inputs are finite; a program needn't handle non-finite values. No bound on the sum of `pattern` or of `filter_mask` on one device may be relied on, other than what follows from the above.
Results may differ from a plain program's by a relative error of at most 0.0045.
Values may be sent and summed in bfloat16 or wider, within the bound.
No kernel may reach another device: no remote copies, remote signals or barrier semaphores. Data moves between devices by JAX's collectives and lax.ppermute only.
A program may use at most 64 MiB of HBM per device.

v0:
```python
import jax
import jax.numpy as jnp
from jax import lax
from jax.sharding import PartitionSpec as P


def shifted(block, axis, distance):
    devices = range(lax.axis_size(axis))
    route = [((i - distance) % len(devices), i) for i in devices]
    return lax.ppermute(block, axis, route)


def extend(blocks, band_reach, fetch):
    row_count = blocks.shape[0]
    hop_count = -(-band_reach // row_count)
    below_rows = []
    above_rows = []
    for distance in range(1, hop_count + 1):
        below_rows.insert(0, fetch(blocks, distance))
        above_rows.append(fetch(blocks, -distance))
    offset = sum((portion.shape[0] for portion in below_rows))
    return (jnp.concatenate(below_rows + [blocks] + above_rows, axis=0), offset)


def band_product(left_blocks, extended, offset, band_reach, out_slots, slot_shift):
    row_count = left_blocks.shape[0]
    slot_count = left_blocks.shape[1]
    ext_slots = extended.shape[1]
    columns = []
    for target in range(out_slots):
        picked = [
            source for source in range(slot_count) if 0 <= target - source + slot_shift < ext_slots
        ]
        lowest = picked[0]
        highest = picked[-1] + 1
        pieces = jnp.stack(
            [
                extended[
                    offset - band_reach + source : offset - band_reach + source + row_count,
                    target - source + slot_shift,
                ]
                for source in range(lowest, highest)
            ],
            axis=1,
        )
        columns.append(
            jnp.einsum(
                "rsab,rsbc->rac",
                left_blocks[:, lowest:highest],
                pieces,
                preferred_element_type=jnp.float32,
            )
        )
    return jnp.stack(columns, axis=1)


def shards(density, pattern, filter_mask):
    band_reach = (pattern.shape[1] - 1) // 2
    wide_count = filter_mask.shape[1]
    masked = density * pattern[:, :, None, None].astype(jnp.bfloat16)
    retain = filter_mask[:, :, None, None].astype(jnp.float32)

    def fetch_density(portion, distance):
        return shifted(portion, ("row", "col"), distance)

    extended, offset = extend(masked, band_reach, fetch_density)
    square = band_product(masked, extended, offset, band_reach, wide_count, 0)
    square_kept = square * retain
    square_round = square_kept.astype(jnp.bfloat16)

    def fetch_square(portion, distance):
        return shifted(portion, ("row", "col"), distance)

    square_ext, square_offset = extend(square_round, band_reach, fetch_square)
    cubed = band_product(masked, square_ext, square_offset, band_reach, wide_count, band_reach)
    return (retain * (3.0 * square_kept - 2.0 * cubed)).astype(jnp.bfloat16)


def solution(mesh):
    in_specs = (
        P(("row", "col"), None, None, None),
        P(("row", "col"), None),
        P(("row", "col"), None),
    )
    out_specs = P(("row", "col"), None, None, None)
    return jax.shard_map(shards, mesh=mesh, in_specs=in_specs, out_specs=out_specs, check_vma=False)
```

profile of v0, /device:TPU:0, one launch (start us, length us, event | category | flops | bytes accessed | tf_op | source)
XLA Modules:
  0.0 529.6 jit_solution(13204573666782345746)
XLA Ops:
  1.8 6.0 %collective-permute-start = (bf16[1,15,128,128]{3,2,1,0:T(8,128)(2,1)S(1)}, bf16[1,15,128,128]{3,2,1,0:T(8,128)(2,1)S(1)}, u32[]{:S(2)}, u32[]{:S(2)}) collective-permute-start(bf16[1,15,128,128]{3,2,1,0:T(8,128)(2,1)S(1)} %broadcast_multiply_fusion), channel_id=1, source_target_pairs={{25,0},{26,1},{27,2},{28,3},{29,4},{30,5},{31,6},{0,7},{1,8},{2,9}... | collective-permute-start | bytes 1474568 | tf_op jit(solution)/shard_map/ppermute | solution.py:10
  8.5 3.2 collective-permute-start.3
  12.3 7.2 %collective-permute-done = bf16[1,15,128,128]{3,2,1,0:T(8,128)(2,1)S(1)} collective-permute-done((bf16[1,15,128,128]{3,2,1,0:T(8,128)(2,1)S(1)}, bf16[1,15,128,128]{3,2,1,0:T(8,128)(2,1)S(1)}, u32[]{:S(2)}, u32[]{:S(2)}) %collective-permute-start) | collective-permute-done | bytes 491552 | tf_op jit(solution)/shard_map/ppermute | solution.py:10
  19.6 10.5 %collective-permute-done.1 = bf16[1,15,128,128]{3,2,1,0:T(8,128)(2,1)S(1)} collective-permute-done((bf16[1,15,128,128]{3,2,1,0:T(8,128)(2,1)S(1)}, bf16[1,15,128,128]{3,2,1,0:T(8,128)(2,1)S(1)}, u32[]{:S(2)}, u32[]{:S(2)}) %collective-permute-start.1) | collective-permute-done | bytes 491552 | tf_op jit(solution)/shard_map/ppermute | solution.py:10
  30.4 10.2 %collective-permute-done.2 = bf16[1,15,128,128]{3,2,1,0:T(8,128)(2,1)S(1)} collective-permute-done((bf16[1,15,128,128]{3,2,1,0:T(8,128)(2,1)S(1)}, bf16[1,15,128,128]{3,2,1,0:T(8,128)(2,1)S(1)}, u32[]{:S(2)}, u32[]{:S(2)}) %collective-permute-start.2) | collective-permute-done | bytes 491552 | tf_op jit(solution)/shard_map/ppermute | solution.py:10
  40.7 25.7 %collective-permute-start.7 = (bf16[1,15,128,128]{3,2,1,0:T(8,128)(2,1)S(1)}, bf16[1,15,128,128]{3,2,1,0:T(8,128)(2,1)S(1)}, u32[]{:S(2)}, u32[]{:S(2)}) collective-permute-start(bf16[1,15,128,128]{3,2,1,0:T(8,128)(2,1)S(1)} %broadcast_multiply_fusion), channel_id=1, source_target_pairs={{1,0},{2,1},{3,2},{4,3},{5,4},{6,5},{7,6},{8,7},{9,8},{10,9},{11,1... | collective-permute-start | bytes 1474568 | tf_op jit(solution)/shard_map/ppermute | solution.py:10
  66.4 27.0 %collective-permute-done.3 = bf16[1,15,128,128]{3,2,1,0:T(8,128)(2,1)S(1)} collective-permute-done((bf16[1,15,128,128]{3,2,1,0:T(8,128)(2,1)S(1)}, bf16[1,15,128,128]{3,2,1,0:T(8,128)(2,1)S(1)}, u32[]{:S(2)}, u32[]{:S(2)}) %collective-permute-start.3) | collective-permute-done | bytes 491552 | tf_op jit(solution)/shard_map/ppermute | solution.py:10
  93.9 3.1 collective-permute-start.9
  97.1 30.6 %collective-permute-start.10 = (bf16[1,15,128,128]{3,2,1,0:T(8,128)(2,1)S(1)}, bf16[1,15,128,128]{3,2,1,0:T(8,128)(2,1)S(1)}, u32[]{:S(2)}, u32[]{:S(2)}) collective-permute-start(bf16[1,15,128,128]{3,2,1,0:T(8,128)(2,1)S(1)} %broadcast_multiply_fusion), channel_id=1, source_target_pairs={{4,0},{5,1},{6,2},{7,3},{8,4},{9,5},{10,6},{11,7},{12,8},{13,9},{1... | collective-permute-start | bytes 1474568 | tf_op jit(solution)/shard_map/ppermute | solution.py:10
  128.3 2.3 collective-permute-start.13
  131.6 44.3 %collective-permute-done.10 = bf16[1,15,128,128]{3,2,1,0:T(8,128)(2,1)S(1)} collective-permute-done((bf16[1,15,128,128]{3,2,1,0:T(8,128)(2,1)S(1)}, bf16[1,15,128,128]{3,2,1,0:T(8,128)(2,1)S(1)}, u32[]{:S(2)}, u32[]{:S(2)}) %collective-permute-start.10) | collective-permute-done | bytes 491552 | tf_op jit(solution)/shard_map/ppermute | solution.py:10
  183.0 3.6 collective-permute-start.18
  186.5 2.2 collective-permute-start.17
  188.7 18.4 %collective-permute-done.14 = bf16[1,29,128,128]{3,2,1,0:T(8,128)(2,1)S(1)} collective-permute-done((bf16[1,29,128,128]{3,2,1,0:T(8,128)(2,1)S(1)}, bf16[1,29,128,128]{3,2,1,0:T(8,128)(2,1)S(1)}, u32[]{:S(2)}, u32[]{:S(2)}) %collective-permute-start.14) | collective-permute-done | bytes 950304 | tf_op jit(solution)/shard_map/ppermute | solution.py:10
  207.2 18.1 %collective-permute-done.15 = bf16[1,29,128,128]{3,2,1,0:T(8,128)(2,1)S(1)} collective-permute-done((bf16[1,29,128,128]{3,2,1,0:T(8,128)(2,1)S(1)}, bf16[1,29,128,128]{3,2,1,0:T(8,128)(2,1)S(1)}, u32[]{:S(2)}, u32[]{:S(2)}) %collective-permute-start.15) | collective-permute-done | bytes 950304 | tf_op jit(solution)/shard_map/ppermute | solution.py:10
  225.4 60.5 %collective-permute-done.16 = bf16[1,29,128,128]{3,2,1,0:T(8,128)(2,1)S(1)} collective-permute-done((bf16[1,29,128,128]{3,2,1,0:T(8,128)(2,1)S(1)}, bf16[1,29,128,128]{3,2,1,0:T(8,128)(2,1)S(1)}, u32[]{:S(2)}, u32[]{:S(2)}) %collective-permute-start.16) | collective-permute-done | bytes 950304 | tf_op jit(solution)/shard_map/ppermute | solution.py:10
  285.9 45.3 %collective-permute-start.21 = (bf16[1,29,128,128]{3,2,1,0:T(8,128)(2,1)S(1)}, bf16[1,29,128,128]{3,2,1,0:T(8,128)(2,1)S(1)}, u32[]{:S(2)}, u32[]{:S(2)}) collective-permute-start(bf16[1,29,128,128]{3,2,1,0:T(8,128)(2,1)S(1)} %multiply_convert_fusion.1), channel_id=1, source_target_pairs={{1,0},{2,1},{3,2},{4,3},{5,4},{6,5},{7,6},{8,7},{9,8},{10,9},{11,1... | collective-permute-start | bytes 2850824 | tf_op jit(solution)/shard_map/ppermute | solution.py:10
  331.3 22.7 %collective-permute-start.22 = (bf16[1,29,128,128]{3,2,1,0:T(8,128)(2,1)S(1)}, bf16[1,29,128,128]{3,2,1,0:T(8,128)(2,1)S(1)}, u32[]{:S(2)}, u32[]{:S(2)}) collective-permute-start(bf16[1,29,128,128]{3,2,1,0:T(8,128)(2,1)S(1)} %multiply_convert_fusion.1), channel_id=1, source_target_pairs={{2,0},{3,1},{4,2},{5,3},{6,4},{7,5},{8,6},{9,7},{10,8},{11,9},{12,... | collective-permute-start | bytes 2850824 | tf_op jit(solution)/shard_map/ppermute | solution.py:10
  354.2 2.3 collective-permute-start.23
  356.6 54.3 %collective-permute-start.24 = (bf16[1,29,128,128]{3,2,1,0:T(8,128)(2,1)S(1)}, bf16[1,29,128,128]{3,2,1,0:T(8,128)(2,1)S(1)}, u32[]{:S(2)}, u32[]{:S(2)}) collective-permute-start(bf16[1,29,128,128]{3,2,1,0:T(8,128)(2,1)S(1)} %multiply_convert_fusion.1), channel_id=1, source_target_pairs={{4,0},{5,1},{6,2},{7,3},{8,4},{9,5},{10,6},{11,7},{12,8},{13,9},{1... | collective-permute-start | bytes 2850824 | tf_op jit(solution)/shard_map/ppermute | solution.py:10
  411.5 2.2 collective-permute-start.27
  413.8 98.6 %collective-permute-done.24 = bf16[1,29,128,128]{3,2,1,0:T(8,128)(2,1)S(1)} collective-permute-done((bf16[1,29,128,128]{3,2,1,0:T(8,128)(2,1)S(1)}, bf16[1,29,128,128]{3,2,1,0:T(8,128)(2,1)S(1)}, u32[]{:S(2)}, u32[]{:S(2)}) %collective-permute-start.24) | collective-permute-done | bytes 950304 | tf_op jit(solution)/shard_map/ppermute | solution.py:10
  512.7 6.8 %collective-permute-done.25 = bf16[1,29,128,128]{3,2,1,0:T(8,128)(2,1)S(1)} collective-permute-done((bf16[1,29,128,128]{3,2,1,0:T(8,128)(2,1)S(1)}, bf16[1,29,128,128]{3,2,1,0:T(8,128)(2,1)S(1)}, u32[]{:S(2)}, u32[]{:S(2)}) %collective-permute-start.25) | collective-permute-done | bytes 950304 | tf_op jit(solution)/shard_map/ppermute | solution.py:10
  528.2 1.4 multiply_convert_fusion
  (170 shorter events, 22.0 us)
Async XLA Ops:
  8.5 84.9 %collective-permute-start.3 = (bf16[1,15,128,128]{3,2,1,0:T(8,128)(2,1)S(1)}, bf16[1,15,128,128]{3,2,1,0:T(8,128)(2,1)S(1)}, u32[]{:S(2)}, u32[]{:S(2)}) collective-permute-start(bf16[1,15,128,128]{3,2,1,0:T(8,128)(2,1)S(1)} %broadcast_multiply_fusion), channel_id=1, source_target_pairs={{28,0},{29,1},{30,2},{31,3},{0,4},{1,5},{2,6},{3,7},{4,8},{5,9},{6... | collective-permute-start | bytes 1474568 | tf_op jit(solution)/shard_map/ppermute | solution.py:10
  11.7 82.2 %collective-permute-start.4 = (bf16[1,15,128,128]{3,2,1,0:T(8,128)(2,1)S(1)}, bf16[1,15,128,128]{3,2,1,0:T(8,128)(2,1)S(1)}, u32[]{:S(2)}, u32[]{:S(2)}) collective-permute-start(bf16[1,15,128,128]{3,2,1,0:T(8,128)(2,1)S(1)} %broadcast_multiply_fusion), channel_id=1, source_target_pairs={{29,0},{30,1},{31,2},{0,3},{1,4},{2,5},{3,6},{4,7},{5,8},{6,9},{7,... | collective-permute-start | bytes 1474568 | tf_op jit(solution)/shard_map/ppermute | solution.py:10
  19.5 77.6 %collective-permute-start.5 = (bf16[1,15,128,128]{3,2,1,0:T(8,128)(2,1)S(1)}, bf16[1,15,128,128]{3,2,1,0:T(8,128)(2,1)S(1)}, u32[]{:S(2)}, u32[]{:S(2)}) collective-permute-start(bf16[1,15,128,128]{3,2,1,0:T(8,128)(2,1)S(1)} %broadcast_multiply_fusion), channel_id=1, source_target_pairs={{30,0},{31,1},{0,2},{1,3},{2,4},{3,5},{4,6},{5,7},{6,8},{7,9},{8,1... | collective-permute-start | bytes 1474568 | tf_op jit(solution)/shard_map/ppermute | solution.py:10
  30.1 97.8 %collective-permute-start.6 = (bf16[1,15,128,128]{3,2,1,0:T(8,128)(2,1)S(1)}, bf16[1,15,128,128]{3,2,1,0:T(8,128)(2,1)S(1)}, u32[]{:S(2)}, u32[]{:S(2)}) collective-permute-start(bf16[1,15,128,128]{3,2,1,0:T(8,128)(2,1)S(1)} %broadcast_multiply_fusion), channel_id=1, source_target_pairs={{31,0},{0,1},{1,2},{2,3},{3,4},{4,5},{5,6},{6,7},{7,8},{8,9},{9,10... | collective-permute-start | bytes 1474568 | tf_op jit(solution)/shard_map/ppermute | solution.py:10
  40.7 87.4 %collective-permute-start.7 = (bf16[1,15,128,128]{3,2,1,0:T(8,128)(2,1)S(1)}, bf16[1,15,128,128]{3,2,1,0:T(8,128)(2,1)S(1)}, u32[]{:S(2)}, u32[]{:S(2)}) collective-permute-start(bf16[1,15,128,128]{3,2,1,0:T(8,128)(2,1)S(1)} %broadcast_multiply_fusion), channel_id=1, source_target_pairs={{1,0},{2,1},{3,2},{4,3},{5,4},{6,5},{7,6},{8,7},{9,8},{10,9},{11,1... | collective-permute-start | bytes 1474568 | tf_op jit(solution)/shard_map/ppermute | solution.py:10
  93.4 34.9 %collective-permute-start.8 = (bf16[1,15,128,128]{3,2,1,0:T(8,128)(2,1)S(1)}, bf16[1,15,128,128]{3,2,1,0:T(8,128)(2,1)S(1)}, u32[]{:S(2)}, u32[]{:S(2)}) collective-permute-start(bf16[1,15,128,128]{3,2,1,0:T(8,128)(2,1)S(1)} %broadcast_multiply_fusion), channel_id=1, source_target_pairs={{2,0},{3,1},{4,2},{5,3},{6,4},{7,5},{8,6},{9,7},{10,8},{11,9},{12,... | collective-permute-start | bytes 1474568 | tf_op jit(solution)/shard_map/ppermute | solution.py:10
  93.9 37.2 %collective-permute-start.9 = (bf16[1,15,128,128]{3,2,1,0:T(8,128)(2,1)S(1)}, bf16[1,15,128,128]{3,2,1,0:T(8,128)(2,1)S(1)}, u32[]{:S(2)}, u32[]{:S(2)}) collective-permute-start(bf16[1,15,128,128]{3,2,1,0:T(8,128)(2,1)S(1)} %broadcast_multiply_fusion), channel_id=1, source_target_pairs={{3,0},{4,1},{5,2},{6,3},{7,4},{8,5},{9,6},{10,7},{11,8},{12,9},{13... | collective-permute-start | bytes 1474568 | tf_op jit(solution)/shard_map/ppermute | solution.py:10
  97.1 78.8 %collective-permute-start.10 = (bf16[1,15,128,128]{3,2,1,0:T(8,128)(2,1)S(1)}, bf16[1,15,128,128]{3,2,1,0:T(8,128)(2,1)S(1)}, u32[]{:S(2)}, u32[]{:S(2)}) collective-permute-start(bf16[1,15,128,128]{3,2,1,0:T(8,128)(2,1)S(1)} %broadcast_multiply_fusion), channel_id=1, source_target_pairs={{4,0},{5,1},{6,2},{7,3},{8,4},{9,5},{10,6},{11,7},{12,8},{13,9},{1... | collective-permute-start | bytes 1474568 | tf_op jit(solution)/shard_map/ppermute | solution.py:10
  127.8 50.0 %collective-permute-start.11 = (bf16[1,15,128,128]{3,2,1,0:T(8,128)(2,1)S(1)}, bf16[1,15,128,128]{3,2,1,0:T(8,128)(2,1)S(1)}, u32[]{:S(2)}, u32[]{:S(2)}) collective-permute-start(bf16[1,15,128,128]{3,2,1,0:T(8,128)(2,1)S(1)} %broadcast_multiply_fusion), channel_id=1, source_target_pairs={{5,0},{6,1},{7,2},{8,3},{9,4},{10,5},{11,6},{12,7},{13,8},{14,9},{... | collective-permute-start | bytes 1474568 | tf_op jit(solution)/shard_map/ppermute | solution.py:10
  128.1 50.4 %collective-permute-start.12 = (bf16[1,15,128,128]{3,2,1,0:T(8,128)(2,1)S(1)}, bf16[1,15,128,128]{3,2,1,0:T(8,128)(2,1)S(1)}, u32[]{:S(2)}, u32[]{:S(2)}) collective-permute-start(bf16[1,15,128,128]{3,2,1,0:T(8,128)(2,1)S(1)} %broadcast_multiply_fusion), channel_id=1, source_target_pairs={{6,0},{7,1},{8,2},{9,3},{10,4},{11,5},{12,6},{13,7},{14,8},{15,9},... | collective-permute-start | bytes 1474568 | tf_op jit(solution)/shard_map/ppermute | solution.py:10
  128.3 50.8 %collective-permute-start.13 = (bf16[1,15,128,128]{3,2,1,0:T(8,128)(2,1)S(1)}, bf16[1,15,128,128]{3,2,1,0:T(8,128)(2,1)S(1)}, u32[]{:S(2)}, u32[]{:S(2)}) collective-permute-start(bf16[1,15,128,128]{3,2,1,0:T(8,128)(2,1)S(1)} %broadcast_multiply_fusion), channel_id=1, source_target_pairs={{7,0},{8,1},{9,2},{10,3},{11,4},{12,5},{13,6},{14,7},{15,8},{16,9}... | collective-permute-start | bytes 1474568 | tf_op jit(solution)/shard_map/ppermute | solution.py:10
  182.9 42.4 %collective-permute-start.15 = (bf16[1,29,128,128]{3,2,1,0:T(8,128)(2,1)S(1)}, bf16[1,29,128,128]{3,2,1,0:T(8,128)(2,1)S(1)}, u32[]{:S(2)}, u32[]{:S(2)}) collective-permute-start(bf16[1,29,128,128]{3,2,1,0:T(8,128)(2,1)S(1)} %multiply_convert_fusion.1), channel_id=1, source_target_pairs={{26,0},{27,1},{28,2},{29,3},{30,4},{31,5},{0,6},{1,7},{2,8},{3,9},... | collective-permute-start | bytes 2850824 | tf_op jit(solution)/shard_map/ppermute | solution.py:10
  183.0 171.2 %collective-permute-start.18 = (bf16[1,29,128,128]{3,2,1,0:T(8,128)(2,1)S(1)}, bf16[1,29,128,128]{3,2,1,0:T(8,128)(2,1)S(1)}, u32[]{:S(2)}, u32[]{:S(2)}) collective-permute-start(bf16[1,29,128,128]{3,2,1,0:T(8,128)(2,1)S(1)} %multiply_convert_fusion.1), channel_id=1, source_target_pairs={{29,0},{30,1},{31,2},{0,3},{1,4},{2,5},{3,6},{4,7},{5,8},{6,9},{7,... | collective-permute-start | bytes 2850824 | tf_op jit(solution)/shard_map/ppermute | solution.py:10
  186.5 144.8 %collective-permute-start.17 = (bf16[1,29,128,128]{3,2,1,0:T(8,128)(2,1)S(1)}, bf16[1,29,128,128]{3,2,1,0:T(8,128)(2,1)S(1)}, u32[]{:S(2)}, u32[]{:S(2)}) collective-permute-start(bf16[1,29,128,128]{3,2,1,0:T(8,128)(2,1)S(1)} %multiply_convert_fusion.1), channel_id=1, source_target_pairs={{28,0},{29,1},{30,2},{31,3},{0,4},{1,5},{2,6},{3,7},{4,8},{5,9},{6... | collective-permute-start | bytes 2850824 | tf_op jit(solution)/shard_map/ppermute | solution.py:10
  188.7 97.2 %collective-permute-start.16 = (bf16[1,29,128,128]{3,2,1,0:T(8,128)(2,1)S(1)}, bf16[1,29,128,128]{3,2,1,0:T(8,128)(2,1)S(1)}, u32[]{:S(2)}, u32[]{:S(2)}) collective-permute-start(bf16[1,29,128,128]{3,2,1,0:T(8,128)(2,1)S(1)} %multiply_convert_fusion.1), channel_id=1, source_target_pairs={{27,0},{28,1},{29,2},{30,3},{31,4},{0,5},{1,6},{2,7},{3,8},{4,9},{... | collective-permute-start | bytes 2850824 | tf_op jit(solution)/shard_map/ppermute | solution.py:10
  207.1 149.4 %collective-permute-start.19 = (bf16[1,29,128,128]{3,2,1,0:T(8,128)(2,1)S(1)}, bf16[1,29,128,128]{3,2,1,0:T(8,128)(2,1)S(1)}, u32[]{:S(2)}, u32[]{:S(2)}) collective-permute-start(bf16[1,29,128,128]{3,2,1,0:T(8,128)(2,1)S(1)} %multiply_convert_fusion.1), channel_id=1, source_target_pairs={{30,0},{31,1},{0,2},{1,3},{2,4},{3,5},{4,6},{5,7},{6,8},{7,9},{8,1... | collective-permute-start | bytes 2850824 | tf_op jit(solution)/shard_map/ppermute | solution.py:10
  225.3 185.8 %collective-permute-start.20 = (bf16[1,29,128,128]{3,2,1,0:T(8,128)(2,1)S(1)}, bf16[1,29,128,128]{3,2,1,0:T(8,128)(2,1)S(1)}, u32[]{:S(2)}, u32[]{:S(2)}) collective-permute-start(bf16[1,29,128,128]{3,2,1,0:T(8,128)(2,1)S(1)} %multiply_convert_fusion.1), channel_id=1, source_target_pairs={{31,0},{0,1},{1,2},{2,3},{3,4},{4,5},{5,6},{6,7},{7,8},{8,9},{9,10... | collective-permute-start | bytes 2850824 | tf_op jit(solution)/shard_map/ppermute | solution.py:10
  285.9 125.5 %collective-permute-start.21 = (bf16[1,29,128,128]{3,2,1,0:T(8,128)(2,1)S(1)}, bf16[1,29,128,128]{3,2,1,0:T(8,128)(2,1)S(1)}, u32[]{:S(2)}, u32[]{:S(2)}) collective-permute-start(bf16[1,29,128,128]{3,2,1,0:T(8,128)(2,1)S(1)} %multiply_convert_fusion.1), channel_id=1, source_target_pairs={{1,0},{2,1},{3,2},{4,3},{5,4},{6,5},{7,6},{8,7},{9,8},{10,9},{11,1... | collective-permute-start | bytes 2850824 | tf_op jit(solution)/shard_map/ppermute | solution.py:10
  331.3 80.2 %collective-permute-start.22 = (bf16[1,29,128,128]{3,2,1,0:T(8,128)(2,1)S(1)}, bf16[1,29,128,128]{3,2,1,0:T(8,128)(2,1)S(1)}, u32[]{:S(2)}, u32[]{:S(2)}) collective-permute-start(bf16[1,29,128,128]{3,2,1,0:T(8,128)(2,1)S(1)} %multiply_convert_fusion.1), channel_id=1, source_target_pairs={{2,0},{3,1},{4,2},{5,3},{6,4},{7,5},{8,6},{9,7},{10,8},{11,9},{12,... | collective-permute-start | bytes 2850824 | tf_op jit(solution)/shard_map/ppermute | solution.py:10
  354.2 59.6 %collective-permute-start.23 = (bf16[1,29,128,128]{3,2,1,0:T(8,128)(2,1)S(1)}, bf16[1,29,128,128]{3,2,1,0:T(8,128)(2,1)S(1)}, u32[]{:S(2)}, u32[]{:S(2)}) collective-permute-start(bf16[1,29,128,128]{3,2,1,0:T(8,128)(2,1)S(1)} %multiply_convert_fusion.1), channel_id=1, source_target_pairs={{3,0},{4,1},{5,2},{6,3},{7,4},{8,5},{9,6},{10,7},{11,8},{12,9},{13... | collective-permute-start | bytes 2850824 | tf_op jit(solution)/shard_map/ppermute | solution.py:10
  356.6 155.9 %collective-permute-start.24 = (bf16[1,29,128,128]{3,2,1,0:T(8,128)(2,1)S(1)}, bf16[1,29,128,128]{3,2,1,0:T(8,128)(2,1)S(1)}, u32[]{:S(2)}, u32[]{:S(2)}) collective-permute-start(bf16[1,29,128,128]{3,2,1,0:T(8,128)(2,1)S(1)} %multiply_convert_fusion.1), channel_id=1, source_target_pairs={{4,0},{5,1},{6,2},{7,3},{8,4},{9,5},{10,6},{11,7},{12,8},{13,9},{1... | collective-permute-start | bytes 2850824 | tf_op jit(solution)/shard_map/ppermute | solution.py:10
  411.0 108.5 %collective-permute-start.25 = (bf16[1,29,128,128]{3,2,1,0:T(8,128)(2,1)S(1)}, bf16[1,29,128,128]{3,2,1,0:T(8,128)(2,1)S(1)}, u32[]{:S(2)}, u32[]{:S(2)}) collective-permute-start(bf16[1,29,128,128]{3,2,1,0:T(8,128)(2,1)S(1)} %multiply_convert_fusion.1), channel_id=1, source_target_pairs={{5,0},{6,1},{7,2},{8,3},{9,4},{10,5},{11,6},{12,7},{13,8},{14,9},{... | collective-permute-start | bytes 2850824 | tf_op jit(solution)/shard_map/ppermute | solution.py:10
  411.4 108.9 %collective-permute-start.26 = (bf16[1,29,128,128]{3,2,1,0:T(8,128)(2,1)S(1)}, bf16[1,29,128,128]{3,2,1,0:T(8,128)(2,1)S(1)}, u32[]{:S(2)}, u32[]{:S(2)}) collective-permute-start(bf16[1,29,128,128]{3,2,1,0:T(8,128)(2,1)S(1)} %multiply_convert_fusion.1), channel_id=1, source_target_pairs={{6,0},{7,1},{8,2},{9,3},{10,4},{11,5},{12,6},{13,7},{14,8},{15,9},... | collective-permute-start | bytes 2850824 | tf_op jit(solution)/shard_map/ppermute | solution.py:10
  411.5 109.6 %collective-permute-start.27 = (bf16[1,29,128,128]{3,2,1,0:T(8,128)(2,1)S(1)}, bf16[1,29,128,128]{3,2,1,0:T(8,128)(2,1)S(1)}, u32[]{:S(2)}, u32[]{:S(2)}) collective-permute-start(bf16[1,29,128,128]{3,2,1,0:T(8,128)(2,1)S(1)} %multiply_convert_fusion.1), channel_id=1, source_target_pairs={{7,0},{8,1},{9,2},{10,3},{11,4},{12,5},{13,6},{14,7},{15,8},{16,9}... | collective-permute-start | bytes 2850824 | tf_op jit(solution)/shard_map/ppermute | solution.py:10
  (4 other events, 97.1 us)
where the time goes:
time: 530 us
  waiting for transfers between devices  303 us (57%)
  starting transfers between devices  205 us (39%)
  matrix products  14.1 us (3%)
    ppermute x28, waiting for transfers between devices, shifted(): return lax.ppermute(block, axis, route)  303 us
    ppermute x28, starting transfers between devices, shifted(): return lax.ppermute(block, axis, route)  205 us
    dot_general x58, matrix products, band_product(): jnp.einsum('rsab,rsbc->rac', left_blocks[:, lowest:highest], pieces, pref...  14.1 us
  transfers between devices with their start and end apart: 28, of which 11 were waited for; matrix products, arithmetic and copies ran while one was open for 1% of the time, Pallas kernels for 0%

commit v1 on v0

v1 whole, which is shorter than its diff:
```python
import functools

import jax
import jax.numpy as jnp
from jax import lax
from jax.experimental import pallas as pl
from jax.experimental.pallas import tpu as pltpu
from jax.sharding import PartitionSpec as P

AXES = ("row", "col")


def window(payload, need):
    groups, width = lax.axis_size("row"), lax.axis_size("col")
    count = groups * width
    here = lax.axis_index("row") * width + lax.axis_index("col")
    steps = jnp.arange(-need, need + 1, dtype=jnp.int32)
    if count <= 2 * need + 4:
        table = lax.all_gather(payload, AXES, axis=0, tiled=False)
        return table, (here + steps) % count
    group = lax.all_gather(payload, "col", axis=0, tiled=False)
    below, above = [], []
    for hop in range(1, -(-need // width) + 1):
        part = min(width, need - (hop - 1) * width)
        up = [(g, (g + hop) % groups) for g in range(groups)]
        down = [(g, (g - hop) % groups) for g in range(groups)]
        below.insert(0, lax.ppermute(group[width - part :], "row", up))
        above.append(lax.ppermute(group[:part], "row", down))
    table = jnp.concatenate(below + [group] + above, axis=0)
    return table, lax.axis_index("col") + need + steps


def purify(reach, edge, where, keep, table, out, dense, square, own, arrived):
    near, far = reach, 2 * reach
    row_base, col_base = far + 1, far + 2
    kept_cols = 2 * far + 1

    def rows(k, n):
        return pl.ds(pl.multiple_of((k + row_base) * edge, edge), n * edge)

    def cols(c, n):
        return pl.ds(pl.multiple_of((c + col_base) * edge, edge), n * edge)

    copies = []
    for k in range(-far, far + 1):
        low = max(k - reach, -far)
        high = min(k + reach, far + 1)
        first = low - (k - reach)
        n = high - low + 1
        copies.append(
            pltpu.make_async_copy(
                table.at[where[k + far], :edge, pl.ds(first * edge, n * edge)],
                dense.at[rows(k, 1), cols(low, n)],
                arrived.at[k + far],
            )
        )
    for copy in copies:
        copy.start()
    zero = jnp.zeros((edge, edge), dense.dtype)
    for k in range(-far, far + 1):
        for c in (k - reach - 1, k + reach + 1):
            if -far - 2 <= c <= far + 1:
                dense[rows(k, 1), cols(c, 1)] = zero
    dense[rows(-far - 1, 1), :] = jnp.zeros((edge, dense.shape[1]), dense.dtype)
    for copy in copies:
        copy.wait()

    def column(index, carry):
        c = 2 * index - far
        for d in range(-far, far + 1, 2):
            r = c - d
            low = max(-reach, -d - reach)
            size = 2 * reach + 2 - abs(d)

            @pl.when((r >= -near - 1) & (r <= near - 1))
            def _():
                s = jnp.dot(
                    dense[rows(r, 2), cols(c + low, size)],
                    dense[rows(c + low, size), cols(c, 2)],
                    preferred_element_type=jnp.float32,
                )
                parts = []
                for i in range(2):
                    line = []
                    for j in range(2):
                        u = jnp.clip(c + j - r - i + far, 0, kept_cols - 1)
                        m = keep[jnp.maximum(r + i + near, 0), u]
                        line.append(s[i * edge : (i + 1) * edge, j * edge : (j + 1) * edge] * m)
                    parts.append(jnp.concatenate(line, axis=1))
                for i in range(2):
                    square[pl.ds(pl.multiple_of((r + i + near + 1) * edge, edge), edge), :] = parts[i].astype(square.dtype)

                @pl.when(r == 0)
                def _():
                    own[...] = parts[0]

        for r in range(-near - 1, near, 2):

            @pl.when((c - r > far) | (c - r < -far))
            def _():
                square[(r + near + 1) * edge : (r + near + 3) * edge, :] = jnp.zeros((2 * edge, 2 * edge), square.dtype)

        cube = jnp.dot(
            dense[rows(0, 1), cols(-near, 2 * near + 1)],
            square[edge:, :],
            preferred_element_type=jnp.float32,
        )
        value = 3.0 * own[...] - 2.0 * cube
        for j in range(2):
            u = 2 * index + j
            m = keep[near, jnp.minimum(u, kept_cols - 1)]

            @pl.when(u < kept_cols)
            def _():
                out[u] = (m * value[:, j * edge : (j + 1) * edge]).astype(out.dtype)

        return carry

    lax.fori_loop(0, far + 1, column, 0)


def shards(density, pattern, filter_mask):
    slots, edge = density.shape[1], density.shape[2]
    wide = filter_mask.shape[1]
    reach = (slots - 1) // 2
    far = 2 * reach
    masked = density[0] * pattern[0][:, None, None].astype(density.dtype)
    flat = jnp.transpose(masked, (1, 0, 2)).reshape(edge, slots * edge)
    note = jnp.zeros((16, slots * edge), density.dtype).at[0, :wide].set(filter_mask[0].astype(density.dtype))
    payload = jnp.concatenate([flat, note], axis=0)
    table, where = window(payload, far)
    keep = table[where[reach : 3 * reach + 1], edge, :wide].astype(jnp.float32)
    smem = pl.BlockSpec(memory_space=pltpu.SMEM)
    result = pl.pallas_call(
        functools.partial(purify, reach, edge),
        out_shape=jax.ShapeDtypeStruct((wide, edge, edge), density.dtype),
        in_specs=[smem, smem, pl.BlockSpec(memory_space=pl.ANY)],
        out_specs=pl.BlockSpec(memory_space=pltpu.VMEM),
        scratch_shapes=[
            pltpu.VMEM(((2 * far + 2) * edge, (2 * far + 4) * edge), density.dtype),
            pltpu.VMEM(((2 * reach + 2) * edge, 2 * edge), density.dtype),
            pltpu.VMEM((edge, 2 * edge), jnp.float32),
            pltpu.SemaphoreType.DMA((2 * far + 1,)),
        ],
        compiler_params=pltpu.CompilerParams(vmem_limit_bytes=56 * 2**20),
        cost_estimate=pl.CostEstimate(flops=16 * 10**9, bytes_accessed=14 * 2**20, transcendentals=0),
    )(where, keep, table)
    return result[None]


def solution(mesh):
    in_specs = (
        P(AXES, None, None, None),
        P(AXES, None),
        P(AXES, None),
    )
    out_specs = P(AXES, None, None, None)
    return jax.shard_map(shards, mesh=mesh, in_specs=in_specs, out_specs=out_specs, check_vma=False)
```

time: 530 us -> 240 us (0.45)
  starting transfers between devices: 205 us -> 0.01 us
  waiting for transfers between devices: 303 us -> 122 us
  local copies, waits for them, and re-layouts: 2.82 us -> 53 us
  Pallas kernels: 0 us -> 48.7 us
  matrix products: 14.1 us -> 0 us
  between operations: 1.08 us -> 13.5 us
    ppermute x28 -> x0, waiting for transfers between devices: 303 us -> none  [shifted(): return lax.ppermute(block, axis, route)]
    ppermute x28 -> x0, starting transfers between devices: 205 us -> none  [shifted(): return lax.ppermute(block, axis, route)]
    all_gather x0 -> x1, waiting for transfers between devices: none -> 122 us  [window(): table = lax.all_gather(payload, AXES, axis=0, tiled=False)]
    gather x0 -> x60, local copies, waits for them, and re-layouts: none -> 50.3 us
    pallas_call x0 -> x1, Pallas kernels: none -> 48.7 us  [shards(): pl.pallas_call(functools.partial(purify, reach, edge), out_shape=jax.Shap...]
    dot_general x58 -> x0, matrix products: 14.1 us -> none  [band_product(): jnp.einsum('rsab,rsbc->rac', left_blocks[:, lowest:highest], pieces, pref...]
  transfers between devices with their start and end apart: 28 -> 1, of which waited for: 11 -> 1; matrix products, arithmetic and copies ran while one was open for 1% -> 0% of each run, Pallas kernels for 0% -> 0%
where the time goes in v1:
time: 240 us; the launch traced here: 239 us
  waiting for transfers between devices  122 us (51%)
  local copies, waits for them, and re-layouts  53 us (22%)
  Pallas kernels  48.7 us (20%)
  between operations  13.5 us (6%)
    all_gather x1, waiting for transfers between devices, window(): table = lax.all_gather(payload, AXES, axis=0, tiled=False)  122 us
    gather x60, local copies, waits for them, and re-layouts  50.3 us
    pallas_call x1, Pallas kernels, shards(): pl.pallas_call(functools.partial(purify, reach, edge), out_shape=jax.Shap...  48.7 us
  transfers between devices with their start and end apart: 1, of which 1 were waited for; matrix products, arithmetic and copies ran while one was open for 0% of the time, Pallas kernels for 0%

profile of v1, /device:TPU:0, one launch (start us, length us, event | category | flops | bytes accessed | tf_op | source)
XLA Modules:
  0.0 239.3 jit_solution(5463515780271783472)
XLA Ops:
  6.5 0.7 convert_bitcast_fusion
  7.2 0.7 convert_element_type.20
  8.0 1.3 copy.10
  9.5 1.1 copy.12
  11.0 121.8 %all-gather.3.cloned.1.call-done = bf16[4608,1920]{1,0:T(8,128)(2,1)} async-done(((bf16[144,1920]{1,0:T(8,128)(2,1)}), bf16[4608,1920]{1,0:T(8,128)(2,1)}) %all-gather.3.cloned.1.call-update) | async-done | bytes 17694736 | tf_op jit(solution)/shard_map/all_gather | solution.py:19
  132.8 50.4 %while.2 = (s32[]{:T(128)}, bf16[32,144,1920]{2,1,0:T(8,128)(2,1)}, s32[15,3]{0,1:T(4,128)S(1)}, bf16[15,29]{1,0:T(8,128)(2,1)S(1)}, s32[]{:T(128)}, /*index=5*/s32[]{:T(128)}) while((s32[]{:T(128)}, bf16[32,144,1920]{2,1,0:T(8,128)(2,1)}, s32[15,3]{0,1:T(4,128)S(1)}, bf16[15,29]{1,0:T(8,128)(2,1)S(1)}, s32[]{:T(128)}, /*index=5*/s32[]{:T(128)}) %tuple.29), condition=%wide.while_cond.1, body=%wide.while_body.1.sunk | while | flops 2 | bytes 377 | solution.py:132
  133.4 2.7 %dynamic-slice_bitcast_fusion.2 = bf16[1,29]{1,0:T(2,128)(2,1)S(1)} fusion(bf16[32,144,1920]{2,1,0:T(8,128)(2,1)} %get-tuple-element.80, s32[]{:T(128)} %bitcast.23, s32[]{:T(128)} %bitcast.24, s32[]{:T(128)} %bitcast.25), kind=kLoop, calls=%fused_computation.clone.1 | loop fusion | bytes 128 | tf_op jit(solution)/shard_map/gather
  136.2 0.6 fusion.6
  136.8 2.7 %dynamic-slice_bitcast_fusion.2 = bf16[1,29]{1,0:T(2,128)(2,1)S(1)} fusion(bf16[32,144,1920]{2,1,0:T(8,128)(2,1)} %get-tuple-element.80, s32[]{:T(128)} %bitcast.23, s32[]{:T(128)} %bitcast.24, s32[]{:T(128)} %bitcast.25), kind=kLoop, calls=%fused_computation.clone.1 | loop fusion | bytes 128 | tf_op jit(solution)/shard_map/gather
  139.6 0.6 fusion.6
  140.2 2.7 %dynamic-slice_bitcast_fusion.2 = bf16[1,29]{1,0:T(2,128)(2,1)S(1)} fusion(bf16[32,144,1920]{2,1,0:T(8,128)(2,1)} %get-tuple-element.80, s32[]{:T(128)} %bitcast.23, s32[]{:T(128)} %bitcast.24, s32[]{:T(128)} %bitcast.25), kind=kLoop, calls=%fused_computation.clone.1 | loop fusion | bytes 128 | tf_op jit(solution)/shard_map/gather
  143.5 2.7 %dynamic-slice_bitcast_fusion.2 = bf16[1,29]{1,0:T(2,128)(2,1)S(1)} fusion(bf16[32,144,1920]{2,1,0:T(8,128)(2,1)} %get-tuple-element.80, s32[]{:T(128)} %bitcast.23, s32[]{:T(128)} %bitcast.24, s32[]{:T(128)} %bitcast.25), kind=kLoop, calls=%fused_computation.clone.1 | loop fusion | bytes 128 | tf_op jit(solution)/shard_map/gather
  146.9 2.6 %dynamic-slice_bitcast_fusion.2 = bf16[1,29]{1,0:T(2,128)(2,1)S(1)} fusion(bf16[32,144,1920]{2,1,0:T(8,128)(2,1)} %get-tuple-element.80, s32[]{:T(128)} %bitcast.23, s32[]{:T(128)} %bitcast.24, s32[]{:T(128)} %bitcast.25), kind=kLoop, calls=%fused_computation.clone.1 | loop fusion | bytes 128 | tf_op jit(solution)/shard_map/gather
  150.2 2.7 %dynamic-slice_bitcast_fusion.2 = bf16[1,29]{1,0:T(2,128)(2,1)S(1)} fusion(bf16[32,144,1920]{2,1,0:T(8,128)(2,1)} %get-tuple-element.80, s32[]{:T(128)} %bitcast.23, s32[]{:T(128)} %bitcast.24, s32[]{:T(128)} %bitcast.25), kind=kLoop, calls=%fused_computation.clone.1 | loop fusion | bytes 128 | tf_op jit(solution)/shard_map/gather
  153.6 2.7 %dynamic-slice_bitcast_fusion.2 = bf16[1,29]{1,0:T(2,128)(2,1)S(1)} fusion(bf16[32,144,1920]{2,1,0:T(8,128)(2,1)} %get-tuple-element.80, s32[]{:T(128)} %bitcast.23, s32[]{:T(128)} %bitcast.24, s32[]{:T(128)} %bitcast.25), kind=kLoop, calls=%fused_computation.clone.1 | loop fusion | bytes 128 | tf_op jit(solution)/shard_map/gather
  156.9 2.7 %dynamic-slice_bitcast_fusion.2 = bf16[1,29]{1,0:T(2,128)(2,1)S(1)} fusion(bf16[32,144,1920]{2,1,0:T(8,128)(2,1)} %get-tuple-element.80, s32[]{:T(128)} %bitcast.23, s32[]{:T(128)} %bitcast.24, s32[]{:T(128)} %bitcast.25), kind=kLoop, calls=%fused_computation.clone.1 | loop fusion | bytes 128 | tf_op jit(solution)/shard_map/gather
  160.3 2.7 %dynamic-slice_bitcast_fusion.2 = bf16[1,29]{1,0:T(2,128)(2,1)S(1)} fusion(bf16[32,144,1920]{2,1,0:T(8,128)(2,1)} %get-tuple-element.80, s32[]{:T(128)} %bitcast.23, s32[]{:T(128)} %bitcast.24, s32[]{:T(128)} %bitcast.25), kind=kLoop, calls=%fused_computation.clone.1 | loop fusion | bytes 128 | tf_op jit(solution)/shard_map/gather
  163.7 2.7 %dynamic-slice_bitcast_fusion.2 = bf16[1,29]{1,0:T(2,128)(2,1)S(1)} fusion(bf16[32,144,1920]{2,1,0:T(8,128)(2,1)} %get-tuple-element.80, s32[]{:T(128)} %bitcast.23, s32[]{:T(128)} %bitcast.24, s32[]{:T(128)} %bitcast.25), kind=kLoop, calls=%fused_computation.clone.1 | loop fusion | bytes 128 | tf_op jit(solution)/shard_map/gather
  167.0 2.7 %dynamic-slice_bitcast_fusion.2 = bf16[1,29]{1,0:T(2,128)(2,1)S(1)} fusion(bf16[32,144,1920]{2,1,0:T(8,128)(2,1)} %get-tuple-element.80, s32[]{:T(128)} %bitcast.23, s32[]{:T(128)} %bitcast.24, s32[]{:T(128)} %bitcast.25), kind=kLoop, calls=%fused_computation.clone.1 | loop fusion | bytes 128 | tf_op jit(solution)/shard_map/gather
  170.4 2.7 %dynamic-slice_bitcast_fusion.2 = bf16[1,29]{1,0:T(2,128)(2,1)S(1)} fusion(bf16[32,144,1920]{2,1,0:T(8,128)(2,1)} %get-tuple-element.80, s32[]{:T(128)} %bitcast.23, s32[]{:T(128)} %bitcast.24, s32[]{:T(128)} %bitcast.25), kind=kLoop, calls=%fused_computation.clone.1 | loop fusion | bytes 128 | tf_op jit(solution)/shard_map/gather
  173.8 2.6 %dynamic-slice_bitcast_fusion.2 = bf16[1,29]{1,0:T(2,128)(2,1)S(1)} fusion(bf16[32,144,1920]{2,1,0:T(8,128)(2,1)} %get-tuple-element.80, s32[]{:T(128)} %bitcast.23, s32[]{:T(128)} %bitcast.24, s32[]{:T(128)} %bitcast.25), kind=kLoop, calls=%fused_computation.clone.1 | loop fusion | bytes 128 | tf_op jit(solution)/shard_map/gather
  177.1 2.6 %dynamic-slice_bitcast_fusion.2 = bf16[1,29]{1,0:T(2,128)(2,1)S(1)} fusion(bf16[32,144,1920]{2,1,0:T(8,128)(2,1)} %get-tuple-element.80, s32[]{:T(128)} %bitcast.23, s32[]{:T(128)} %bitcast.24, s32[]{:T(128)} %bitcast.25), kind=kLoop, calls=%fused_computation.clone.1 | loop fusion | bytes 128 | tf_op jit(solution)/shard_map/gather
  180.5 2.7 %dynamic-slice_bitcast_fusion.2 = bf16[1,29]{1,0:T(2,128)(2,1)S(1)} fusion(bf16[32,144,1920]{2,1,0:T(8,128)(2,1)} %get-tuple-element.80, s32[]{:T(128)} %bitcast.23, s32[]{:T(128)} %bitcast.24, s32[]{:T(128)} %bitcast.25), kind=kLoop, calls=%fused_computation.clone.1 | loop fusion | bytes 128 | tf_op jit(solution)/shard_map/gather
  183.7 48.7 %shard_map.37 = bf16[29,128,128]{2,1,0:T(8,128)(2,1)} custom-call(s32[29]{0:T(128)} %copy-done, f32[15,29]{1,0:T(8,128)} %convert_element_type.21.keep, bf16[32,144,1920]{2,1,0:T(8,128)(2,1)} %get-tuple-element.89), custom_call_target="tpu_custom_call" | custom-call | flops 16000000000 | bytes 14680064 | tf_op jit(solution)/shard_map/pallas_call | solution.py:134
  (57 shorter events, 10.6 us)
Async XLA Ops:
  6.5 126.2 %all-gather.3.cloned.1.call-start = ((), (), s32[]{:S(2)}) async-start(), calls=%async_computation | async-start | bytes 18247680 | tf_op jit(solution)/shard_map/all_gather | solution.py:19
  10.8 172.9 %copy-start = (s32[29]{0:T(128)}, s32[29]{0:T(128)S(1)}, u32[]{:S(2)}) copy-start(s32[29]{0:T(128)S(1)} %and_select_fusion.where) | copy-start | bytes 352
Sparse Core Ops, SparseCore 0:
  10.7 121.9 all-gather.2

commit v2 on v0

v2 whole, which is shorter than its diff:
```python
import functools

import jax
import jax.numpy as jnp
from jax import lax
from jax.experimental import pallas as pl
from jax.experimental.pallas import tpu as pltpu
from jax.sharding import Mesh, PartitionSpec as P

NOTE = 16
CORES = 2


def window(payload, need):
    width = lax.axis_size("col")
    groups = lax.axis_size("y") * CORES
    count = groups * width
    core, column = lax.axis_index("core"), lax.axis_index("col")
    group = lax.axis_index("y") * CORES + core
    steps = jnp.arange(-need, need + 1, dtype=jnp.int32)
    if count <= 2 * need + 4:
        mine = lax.all_gather(payload, ("y", "col"), axis=0, tiled=False)
        other = lax.ppermute(mine, "core", [(0, 1), (1, 0)])
        row = (group * width + column + steps) % count
        far_group = row // width
        return (mine, other), (far_group % CORES != core).astype(jnp.int32), far_group // CORES * width + row % width
    block = lax.all_gather(payload, "col", axis=0, tiled=False)
    below, above = [], []
    for hop in range(1, -(-need // width) + 1):
        part = min(width, need - (hop - 1) * width)
        up = [(g, (g + hop) % groups) for g in range(groups)]
        down = [(g, (g - hop) % groups) for g in range(groups)]
        below.insert(0, lax.ppermute(block[width - part :], ("y", "core"), up))
        above.append(lax.ppermute(block[:part], ("y", "core"), down))
    tables = below + [block] + above
    place, which, start = column + need + steps, jnp.zeros_like(steps), jnp.zeros_like(steps)
    edge = 0
    for t, table in enumerate(tables):
        which, start = jnp.where(place >= edge, t, which), jnp.where(place >= edge, edge, start)
        edge += table.shape[0]
    return tuple(tables), which, place - start


def purify(reach, edge, count, which, where, *refs):
    tables, (out, band, square, own, notes, keep, arrived, noted) = refs[:count], refs[count:]
    far = 2 * reach
    slots, wide = 2 * reach + 1, 4 * reach + 1
    kind = band.dtype

    def span(first, n):
        first = first * edge
        return pl.ds(first if isinstance(first, int) else pl.multiple_of(first, edge), n * edge)

    def fetch(k, carry):
        for t, table in enumerate(tables):

            @pl.when(which[k] == t)
            def _():
                for s in range(slots):
                    pltpu.make_async_copy(
                        table.at[where[k], pl.ds(s * edge, edge)],
                        band.at[span(k, 1), pl.ds((s + 1) * edge, edge)],
                        arrived.at[k],
                    ).start()

                @pl.when((k >= reach) & (k <= 3 * reach))
                def _():
                    pltpu.make_async_copy(
                        table.at[where[k], pl.ds(slots * edge, NOTE)], notes.at[k - reach], noted
                    ).start()

        return carry

    lax.fori_loop(0, 2 * far + 1, fetch, 0)

    def ready(k):
        whole = tables[0].at[0, pl.ds(0, slots * edge)]
        pltpu.make_async_copy(whole, band.at[pl.ds(0, slots * edge), pl.ds(0, edge)], arrived.at[k]).wait()

    def clear(k, carry):
        zero = jnp.zeros((edge, edge), kind)
        band[span(k, 1), pl.ds(0, edge)] = zero
        band[span(k, 1), pl.ds((slots + 1) * edge, edge)] = zero
        return carry

    lax.fori_loop(0, 2 * far + 2, clear, 0)
    band[span(2 * far + 1, 1), :] = jnp.zeros((edge, band.shape[1]), kind)

    def clear_square(r, carry):
        zero = jnp.zeros((edge, edge), kind)
        square[span(r, 1), pl.ds(0, edge)] = zero
        square[span(r, 1), pl.ds((wide + 1) * edge, edge)] = zero
        return carry

    lax.fori_loop(0, slots + 1, clear_square, 0)

    for r in range(slots):
        pltpu.make_async_copy(tables[0].at[0, pl.ds(0, NOTE)], notes.at[r], noted).wait()
    notes[slots] = jnp.zeros(notes.shape[1:], kind)
    spots = keep.shape[1]
    diagonal = lax.broadcasted_iota(jnp.int32, (spots, edge), 0) == lax.broadcasted_iota(jnp.int32, (spots, edge), 1)

    def spread(r, carry):
        line = notes[r].astype(jnp.float32)[:1]
        value = jnp.sum(jnp.where(diagonal, line, 0.0), axis=1, keepdims=True)
        keep[r] = jnp.broadcast_to(value, (spots, edge))
        return carry

    lax.fori_loop(0, slots + 1, spread, 0)

    for k in range(far):
        ready(k)

    def row_pair(pair, carry):
        r = 2 * pair
        ready(r + far)

        @pl.when(r + far + 1 <= 2 * far)
        def _():
            ready(r + far + 1)

        middle = jnp.where((r == reach) | (r + 1 == reach), 1, 0)
        for d in range(-far, far + 1, 2):
            low, high = max(-reach, d - reach), min(reach + 1, d + reach + 1)
            size = high - low + 1
            left = jnp.concatenate(
                [
                    band[span(r + reach, 1), pl.ds((low + reach + 1) * edge, size * edge)],
                    band[span(r + reach + 1, 1), pl.ds((low + reach) * edge, size * edge)],
                ],
                axis=0,
            )
            right = jnp.concatenate(
                [
                    band[span(r + reach + e, 1), pl.ds((d - e + reach + 1) * edge, 2 * edge)]
                    for e in range(low, high + 1)
                ],
                axis=0,
            )
            product = jnp.dot(left, right, preferred_element_type=jnp.float32)
            for i in range(2):
                u = d + far - i
                mask = jnp.concatenate(
                    [keep[r + i, pl.ds(min(max(u + j, 0), wide - 1), 1), :] for j in range(2)], axis=1
                )
                kept = product[i * edge : (i + 1) * edge] * mask
                square[span(r + i, 1), pl.ds((u + 1) * edge, 2 * edge)] = kept.astype(kind)
                if i == reach % 2:
                    own[middle, :, pl.ds((u + 1) * edge, 2 * edge)] = kept
        return carry

    lax.fori_loop(0, (slots + 1) // 2, row_pair, 0)

    for c in range(-far, far + 1, 2):
        low, high = max(-reach, c - far), min(reach, c + far + 1)
        left = band[span(far, 1), pl.ds((low + reach + 1) * edge, (high - low + 1) * edge)]
        right = jnp.concatenate(
            [square[span(r + reach, 1), pl.ds((c - r + far + 1) * edge, 2 * edge)] for r in range(low, high + 1)],
            axis=0,
        )
        cube = jnp.dot(left, right, preferred_element_type=jnp.float32)
        for j in range(2):
            u = c + far + j
            if u < wide:
                kept = own[1, :, pl.ds((u + 1) * edge, edge)]
                value = 3.0 * kept - 2.0 * cube[:, j * edge : (j + 1) * edge]
                out[u] = (keep[reach, pl.ds(u, 1), :] * value).astype(out.dtype)


def shards(density, pattern, filter_mask):
    slots, edge = density.shape[1], density.shape[2]
    wide = filter_mask.shape[1]
    reach = (slots - 1) // 2
    far = 2 * reach
    masked = density[0] * pattern[0][:, None, None].astype(density.dtype)
    note = jnp.zeros((NOTE, edge), density.dtype).at[0, :wide].set(filter_mask[0].astype(density.dtype))
    payload = jnp.concatenate([masked.reshape(slots * edge, edge), note], axis=0)
    tables, which, where = window(payload, far)
    smem = pl.BlockSpec(memory_space=pltpu.SMEM)
    result = pl.pallas_call(
        functools.partial(purify, reach, edge, len(tables)),
        out_shape=jax.ShapeDtypeStruct((wide, edge, edge), density.dtype),
        in_specs=[smem, smem] + [pl.BlockSpec(memory_space=pl.ANY)] * len(tables),
        out_specs=pl.BlockSpec(memory_space=pltpu.VMEM),
        scratch_shapes=[
            pltpu.VMEM(((2 * far + 2) * edge, (slots + 2) * edge), density.dtype),
            pltpu.VMEM(((slots + 1) * edge, (wide + 2) * edge), density.dtype),
            pltpu.VMEM((2, edge, (wide + 2) * edge), jnp.float32),
            pltpu.VMEM((slots + 1, NOTE, edge), density.dtype),
            pltpu.VMEM((slots + 1, -(-wide // 8) * 8, edge), jnp.float32),
            pltpu.SemaphoreType.DMA((2 * far + 1,)),
            pltpu.SemaphoreType.DMA,
        ],
        compiler_params=pltpu.CompilerParams(vmem_limit_bytes=56 * 2**20),
        cost_estimate=pl.CostEstimate(flops=17 * 10**9, bytes_accessed=15 * 2**20, transcendentals=0),
    )(which, where, *tables)
    return result[None]


def solution(mesh):
    groups, width = mesh.devices.shape
    devices = Mesh(mesh.devices.reshape(groups // CORES, CORES, width), ("y", "core", "col"))
    axes = ("y", "core", "col")
    in_specs = (P(axes, None, None, None), P(axes, None), P(axes, None))
    out_specs = P(axes, None, None, None)
    return jax.shard_map(shards, mesh=devices, in_specs=in_specs, out_specs=out_specs, check_vma=False)
```

time: 530 us -> 170 us (0.32)
  starting transfers between devices: 205 us -> 0.01 us
  waiting for transfers between devices: 303 us -> 123 us
  Pallas kernels: 0 us -> 28 us
  matrix products: 14.1 us -> 0 us
  between operations: 1.08 us -> 13.4 us
    ppermute x28 -> x1, waiting for transfers between devices: 303 us -> 11.8 us  [window(): other = lax.ppermute(mine, 'core', [(0, 1), (1, 0)])]
    ppermute x28 -> x1, starting transfers between devices: 205 us -> 0.01 us  [window(): other = lax.ppermute(mine, 'core', [(0, 1), (1, 0)])]
    all_gather x0 -> x1, waiting for transfers between devices: none -> 112 us  [window(): mine = lax.all_gather(payload, ('y', 'col'), axis=0, tiled=False)]
    pallas_call x0 -> x1, Pallas kernels: none -> 28 us  [shards(): pl.pallas_call(functools.partial(purify, reach, edge, len(tables)), out_s...]
    dot_general x58 -> x0, matrix products: 14.1 us -> none  [band_product(): jnp.einsum('rsab,rsbc->rac', left_blocks[:, lowest:highest], pieces, pref...]
  transfers between devices with their start and end apart: 28 -> 2, of which waited for: 11 -> 2; matrix products, arithmetic and copies ran while one was open for 1% -> 1% of each run, Pallas kernels for 0% -> 0%
where the time goes in v2:
time: 170 us; the launch traced here: 169 us
  waiting for transfers between devices  123 us (72%)
  Pallas kernels  28 us (16%)
  between operations  13.4 us (8%)
  other arithmetic  4.57 us (3%)
    all_gather x1, waiting for transfers between devices, window(): mine = lax.all_gather(payload, ('y', 'col'), axis=0, tiled=False)  112 us
    pallas_call x1, Pallas kernels, shards(): pl.pallas_call(functools.partial(purify, reach, edge, len(tables)), out_s...  28 us
    ppermute x1, waiting for transfers between devices, window(): other = lax.ppermute(mine, 'core', [(0, 1), (1, 0)])  11.8 us
  transfers between devices with their start and end apart: 2, of which 2 were waited for; matrix products, arithmetic and copies ran while one was open for 1% of the time, Pallas kernels for 0%

profile of v2, /device:TPU:0, one launch (start us, length us, event | category | flops | bytes accessed | tf_op | source)
XLA Modules:
  0.0 169.3 jit_solution(8357893497186919983)
XLA Ops:
  6.5 0.0 all-gather.3.cloned.1.call-start
  6.5 0.7 convert_bitcast_fusion
  7.2 0.7 convert_element_type.21
  7.9 0.1 broadcast_bitcast_fusion
  7.9 1.3 bitcast_multiply_fusion
  9.3 0.8 fusion.1
  10.1 0.0 all-gather.3.cloned.1.call-update
  10.1 111.5 %all-gather.3.cloned.1.call-done = bf16[30976,128]{1,0:T(8,128)(2,1)} async-done(((bf16[1936,128]{1,0:T(8,128)(2,1)}), bf16[30976,128]{1,0:T(8,128)(2,1)}) %all-gather.3.cloned.1.call-update) | async-done | bytes 7929872 | tf_op jit(solution)/shard_map/all_gather | solution.py:22
  121.6 0.0 collective-permute-start
  121.6 0.5 compare_convert_fusion.which
  122.2 0.5 fusion.2.where
  122.7 11.8 %collective-permute-done.refs_1_ = bf16[16,1936,128]{2,1,0:T(8,128)(2,1)} collective-permute-done((bf16[16,1936,128]{2,1,0:T(8,128)(2,1)}, bf16[16,1936,128]{2,1,0:T(8,128)(2,1)}, u32[]{:S(2)}, u32[]{:S(2)}) %collective-permute-start) | collective-permute-done | bytes 7929888 | tf_op jit(solution)/shard_map/ppermute | solution.py:23
  134.5 28.0 %shard_map.37 = bf16[29,128,128]{2,1,0:T(8,128)(2,1)} custom-call(s32[29]{0:T(128)} %compare_convert_fusion.which, s32[29]{0:T(128)} %fusion.2.where, bf16[16,1936,128]{2,1,0:T(8,128)(2,1)} %bitcast.9, bf16[16,1936,128]{2,1,0:T(8,128)(2,1)} %collective-permute-done.refs_1_), custom_call_target="tpu_custom_call" | custom-call | flops 16999999488 | bytes 15728640 | tf_op jit(solution)/shard_map/pallas_call | solution.py:180
Async XLA Ops:
  6.5 115.1 %all-gather.3.cloned.1.call-start = ((), (), s32[]{:S(2)}) async-start(), calls=%async_computation | async-start | bytes 8425472 | tf_op jit(solution)/shard_map/all_gather | solution.py:22
  121.6 12.8 %collective-permute-start = (bf16[16,1936,128]{2,1,0:T(8,128)(2,1)}, bf16[16,1936,128]{2,1,0:T(8,128)(2,1)}, u32[]{:S(2)}, u32[]{:S(2)}) collective-permute-start(bf16[16,1936,128]{2,1,0:T(8,128)(2,1)} %bitcast.8), channel_id=1, source_target_pairs={{0,8},{8,0},{1,9},{9,1},{2,10},{10,2},{3,11},{11,3},{4,12},{12,4},... | collective-permute-start | bytes 23789576 | tf_op jit(solution)/shard_map/ppermute | solution.py:23
Sparse Core Ops, SparseCore 0:
  10.2 111.3 all-gather.2

commit v3 on v2

--- a/solution.py
+++ b/solution.py
@@ -5,76 +5,114 @@
 from jax import lax
 from jax.experimental import pallas as pl
 from jax.experimental.pallas import tpu as pltpu
-from jax.sharding import Mesh, PartitionSpec as P
+from jax.sharding import PartitionSpec as P
 
 NOTE = 16
-CORES = 2
-
-
-def window(payload, need):
-    width = lax.axis_size("col")
-    groups = lax.axis_size("y") * CORES
+AXES = ("row", "col")
+
+
+def cube(payload, count, half):
+    def swap(value, mask):
+        return lax.ppermute(value, AXES, [(i, i ^ mask) for i in range(count)])
+
+    x, core, y = 1, 8, 16
+    rows = {0: [payload]}
+    for z in (2, 4, 6):
+        rows[z] = [swap(payload, z)]
+    for z in (0, 2, 4, 6):
+        rows[z | x] = [swap(rows[z][0], x)]
+        rows[z | y] = [swap(rows[z][0], y)]
+        if z == 2:
+            continue
+        rows[z | x | y] = [swap(rows[z | y][0][:half], x), swap(rows[z | x][0][half:], y)]
+        if z == 0:
+            rows[2 | x | y] = [swap(piece, 2) for piece in rows[x | y]]
+    for mask in list(rows):
+        rows[mask | core] = [swap(piece, core) for piece in rows[mask]]
+    return rows
+
+
+def window(payload, need, half):
+    groups, width = lax.axis_size("row"), lax.axis_size("col")
     count = groups * width
-    core, column = lax.axis_index("core"), lax.axis_index("col")
-    group = lax.axis_index("y") * CORES + core
-    steps = jnp.arange(-need, need + 1, dtype=jnp.int32)
-    if count <= 2 * need + 4:
-        mine = lax.all_gather(payload, ("y", "col"), axis=0, tiled=False)
-        other = lax.ppermute(mine, "core", [(0, 1), (1, 0)])
-        row = (group * width + column + steps) % count
-        far_group = row // width
-        return (mine, other), (far_group % CORES != core).astype(jnp.int32), far_group // CORES * width + row % width
-    block = lax.all_gather(payload, "col", axis=0, tiled=False)
-    below, above = [], []
-    for hop in range(1, -(-need // width) + 1):
-        part = min(width, need - (hop - 1) * width)
-        up = [(g, (g + hop) % groups) for g in range(groups)]
-        down = [(g, (g - hop) % groups) for g in range(groups)]
-        below.insert(0, lax.ppermute(block[width - part :], ("y", "core"), up))
-        above.append(lax.ppermute(block[:part], ("y", "core"), down))
-    tables = below + [block] + above
-    place, which, start = column + need + steps, jnp.zeros_like(steps), jnp.zeros_like(steps)
-    edge = 0
-    for t, table in enumerate(tables):
-        which, start = jnp.where(place >= edge, t, which), jnp.where(place >= edge, edge, start)
-        edge += table.shape[0]
-    return tuple(tables), which, place - start
-
-
-def purify(reach, edge, count, which, where, *refs):
+    size = payload.shape[0]
+    column = lax.axis_index("col")
+    here = lax.axis_index("row") * width + column
+    pieces, offsets = [], []
+    if (groups, width) == (4, 8):
+        for mask, arrays in sorted(cube(payload, count, half).items()):
+            start = 0
+            for array in arrays:
+                pieces.append((array, 1, start))
+                offsets.append((((here ^ mask) - here + count // 2) % count - count // 2)[None])
+                start += array.shape[0]
+    else:
+        block = lax.all_gather(payload, "col", axis=0, tiled=True)
+        pieces.append((block, width, 0))
+        offsets.append(jnp.arange(width, dtype=jnp.int32) - column)
+        for hop in range(1, -(-need // width) + 1):
+            part = min(width, need - (hop - 1) * width)
+            up = [(g, (g + hop) % groups) for g in range(groups)]
+            down = [(g, (g - hop) % groups) for g in range(groups)]
+            steps = jnp.arange(part, dtype=jnp.int32) - column
+            pieces.append((lax.ppermute(block[(width - part) * size :], "row", up), part, 0))
+            offsets.append(steps - (hop - 1) * width - part)
+            pieces.append((lax.ppermute(block[: part * size], "row", down), part, 0))
+            offsets.append(steps + hop * width)
+    offsets = jnp.concatenate(offsets).astype(jnp.int32)
+    return pieces, jnp.where(jnp.abs(offsets) <= need, offsets + need, -1)
+
+
+def purify(reach, edge, layout, place, *refs):
+    count = len(layout)
     tables, (out, band, square, own, notes, keep, arrived, noted) = refs[:count], refs[count:]
     far = 2 * reach
     slots, wide = 2 * reach + 1, 4 * reach + 1
     kind = band.dtype
+    size = slots * edge + NOTE
 
     def span(first, n):
         first = first * edge
         return pl.ds(first if isinstance(first, int) else pl.multiple_of(first, edge), n * edge)
 
-    def fetch(k, carry):
-        for t, table in enumerate(tables):
-
-            @pl.when(which[k] == t)
+    base = 0
+    for table, (number, start) in zip(tables, layout):
+        held = table.shape[0] // number
+        first, last = start // edge, min((start + held) // edge, slots)
+
+        def fetch(j, carry, table=table, base=base, start=start, held=held, first=first, last=last):
+            k = place[base + j]
+            begin = j * held - start
+
+            @pl.when(k >= 0)
             def _():
-                for s in range(slots):
+                def block(s, carry):
                     pltpu.make_async_copy(
-                        table.at[where[k], pl.ds(s * edge, edge)],
-                        band.at[span(k, 1), pl.ds((s + 1) * edge, edge)],
+                        table.at[pl.ds(pl.multiple_of(begin + s * edge, 16), edge)],
+                        band.at[span(k, 1), span(s + 1, 1)],
                         arrived.at[k],
                     ).start()
-
-                @pl.when((k >= reach) & (k <= 3 * reach))
-                def _():
-                    pltpu.make_async_copy(
-                        table.at[where[k], pl.ds(slots * edge, NOTE)], notes.at[k - reach], noted
-                    ).start()
-
-        return carry
-
-    lax.fori_loop(0, 2 * far + 1, fetch, 0)
+                    return carry
+
+                lax.fori_loop(first, last, block, 0)
+
+                if start + held == size:
+
+                    @pl.when((k >= reach) & (k <= 3 * reach))
+                    def _():
+                        pltpu.make_async_copy(
+                            table.at[pl.ds(pl.multiple_of(begin + slots * edge, 16), NOTE)],
+                            notes.at[k - reach],
+                            noted,
+                        ).start()
+
+            return carry
+
+        lax.fori_loop(0, number, fetch, 0)
+        base += number
 
     def ready(k):
-        whole = tables[0].at[0, pl.ds(0, slots * edge)]
+        whole = tables[0].at[pl.ds(0, slots * edge)]
         pltpu.make_async_copy(whole, band.at[pl.ds(0, slots * edge), pl.ds(0, edge)], arrived.at[k]).wait()
 
     def clear(k, carry):
@@ -95,7 +133,7 @@
     lax.fori_loop(0, slots + 1, clear_square, 0)
 
     for r in range(slots):
-        pltpu.make_async_copy(tables[0].at[0, pl.ds(0, NOTE)], notes.at[r], noted).wait()
+        pltpu.make_async_copy(tables[0].at[pl.ds(0, NOTE)], notes.at[r], noted).wait()
     notes[slots] = jnp.zeros(notes.shape[1:], kind)
     spots = keep.shape[1]
     diagonal = lax.broadcasted_iota(jnp.int32, (spots, edge), 0) == lax.broadcasted_iota(jnp.int32, (spots, edge), 1)
@@ -175,12 +213,15 @@
     masked = density[0] * pattern[0][:, None, None].astype(density.dtype)
     note = jnp.zeros((NOTE, edge), density.dtype).at[0, :wide].set(filter_mask[0].astype(density.dtype))
     payload = jnp.concatenate([masked.reshape(slots * edge, edge), note], axis=0)
-    tables, which, where = window(payload, far)
+    half = -(-slots // 2) * edge
+    pieces, place = window(payload, far, half)
+    tables = [array for array, _, _ in pieces]
+    layout = [(number, start) for _, number, start in pieces]
     smem = pl.BlockSpec(memory_space=pltpu.SMEM)
     result = pl.pallas_call(
-        functools.partial(purify, reach, edge, len(tables)),
+        functools.partial(purify, reach, edge, layout),
         out_shape=jax.ShapeDtypeStruct((wide, edge, edge), density.dtype),
-        in_specs=[smem, smem] + [pl.BlockSpec(memory_space=pl.ANY)] * len(tables),
+        in_specs=[smem] + [pl.BlockSpec(memory_space=pl.ANY)] * len(tables),
         out_specs=pl.BlockSpec(memory_space=pltpu.VMEM),
         scratch_shapes=[
             pltpu.VMEM(((2 * far + 2) * edge, (slots + 2) * edge), density.dtype),
@@ -193,14 +234,11 @@
         ],
         compiler_params=pltpu.CompilerParams(vmem_limit_bytes=56 * 2**20),
         cost_estimate=pl.CostEstimate(flops=17 * 10**9, bytes_accessed=15 * 2**20, transcendentals=0),
-    )(which, where, *tables)
+    )(place, *tables)
     return result[None]
 
 
 def solution(mesh):
-    groups, width = mesh.devices.shape
-    devices = Mesh(mesh.devices.reshape(groups // CORES, CORES, width), ("y", "core", "col"))
-    axes = ("y", "core", "col")
-    in_specs = (P(axes, None, None, None), P(axes, None), P(axes, None))
-    out_specs = P(axes, None, None, None)
-    return jax.shard_map(shards, mesh=devices, in_specs=in_specs, out_specs=out_specs, check_vma=False)
+    in_specs = (P(AXES, None, None, None), P(AXES, None), P(AXES, None))
+    out_specs = P(AXES, None, None, None)
+    return jax.shard_map(shards, mesh=mesh, in_specs=in_specs, out_specs=out_specs, check_vma=False)

time: 170 us -> 142 us (0.84)
  waiting for transfers between devices: 123 us -> 80.4 us
  starting transfers between devices: 0.01 us -> 24.2 us
  between operations: 13.4 us -> 0.78 us
  local copies, waits for them, and re-layouts: 0.07 us -> 3.64 us
  other arithmetic: 4.57 us -> 2.6 us
  Pallas kernels: 28 us -> 29.8 us
    all_gather x1 -> x0, waiting for transfers between devices: 112 us -> none  [window(): mine = lax.all_gather(payload, ('y', 'col'), axis=0, tiled=False)]
    ppermute x1 -> x39, waiting for transfers between devices: 11.8 us -> 80.4 us  [swap(): return lax.ppermute(value, AXES, [(i, i ^ mask) for i in range(count)])]
    ppermute x1 -> x39, starting transfers between devices: 0.01 us -> 24.2 us  [swap(): return lax.ppermute(value, AXES, [(i, i ^ mask) for i in range(count)])]
    unnamed x0 -> x68, local copies, waits for them, and re-layouts: none -> 3.35 us
    pallas_call x1, Pallas kernels: 28 us -> 29.8 us  [shards(): pl.pallas_call(functools.partial(purify, reach, edge, layout), out_shape=...]
  transfers between devices with their start and end apart: 2 -> 39, of which waited for: 2 -> 15; matrix products, arithmetic and copies ran while one was open for 1% -> 1% of each run, Pallas kernels for 0% -> 0%
where the time goes in v3:
time: 142 us; the launch traced here: 141 us
  waiting for transfers between devices  80.4 us (57%)
  Pallas kernels  29.8 us (21%)
  starting transfers between devices  24.2 us (17%)
  local copies, waits for them, and re-layouts  3.64 us (3%)
  other arithmetic  2.6 us (2%)
    ppermute x39, waiting for transfers between devices, swap(): return lax.ppermute(value, AXES, [(i, i ^ mask) for i in range(count)])  80.4 us
    pallas_call x1, Pallas kernels, shards(): pl.pallas_call(functools.partial(purify, reach, edge, layout), out_shape=...  29.8 us
    ppermute x39, starting transfers between devices, swap(): return lax.ppermute(value, AXES, [(i, i ^ mask) for i in range(count)])  24.2 us
    unnamed x68, local copies, waits for them, and re-layouts  3.35 us
  transfers between devices with their start and end apart: 39, of which 15 were waited for; matrix products, arithmetic and copies ran while one was open for 1% of the time, Pallas kernels for 0%

profile of v3, /device:TPU:0, one launch (start us, length us, event | category | flops | bytes accessed | tf_op | source)
XLA Modules:
  0.0 141.4 jit_solution(8483216229270355714)
XLA Ops:
  0.8 1.3 bitcast_multiply_fusion
  2.2 3.0 %collective-permute-start = (bf16[1936,128]{1,0:T(8,128)(2,1)S(1)}, bf16[1936,128]{1,0:T(8,128)(2,1)S(1)}, u32[]{:S(2)}, u32[]{:S(2)}) collective-permute-start(bf16[1936,128]{1,0:T(8,128)(2,1)S(1)} %fusion.1.refs_0_), channel_id=1, source_target_pairs={{0,1},{1,0},{2,3},{3,2},{4,5},{5,4},{6,7},{7,6},{8,9},{9,8},{10,11... | collective-permute-start | bytes 1486856 | tf_op jit(solution)/shard_map/ppermute | solution.py:16
  5.2 1.5 %collective-permute-start.15 = (bf16[1936,128]{1,0:T(8,128)(2,1)S(1)}, bf16[1936,128]{1,0:T(8,128)(2,1)S(1)}, u32[]{:S(2)}, u32[]{:S(2)}) collective-permute-start(bf16[1936,128]{1,0:T(8,128)(2,1)S(1)} %fusion.1.refs_0_), channel_id=1, source_target_pairs={{0,16},{1,17},{2,18},{3,19},{4,20},{5,21},{6,22},{7,23},{8,24},{9,... | collective-permute-start | bytes 1486856 | tf_op jit(solution)/shard_map/ppermute | solution.py:16
  6.7 3.6 %collective-permute-start.5 = (bf16[1936,128]{1,0:T(8,128)(2,1)S(1)}, bf16[1936,128]{1,0:T(8,128)(2,1)S(1)}, u32[]{:S(2)}, u32[]{:S(2)}) collective-permute-start(bf16[1936,128]{1,0:T(8,128)(2,1)S(1)} %fusion.1.refs_0_), channel_id=1, source_target_pairs={{0,6},{1,7},{2,4},{3,5},{4,2},{5,3},{6,0},{7,1},{8,14},{9,15},{10,... | collective-permute-start | bytes 1486856 | tf_op jit(solution)/shard_map/ppermute | solution.py:16
  10.3 6.2 %collective-permute-done.refs_1_ = bf16[1936,128]{1,0:T(8,128)(2,1)S(1)} collective-permute-done((bf16[1936,128]{1,0:T(8,128)(2,1)S(1)}, bf16[1936,128]{1,0:T(8,128)(2,1)S(1)}, u32[]{:S(2)}, u32[]{:S(2)}) %collective-permute-start) | collective-permute-done | bytes 495648 | tf_op jit(solution)/shard_map/ppermute | solution.py:16
  16.5 1.8 %collective-permute-start.1 = (bf16[1936,128]{1,0:T(8,128)(2,1)S(1)}, bf16[1936,128]{1,0:T(8,128)(2,1)S(1)}, u32[]{:S(2)}, u32[]{:S(2)}) collective-permute-start(bf16[1936,128]{1,0:T(8,128)(2,1)S(1)} %fusion.1.refs_0_), channel_id=1, source_target_pairs={{0,2},{1,3},{2,0},{3,1},{4,6},{5,7},{6,4},{7,5},{8,10},{9,11},{10,... | collective-permute-start | bytes 1486856 | tf_op jit(solution)/shard_map/ppermute | solution.py:16
  18.3 1.6 %collective-permute-start.17 = (bf16[912,128]{1,0:T(8,128)(2,1)S(1)}, bf16[912,128]{1,0:T(8,128)(2,1)S(1)}, u32[]{:S(2)}, u32[]{:S(2)}) collective-permute-start(bf16[912,128]{1,0:T(8,128)(2,1)S(1)} %slice.41), channel_id=1, source_target_pairs={{0,16},{1,17},{2,18},{3,19},{4,20},{5,21},{6,22},{7,23},{8,24},{9,... | collective-permute-start | bytes 700424 | tf_op jit(solution)/shard_map/ppermute | solution.py:16
  20.0 1.6 %collective-permute-start.16 = (bf16[1024,128]{1,0:T(8,128)(2,1)S(1)}, bf16[1024,128]{1,0:T(8,128)(2,1)S(1)}, u32[]{:S(2)}, u32[]{:S(2)}) collective-permute-start(bf16[1024,128]{1,0:T(8,128)(2,1)S(1)} %slice.40), channel_id=1, source_target_pairs={{0,1},{1,0},{2,3},{3,2},{4,5},{5,4},{6,7},{7,6},{8,9},{9,8},{10,11... | collective-permute-start | bytes 786440 | tf_op jit(solution)/shard_map/ppermute | solution.py:16
  21.5 1.2 collective-permute-done.5.refs_6_
  22.7 2.0 %collective-permute-done.17.refs_18_ = bf16[912,128]{1,0:T(8,128)(2,1)S(1)} collective-permute-done((bf16[912,128]{1,0:T(8,128)(2,1)S(1)}, bf16[912,128]{1,0:T(8,128)(2,1)S(1)}, u32[]{:S(2)}, u32[]{:S(2)}) %collective-permute-start.17) | collective-permute-done | bytes 233504 | tf_op jit(solution)/shard_map/ppermute | solution.py:16
  24.7 28.6 %collective-permute-done.3.refs_4_ = bf16[1936,128]{1,0:T(8,128)(2,1)S(1)} collective-permute-done((bf16[1936,128]{1,0:T(8,128)(2,1)S(1)}, bf16[1936,128]{1,0:T(8,128)(2,1)S(1)}, u32[]{:S(2)}, u32[]{:S(2)}) %collective-permute-start.3) | collective-permute-done | bytes 495648 | tf_op jit(solution)/shard_map/ppermute | solution.py:16
  54.5 6.1 %collective-permute-done.20.refs_21_ = bf16[912,128]{1,0:T(8,128)(2,1)S(1)} collective-permute-done((bf16[912,128]{1,0:T(8,128)(2,1)S(1)}, bf16[912,128]{1,0:T(8,128)(2,1)S(1)}, u32[]{:S(2)}, u32[]{:S(2)}) %collective-permute-start.20) | collective-permute-done | bytes 233504 | tf_op jit(solution)/shard_map/ppermute | solution.py:16
  61.9 5.7 %collective-permute-done.24.refs_25_ = bf16[1936,128]{1,0:T(8,128)(2,1)S(1)} collective-permute-done((bf16[1936,128]{1,0:T(8,128)(2,1)S(1)}, bf16[1936,128]{1,0:T(8,128)(2,1)S(1)}, u32[]{:S(2)}, u32[]{:S(2)}) %collective-permute-start.24) | collective-permute-done | bytes 495648 | tf_op jit(solution)/shard_map/ppermute | solution.py:16
  68.7 9.5 %collective-permute-done.21.refs_22_ = bf16[1936,128]{1,0:T(8,128)(2,1)S(1)} collective-permute-done((bf16[1936,128]{1,0:T(8,128)(2,1)S(1)}, bf16[1936,128]{1,0:T(8,128)(2,1)S(1)}, u32[]{:S(2)}, u32[]{:S(2)}) %collective-permute-start.21) | collective-permute-done | bytes 495648 | tf_op jit(solution)/shard_map/ppermute | solution.py:16
  79.3 8.3 %collective-permute-done.18.refs_19_ = bf16[1936,128]{1,0:T(8,128)(2,1)} collective-permute-done((bf16[1936,128]{1,0:T(8,128)(2,1)S(1)}, bf16[1936,128]{1,0:T(8,128)(2,1)}, u32[]{:S(2)}, u32[]{:S(2)}) %collective-permute-start.18) | collective-permute-done | bytes 495648 | tf_op jit(solution)/shard_map/ppermute | solution.py:16
  87.7 1.7 %collective-permute-start.19 = (bf16[1024,128]{1,0:T(8,128)(2,1)S(1)}, bf16[1024,128]{1,0:T(8,128)(2,1)S(1)}, u32[]{:S(2)}, u32[]{:S(2)}) collective-permute-start(bf16[1024,128]{1,0:T(8,128)(2,1)S(1)} %collective-permute-done.16.refs_17_), channel_id=1, source_target_pairs={{0,2},{1,3},{2,0},{3,1},{4,6},{5,7},{6,4},{7,5},{8,10},{9,11},{10,... | collective-permute-start | bytes 786440 | tf_op jit(solution)/shard_map/ppermute | solution.py:16
  91.5 1.6 %collective-permute-start.22 = (bf16[1024,128]{1,0:T(8,128)(2,1)S(1)}, bf16[1024,128]{1,0:T(8,128)(2,1)}, u32[]{:S(2)}, u32[]{:S(2)}) collective-permute-start(bf16[1024,128]{1,0:T(8,128)(2,1)S(1)} %slice.42), channel_id=1, source_target_pairs={{0,1},{1,0},{2,3},{3,2},{4,5},{5,4},{6,7},{7,6},{8,9},{9,8},{10,11... | collective-permute-start | bytes 786440 | tf_op jit(solution)/shard_map/ppermute | solution.py:16
  93.0 1.7 %collective-permute-done.19.refs_20_ = bf16[1024,128]{1,0:T(8,128)(2,1)S(1)} collective-permute-done((bf16[1024,128]{1,0:T(8,128)(2,1)S(1)}, bf16[1024,128]{1,0:T(8,128)(2,1)S(1)}, u32[]{:S(2)}, u32[]{:S(2)}) %collective-permute-start.19) | collective-permute-done | bytes 262176 | tf_op jit(solution)/shard_map/ppermute | solution.py:16
  95.4 2.2 %collective-permute-done.26.refs_27_ = bf16[912,128]{1,0:T(8,128)(2,1)S(1)} collective-permute-done((bf16[912,128]{1,0:T(8,128)(2,1)S(1)}, bf16[912,128]{1,0:T(8,128)(2,1)S(1)}, u32[]{:S(2)}, u32[]{:S(2)}) %collective-permute-start.26) | collective-permute-done | bytes 233504 | tf_op jit(solution)/shard_map/ppermute | solution.py:16
  97.6 5.3 %collective-permute-done.23.refs_24_ = bf16[912,128]{1,0:T(8,128)(2,1)S(1)} collective-permute-done((bf16[912,128]{1,0:T(8,128)(2,1)S(1)}, bf16[912,128]{1,0:T(8,128)(2,1)S(1)}, u32[]{:S(2)}, u32[]{:S(2)}) %collective-permute-start.23) | collective-permute-done | bytes 233504 | tf_op jit(solution)/shard_map/ppermute | solution.py:16
  103.4 0.9 collective-permute-done.22.refs_23_
  104.8 1.0 collective-permute-done.38.refs_39_
  108.8 1.4 %collective-permute-done.10.refs_11_ = bf16[1936,128]{1,0:T(8,128)(2,1)} collective-permute-done((bf16[1936,128]{1,0:T(8,128)(2,1)}, bf16[1936,128]{1,0:T(8,128)(2,1)}, u32[]{:S(2)}, u32[]{:S(2)}) %collective-permute-start.10) | collective-permute-done | bytes 495648 | tf_op jit(solution)/shard_map/ppermute | solution.py:16
  111.6 29.8 %shard_map.37 = bf16[29,128,128]{2,1,0:T(8,128)(2,1)} custom-call(s32[40]{0:T(128)} %compare_select_fusion.place, bf16[1936,128]{1,0:T(8,128)(2,1)} %copy-done, bf16[1936,128]{1,0:T(8,128)(2,1)} %copy-done.4, bf16[1936,128]{1,0:T(8,128)(2,1)} %copy-done.10, bf16[1936,128]{1,0:T(8,128)(2,1)} %collective-permute-done.2.refs_3_, bf16[1936,128]{1,0:T(8,128)(2,1)} %copy-done.9, ...), custom_call_target="tpu_custom_call" | custom-call | flops 16999999488 | bytes 15728640 | tf_op jit(solution)/shard_map/pallas_call | solution.py:221
  (136 shorter events, 13.0 us)
Async XLA Ops:
  2.2 14.3 %collective-permute-start = (bf16[1936,128]{1,0:T(8,128)(2,1)S(1)}, bf16[1936,128]{1,0:T(8,128)(2,1)S(1)}, u32[]{:S(2)}, u32[]{:S(2)}) collective-permute-start(bf16[1936,128]{1,0:T(8,128)(2,1)S(1)} %fusion.1.refs_0_), channel_id=1, source_target_pairs={{0,1},{1,0},{2,3},{3,2},{4,5},{5,4},{6,7},{7,6},{8,9},{9,8},{10,11... | collective-permute-start | bytes 1486856 | tf_op jit(solution)/shard_map/ppermute | solution.py:16
  5.2 13.2 %collective-permute-start.15 = (bf16[1936,128]{1,0:T(8,128)(2,1)S(1)}, bf16[1936,128]{1,0:T(8,128)(2,1)S(1)}, u32[]{:S(2)}, u32[]{:S(2)}) collective-permute-start(bf16[1936,128]{1,0:T(8,128)(2,1)S(1)} %fusion.1.refs_0_), channel_id=1, source_target_pairs={{0,16},{1,17},{2,18},{3,19},{4,20},{5,21},{6,22},{7,23},{8,24},{9,... | collective-permute-start | bytes 1486856 | tf_op jit(solution)/shard_map/ppermute | solution.py:16
  6.7 13.3 %collective-permute-start.7 = (bf16[1936,128]{1,0:T(8,128)(2,1)S(1)}, bf16[1936,128]{1,0:T(8,128)(2,1)S(1)}, u32[]{:S(2)}, u32[]{:S(2)}) collective-permute-start(bf16[1936,128]{1,0:T(8,128)(2,1)S(1)} %fusion.1.refs_0_), channel_id=1, source_target_pairs={{0,8},{1,9},{2,10},{3,11},{4,12},{5,13},{6,14},{7,15},{8,0},{9,1},... | collective-permute-start | bytes 1486856 | tf_op jit(solution)/shard_map/ppermute | solution.py:16
  6.7 16.0 %collective-permute-start.5 = (bf16[1936,128]{1,0:T(8,128)(2,1)S(1)}, bf16[1936,128]{1,0:T(8,128)(2,1)S(1)}, u32[]{:S(2)}, u32[]{:S(2)}) collective-permute-start(bf16[1936,128]{1,0:T(8,128)(2,1)S(1)} %fusion.1.refs_0_), channel_id=1, source_target_pairs={{0,6},{1,7},{2,4},{3,5},{4,2},{5,3},{6,0},{7,1},{8,14},{9,15},{10,... | collective-permute-start | bytes 1486856 | tf_op jit(solution)/shard_map/ppermute | solution.py:16
  10.3 43.0 %collective-permute-start.3 = (bf16[1936,128]{1,0:T(8,128)(2,1)S(1)}, bf16[1936,128]{1,0:T(8,128)(2,1)S(1)}, u32[]{:S(2)}, u32[]{:S(2)}) collective-permute-start(bf16[1936,128]{1,0:T(8,128)(2,1)S(1)} %fusion.1.refs_0_), channel_id=1, source_target_pairs={{0,4},{1,5},{2,6},{3,7},{4,0},{5,1},{6,2},{7,3},{8,12},{9,13},{10,... | collective-permute-start | bytes 1486856 | tf_op jit(solution)/shard_map/ppermute | solution.py:16
  16.5 36.8 %collective-permute-start.1 = (bf16[1936,128]{1,0:T(8,128)(2,1)S(1)}, bf16[1936,128]{1,0:T(8,128)(2,1)S(1)}, u32[]{:S(2)}, u32[]{:S(2)}) collective-permute-start(bf16[1936,128]{1,0:T(8,128)(2,1)S(1)} %fusion.1.refs_0_), channel_id=1, source_target_pairs={{0,2},{1,3},{2,0},{3,1},{4,6},{5,7},{6,4},{7,5},{8,10},{9,11},{10,... | collective-permute-start | bytes 1486856 | tf_op jit(solution)/shard_map/ppermute | solution.py:16
  20.0 33.9 %collective-permute-start.16 = (bf16[1024,128]{1,0:T(8,128)(2,1)S(1)}, bf16[1024,128]{1,0:T(8,128)(2,1)S(1)}, u32[]{:S(2)}, u32[]{:S(2)}) collective-permute-start(bf16[1024,128]{1,0:T(8,128)(2,1)S(1)} %slice.40), channel_id=1, source_target_pairs={{0,1},{1,0},{2,3},{3,2},{4,5},{5,4},{6,7},{7,6},{8,9},{9,8},{10,11... | collective-permute-start | bytes 786440 | tf_op jit(solution)/shard_map/ppermute | solution.py:16
  22.7 38.4 %collective-permute-start.27 = (bf16[1936,128]{1,0:T(8,128)(2,1)S(1)}, bf16[1936,128]{1,0:T(8,128)(2,1)S(1)}, u32[]{:S(2)}, u32[]{:S(2)}) collective-permute-start(bf16[1936,128]{1,0:T(8,128)(2,1)S(1)} %collective-permute-done.15.refs_16_), channel_id=1, source_target_pairs={{0,8},{1,9},{2,10},{3,11},{4,12},{5,13},{6,14},{7,15},{8,0},{9,1},... | collective-permute-start | bytes 1486856 | tf_op jit(solution)/shard_map/ppermute | solution.py:16
  24.7 29.2 %collective-permute-start.29 = (bf16[912,128]{1,0:T(8,128)(2,1)S(1)}, bf16[912,128]{1,0:T(8,128)(2,1)S(1)}, u32[]{:S(2)}, u32[]{:S(2)}) collective-permute-start(bf16[912,128]{1,0:T(8,128)(2,1)S(1)} %collective-permute-done.17.refs_18_), channel_id=1, source_target_pairs={{0,8},{1,9},{2,10},{3,11},{4,12},{5,13},{6,14},{7,15},{8,0},{9,1},... | collective-permute-start | bytes 700424 | tf_op jit(solution)/shard_map/ppermute | solution.py:16
  53.3 14.3 %collective-permute-start.24 = (bf16[1936,128]{1,0:T(8,128)(2,1)S(1)}, bf16[1936,128]{1,0:T(8,128)(2,1)S(1)}, u32[]{:S(2)}, u32[]{:S(2)}) collective-permute-start(bf16[1936,128]{1,0:T(8,128)(2,1)S(1)} %collective-permute-done.5.refs_6_), channel_id=1, source_target_pairs={{0,16},{1,17},{2,18},{3,19},{4,20},{5,21},{6,22},{7,23},{8,24},{9,... | collective-permute-start | bytes 1486856 | tf_op jit(solution)/shard_map/ppermute | solution.py:16
  53.9 14.2 %collective-permute-start.13 = (bf16[1936,128]{1,0:T(8,128)(2,1)S(1)}, bf16[1936,128]{1,0:T(8,128)(2,1)S(1)}, u32[]{:S(2)}, u32[]{:S(2)}) collective-permute-start(bf16[1936,128]{1,0:T(8,128)(2,1)S(1)} %collective-permute-done.5.refs_6_), channel_id=1, source_target_pairs={{0,8},{1,9},{2,10},{3,11},{4,12},{5,13},{6,14},{7,15},{8,0},{9,1},... | collective-permute-start | bytes 1486856 | tf_op jit(solution)/shard_map/ppermute | solution.py:16
  53.9 14.7 %collective-permute-start.6 = (bf16[1936,128]{1,0:T(8,128)(2,1)S(1)}, bf16[1936,128]{1,0:T(8,128)(2,1)S(1)}, u32[]{:S(2)}, u32[]{:S(2)}) collective-permute-start(bf16[1936,128]{1,0:T(8,128)(2,1)S(1)} %collective-permute-done.5.refs_6_), channel_id=1, source_target_pairs={{0,1},{1,0},{2,3},{3,2},{4,5},{5,4},{6,7},{7,6},{8,9},{9,8},{10,11... | collective-permute-start | bytes 1486856 | tf_op jit(solution)/shard_map/ppermute | solution.py:16
  60.6 17.6 %collective-permute-start.21 = (bf16[1936,128]{1,0:T(8,128)(2,1)S(1)}, bf16[1936,128]{1,0:T(8,128)(2,1)S(1)}, u32[]{:S(2)}, u32[]{:S(2)}) collective-permute-start(bf16[1936,128]{1,0:T(8,128)(2,1)S(1)} %collective-permute-done.3.refs_4_), channel_id=1, source_target_pairs={{0,16},{1,17},{2,18},{3,19},{4,20},{5,21},{6,22},{7,23},{8,24},{9,... | collective-permute-start | bytes 1486856 | tf_op jit(solution)/shard_map/ppermute | solution.py:16
  61.1 17.6 %collective-permute-start.11 = (bf16[1936,128]{1,0:T(8,128)(2,1)S(1)}, bf16[1936,128]{1,0:T(8,128)(2,1)S(1)}, u32[]{:S(2)}, u32[]{:S(2)}) collective-permute-start(bf16[1936,128]{1,0:T(8,128)(2,1)S(1)} %collective-permute-done.3.refs_4_), channel_id=1, source_target_pairs={{0,8},{1,9},{2,10},{3,11},{4,12},{5,13},{6,14},{7,15},{8,0},{9,1},... | collective-permute-start | bytes 1486856 | tf_op jit(solution)/shard_map/ppermute | solution.py:16
  67.6 11.2 %collective-permute-start.4 = (bf16[1936,128]{1,0:T(8,128)(2,1)S(1)}, bf16[1936,128]{1,0:T(8,128)(2,1)S(1)}, u32[]{:S(2)}, u32[]{:S(2)}) collective-permute-start(bf16[1936,128]{1,0:T(8,128)(2,1)S(1)} %collective-permute-done.3.refs_4_), channel_id=1, source_target_pairs={{0,1},{1,0},{2,3},{3,2},{4,5},{5,4},{6,7},{7,6},{8,9},{9,8},{10,11... | collective-permute-start | bytes 1486856 | tf_op jit(solution)/shard_map/ppermute | solution.py:16
  68.1 19.5 %collective-permute-start.18 = (bf16[1936,128]{1,0:T(8,128)(2,1)S(1)}, bf16[1936,128]{1,0:T(8,128)(2,1)}, u32[]{:S(2)}, u32[]{:S(2)}) collective-permute-start(bf16[1936,128]{1,0:T(8,128)(2,1)S(1)} %collective-permute-done.1.refs_2_), channel_id=1, source_target_pairs={{0,16},{1,17},{2,18},{3,19},{4,20},{5,21},{6,22},{7,23},{8,24},{9,... | collective-permute-start | bytes 1486856 | tf_op jit(solution)/shard_map/ppermute | solution.py:16
  68.6 20.8 %collective-permute-start.9 = (bf16[1936,128]{1,0:T(8,128)(2,1)S(1)}, bf16[1936,128]{1,0:T(8,128)(2,1)S(1)}, u32[]{:S(2)}, u32[]{:S(2)}) collective-permute-start(bf16[1936,128]{1,0:T(8,128)(2,1)S(1)} %collective-permute-done.1.refs_2_), channel_id=1, source_target_pairs={{0,8},{1,9},{2,10},{3,11},{4,12},{5,13},{6,14},{7,15},{8,0},{9,1},... | collective-permute-start | bytes 1486856 | tf_op jit(solution)/shard_map/ppermute | solution.py:16
  78.2 11.3 %collective-permute-start.2 = (bf16[1936,128]{1,0:T(8,128)(2,1)S(1)}, bf16[1936,128]{1,0:T(8,128)(2,1)}, u32[]{:S(2)}, u32[]{:S(2)}) collective-permute-start(bf16[1936,128]{1,0:T(8,128)(2,1)S(1)} %collective-permute-done.1.refs_2_), channel_id=1, source_target_pairs={{0,1},{1,0},{2,3},{3,2},{4,5},{5,4},{6,7},{7,6},{8,9},{9,8},{10,11... | collective-permute-start | bytes 1486856 | tf_op jit(solution)/shard_map/ppermute | solution.py:16
  78.8 12.0 %collective-permute-start.8 = (bf16[1936,128]{1,0:T(8,128)(2,1)S(1)}, bf16[1936,128]{1,0:T(8,128)(2,1)S(1)}, u32[]{:S(2)}, u32[]{:S(2)}) collective-permute-start(bf16[1936,128]{1,0:T(8,128)(2,1)S(1)} %collective-permute-done.refs_1_), channel_id=1, source_target_pairs={{0,8},{1,9},{2,10},{3,11},{4,12},{5,13},{6,14},{7,15},{8,0},{9,1},... | collective-permute-start | bytes 1486856 | tf_op jit(solution)/shard_map/ppermute | solution.py:16
  78.8 12.6 %collective-permute-start.28 = (bf16[1024,128]{1,0:T(8,128)(2,1)S(1)}, bf16[1024,128]{1,0:T(8,128)(2,1)S(1)}, u32[]{:S(2)}, u32[]{:S(2)}) collective-permute-start(bf16[1024,128]{1,0:T(8,128)(2,1)S(1)} %collective-permute-done.16.refs_17_), channel_id=1, source_target_pairs={{0,8},{1,9},{2,10},{3,11},{4,12},{5,13},{6,14},{7,15},{8,0},{9,1},... | collective-permute-start | bytes 786440 | tf_op jit(solution)/shard_map/ppermute | solution.py:16
  90.8 12.1 %collective-permute-start.25 = (bf16[1024,128]{1,0:T(8,128)(2,1)S(1)}, bf16[1024,128]{1,0:T(8,128)(2,1)}, u32[]{:S(2)}, u32[]{:S(2)}) collective-permute-start(bf16[1024,128]{1,0:T(8,128)(2,1)S(1)} %slice.44), channel_id=1, source_target_pairs={{0,1},{1,0},{2,3},{3,2},{4,5},{5,4},{6,7},{7,6},{8,9},{9,8},{10,11... | collective-permute-start | bytes 786440 | tf_op jit(solution)/shard_map/ppermute | solution.py:16
  91.5 12.8 %collective-permute-start.22 = (bf16[1024,128]{1,0:T(8,128)(2,1)S(1)}, bf16[1024,128]{1,0:T(8,128)(2,1)}, u32[]{:S(2)}, u32[]{:S(2)}) collective-permute-start(bf16[1024,128]{1,0:T(8,128)(2,1)S(1)} %slice.42), channel_id=1, source_target_pairs={{0,1},{1,0},{2,3},{3,2},{4,5},{5,4},{6,7},{7,6},{8,9},{9,8},{10,11... | collective-permute-start | bytes 786440 | tf_op jit(solution)/shard_map/ppermute | solution.py:16
  94.8 9.5 %collective-permute-start.31 = (bf16[1024,128]{1,0:T(8,128)(2,1)S(1)}, bf16[1024,128]{1,0:T(8,128)(2,1)S(1)}, u32[]{:S(2)}, u32[]{:S(2)}) collective-permute-start(bf16[1024,128]{1,0:T(8,128)(2,1)S(1)} %collective-permute-done.19.refs_20_), channel_id=1, source_target_pairs={{0,8},{1,9},{2,10},{3,11},{4,12},{5,13},{6,14},{7,15},{8,0},{9,1},... | collective-permute-start | bytes 786440 | tf_op jit(solution)/shard_map/ppermute | solution.py:16
  97.6 8.7 %collective-permute-start.36 = (bf16[1936,128]{1,0:T(8,128)(2,1)S(1)}, bf16[1936,128]{1,0:T(8,128)(2,1)S(1)}, u32[]{:S(2)}, u32[]{:S(2)}) collective-permute-start(bf16[1936,128]{1,0:T(8,128)(2,1)S(1)} %collective-permute-done.24.refs_25_), channel_id=1, source_target_pairs={{0,8},{1,9},{2,10},{3,11},{4,12},{5,13},{6,14},{7,15},{8,0},{9,1},... | collective-permute-start | bytes 1486856 | tf_op jit(solution)/shard_map/ppermute | solution.py:16
  (49 other events, 868.7 us)

commit v4 on v3

--- a/solution.py
+++ b/solution.py
@@ -15,20 +15,32 @@
     def swap(value, mask):
         return lax.ppermute(value, AXES, [(i, i ^ mask) for i in range(count)])
 
-    x, core, y = 1, 8, 16
+    x, z1, z2, z3, core, y = 1, 2, 4, 6, 8, 16
     rows = {0: [payload]}
-    for z in (2, 4, 6):
-        rows[z] = [swap(payload, z)]
-    for z in (0, 2, 4, 6):
-        rows[z | x] = [swap(rows[z][0], x)]
-        rows[z | y] = [swap(rows[z][0], y)]
-        if z == 2:
-            continue
+
+    def send(target, source, mask):
+        rows[target] = [swap(piece, mask) for piece in rows[source]]
+
+    def corner(z):
         rows[z | x | y] = [swap(rows[z | y][0][:half], x), swap(rows[z | x][0][half:], y)]
-        if z == 0:
-            rows[2 | x | y] = [swap(piece, 2) for piece in rows[x | y]]
+
+    send(x, 0, x)
+    send(y, 0, y)
+    send(z1, 0, z1)
+    send(z3, 0, z3)
+    corner(0)
+    send(z1 | x, z1, x)
+    send(z1 | y, z1, y)
+    send(z2, z3, z1)
+    send(z3 | x, z3, x)
+    send(z3 | y, z3, y)
+    send(z1 | x | y, x | y, z1)
+    send(z3 | x | y, x | y, z3)
+    send(z2 | x, z2, x)
+    send(z2 | y, z2, y)
+    corner(z2)
     for mask in list(rows):
-        rows[mask | core] = [swap(piece, core) for piece in rows[mask]]
+        send(mask | core, mask, core)
     return rows
 
 

time: 142 us -> 134 us (0.944)
  waiting for transfers between devices: 80.4 us -> 68.3 us
  starting transfers between devices: 24.2 us -> 32 us
  local copies, waits for them, and re-layouts: 3.64 us -> 0.69 us
    ppermute x39, waiting for transfers between devices: 80.4 us -> 68.3 us  [swap(): return lax.ppermute(value, AXES, [(i, i ^ mask) for i in range(count)])]
    ppermute x39, starting transfers between devices: 24.2 us -> 32 us  [swap(): return lax.ppermute(value, AXES, [(i, i ^ mask) for i in range(count)])]
    unnamed x68 -> x70, local copies, waits for them, and re-layouts: 3.35 us -> 0.43 us
  transfers between devices with their start and end apart: 39 -> 39, of which waited for: 15 -> 16; matrix products, arithmetic and copies ran while one was open for 1% -> 1% of each run, Pallas kernels for 0% -> 0%
where the time goes in v4:
time: 134 us
  waiting for transfers between devices  68.3 us (51%)
  starting transfers between devices  32 us (24%)
  Pallas kernels  29.8 us (22%)
  other arithmetic  2.58 us (2%)
    ppermute x39, waiting for transfers between devices, swap(): return lax.ppermute(value, AXES, [(i, i ^ mask) for i in range(count)])  68.3 us
    ppermute x39, starting transfers between devices, swap(): return lax.ppermute(value, AXES, [(i, i ^ mask) for i in range(count)])  32 us
    pallas_call x1, Pallas kernels, shards(): pl.pallas_call(functools.partial(purify, reach, edge, layout), out_shape=...  29.8 us
  transfers between devices with their start and end apart: 39, of which 16 were waited for; matrix products, arithmetic and copies ran while one was open for 1% of the time, Pallas kernels for 0%

profile of v4, /device:TPU:0, one launch (start us, length us, event | category | flops | bytes accessed | tf_op | source)
XLA Modules:
  0.0 134.1 jit_solution(2701736307180996336)
XLA Ops:
  0.8 1.3 %bitcast_multiply_fusion = bf16[1920,128]{1,0:T(8,128)(2,1)S(1)} fusion(bf16[1,15,128,128]{3,2,1,0:T(8,128)(2,1)} %param.5, bf16[1920]{0:T(1024)(128)(2,1)S(1)} %broadcast_bitcast_fusion), kind=kLoop, calls=%fused_computation.3 | loop fusion | flops 245760 | bytes 986880 | tf_op jit(solution)/shard_map/mul | solution.py:225
  2.2 3.0 %collective-permute-start = (bf16[1936,128]{1,0:T(8,128)(2,1)S(1)}, bf16[1936,128]{1,0:T(8,128)(2,1)S(1)}, u32[]{:S(2)}, u32[]{:S(2)}) collective-permute-start(bf16[1936,128]{1,0:T(8,128)(2,1)S(1)} %fusion.1.refs_0_), channel_id=1, source_target_pairs={{0,1},{1,0},{2,3},{3,2},{4,5},{5,4},{6,7},{7,6},{8,9},{9,8},{10,11... | collective-permute-start | bytes 1486856 | tf_op jit(solution)/shard_map/ppermute | solution.py:16
  5.2 1.5 %collective-permute-start.15 = (bf16[1936,128]{1,0:T(8,128)(2,1)S(1)}, bf16[1936,128]{1,0:T(8,128)(2,1)S(1)}, u32[]{:S(2)}, u32[]{:S(2)}) collective-permute-start(bf16[1936,128]{1,0:T(8,128)(2,1)S(1)} %fusion.1.refs_0_), channel_id=1, source_target_pairs={{0,16},{1,17},{2,18},{3,19},{4,20},{5,21},{6,22},{7,23},{8,24},{9,... | collective-permute-start | bytes 1486856 | tf_op jit(solution)/shard_map/ppermute | solution.py:16
  6.7 3.6 %collective-permute-start.3 = (bf16[1936,128]{1,0:T(8,128)(2,1)S(1)}, bf16[1936,128]{1,0:T(8,128)(2,1)S(1)}, u32[]{:S(2)}, u32[]{:S(2)}) collective-permute-start(bf16[1936,128]{1,0:T(8,128)(2,1)S(1)} %fusion.1.refs_0_), channel_id=1, source_target_pairs={{0,6},{1,7},{2,4},{3,5},{4,2},{5,3},{6,0},{7,1},{8,14},{9,15},{10,... | collective-permute-start | bytes 1486856 | tf_op jit(solution)/shard_map/ppermute | solution.py:16
  10.3 6.2 %collective-permute-done.refs_1_ = bf16[1936,128]{1,0:T(8,128)(2,1)S(1)} collective-permute-done((bf16[1936,128]{1,0:T(8,128)(2,1)S(1)}, bf16[1936,128]{1,0:T(8,128)(2,1)S(1)}, u32[]{:S(2)}, u32[]{:S(2)}) %collective-permute-start) | collective-permute-done | bytes 495648 | tf_op jit(solution)/shard_map/ppermute | solution.py:16
  16.5 1.8 %collective-permute-start.17 = (bf16[912,128]{1,0:T(8,128)(2,1)S(1)}, bf16[912,128]{1,0:T(8,128)(2,1)S(1)}, u32[]{:S(2)}, u32[]{:S(2)}) collective-permute-start(bf16[912,128]{1,0:T(8,128)(2,1)S(1)} %slice.33), channel_id=1, source_target_pairs={{0,16},{1,17},{2,18},{3,19},{4,20},{5,21},{6,22},{7,23},{8,24},{9,... | collective-permute-start | bytes 700424 | tf_op jit(solution)/shard_map/ppermute | solution.py:16
  18.4 1.6 %collective-permute-start.16 = (bf16[1024,128]{1,0:T(8,128)(2,1)S(1)}, bf16[1024,128]{1,0:T(8,128)(2,1)S(1)}, u32[]{:S(2)}, u32[]{:S(2)}) collective-permute-start(bf16[1024,128]{1,0:T(8,128)(2,1)S(1)} %slice.32), channel_id=1, source_target_pairs={{0,1},{1,0},{2,3},{3,2},{4,5},{5,4},{6,7},{7,6},{8,9},{9,8},{10,11... | collective-permute-start | bytes 786440 | tf_op jit(solution)/shard_map/ppermute | solution.py:16
  19.9 2.7 %collective-permute-done.3.refs_6_ = bf16[1936,128]{1,0:T(8,128)(2,1)S(1)} collective-permute-done((bf16[1936,128]{1,0:T(8,128)(2,1)S(1)}, bf16[1936,128]{1,0:T(8,128)(2,1)S(1)}, u32[]{:S(2)}, u32[]{:S(2)}) %collective-permute-start.3) | collective-permute-done | bytes 495648 | tf_op jit(solution)/shard_map/ppermute | solution.py:16
  23.4 9.5 %collective-permute-done.1.refs_2_ = bf16[1936,128]{1,0:T(8,128)(2,1)S(1)} collective-permute-done((bf16[1936,128]{1,0:T(8,128)(2,1)S(1)}, bf16[1936,128]{1,0:T(8,128)(2,1)S(1)}, u32[]{:S(2)}, u32[]{:S(2)}) %collective-permute-start.1) | collective-permute-done | bytes 495648 | tf_op jit(solution)/shard_map/ppermute | solution.py:16
  33.0 1.6 %collective-permute-start.26 = (bf16[912,128]{1,0:T(8,128)(2,1)S(1)}, bf16[912,128]{1,0:T(8,128)(2,1)S(1)}, u32[]{:S(2)}, u32[]{:S(2)}) collective-permute-start(bf16[912,128]{1,0:T(8,128)(2,1)S(1)} %collective-permute-done.17.refs_18_), channel_id=1, source_target_pairs={{0,6},{1,7},{2,4},{3,5},{4,2},{5,3},{6,0},{7,1},{8,14},{9,15},{10,... | collective-permute-start | bytes 700424 | tf_op jit(solution)/shard_map/ppermute | solution.py:16
  35.3 7.3 %collective-permute-done.26.refs_27_ = bf16[912,128]{1,0:T(8,128)(2,1)S(1)} collective-permute-done((bf16[912,128]{1,0:T(8,128)(2,1)S(1)}, bf16[912,128]{1,0:T(8,128)(2,1)S(1)}, u32[]{:S(2)}, u32[]{:S(2)}) %collective-permute-start.26) | collective-permute-done | bytes 233504 | tf_op jit(solution)/shard_map/ppermute | solution.py:16
  42.5 4.5 %collective-permute-start.20 = (bf16[912,128]{1,0:T(8,128)(2,1)S(1)}, bf16[912,128]{1,0:T(8,128)(2,1)S(1)}, u32[]{:S(2)}, u32[]{:S(2)}) collective-permute-start(bf16[912,128]{1,0:T(8,128)(2,1)S(1)} %collective-permute-done.17.refs_18_), channel_id=1, source_target_pairs={{0,2},{1,3},{2,0},{3,1},{4,6},{5,7},{6,4},{7,5},{8,10},{9,11},{10,... | collective-permute-start | bytes 700424 | tf_op jit(solution)/shard_map/ppermute | solution.py:16
  47.0 4.8 %collective-permute-done.20.refs_21_ = bf16[912,128]{1,0:T(8,128)(2,1)S(1)} collective-permute-done((bf16[912,128]{1,0:T(8,128)(2,1)S(1)}, bf16[912,128]{1,0:T(8,128)(2,1)S(1)}, u32[]{:S(2)}, u32[]{:S(2)}) %collective-permute-start.20) | collective-permute-done | bytes 233504 | tf_op jit(solution)/shard_map/ppermute | solution.py:16
  51.9 1.7 %collective-permute-start.4 = (bf16[1936,128]{1,0:T(8,128)(2,1)S(1)}, bf16[1936,128]{1,0:T(8,128)(2,1)S(1)}, u32[]{:S(2)}, u32[]{:S(2)}) collective-permute-start(bf16[1936,128]{1,0:T(8,128)(2,1)S(1)} %collective-permute-done.3.refs_6_), channel_id=1, source_target_pairs={{0,2},{1,3},{2,0},{3,1},{4,6},{5,7},{6,4},{7,5},{8,10},{9,11},{10,... | collective-permute-start | bytes 1486856 | tf_op jit(solution)/shard_map/ppermute | solution.py:16
  55.4 8.0 %collective-permute-done.4.refs_4_ = bf16[1936,128]{1,0:T(8,128)(2,1)S(1)} collective-permute-done((bf16[1936,128]{1,0:T(8,128)(2,1)S(1)}, bf16[1936,128]{1,0:T(8,128)(2,1)S(1)}, u32[]{:S(2)}, u32[]{:S(2)}) %collective-permute-start.4) | collective-permute-done | bytes 495648 | tf_op jit(solution)/shard_map/ppermute | solution.py:16
  63.4 3.3 %collective-permute-start.25 = (bf16[1024,128]{1,0:T(8,128)(2,1)S(1)}, bf16[1024,128]{1,0:T(8,128)(2,1)S(1)}, u32[]{:S(2)}, u32[]{:S(2)}) collective-permute-start(bf16[1024,128]{1,0:T(8,128)(2,1)S(1)} %collective-permute-done.16.refs_17_), channel_id=1, source_target_pairs={{0,6},{1,7},{2,4},{3,5},{4,2},{5,3},{6,0},{7,1},{8,14},{9,15},{10,... | collective-permute-start | bytes 786440 | tf_op jit(solution)/shard_map/ppermute | solution.py:16
  69.5 5.0 %collective-permute-done.25.refs_26_ = bf16[1024,128]{1,0:T(8,128)(2,1)S(1)} collective-permute-done((bf16[1024,128]{1,0:T(8,128)(2,1)S(1)}, bf16[1024,128]{1,0:T(8,128)(2,1)S(1)}, u32[]{:S(2)}, u32[]{:S(2)}) %collective-permute-start.25) | collective-permute-done | bytes 262176 | tf_op jit(solution)/shard_map/ppermute | solution.py:16
  74.5 3.0 %collective-permute-done.19.refs_20_ = bf16[1024,128]{1,0:T(8,128)(2,1)S(1)} collective-permute-done((bf16[1024,128]{1,0:T(8,128)(2,1)S(1)}, bf16[1024,128]{1,0:T(8,128)(2,1)S(1)}, u32[]{:S(2)}, u32[]{:S(2)}) %collective-permute-start.19) | collective-permute-done | bytes 262176 | tf_op jit(solution)/shard_map/ppermute | solution.py:16
  78.0 1.3 collective-permute-done.32.refs_33_
  82.8 11.3 %collective-permute-done.5.refs_5_ = bf16[1936,128]{1,0:T(8,128)(2,1)S(1)} collective-permute-done((bf16[1936,128]{1,0:T(8,128)(2,1)S(1)}, bf16[1936,128]{1,0:T(8,128)(2,1)S(1)}, u32[]{:S(2)}, u32[]{:S(2)}) %collective-permute-start.5) | collective-permute-done | bytes 495648 | tf_op jit(solution)/shard_map/ppermute | solution.py:16
  94.1 1.8 %collective-permute-start.23 = (bf16[912,128]{1,0:T(8,128)(2,1)S(1)}, bf16[912,128]{1,0:T(8,128)(2,1)}, u32[]{:S(2)}, u32[]{:S(2)}) collective-permute-start(bf16[912,128]{1,0:T(8,128)(2,1)S(1)} %slice.35), channel_id=1, source_target_pairs={{0,16},{1,17},{2,18},{3,19},{4,20},{5,21},{6,22},{7,23},{8,24},{9,... | collective-permute-start | bytes 700424 | tf_op jit(solution)/shard_map/ppermute | solution.py:16
  95.9 2.9 %collective-permute-done.22.refs_23_ = bf16[1024,128]{1,0:T(8,128)(2,1)S(1)} collective-permute-done((bf16[1024,128]{1,0:T(8,128)(2,1)S(1)}, bf16[1024,128]{1,0:T(8,128)(2,1)S(1)}, u32[]{:S(2)}, u32[]{:S(2)}) %collective-permute-start.22) | collective-permute-done | bytes 262176 | tf_op jit(solution)/shard_map/ppermute | solution.py:16
  99.6 2.8 %collective-permute-done.23.refs_24_ = bf16[912,128]{1,0:T(8,128)(2,1)} collective-permute-done((bf16[912,128]{1,0:T(8,128)(2,1)S(1)}, bf16[912,128]{1,0:T(8,128)(2,1)}, u32[]{:S(2)}, u32[]{:S(2)}) %collective-permute-start.23) | collective-permute-done | bytes 233504 | tf_op jit(solution)/shard_map/ppermute | solution.py:16
  104.3 29.8 %shard_map.37 = bf16[29,128,128]{2,1,0:T(8,128)(2,1)} custom-call(s32[40]{0:T(128)} %compare_select_fusion.place, bf16[1936,128]{1,0:T(8,128)(2,1)} %copy-done, bf16[1936,128]{1,0:T(8,128)(2,1)} %copy-done.3, bf16[1936,128]{1,0:T(8,128)(2,1)} %copy-done.7, bf16[1936,128]{1,0:T(8,128)(2,1)} %collective-permute-done.2.refs_3_, bf16[1936,128]{1,0:T(8,128)(2,1)} %copy-done.12, ...), custom_call_target="tpu_custom_call" | custom-call | flops 16999999488 | bytes 15728640 | tf_op jit(solution)/shard_map/pallas_call | solution.py:233
  (136 shorter events, 12.9 us)
Async XLA Ops:
  2.2 14.3 %collective-permute-start = (bf16[1936,128]{1,0:T(8,128)(2,1)S(1)}, bf16[1936,128]{1,0:T(8,128)(2,1)S(1)}, u32[]{:S(2)}, u32[]{:S(2)}) collective-permute-start(bf16[1936,128]{1,0:T(8,128)(2,1)S(1)} %fusion.1.refs_0_), channel_id=1, source_target_pairs={{0,1},{1,0},{2,3},{3,2},{4,5},{5,4},{6,7},{7,6},{8,9},{9,8},{10,11... | collective-permute-start | bytes 1486856 | tf_op jit(solution)/shard_map/ppermute | solution.py:16
  5.2 13.2 %collective-permute-start.15 = (bf16[1936,128]{1,0:T(8,128)(2,1)S(1)}, bf16[1936,128]{1,0:T(8,128)(2,1)S(1)}, u32[]{:S(2)}, u32[]{:S(2)}) collective-permute-start(bf16[1936,128]{1,0:T(8,128)(2,1)S(1)} %fusion.1.refs_0_), channel_id=1, source_target_pairs={{0,16},{1,17},{2,18},{3,19},{4,20},{5,21},{6,22},{7,23},{8,24},{9,... | collective-permute-start | bytes 1486856 | tf_op jit(solution)/shard_map/ppermute | solution.py:16
  6.7 13.2 %collective-permute-start.7 = (bf16[1936,128]{1,0:T(8,128)(2,1)S(1)}, bf16[1936,128]{1,0:T(8,128)(2,1)S(1)}, u32[]{:S(2)}, u32[]{:S(2)}) collective-permute-start(bf16[1936,128]{1,0:T(8,128)(2,1)S(1)} %fusion.1.refs_0_), channel_id=1, source_target_pairs={{0,8},{1,9},{2,10},{3,11},{4,12},{5,13},{6,14},{7,15},{8,0},{9,1},... | collective-permute-start | bytes 1486856 | tf_op jit(solution)/shard_map/ppermute | solution.py:16
  6.7 16.0 %collective-permute-start.3 = (bf16[1936,128]{1,0:T(8,128)(2,1)S(1)}, bf16[1936,128]{1,0:T(8,128)(2,1)S(1)}, u32[]{:S(2)}, u32[]{:S(2)}) collective-permute-start(bf16[1936,128]{1,0:T(8,128)(2,1)S(1)} %fusion.1.refs_0_), channel_id=1, source_target_pairs={{0,6},{1,7},{2,4},{3,5},{4,2},{5,3},{6,0},{7,1},{8,14},{9,15},{10,... | collective-permute-start | bytes 1486856 | tf_op jit(solution)/shard_map/ppermute | solution.py:16
  10.3 22.7 %collective-permute-start.1 = (bf16[1936,128]{1,0:T(8,128)(2,1)S(1)}, bf16[1936,128]{1,0:T(8,128)(2,1)S(1)}, u32[]{:S(2)}, u32[]{:S(2)}) collective-permute-start(bf16[1936,128]{1,0:T(8,128)(2,1)S(1)} %fusion.1.refs_0_), channel_id=1, source_target_pairs={{0,2},{1,3},{2,0},{3,1},{4,6},{5,7},{6,4},{7,5},{8,10},{9,11},{10,... | collective-permute-start | bytes 1486856 | tf_op jit(solution)/shard_map/ppermute | solution.py:16
  18.4 16.3 %collective-permute-start.16 = (bf16[1024,128]{1,0:T(8,128)(2,1)S(1)}, bf16[1024,128]{1,0:T(8,128)(2,1)S(1)}, u32[]{:S(2)}, u32[]{:S(2)}) collective-permute-start(bf16[1024,128]{1,0:T(8,128)(2,1)S(1)} %slice.32), channel_id=1, source_target_pairs={{0,1},{1,0},{2,3},{3,2},{4,5},{5,4},{6,7},{7,6},{8,9},{9,8},{10,11... | collective-permute-start | bytes 786440 | tf_op jit(solution)/shard_map/ppermute | solution.py:16
  19.9 33.7 %collective-permute-start.27 = (bf16[1936,128]{1,0:T(8,128)(2,1)S(1)}, bf16[1936,128]{1,0:T(8,128)(2,1)S(1)}, u32[]{:S(2)}, u32[]{:S(2)}) collective-permute-start(bf16[1936,128]{1,0:T(8,128)(2,1)S(1)} %collective-permute-done.15.refs_16_), channel_id=1, source_target_pairs={{0,8},{1,9},{2,10},{3,11},{4,12},{5,13},{6,14},{7,15},{8,0},{9,1},... | collective-permute-start | bytes 1486856 | tf_op jit(solution)/shard_map/ppermute | solution.py:16
  22.7 32.0 %collective-permute-start.24 = (bf16[1936,128]{1,0:T(8,128)(2,1)S(1)}, bf16[1936,128]{1,0:T(8,128)(2,1)S(1)}, u32[]{:S(2)}, u32[]{:S(2)}) collective-permute-start(bf16[1936,128]{1,0:T(8,128)(2,1)S(1)} %collective-permute-done.3.refs_6_), channel_id=1, source_target_pairs={{0,16},{1,17},{2,18},{3,19},{4,20},{5,21},{6,22},{7,23},{8,24},{9,... | collective-permute-start | bytes 1486856 | tf_op jit(solution)/shard_map/ppermute | solution.py:16
  23.4 11.2 %collective-permute-start.29 = (bf16[912,128]{1,0:T(8,128)(2,1)S(1)}, bf16[912,128]{1,0:T(8,128)(2,1)S(1)}, u32[]{:S(2)}, u32[]{:S(2)}) collective-permute-start(bf16[912,128]{1,0:T(8,128)(2,1)S(1)} %collective-permute-done.17.refs_18_), channel_id=1, source_target_pairs={{0,8},{1,9},{2,10},{3,11},{4,12},{5,13},{6,14},{7,15},{8,0},{9,1},... | collective-permute-start | bytes 700424 | tf_op jit(solution)/shard_map/ppermute | solution.py:16
  34.6 20.0 %collective-permute-start.13 = (bf16[1936,128]{1,0:T(8,128)(2,1)S(1)}, bf16[1936,128]{1,0:T(8,128)(2,1)S(1)}, u32[]{:S(2)}, u32[]{:S(2)}) collective-permute-start(bf16[1936,128]{1,0:T(8,128)(2,1)S(1)} %collective-permute-done.3.refs_6_), channel_id=1, source_target_pairs={{0,8},{1,9},{2,10},{3,11},{4,12},{5,13},{6,14},{7,15},{8,0},{9,1},... | collective-permute-start | bytes 1486856 | tf_op jit(solution)/shard_map/ppermute | solution.py:16
  34.7 20.6 %collective-permute-start.6 = (bf16[1936,128]{1,0:T(8,128)(2,1)S(1)}, bf16[1936,128]{1,0:T(8,128)(2,1)S(1)}, u32[]{:S(2)}, u32[]{:S(2)}) collective-permute-start(bf16[1936,128]{1,0:T(8,128)(2,1)S(1)} %collective-permute-done.3.refs_6_), channel_id=1, source_target_pairs={{0,1},{1,0},{2,3},{3,2},{4,5},{5,4},{6,7},{7,6},{8,9},{9,8},{10,11... | collective-permute-start | bytes 1486856 | tf_op jit(solution)/shard_map/ppermute | solution.py:16
  51.9 11.6 %collective-permute-start.4 = (bf16[1936,128]{1,0:T(8,128)(2,1)S(1)}, bf16[1936,128]{1,0:T(8,128)(2,1)S(1)}, u32[]{:S(2)}, u32[]{:S(2)}) collective-permute-start(bf16[1936,128]{1,0:T(8,128)(2,1)S(1)} %collective-permute-done.3.refs_6_), channel_id=1, source_target_pairs={{0,2},{1,3},{2,0},{3,1},{4,6},{5,7},{6,4},{7,5},{8,10},{9,11},{10,... | collective-permute-start | bytes 1486856 | tf_op jit(solution)/shard_map/ppermute | solution.py:16
  53.6 13.1 %collective-permute-start.18 = (bf16[1936,128]{1,0:T(8,128)(2,1)S(1)}, bf16[1936,128]{1,0:T(8,128)(2,1)S(1)}, u32[]{:S(2)}, u32[]{:S(2)}) collective-permute-start(bf16[1936,128]{1,0:T(8,128)(2,1)S(1)} %collective-permute-done.1.refs_2_), channel_id=1, source_target_pairs={{0,16},{1,17},{2,18},{3,19},{4,20},{5,21},{6,22},{7,23},{8,24},{9,... | collective-permute-start | bytes 1486856 | tf_op jit(solution)/shard_map/ppermute | solution.py:16
  54.6 12.7 %collective-permute-start.9 = (bf16[1936,128]{1,0:T(8,128)(2,1)S(1)}, bf16[1936,128]{1,0:T(8,128)(2,1)S(1)}, u32[]{:S(2)}, u32[]{:S(2)}) collective-permute-start(bf16[1936,128]{1,0:T(8,128)(2,1)S(1)} %collective-permute-done.1.refs_2_), channel_id=1, source_target_pairs={{0,8},{1,9},{2,10},{3,11},{4,12},{5,13},{6,14},{7,15},{8,0},{9,1},... | collective-permute-start | bytes 1486856 | tf_op jit(solution)/shard_map/ppermute | solution.py:16
  54.7 13.8 %collective-permute-start.2 = (bf16[1936,128]{1,0:T(8,128)(2,1)S(1)}, bf16[1936,128]{1,0:T(8,128)(2,1)}, u32[]{:S(2)}, u32[]{:S(2)}) collective-permute-start(bf16[1936,128]{1,0:T(8,128)(2,1)S(1)} %collective-permute-done.1.refs_2_), channel_id=1, source_target_pairs={{0,1},{1,0},{2,3},{3,2},{4,5},{5,4},{6,7},{7,6},{8,9},{9,8},{10,11... | collective-permute-start | bytes 1486856 | tf_op jit(solution)/shard_map/ppermute | solution.py:16
  55.3 14.2 %collective-permute-start.8 = (bf16[1936,128]{1,0:T(8,128)(2,1)S(1)}, bf16[1936,128]{1,0:T(8,128)(2,1)S(1)}, u32[]{:S(2)}, u32[]{:S(2)}) collective-permute-start(bf16[1936,128]{1,0:T(8,128)(2,1)S(1)} %collective-permute-done.refs_1_), channel_id=1, source_target_pairs={{0,8},{1,9},{2,10},{3,11},{4,12},{5,13},{6,14},{7,15},{8,0},{9,1},... | collective-permute-start | bytes 1486856 | tf_op jit(solution)/shard_map/ppermute | solution.py:16
  63.4 11.0 %collective-permute-start.25 = (bf16[1024,128]{1,0:T(8,128)(2,1)S(1)}, bf16[1024,128]{1,0:T(8,128)(2,1)S(1)}, u32[]{:S(2)}, u32[]{:S(2)}) collective-permute-start(bf16[1024,128]{1,0:T(8,128)(2,1)S(1)} %collective-permute-done.16.refs_17_), channel_id=1, source_target_pairs={{0,6},{1,7},{2,4},{3,5},{4,2},{5,3},{6,0},{7,1},{8,14},{9,15},{10,... | collective-permute-start | bytes 786440 | tf_op jit(solution)/shard_map/ppermute | solution.py:16
  66.7 10.7 %collective-permute-start.19 = (bf16[1024,128]{1,0:T(8,128)(2,1)S(1)}, bf16[1024,128]{1,0:T(8,128)(2,1)S(1)}, u32[]{:S(2)}, u32[]{:S(2)}) collective-permute-start(bf16[1024,128]{1,0:T(8,128)(2,1)S(1)} %collective-permute-done.16.refs_17_), channel_id=1, source_target_pairs={{0,2},{1,3},{2,0},{3,1},{4,6},{5,7},{6,4},{7,5},{8,10},{9,11},{10,... | collective-permute-start | bytes 786440 | tf_op jit(solution)/shard_map/ppermute | solution.py:16
  68.5 12.9 %collective-permute-start.21 = (bf16[1936,128]{1,0:T(8,128)(2,1)S(1)}, bf16[1936,128]{1,0:T(8,128)(2,1)S(1)}, u32[]{:S(2)}, u32[]{:S(2)}) collective-permute-start(bf16[1936,128]{1,0:T(8,128)(2,1)S(1)} %collective-permute-done.4.refs_4_), channel_id=1, source_target_pairs={{0,16},{1,17},{2,18},{3,19},{4,20},{5,21},{6,22},{7,23},{8,24},{9,... | collective-permute-start | bytes 1486856 | tf_op jit(solution)/shard_map/ppermute | solution.py:16
  79.8 14.2 %collective-permute-start.5 = (bf16[1936,128]{1,0:T(8,128)(2,1)S(1)}, bf16[1936,128]{1,0:T(8,128)(2,1)S(1)}, u32[]{:S(2)}, u32[]{:S(2)}) collective-permute-start(bf16[1936,128]{1,0:T(8,128)(2,1)S(1)} %collective-permute-done.4.refs_4_), channel_id=1, source_target_pairs={{0,1},{1,0},{2,3},{3,2},{4,5},{5,4},{6,7},{7,6},{8,9},{9,8},{10,11... | collective-permute-start | bytes 1486856 | tf_op jit(solution)/shard_map/ppermute | solution.py:16
  81.5 12.6 %collective-permute-start.30 = (bf16[1936,128]{1,0:T(8,128)(2,1)S(1)}, bf16[1936,128]{1,0:T(8,128)(2,1)S(1)}, u32[]{:S(2)}, u32[]{:S(2)}) collective-permute-start(bf16[1936,128]{1,0:T(8,128)(2,1)S(1)} %collective-permute-done.18.refs_19_), channel_id=1, source_target_pairs={{0,8},{1,9},{2,10},{3,11},{4,12},{5,13},{6,14},{7,15},{8,0},{9,1},... | collective-permute-start | bytes 1486856 | tf_op jit(solution)/shard_map/ppermute | solution.py:16
  81.6 17.3 %collective-permute-start.22 = (bf16[1024,128]{1,0:T(8,128)(2,1)S(1)}, bf16[1024,128]{1,0:T(8,128)(2,1)S(1)}, u32[]{:S(2)}, u32[]{:S(2)}) collective-permute-start(bf16[1024,128]{1,0:T(8,128)(2,1)S(1)} %slice.34), channel_id=1, source_target_pairs={{0,1},{1,0},{2,3},{3,2},{4,5},{5,4},{6,7},{7,6},{8,9},{9,8},{10,11... | collective-permute-start | bytes 786440 | tf_op jit(solution)/shard_map/ppermute | solution.py:16
  82.3 20.8 %collective-permute-start.10 = (bf16[1936,128]{1,0:T(8,128)(2,1)}, bf16[1936,128]{1,0:T(8,128)(2,1)S(1)}, u32[]{:S(2)}, u32[]{:S(2)}) collective-permute-start(bf16[1936,128]{1,0:T(8,128)(2,1)} %collective-permute-done.2.refs_3_), channel_id=1, source_target_pairs={{0,8},{1,9},{2,10},{3,11},{4,12},{5,13},{6,14},{7,15},{8,0},{9,1},... | collective-permute-start | bytes 1486856 | tf_op jit(solution)/shard_map/ppermute | solution.py:16
  82.5 21.8 %collective-permute-start.33 = (bf16[1936,128]{1,0:T(8,128)(2,1)S(1)}, bf16[1936,128]{1,0:T(8,128)(2,1)}, u32[]{:S(2)}, u32[]{:S(2)}) collective-permute-start(bf16[1936,128]{1,0:T(8,128)(2,1)S(1)} %collective-permute-done.21.refs_22_), channel_id=1, source_target_pairs={{0,8},{1,9},{2,10},{3,11},{4,12},{5,13},{6,14},{7,15},{8,0},{9,1},... | collective-permute-start | bytes 1486856 | tf_op jit(solution)/shard_map/ppermute | solution.py:16
  (50 other events, 991.7 us)

commit v5 on v3

--- a/solution.py
+++ b/solution.py
@@ -11,28 +11,63 @@
 AXES = ("row", "col")
 
 
-def cube(payload, count, half):
+def cube(own, count, here):
+    x, z1, z2, z3, core, y = 1, 2, 4, 6, 8, 16
+
+    def inner(i):
+        return (i // 2) % 4 in (1, 2)
+
     def swap(value, mask):
         return lax.ppermute(value, AXES, [(i, i ^ mask) for i in range(count)])
 
-    x, core, y = 1, 8, 16
-    rows = {0: [payload]}
-    for z in (2, 4, 6):
-        rows[z] = [swap(payload, z)]
-    for z in (0, 2, 4, 6):
-        rows[z | x] = [swap(rows[z][0], x)]
-        rows[z | y] = [swap(rows[z][0], y)]
-        if z == 2:
-            continue
-        rows[z | x | y] = [swap(rows[z | y][0][:half], x), swap(rows[z | x][0][half:], y)]
-        if z == 0:
-            rows[2 | x | y] = [swap(piece, 2) for piece in rows[x | y]]
-    for mask in list(rows):
-        rows[mask | core] = [swap(piece, core) for piece in rows[mask]]
-    return rows
-
-
-def window(payload, need, half):
+    def middle(value):
+        return lax.ppermute(value, AXES, [(i, i ^ z3) for i in range(count) if inner(i)])
+
+    def outward(value):
+        return lax.ppermute(value, AXES, [(i, i ^ z1) for i in range(count) if inner(i)])
+
+    within = ((here // 2) % 4 == 1) | ((here // 2) % 4 == 2)
+    near, far = jnp.where(within, z3, z2), jnp.where(within, z2, z3)
+    both = lax.optimization_barrier
+    found = []
+
+    def cross(*rows):
+        arrays = [array for array, _ in rows]
+        masks = [mask for _, mask in rows]
+        found.extend((array, [mask]) for array, mask in rows)
+        batch = swap(jnp.concatenate(arrays, axis=0) if len(arrays) > 1 else arrays[0], core)
+        found.append((batch, [jnp.where(mask >= 0, mask | core, -1) for mask in masks]))
+        return len(found) - 1
+
+    def finish(spot, *arrays):
+        batch, *arrays = both((found[spot][0],) + arrays)
+        found[spot] = (batch, found[spot][1])
+        return arrays
+
+    x0, y0, f, b2 = swap(own, x), swap(own, y), swap(own, z1), middle(own)
+    spot = cross((own, 0))
+    x0, y0, f, b2 = finish(spot, x0, y0, f, b2)
+    d0, yf, c3, b4 = swap(y0, x), swap(f, y), middle(f), outward(b2)
+    spot = cross((x0, x), (y0, y), (f, z1))
+    d0, yf, c3, b4, b2, f = finish(spot, d0, yf, c3, b4, b2, f)
+    b = jnp.where(within, b2, b4)
+    xb, yb, c5, db2 = swap(b, x), swap(b, y), outward(c3), middle(d0)
+    spot = cross((d0, x | y), (yf, z1 | y), (b, near))
+    xb, yb, c5, db2, c3, d0, f = finish(spot, xb, yb, c5, db2, c3, d0, f)
+    c = jnp.where(within, c3, c5)
+    xc, yc, df = swap(c, x), swap(c, y), swap(d0, z1)
+    spot = cross((xb, near | x), (yb, near | y), (c, far))
+    xc, yc, df, f, db2 = finish(spot, xc, yc, df, f, db2)
+    xf, dc, db4 = swap(f, x), swap(xc, y), outward(db2)
+    spot = cross((xc, far | x), (yc, far | y), (df, z1 | x | y), (db2, jnp.where(within, z3 | x | y, -1)))
+    xf, dc, db4 = finish(spot, xf, dc, db4)
+    cross((xf, z1 | x))
+    cross((dc, far | x | y))
+    cross((db4, jnp.where(within, -1, z2 | x | y)))
+    return found
+
+
+def window(payload, need):
     groups, width = lax.axis_size("row"), lax.axis_size("col")
     count = groups * width
     size = payload.shape[0]
@@ -40,24 +75,23 @@
     here = lax.axis_index("row") * width + column
     pieces, offsets = [], []
     if (groups, width) == (4, 8):
-        for mask, arrays in sorted(cube(payload, count, half).items()):
-            start = 0
-            for array in arrays:
-                pieces.append((array, 1, start))
-                offsets.append((((here ^ mask) - here + count // 2) % count - count // 2)[None])
-                start += array.shape[0]
+        for array, masks in cube(payload, count, here):
+            pieces.append((array, len(masks)))
+            for mask in masks:
+                offset = ((here ^ mask) - here + count // 2) % count - count // 2
+                offsets.append(jnp.where(mask >= 0, offset, need + 1)[None])
     else:
         block = lax.all_gather(payload, "col", axis=0, tiled=True)
-        pieces.append((block, width, 0))
+        pieces.append((block, width))
         offsets.append(jnp.arange(width, dtype=jnp.int32) - column)
         for hop in range(1, -(-need // width) + 1):
             part = min(width, need - (hop - 1) * width)
             up = [(g, (g + hop) % groups) for g in range(groups)]
             down = [(g, (g - hop) % groups) for g in range(groups)]
             steps = jnp.arange(part, dtype=jnp.int32) - column
-            pieces.append((lax.ppermute(block[(width - part) * size :], "row", up), part, 0))
+            pieces.append((lax.ppermute(block[(width - part) * size :], "row", up), part))
             offsets.append(steps - (hop - 1) * width - part)
-            pieces.append((lax.ppermute(block[: part * size], "row", down), part, 0))
+            pieces.append((lax.ppermute(block[: part * size], "row", down), part))
             offsets.append(steps + hop * width)
     offsets = jnp.concatenate(offsets).astype(jnp.int32)
     return pieces, jnp.where(jnp.abs(offsets) <= need, offsets + need, -1)
@@ -76,13 +110,11 @@
         return pl.ds(first if isinstance(first, int) else pl.multiple_of(first, edge), n * edge)
 
     base = 0
-    for table, (number, start) in zip(tables, layout):
-        held = table.shape[0] // number
-        first, last = start // edge, min((start + held) // edge, slots)
-
-        def fetch(j, carry, table=table, base=base, start=start, held=held, first=first, last=last):
+    for table, number in zip(tables, layout):
+
+        def fetch(j, carry, table=table, base=base):
             k = place[base + j]
-            begin = j * held - start
+            begin = j * size
 
             @pl.when(k >= 0)
             def _():
@@ -94,17 +126,13 @@
                     ).start()
                     return carry
 
-                lax.fori_loop(first, last, block, 0)
-
-                if start + held == size:
-
-                    @pl.when((k >= reach) & (k <= 3 * reach))
-                    def _():
-                        pltpu.make_async_copy(
-                            table.at[pl.ds(pl.multiple_of(begin + slots * edge, 16), NOTE)],
-                            notes.at[k - reach],
-                            noted,
-                        ).start()
+                lax.fori_loop(0, slots, block, 0)
+
+                @pl.when((k >= reach) & (k <= 3 * reach))
+                def _():
+                    pltpu.make_async_copy(
+                        table.at[pl.ds(pl.multiple_of(begin + slots * edge, 16), NOTE)], notes.at[k - reach], noted
+                    ).start()
 
             return carry
 
@@ -213,10 +241,9 @@
     masked = density[0] * pattern[0][:, None, None].astype(density.dtype)
     note = jnp.zeros((NOTE, edge), density.dtype).at[0, :wide].set(filter_mask[0].astype(density.dtype))
     payload = jnp.concatenate([masked.reshape(slots * edge, edge), note], axis=0)
-    half = -(-slots // 2) * edge
-    pieces, place = window(payload, far, half)
-    tables = [array for array, _, _ in pieces]
-    layout = [(number, start) for _, number, start in pieces]
+    pieces, place = window(payload, far)
+    tables = [array for array, _ in pieces]
+    layout = [number for _, number in pieces]
     smem = pl.BlockSpec(memory_space=pltpu.SMEM)
     result = pl.pallas_call(
         functools.partial(purify, reach, edge, layout),

time: 142 us -> 134 us (0.944)
  waiting for transfers between devices: 80.4 us -> 65.2 us
  starting transfers between devices: 24.2 us -> 28.5 us
  other arithmetic: 2.6 us -> 6.22 us
    ppermute x39 -> x20, waiting for transfers between devices: 80.4 us -> 48.2 us  [swap(): return lax.ppermute(value, AXES, [(i, i ^ mask) for i in range(count)])]
    ppermute x0 -> x6, waiting for transfers between devices: none -> 17.1 us  [the longest x3 17 us: outward(): lax.ppermute(value, AXES, [(i, i ^ z1) for i in range(count) if inner(i)])]
    ppermute x0 -> x6, starting transfers between devices: none -> 7.45 us  [the longest x3 3.85 us: outward(): lax.ppermute(value, AXES, [(i, i ^ z1) for i in range(count) if inner(i)])]
    ppermute x39 -> x20, starting transfers between devices: 24.2 us -> 21 us  [swap(): return lax.ppermute(value, AXES, [(i, i ^ mask) for i in range(count)])]
    concatenate x0 -> x4, other arithmetic: none -> 1.78 us  [cross(): jnp.concatenate(arrays, axis=0)]
    unnamed x68 -> x36, local copies, waits for them, and re-layouts: 3.35 us -> 2.96 us
  transfers between devices with their start and end apart: 39 -> 26, of which waited for: 15 -> 16; matrix products, arithmetic and copies ran while one was open for 1% -> 1% of each run, Pallas kernels for 0% -> 0%
where the time goes in v5:
time: 134 us
  waiting for transfers between devices  65.2 us (49%)
  Pallas kernels  29.7 us (22%)
  starting transfers between devices  28.5 us (21%)
  other arithmetic  6.22 us (5%)
  local copies, waits for them, and re-layouts  3.14 us (2%)
    ppermute x20, waiting for transfers between devices, swap(): return lax.ppermute(value, AXES, [(i, i ^ mask) for i in range(count)])  48.2 us
    pallas_call x1, Pallas kernels, shards(): pl.pallas_call(functools.partial(purify, reach, edge, layout), out_shape=...  29.7 us
    ppermute x20, starting transfers between devices, swap(): return lax.ppermute(value, AXES, [(i, i ^ mask) for i in range(count)])  21 us
    ppermute x3, waiting for transfers between devices, outward(): lax.ppermute(value, AXES, [(i, i ^ z1) for i in range(count) if inner(i)])  17 us
    ppermute x3, starting transfers between devices, outward(): lax.ppermute(value, AXES, [(i, i ^ z1) for i in range(count) if inner(i)])  3.85 us
    ppermute x3, starting transfers between devices, middle(): lax.ppermute(value, AXES, [(i, i ^ z3) for i in range(count) if inner(i)])  3.59 us
    unnamed x36, local copies, waits for them, and re-layouts  2.96 us
  transfers between devices with their start and end apart: 26, of which 16 were waited for; matrix products, arithmetic and copies ran while one was open for 1% of the time, Pallas kernels for 0%

profile of v5, /device:TPU:0, one launch (start us, length us, event | category | flops | bytes accessed | tf_op | source)
XLA Modules:
  0.0 133.8 jit_solution(333716201728129771)
XLA Ops:
  1.4 1.3 %bitcast_multiply_fusion = bf16[1920,128]{1,0:T(8,128)(2,1)S(1)} fusion(bf16[1,15,128,128]{3,2,1,0:T(8,128)(2,1)} %param.5, bf16[1920]{0:T(1024)(128)(2,1)S(1)} %broadcast_bitcast_fusion), kind=kLoop, calls=%fused_computation.9 | loop fusion | flops 245760 | bytes 986880 | tf_op jit(solution)/shard_map/mul | solution.py:241
  2.8 1.4 %collective-permute-start.4 = (bf16[1936,128]{1,0:T(8,128)(2,1)S(1)}, bf16[1936,128]{1,0:T(8,128)(2,1)}, u32[]{:S(2)}, u32[]{:S(2)}) collective-permute-start(bf16[1936,128]{1,0:T(8,128)(2,1)S(1)} %fusion.1.refs_0_), channel_id=1, source_target_pairs={{2,4},{3,5},{4,2},{5,3},{10,12},{11,13},{12,10},{13,11},{18,20},{1... | collective-permute-start | bytes 1486856 | tf_op jit(solution)/shard_map/ppermute | solution.py:24
  4.2 5.1 %collective-permute-start.3 = (bf16[1936,128]{1,0:T(8,128)(2,1)S(1)}, bf16[1936,128]{1,0:T(8,128)(2,1)S(1)}, u32[]{:S(2)}, u32[]{:S(2)}) collective-permute-start(bf16[1936,128]{1,0:T(8,128)(2,1)S(1)} %fusion.1.refs_0_), channel_id=1, source_target_pairs={{0,2},{1,3},{2,0},{3,1},{4,6},{5,7},{6,4},{7,5},{8,10},{9,11},{10,... | collective-permute-start | bytes 1486856 | tf_op jit(solution)/shard_map/ppermute | solution.py:21
  9.4 1.5 %collective-permute-start.2 = (bf16[1936,128]{1,0:T(8,128)(2,1)S(1)}, bf16[1936,128]{1,0:T(8,128)(2,1)S(1)}, u32[]{:S(2)}, u32[]{:S(2)}) collective-permute-start(bf16[1936,128]{1,0:T(8,128)(2,1)S(1)} %fusion.1.refs_0_), channel_id=1, source_target_pairs={{0,16},{1,17},{2,18},{3,19},{4,20},{5,21},{6,22},{7,23},{8,24},{9,... | collective-permute-start | bytes 1486856 | tf_op jit(solution)/shard_map/ppermute | solution.py:21
  10.9 1.5 %collective-permute-start.1 = (bf16[1936,128]{1,0:T(8,128)(2,1)S(1)}, bf16[1936,128]{1,0:T(8,128)(2,1)S(1)}, u32[]{:S(2)}, u32[]{:S(2)}) collective-permute-start(bf16[1936,128]{1,0:T(8,128)(2,1)S(1)} %fusion.1.refs_0_), channel_id=1, source_target_pairs={{0,1},{1,0},{2,3},{3,2},{4,5},{5,4},{6,7},{7,6},{8,9},{9,8},{10,11... | collective-permute-start | bytes 1486856 | tf_op jit(solution)/shard_map/ppermute | solution.py:21
  12.4 8.0 %collective-permute-done.3.refs_4_ = bf16[1936,128]{1,0:T(8,128)(2,1)S(1)} collective-permute-done((bf16[1936,128]{1,0:T(8,128)(2,1)S(1)}, bf16[1936,128]{1,0:T(8,128)(2,1)S(1)}, u32[]{:S(2)}, u32[]{:S(2)}) %collective-permute-start.3) | collective-permute-done | bytes 495648 | tf_op jit(solution)/shard_map/ppermute | solution.py:21
  20.4 1.5 %collective-permute-done.2.refs_3_ = bf16[1936,128]{1,0:T(8,128)(2,1)S(1)} collective-permute-done((bf16[1936,128]{1,0:T(8,128)(2,1)S(1)}, bf16[1936,128]{1,0:T(8,128)(2,1)S(1)}, u32[]{:S(2)}, u32[]{:S(2)}) %collective-permute-start.2) | collective-permute-done | bytes 495648 | tf_op jit(solution)/shard_map/ppermute | solution.py:21
  23.3 1.3 collective-permute-start.9
  24.6 1.6 %collective-permute-start.6 = (bf16[1936,128]{1,0:T(8,128)(2,1)S(1)}, bf16[1936,128]{1,0:T(8,128)(2,1)}, u32[]{:S(2)}, u32[]{:S(2)}) collective-permute-start(bf16[1936,128]{1,0:T(8,128)(2,1)S(1)} %collective-permute-done.2.refs_3_), channel_id=1, source_target_pairs={{0,1},{1,0},{2,3},{3,2},{4,5},{5,4},{6,7},{7,6},{8,9},{9,8},{10,11... | collective-permute-start | bytes 1486856 | tf_op jit(solution)/shard_map/ppermute | solution.py:21
  26.2 1.5 %collective-permute-start.8 = (bf16[1936,128]{1,0:T(8,128)(2,1)S(1)}, bf16[1936,128]{1,0:T(8,128)(2,1)}, u32[]{:S(2)}, u32[]{:S(2)}) collective-permute-start(bf16[1936,128]{1,0:T(8,128)(2,1)S(1)} %collective-permute-done.3.refs_4_), channel_id=1, source_target_pairs={{2,4},{3,5},{4,2},{5,3},{10,12},{11,13},{12,10},{13,11},{18,20},{1... | collective-permute-start | bytes 1486856 | tf_op jit(solution)/shard_map/ppermute | solution.py:24
  28.1 11.1 %collective-permute-done.9 = bf16[1936,128]{1,0:T(8,128)(2,1)} collective-permute-done((bf16[1936,128]{1,0:T(8,128)(2,1)}, bf16[1936,128]{1,0:T(8,128)(2,1)}, u32[]{:S(2)}, u32[]{:S(2)}) %collective-permute-start.9) | collective-permute-done | bytes 495648 | tf_op jit(solution)/shard_map/ppermute | solution.py:27
  39.2 1.9 %collective-permute-done.7.refs_7_ = bf16[1936,128]{1,0:T(8,128)(2,1)} collective-permute-done((bf16[1936,128]{1,0:T(8,128)(2,1)S(1)}, bf16[1936,128]{1,0:T(8,128)(2,1)}, u32[]{:S(2)}, u32[]{:S(2)}) %collective-permute-start.7) | collective-permute-done | bytes 495648 | tf_op jit(solution)/shard_map/ppermute | solution.py:21
  42.3 1.5 %pad_maximum_fusion.2 = bf16[5808,128]{1,0:T(8,128)(2,1)S(1)} fusion(bf16[1936,128]{1,0:T(8,128)(2,1)S(1)} %broadcast_select_fusion.1.refs_8_, bf16[1936,128]{1,0:T(8,128)(2,1)} %collective-permute-done.7.refs_7_, bf16[1936,128]{1,0:T(8,128)(2,1)} %collective-permute-done.6.refs_6_), kind=kLoop, calls=%fused_computation.2 | loop fusion | flops 4460544 | bytes 2973696 | tf_op jit(solution)/shard_map/concatenate | solution.py:38
  46.9 10.6 %collective-permute-done.12.refs_11_ = bf16[1936,128]{1,0:T(8,128)(2,1)S(1)} collective-permute-done((bf16[1936,128]{1,0:T(8,128)(2,1)S(1)}, bf16[1936,128]{1,0:T(8,128)(2,1)S(1)}, u32[]{:S(2)}, u32[]{:S(2)}) %collective-permute-start.12) | collective-permute-done | bytes 495648 | tf_op jit(solution)/shard_map/ppermute | solution.py:21
  57.8 3.7 %collective-permute-done.13 = bf16[1936,128]{1,0:T(8,128)(2,1)S(1)} collective-permute-done((bf16[1936,128]{1,0:T(8,128)(2,1)}, bf16[1936,128]{1,0:T(8,128)(2,1)S(1)}, u32[]{:S(2)}, u32[]{:S(2)}) %collective-permute-start.13) | collective-permute-done | bytes 495648 | tf_op jit(solution)/shard_map/ppermute | solution.py:27
  63.0 1.6 %collective-permute-start.17 = (bf16[1936,128]{1,0:T(8,128)(2,1)S(1)}, bf16[1936,128]{1,0:T(8,128)(2,1)S(1)}, u32[]{:S(2)}, u32[]{:S(2)}) collective-permute-start(bf16[1936,128]{1,0:T(8,128)(2,1)S(1)} %broadcast_select_fusion.refs_12_), channel_id=1, source_target_pairs={{0,16},{1,17},{2,18},{3,19},{4,20},{5,21},{6,22},{7,23},{8,24},{9,... | collective-permute-start | bytes 1486856 | tf_op jit(solution)/shard_map/ppermute | solution.py:21
  64.6 1.5 %collective-permute-start.16 = (bf16[1936,128]{1,0:T(8,128)(2,1)S(1)}, bf16[1936,128]{1,0:T(8,128)(2,1)S(1)}, u32[]{:S(2)}, u32[]{:S(2)}) collective-permute-start(bf16[1936,128]{1,0:T(8,128)(2,1)S(1)} %broadcast_select_fusion.refs_12_), channel_id=1, source_target_pairs={{0,1},{1,0},{2,3},{3,2},{4,5},{5,4},{6,7},{7,6},{8,9},{9,8},{10,11... | collective-permute-start | bytes 1486856 | tf_op jit(solution)/shard_map/ppermute | solution.py:21
  66.0 4.7 %collective-permute-start.18 = (bf16[1936,128]{1,0:T(8,128)(2,1)}, bf16[1936,128]{1,0:T(8,128)(2,1)S(1)}, u32[]{:S(2)}, u32[]{:S(2)}) collective-permute-start(bf16[1936,128]{1,0:T(8,128)(2,1)} %collective-permute-done.6.refs_6_), channel_id=1, source_target_pairs={{0,2},{1,3},{2,0},{3,1},{4,6},{5,7},{6,4},{7,5},{8,10},{9,11},{10,... | collective-permute-start | bytes 1486856 | tf_op jit(solution)/shard_map/ppermute | solution.py:21
  70.8 5.9 %collective-permute-done.17.refs_15_ = bf16[1936,128]{1,0:T(8,128)(2,1)S(1)} collective-permute-done((bf16[1936,128]{1,0:T(8,128)(2,1)S(1)}, bf16[1936,128]{1,0:T(8,128)(2,1)S(1)}, u32[]{:S(2)}, u32[]{:S(2)}) %collective-permute-start.17) | collective-permute-done | bytes 495648 | tf_op jit(solution)/shard_map/ppermute | solution.py:21
  77.9 4.4 %collective-permute-done.18.refs_16_ = bf16[1936,128]{1,0:T(8,128)(2,1)S(1)} collective-permute-done((bf16[1936,128]{1,0:T(8,128)(2,1)}, bf16[1936,128]{1,0:T(8,128)(2,1)S(1)}, u32[]{:S(2)}, u32[]{:S(2)}) %collective-permute-start.18) | collective-permute-done | bytes 495648 | tf_op jit(solution)/shard_map/ppermute | solution.py:21
  85.0 11.3 %collective-permute-done.20.refs_19_ = bf16[1936,128]{1,0:T(8,128)(2,1)S(1)} collective-permute-done((bf16[1936,128]{1,0:T(8,128)(2,1)S(1)}, bf16[1936,128]{1,0:T(8,128)(2,1)S(1)}, u32[]{:S(2)}, u32[]{:S(2)}) %collective-permute-start.20) | collective-permute-done | bytes 495648 | tf_op jit(solution)/shard_map/ppermute | solution.py:21
  96.5 2.2 %collective-permute-done.22.refs_23_ = bf16[1936,128]{1,0:T(8,128)(2,1)} collective-permute-done((bf16[1936,128]{1,0:T(8,128)(2,1)S(1)}, bf16[1936,128]{1,0:T(8,128)(2,1)}, u32[]{:S(2)}, u32[]{:S(2)}) %collective-permute-start.22) | collective-permute-done | bytes 495648 | tf_op jit(solution)/shard_map/ppermute | solution.py:27
  98.8 1.3 copy-done.12
  104.1 29.7 %shard_map.37 = bf16[29,128,128]{2,1,0:T(8,128)(2,1)} custom-call(s32[34]{0:T(128)} %compare_select_fusion.place, bf16[1936,128]{1,0:T(8,128)(2,1)} %copy-done.2, bf16[1936,128]{1,0:T(8,128)(2,1)} %collective-permute-done.refs_1_, bf16[1936,128]{1,0:T(8,128)(2,1)} %copy-done.5, bf16[1936,128]{1,0:T(8,128)(2,1)} %copy-done.4, bf16[1936,128]{1,0:T(8,128)(2,1)} %copy-done.3, ...), custom_call_target="tpu_custom_call" | custom-call | flops 16999999488 | bytes 15728640 | tf_op jit(solution)/shard_map/pallas_call | solution.py:248
  (78 shorter events, 16.5 us)
Async XLA Ops:
  2.8 9.6 %collective-permute-start.4 = (bf16[1936,128]{1,0:T(8,128)(2,1)S(1)}, bf16[1936,128]{1,0:T(8,128)(2,1)}, u32[]{:S(2)}, u32[]{:S(2)}) collective-permute-start(bf16[1936,128]{1,0:T(8,128)(2,1)S(1)} %fusion.1.refs_0_), channel_id=1, source_target_pairs={{2,4},{3,5},{4,2},{5,3},{10,12},{11,13},{12,10},{13,11},{18,20},{1... | collective-permute-start | bytes 1486856 | tf_op jit(solution)/shard_map/ppermute | solution.py:24
  4.2 16.2 %collective-permute-start.3 = (bf16[1936,128]{1,0:T(8,128)(2,1)S(1)}, bf16[1936,128]{1,0:T(8,128)(2,1)S(1)}, u32[]{:S(2)}, u32[]{:S(2)}) collective-permute-start(bf16[1936,128]{1,0:T(8,128)(2,1)S(1)} %fusion.1.refs_0_), channel_id=1, source_target_pairs={{0,2},{1,3},{2,0},{3,1},{4,6},{5,7},{6,4},{7,5},{8,10},{9,11},{10,... | collective-permute-start | bytes 1486856 | tf_op jit(solution)/shard_map/ppermute | solution.py:21
  9.4 12.5 %collective-permute-start.2 = (bf16[1936,128]{1,0:T(8,128)(2,1)S(1)}, bf16[1936,128]{1,0:T(8,128)(2,1)S(1)}, u32[]{:S(2)}, u32[]{:S(2)}) collective-permute-start(bf16[1936,128]{1,0:T(8,128)(2,1)S(1)} %fusion.1.refs_0_), channel_id=1, source_target_pairs={{0,16},{1,17},{2,18},{3,19},{4,20},{5,21},{6,22},{7,23},{8,24},{9,... | collective-permute-start | bytes 1486856 | tf_op jit(solution)/shard_map/ppermute | solution.py:21
  10.9 12.2 %collective-permute-start.1 = (bf16[1936,128]{1,0:T(8,128)(2,1)S(1)}, bf16[1936,128]{1,0:T(8,128)(2,1)S(1)}, u32[]{:S(2)}, u32[]{:S(2)}) collective-permute-start(bf16[1936,128]{1,0:T(8,128)(2,1)S(1)} %fusion.1.refs_0_), channel_id=1, source_target_pairs={{0,1},{1,0},{2,3},{3,2},{4,5},{5,4},{6,7},{7,6},{8,9},{9,8},{10,11... | collective-permute-start | bytes 1486856 | tf_op jit(solution)/shard_map/ppermute | solution.py:21
  12.4 10.7 %collective-permute-start = (bf16[1936,128]{1,0:T(8,128)(2,1)S(1)}, bf16[1936,128]{1,0:T(8,128)(2,1)}, u32[]{:S(2)}, u32[]{:S(2)}) collective-permute-start(bf16[1936,128]{1,0:T(8,128)(2,1)S(1)} %fusion.1.refs_0_), channel_id=1, source_target_pairs={{0,8},{1,9},{2,10},{3,11},{4,12},{5,13},{6,14},{7,15},{8,0},{9,1},... | collective-permute-start | bytes 1486856 | tf_op jit(solution)/shard_map/ppermute | solution.py:21
  23.2 17.9 %collective-permute-start.5 = (bf16[5808,128]{1,0:T(8,128)(2,1)S(1)}, bf16[5808,128]{1,0:T(8,128)(2,1)}, u32[]{:S(2)}, u32[]{:S(2)}) collective-permute-start(bf16[5808,128]{1,0:T(8,128)(2,1)S(1)} %pad_maximum_fusion.1), channel_id=1, source_target_pairs={{0,8},{1,9},{2,10},{3,11},{4,12},{5,13},{6,14},{7,15},{8,0},{9,1},... | collective-permute-start | bytes 4460552 | tf_op jit(solution)/shard_map/ppermute | solution.py:21
  23.3 15.9 %collective-permute-start.9 = (bf16[1936,128]{1,0:T(8,128)(2,1)}, bf16[1936,128]{1,0:T(8,128)(2,1)}, u32[]{:S(2)}, u32[]{:S(2)}) collective-permute-start(bf16[1936,128]{1,0:T(8,128)(2,1)} %collective-permute-done.4), channel_id=1, source_target_pairs={{2,0},{3,1},{4,6},{5,7},{10,8},{11,9},{12,14},{13,15},{18,16},{19,... | collective-permute-start | bytes 1486856 | tf_op jit(solution)/shard_map/ppermute | solution.py:27
  24.6 14.6 %collective-permute-start.6 = (bf16[1936,128]{1,0:T(8,128)(2,1)S(1)}, bf16[1936,128]{1,0:T(8,128)(2,1)}, u32[]{:S(2)}, u32[]{:S(2)}) collective-permute-start(bf16[1936,128]{1,0:T(8,128)(2,1)S(1)} %collective-permute-done.2.refs_3_), channel_id=1, source_target_pairs={{0,1},{1,0},{2,3},{3,2},{4,5},{5,4},{6,7},{7,6},{8,9},{9,8},{10,11... | collective-permute-start | bytes 1486856 | tf_op jit(solution)/shard_map/ppermute | solution.py:21
  26.2 13.1 %collective-permute-start.8 = (bf16[1936,128]{1,0:T(8,128)(2,1)S(1)}, bf16[1936,128]{1,0:T(8,128)(2,1)}, u32[]{:S(2)}, u32[]{:S(2)}) collective-permute-start(bf16[1936,128]{1,0:T(8,128)(2,1)S(1)} %collective-permute-done.3.refs_4_), channel_id=1, source_target_pairs={{2,4},{3,5},{4,2},{5,3},{10,12},{11,13},{12,10},{13,11},{18,20},{1... | collective-permute-start | bytes 1486856 | tf_op jit(solution)/shard_map/ppermute | solution.py:24
  27.6 13.5 %collective-permute-start.7 = (bf16[1936,128]{1,0:T(8,128)(2,1)S(1)}, bf16[1936,128]{1,0:T(8,128)(2,1)}, u32[]{:S(2)}, u32[]{:S(2)}) collective-permute-start(bf16[1936,128]{1,0:T(8,128)(2,1)S(1)} %collective-permute-done.3.refs_4_), channel_id=1, source_target_pairs={{0,16},{1,17},{2,18},{3,19},{4,20},{5,21},{6,22},{7,23},{8,24},{9,... | collective-permute-start | bytes 1486856 | tf_op jit(solution)/shard_map/ppermute | solution.py:21
  43.7 17.8 %collective-permute-start.10 = (bf16[5808,128]{1,0:T(8,128)(2,1)S(1)}, bf16[5808,128]{1,0:T(8,128)(2,1)S(1)}, u32[]{:S(2)}, u32[]{:S(2)}) collective-permute-start(bf16[5808,128]{1,0:T(8,128)(2,1)S(1)} %pad_maximum_fusion.2), channel_id=1, source_target_pairs={{0,8},{1,9},{2,10},{3,11},{4,12},{5,13},{6,14},{7,15},{8,0},{9,1},... | collective-permute-start | bytes 4460552 | tf_op jit(solution)/shard_map/ppermute | solution.py:21
  43.8 13.7 %collective-permute-start.12 = (bf16[1936,128]{1,0:T(8,128)(2,1)S(1)}, bf16[1936,128]{1,0:T(8,128)(2,1)S(1)}, u32[]{:S(2)}, u32[]{:S(2)}) collective-permute-start(bf16[1936,128]{1,0:T(8,128)(2,1)S(1)} %broadcast_select_fusion.1.refs_8_), channel_id=1, source_target_pairs={{0,16},{1,17},{2,18},{3,19},{4,20},{5,21},{6,22},{7,23},{8,24},{9,... | collective-permute-start | bytes 1486856 | tf_op jit(solution)/shard_map/ppermute | solution.py:21
  44.4 13.4 %collective-permute-start.11 = (bf16[1936,128]{1,0:T(8,128)(2,1)S(1)}, bf16[1936,128]{1,0:T(8,128)(2,1)S(1)}, u32[]{:S(2)}, u32[]{:S(2)}) collective-permute-start(bf16[1936,128]{1,0:T(8,128)(2,1)S(1)} %broadcast_select_fusion.1.refs_8_), channel_id=1, source_target_pairs={{0,1},{1,0},{2,3},{3,2},{4,5},{5,4},{6,7},{7,6},{8,9},{9,8},{10,11... | collective-permute-start | bytes 1486856 | tf_op jit(solution)/shard_map/ppermute | solution.py:21
  44.9 16.6 %collective-permute-start.13 = (bf16[1936,128]{1,0:T(8,128)(2,1)}, bf16[1936,128]{1,0:T(8,128)(2,1)S(1)}, u32[]{:S(2)}, u32[]{:S(2)}) collective-permute-start(bf16[1936,128]{1,0:T(8,128)(2,1)} %collective-permute-done.8), channel_id=1, source_target_pairs={{2,0},{3,1},{4,6},{5,7},{10,8},{11,9},{12,14},{13,15},{18,16},{19,... | collective-permute-start | bytes 1486856 | tf_op jit(solution)/shard_map/ppermute | solution.py:27
  46.2 15.3 %collective-permute-start.14 = (bf16[1936,128]{1,0:T(8,128)(2,1)}, bf16[1936,128]{1,0:T(8,128)(2,1)S(1)}, u32[]{:S(2)}, u32[]{:S(2)}) collective-permute-start(bf16[1936,128]{1,0:T(8,128)(2,1)} %collective-permute-done.6.refs_6_), channel_id=1, source_target_pairs={{2,4},{3,5},{4,2},{5,3},{10,12},{11,13},{12,10},{13,11},{18,20},{1... | collective-permute-start | bytes 1486856 | tf_op jit(solution)/shard_map/ppermute | solution.py:24
  62.9 19.4 %collective-permute-start.15 = (bf16[5808,128]{1,0:T(8,128)(2,1)S(1)}, bf16[5808,128]{1,0:T(8,128)(2,1)}, u32[]{:S(2)}, u32[]{:S(2)}) collective-permute-start(bf16[5808,128]{1,0:T(8,128)(2,1)S(1)} %pad_maximum_fusion.3), channel_id=1, source_target_pairs={{0,8},{1,9},{2,10},{3,11},{4,12},{5,13},{6,14},{7,15},{8,0},{9,1},... | collective-permute-start | bytes 4460552 | tf_op jit(solution)/shard_map/ppermute | solution.py:21
  63.0 13.7 %collective-permute-start.17 = (bf16[1936,128]{1,0:T(8,128)(2,1)S(1)}, bf16[1936,128]{1,0:T(8,128)(2,1)S(1)}, u32[]{:S(2)}, u32[]{:S(2)}) collective-permute-start(bf16[1936,128]{1,0:T(8,128)(2,1)S(1)} %broadcast_select_fusion.refs_12_), channel_id=1, source_target_pairs={{0,16},{1,17},{2,18},{3,19},{4,20},{5,21},{6,22},{7,23},{8,24},{9,... | collective-permute-start | bytes 1486856 | tf_op jit(solution)/shard_map/ppermute | solution.py:21
  64.6 13.4 %collective-permute-start.16 = (bf16[1936,128]{1,0:T(8,128)(2,1)S(1)}, bf16[1936,128]{1,0:T(8,128)(2,1)S(1)}, u32[]{:S(2)}, u32[]{:S(2)}) collective-permute-start(bf16[1936,128]{1,0:T(8,128)(2,1)S(1)} %broadcast_select_fusion.refs_12_), channel_id=1, source_target_pairs={{0,1},{1,0},{2,3},{3,2},{4,5},{5,4},{6,7},{7,6},{8,9},{9,8},{10,11... | collective-permute-start | bytes 1486856 | tf_op jit(solution)/shard_map/ppermute | solution.py:21
  66.0 16.3 %collective-permute-start.18 = (bf16[1936,128]{1,0:T(8,128)(2,1)}, bf16[1936,128]{1,0:T(8,128)(2,1)S(1)}, u32[]{:S(2)}, u32[]{:S(2)}) collective-permute-start(bf16[1936,128]{1,0:T(8,128)(2,1)} %collective-permute-done.6.refs_6_), channel_id=1, source_target_pairs={{0,2},{1,3},{2,0},{3,1},{4,6},{5,7},{6,4},{7,5},{8,10},{9,11},{10,... | collective-permute-start | bytes 1486856 | tf_op jit(solution)/shard_map/ppermute | solution.py:21
  82.5 16.3 %collective-permute-start.19 = (bf16[7744,128]{1,0:T(8,128)(2,1)S(1)}, bf16[7744,128]{1,0:T(8,128)(2,1)S(1)}, u32[]{:S(2)}, u32[]{:S(2)}) collective-permute-start(bf16[7744,128]{1,0:T(8,128)(2,1)S(1)} %pad_maximum_fusion), channel_id=1, source_target_pairs={{0,8},{1,9},{2,10},{3,11},{4,12},{5,13},{6,14},{7,15},{8,0},{9,1},... | collective-permute-start | bytes 5947400 | tf_op jit(solution)/shard_map/ppermute | solution.py:21
  82.6 13.7 %collective-permute-start.20 = (bf16[1936,128]{1,0:T(8,128)(2,1)S(1)}, bf16[1936,128]{1,0:T(8,128)(2,1)S(1)}, u32[]{:S(2)}, u32[]{:S(2)}) collective-permute-start(bf16[1936,128]{1,0:T(8,128)(2,1)S(1)} %collective-permute-done.3.refs_4_), channel_id=1, source_target_pairs={{0,1},{1,0},{2,3},{3,2},{4,5},{5,4},{6,7},{7,6},{8,9},{9,8},{10,11... | collective-permute-start | bytes 1486856 | tf_op jit(solution)/shard_map/ppermute | solution.py:21
  83.2 13.4 %collective-permute-start.21 = (bf16[1936,128]{1,0:T(8,128)(2,1)S(1)}, bf16[1936,128]{1,0:T(8,128)(2,1)S(1)}, u32[]{:S(2)}, u32[]{:S(2)}) collective-permute-start(bf16[1936,128]{1,0:T(8,128)(2,1)S(1)} %collective-permute-done.16.refs_14_), channel_id=1, source_target_pairs={{0,16},{1,17},{2,18},{3,19},{4,20},{5,21},{6,22},{7,23},{8,24},{9,... | collective-permute-start | bytes 1486856 | tf_op jit(solution)/shard_map/ppermute | solution.py:21
  83.7 15.1 %collective-permute-start.22 = (bf16[1936,128]{1,0:T(8,128)(2,1)S(1)}, bf16[1936,128]{1,0:T(8,128)(2,1)}, u32[]{:S(2)}, u32[]{:S(2)}) collective-permute-start(bf16[1936,128]{1,0:T(8,128)(2,1)S(1)} %collective-permute-done.14.refs_17_), channel_id=1, source_target_pairs={{2,0},{3,1},{4,6},{5,7},{10,8},{11,9},{12,14},{13,15},{18,16},{19,... | collective-permute-start | bytes 1486856 | tf_op jit(solution)/shard_map/ppermute | solution.py:27
  100.1 3.3 %collective-permute-start.24 = (bf16[1936,128]{1,0:T(8,128)(2,1)S(1)}, bf16[1936,128]{1,0:T(8,128)(2,1)S(1)}, u32[]{:S(2)}, u32[]{:S(2)}) collective-permute-start(bf16[1936,128]{1,0:T(8,128)(2,1)S(1)} %collective-permute-done.21.refs_21_), channel_id=1, source_target_pairs={{0,8},{1,9},{2,10},{3,11},{4,12},{5,13},{6,14},{7,15},{8,0},{9,1},... | collective-permute-start | bytes 1486856 | tf_op jit(solution)/shard_map/ppermute | solution.py:21
  (20 other events, 303.3 us)

commit v6 on v5

--- a/solution.py
+++ b/solution.py
@@ -32,9 +32,10 @@
     found = []
 
     def cross(*rows):
+        rows = [(array, mask if isinstance(mask, tuple) else (mask,)) for array, mask in rows]
         arrays = [array for array, _ in rows]
-        masks = [mask for _, mask in rows]
-        found.extend((array, [mask]) for array, mask in rows)
+        masks = [mask for _, group in rows for mask in group]
+        found.extend(rows)
         batch = swap(jnp.concatenate(arrays, axis=0) if len(arrays) > 1 else arrays[0], core)
         found.append((batch, [jnp.where(mask >= 0, mask | core, -1) for mask in masks]))
         return len(found) - 1
@@ -44,26 +45,32 @@
         found[spot] = (batch, found[spot][1])
         return arrays
 
-    x0, y0, f, b2 = swap(own, x), swap(own, y), swap(own, z1), middle(own)
-    spot = cross((own, 0))
-    x0, y0, f, b2 = finish(spot, x0, y0, f, b2)
-    d0, yf, c3, b4 = swap(y0, x), swap(f, y), middle(f), outward(b2)
-    spot = cross((x0, x), (y0, y), (f, z1))
-    d0, yf, c3, b4, b2, f = finish(spot, d0, yf, c3, b4, b2, f)
+    x0, y0, d0, f, b2 = swap(own, x), swap(own, y), swap(own, x | y), swap(own, z1), middle(own)
+    f, b2 = both((f, b2))
+    c3, b4 = middle(f), outward(b2)
+    own, x0, y0, d0, f, b2, c3, b4 = both((own, x0, y0, d0, f, b2, c3, b4))
     b = jnp.where(within, b2, b4)
-    xb, yb, c5, db2 = swap(b, x), swap(b, y), outward(c3), middle(d0)
-    spot = cross((d0, x | y), (yf, z1 | y), (b, near))
-    xb, yb, c5, db2, c3, d0, f = finish(spot, xb, yb, c5, db2, c3, d0, f)
-    c = jnp.where(within, c3, c5)
-    xc, yc, df = swap(c, x), swap(c, y), swap(d0, z1)
-    spot = cross((xb, near | x), (yb, near | y), (c, far))
-    xc, yc, df, f, db2 = finish(spot, xc, yc, df, f, db2)
-    xf, dc, db4 = swap(f, x), swap(xc, y), outward(db2)
-    spot = cross((xc, far | x), (yc, far | y), (df, z1 | x | y), (db2, jnp.where(within, z3 | x | y, -1)))
-    xf, dc, db4 = finish(spot, xf, dc, db4)
-    cross((xf, z1 | x))
-    cross((dc, far | x | y))
-    cross((db4, jnp.where(within, -1, z2 | x | y)))
+    pair = jnp.concatenate([f, b], axis=0)
+    xfb, yfb, db2 = swap(pair, x), swap(pair, y), middle(d0)
+    across = swap(jnp.concatenate([c3, d0], axis=0), z1)
+    spot = cross((own, 0), (x0, x), (y0, y), (d0, x | y), (f, z1), (b, near))
+    xfb, yfb, db2, across = finish(spot, xfb, yfb, db2, across)
+    size = own.shape[0]
+    c, df = jnp.where(within, c3, across[:size]), across[size:]
+    xc, yc, db4 = swap(c, x), swap(c, y), outward(db2)
+    spot = cross(
+        (c, far),
+        (xfb, (z1 | x, near | x)),
+        (yfb, (z1 | y, near | y)),
+        (df, z1 | x | y),
+        (db2, jnp.where(within, z3 | x | y, -1)),
+    )
+    xc, yc, db4 = finish(spot, xc, yc, db4)
+    half = size // 2 // 16 * 16
+    first, second = swap(yc[:half], x), swap(xc[half:], y)
+    spots = [cross((xc, far | x)), cross((yc, far | y)), cross((db4, jnp.where(within, -1, z2 | x | y)))]
+    first, second = finish(spots[0], first, second)
+    cross((jnp.concatenate([first, second], axis=0), far | x | y))
     return found
 
 

time: 134 us -> 129 us (0.963)
  starting transfers between devices: 28.5 us -> 19.4 us
  waiting for transfers between devices: 65.2 us -> 67.9 us
  local copies, waits for them, and re-layouts: 3.14 us -> 5.19 us
  other arithmetic: 6.22 us -> 4.73 us
    ppermute x20 -> x17, waiting for transfers between devices: 48.2 us -> 60.2 us  [swap(): return lax.ppermute(value, AXES, [(i, i ^ mask) for i in range(count)])]
    ppermute x3 -> x2, waiting for transfers between devices: 17 us -> 7.73 us  [outward(): lax.ppermute(value, AXES, [(i, i ^ z1) for i in range(count) if inner(i)])]
    ppermute x20 -> x17, starting transfers between devices: 21 us -> 14.8 us  [swap(): return lax.ppermute(value, AXES, [(i, i ^ mask) for i in range(count)])]
    unnamed x36 -> x47, local copies, waits for them, and re-layouts: 2.96 us -> 4.87 us
    ppermute x3, starting transfers between devices: 3.59 us -> 2.06 us  [middle(): lax.ppermute(value, AXES, [(i, i ^ z3) for i in range(count) if inner(i)])]
    ppermute x3 -> x2, starting transfers between devices: 3.85 us -> 2.57 us  [outward(): lax.ppermute(value, AXES, [(i, i ^ z1) for i in range(count) if inner(i)])]
  transfers between devices with their start and end apart: 26 -> 22, of which waited for: 16 -> 12; matrix products, arithmetic and copies ran while one was open for 1% -> 1% of each run, Pallas kernels for 0% -> 0%
where the time goes in v6:
time: 129 us; the launch traced here: 128 us
  waiting for transfers between devices  67.9 us (53%)
  Pallas kernels  29.7 us (23%)
  starting transfers between devices  19.4 us (15%)
  local copies, waits for them, and re-layouts  5.19 us (4%)
  other arithmetic  4.73 us (4%)
    ppermute x17, waiting for transfers between devices, swap(): return lax.ppermute(value, AXES, [(i, i ^ mask) for i in range(count)])  60.2 us
    pallas_call x1, Pallas kernels, shards(): pl.pallas_call(functools.partial(purify, reach, edge, layout), out_shape=...  29.7 us
    ppermute x17, starting transfers between devices, swap(): return lax.ppermute(value, AXES, [(i, i ^ mask) for i in range(count)])  14.8 us
    ppermute x2, waiting for transfers between devices, outward(): lax.ppermute(value, AXES, [(i, i ^ z1) for i in range(count) if inner(i)])  7.73 us
    unnamed x47, local copies, waits for them, and re-layouts  4.87 us
  transfers between devices with their start and end apart: 22, of which 12 were waited for; matrix products, arithmetic and copies ran while one was open for 1% of the time, Pallas kernels for 0%

profile of v6, /device:TPU:0, one launch (start us, length us, event | category | flops | bytes accessed | tf_op | source)
XLA Modules:
  0.0 128.2 jit_solution(12952812983119091572)
XLA Ops:
  1.4 1.3 %bitcast_multiply_fusion = bf16[1920,128]{1,0:T(8,128)(2,1)S(1)} fusion(bf16[1,15,128,128]{3,2,1,0:T(8,128)(2,1)} %param.5, bf16[1920]{0:T(1024)(128)(2,1)S(1)} %broadcast_bitcast_fusion), kind=kLoop, calls=%fused_computation.7 | loop fusion | flops 245760 | bytes 986880 | tf_op jit(solution)/shard_map/mul | solution.py:248
  2.8 3.1 %collective-permute-start.3 = (bf16[1936,128]{1,0:T(8,128)(2,1)S(1)}, bf16[1936,128]{1,0:T(8,128)(2,1)S(1)}, u32[]{:S(2)}, u32[]{:S(2)}) collective-permute-start(bf16[1936,128]{1,0:T(8,128)(2,1)S(1)} %fusion.1.refs_0_), channel_id=1, source_target_pairs={{0,2},{1,3},{2,0},{3,1},{4,6},{5,7},{6,4},{7,5},{8,10},{9,11},{10,... | collective-permute-start | bytes 1486856 | tf_op jit(solution)/shard_map/ppermute | solution.py:21
  6.6 1.6 %collective-permute-start = (bf16[1936,128]{1,0:T(8,128)(2,1)S(1)}, bf16[1936,128]{1,0:T(8,128)(2,1)S(1)}, u32[]{:S(2)}, u32[]{:S(2)}) collective-permute-start(bf16[1936,128]{1,0:T(8,128)(2,1)S(1)} %fusion.1.refs_0_), channel_id=1, source_target_pairs={{0,1},{1,0},{2,3},{3,2},{4,5},{5,4},{6,7},{7,6},{8,9},{9,8},{10,11... | collective-permute-start | bytes 1486856 | tf_op jit(solution)/shard_map/ppermute | solution.py:21
  8.1 1.5 %collective-permute-start.1 = (bf16[1936,128]{1,0:T(8,128)(2,1)S(1)}, bf16[1936,128]{1,0:T(8,128)(2,1)S(1)}, u32[]{:S(2)}, u32[]{:S(2)}) collective-permute-start(bf16[1936,128]{1,0:T(8,128)(2,1)S(1)} %fusion.1.refs_0_), channel_id=1, source_target_pairs={{0,16},{1,17},{2,18},{3,19},{4,20},{5,21},{6,22},{7,23},{8,24},{9,... | collective-permute-start | bytes 1486856 | tf_op jit(solution)/shard_map/ppermute | solution.py:21
  10.1 7.1 %collective-permute-done.3.refs_4_ = bf16[1936,128]{1,0:T(8,128)(2,1)S(1)} collective-permute-done((bf16[1936,128]{1,0:T(8,128)(2,1)S(1)}, bf16[1936,128]{1,0:T(8,128)(2,1)S(1)}, u32[]{:S(2)}, u32[]{:S(2)}) %collective-permute-start.3) | collective-permute-done | bytes 495648 | tf_op jit(solution)/shard_map/ppermute | solution.py:21
  17.9 1.3 %collective-permute-start.6 = (bf16[1936,128]{1,0:T(8,128)(2,1)S(1)}, bf16[1936,128]{1,0:T(8,128)(2,1)}, u32[]{:S(2)}, u32[]{:S(2)}) collective-permute-start(bf16[1936,128]{1,0:T(8,128)(2,1)S(1)} %collective-permute-done.4), channel_id=1, source_target_pairs={{2,0},{3,1},{4,6},{5,7},{10,8},{11,9},{12,14},{13,15},{18,16},{19,... | collective-permute-start | bytes 1486856 | tf_op jit(solution)/shard_map/ppermute | solution.py:27
  19.2 1.6 %collective-permute-done.refs_1_ = bf16[1936,128]{1,0:T(8,128)(2,1)S(1)} collective-permute-done((bf16[1936,128]{1,0:T(8,128)(2,1)S(1)}, bf16[1936,128]{1,0:T(8,128)(2,1)S(1)}, u32[]{:S(2)}, u32[]{:S(2)}) %collective-permute-start) | collective-permute-done | bytes 495648 | tf_op jit(solution)/shard_map/ppermute | solution.py:21
  20.9 10.4 %collective-permute-done.1.refs_2_ = bf16[1936,128]{1,0:T(8,128)(2,1)S(1)} collective-permute-done((bf16[1936,128]{1,0:T(8,128)(2,1)S(1)}, bf16[1936,128]{1,0:T(8,128)(2,1)S(1)}, u32[]{:S(2)}, u32[]{:S(2)}) %collective-permute-start.1) | collective-permute-done | bytes 495648 | tf_op jit(solution)/shard_map/ppermute | solution.py:21
  31.3 5.6 %collective-permute-done.6 = bf16[1936,128]{1,0:T(8,128)(2,1)} collective-permute-done((bf16[1936,128]{1,0:T(8,128)(2,1)S(1)}, bf16[1936,128]{1,0:T(8,128)(2,1)}, u32[]{:S(2)}, u32[]{:S(2)}) %collective-permute-start.6) | collective-permute-done | bytes 495648 | tf_op jit(solution)/shard_map/ppermute | solution.py:27
  37.2 1.2 constant_dynamic-update-slice_fusion
  38.6 1.6 %collective-permute-start.8 = (bf16[3872,128]{1,0:T(8,128)(2,1)S(1)}, bf16[3872,128]{1,0:T(8,128)(2,1)S(1)}, u32[]{:S(2)}, u32[]{:S(2)}) collective-permute-start(bf16[3872,128]{1,0:T(8,128)(2,1)S(1)} %pad_maximum_fusion), channel_id=1, source_target_pairs={{0,1},{1,0},{2,3},{3,2},{4,5},{5,4},{6,7},{7,6},{8,9},{9,8},{10,11... | collective-permute-start | bytes 2973704 | tf_op jit(solution)/shard_map/ppermute | solution.py:21
  40.2 1.5 %collective-permute-start.9 = (bf16[3872,128]{1,0:T(8,128)(2,1)S(1)}, bf16[3872,128]{1,0:T(8,128)(2,1)S(1)}, u32[]{:S(2)}, u32[]{:S(2)}) collective-permute-start(bf16[3872,128]{1,0:T(8,128)(2,1)S(1)} %pad_maximum_fusion), channel_id=1, source_target_pairs={{0,16},{1,17},{2,18},{3,19},{4,20},{5,21},{6,22},{7,23},{8,24},{9,... | collective-permute-start | bytes 2973704 | tf_op jit(solution)/shard_map/ppermute | solution.py:21
  42.6 20.4 %collective-permute-done.8.refs_8_ = bf16[3872,128]{1,0:T(8,128)(2,1)S(1)} collective-permute-done((bf16[3872,128]{1,0:T(8,128)(2,1)S(1)}, bf16[3872,128]{1,0:T(8,128)(2,1)S(1)}, u32[]{:S(2)}, u32[]{:S(2)}) %collective-permute-start.8) | collective-permute-done | bytes 991264 | tf_op jit(solution)/shard_map/ppermute | solution.py:21
  63.0 1.2 collective-permute-done.9.refs_9_
  64.2 1.4 %collective-permute-done.11 = bf16[3872,128]{1,0:T(8,128)(2,1)S(1)} collective-permute-done((bf16[3872,128]{1,0:T(8,128)(2,1)S(1)}, bf16[3872,128]{1,0:T(8,128)(2,1)S(1)}, u32[]{:S(2)}, u32[]{:S(2)}) %collective-permute-start.11) | collective-permute-done | bytes 991264 | tf_op jit(solution)/shard_map/ppermute | solution.py:21
  66.0 1.2 copy-done.14
  69.4 1.3 collective-permute-start.15
  70.7 11.3 %collective-permute-done.13.refs_13_ = bf16[1936,128]{1,0:T(8,128)(2,1)S(1)} collective-permute-done((bf16[1936,128]{1,0:T(8,128)(2,1)S(1)}, bf16[1936,128]{1,0:T(8,128)(2,1)S(1)}, u32[]{:S(2)}, u32[]{:S(2)}) %collective-permute-start.13) | collective-permute-done | bytes 495648 | tf_op jit(solution)/shard_map/ppermute | solution.py:21
  82.2 2.2 %collective-permute-done.15.refs_17_ = bf16[1936,128]{1,0:T(8,128)(2,1)S(1)} collective-permute-done((bf16[1936,128]{1,0:T(8,128)(2,1)S(1)}, bf16[1936,128]{1,0:T(8,128)(2,1)S(1)}, u32[]{:S(2)}, u32[]{:S(2)}) %collective-permute-start.15) | collective-permute-done | bytes 495648 | tf_op jit(solution)/shard_map/ppermute | solution.py:27
  84.4 1.7 %copy-done.13 = bf16[13552,128]{1,0:T(8,128)(2,1)} copy-done((bf16[13552,128]{1,0:T(8,128)(2,1)}, bf16[13552,128]{1,0:T(8,128)(2,1)S(1)}, u32[]{:S(2)}) %copy-start.13) | copy-done | bytes 3469336
  86.1 1.5 %collective-permute-start.18 = (bf16[976,128]{1,0:T(8,128)(2,1)S(1)}, bf16[976,128]{1,0:T(8,128)(2,1)S(1)}, u32[]{:S(2)}, u32[]{:S(2)}) collective-permute-start(bf16[976,128]{1,0:T(8,128)(2,1)S(1)} %slice.31), channel_id=1, source_target_pairs={{0,16},{1,17},{2,18},{3,19},{4,20},{5,21},{6,22},{7,23},{8,24},{9,... | collective-permute-start | bytes 749576 | tf_op jit(solution)/shard_map/ppermute | solution.py:21
  87.7 1.6 %collective-permute-start.17 = (bf16[960,128]{1,0:T(8,128)(2,1)S(1)}, bf16[960,128]{1,0:T(8,128)(2,1)S(1)}, u32[]{:S(2)}, u32[]{:S(2)}) collective-permute-start(bf16[960,128]{1,0:T(8,128)(2,1)S(1)} %slice.30), channel_id=1, source_target_pairs={{0,1},{1,0},{2,3},{3,2},{4,5},{5,4},{6,7},{7,6},{8,9},{9,8},{10,11... | collective-permute-start | bytes 737288 | tf_op jit(solution)/shard_map/ppermute | solution.py:21
  89.7 6.1 %collective-permute-done.17 = bf16[960,128]{1,0:T(8,128)(2,1)S(1)} collective-permute-done((bf16[960,128]{1,0:T(8,128)(2,1)S(1)}, bf16[960,128]{1,0:T(8,128)(2,1)S(1)}, u32[]{:S(2)}, u32[]{:S(2)}) %collective-permute-start.17) | collective-permute-done | bytes 245792 | tf_op jit(solution)/shard_map/ppermute | solution.py:21
  98.5 29.7 %shard_map.37 = bf16[29,128,128]{2,1,0:T(8,128)(2,1)} custom-call(s32[34]{0:T(128)} %compare_select_fusion.place, bf16[1936,128]{1,0:T(8,128)(2,1)} %copy-done, bf16[1936,128]{1,0:T(8,128)(2,1)} %copy-done.6, bf16[1936,128]{1,0:T(8,128)(2,1)} %copy-done.7, bf16[1936,128]{1,0:T(8,128)(2,1)} %copy-done.2, bf16[1936,128]{1,0:T(8,128)(2,1)} %copy-done.1, ...), custom_call_target="tpu_custom_call" | custom-call | flops 16999999488 | bytes 15728640 | tf_op jit(solution)/shard_map/pallas_call | solution.py:255
  (83 shorter events, 9.7 us)
Async XLA Ops:
  2.8 35.6 %copy-start = (bf16[1936,128]{1,0:T(8,128)(2,1)}, bf16[1936,128]{1,0:T(8,128)(2,1)S(1)}, u32[]{:S(2)}) copy-start(bf16[1936,128]{1,0:T(8,128)(2,1)S(1)} %fusion.1.refs_0_) | copy-start | bytes 1486852
  2.8 14.4 %collective-permute-start.3 = (bf16[1936,128]{1,0:T(8,128)(2,1)S(1)}, bf16[1936,128]{1,0:T(8,128)(2,1)S(1)}, u32[]{:S(2)}, u32[]{:S(2)}) collective-permute-start(bf16[1936,128]{1,0:T(8,128)(2,1)S(1)} %fusion.1.refs_0_), channel_id=1, source_target_pairs={{0,2},{1,3},{2,0},{3,1},{4,6},{5,7},{6,4},{7,5},{8,10},{9,11},{10,... | collective-permute-start | bytes 1486856 | tf_op jit(solution)/shard_map/ppermute | solution.py:21
  5.9 11.3 %collective-permute-start.4 = (bf16[1936,128]{1,0:T(8,128)(2,1)S(1)}, bf16[1936,128]{1,0:T(8,128)(2,1)S(1)}, u32[]{:S(2)}, u32[]{:S(2)}) collective-permute-start(bf16[1936,128]{1,0:T(8,128)(2,1)S(1)} %fusion.1.refs_0_), channel_id=1, source_target_pairs={{2,4},{3,5},{4,2},{5,3},{10,12},{11,13},{12,10},{13,11},{18,20},{1... | collective-permute-start | bytes 1486856 | tf_op jit(solution)/shard_map/ppermute | solution.py:24
  6.6 14.3 %collective-permute-start = (bf16[1936,128]{1,0:T(8,128)(2,1)S(1)}, bf16[1936,128]{1,0:T(8,128)(2,1)S(1)}, u32[]{:S(2)}, u32[]{:S(2)}) collective-permute-start(bf16[1936,128]{1,0:T(8,128)(2,1)S(1)} %fusion.1.refs_0_), channel_id=1, source_target_pairs={{0,1},{1,0},{2,3},{3,2},{4,5},{5,4},{6,7},{7,6},{8,9},{9,8},{10,11... | collective-permute-start | bytes 1486856 | tf_op jit(solution)/shard_map/ppermute | solution.py:21
  8.1 23.1 %collective-permute-start.1 = (bf16[1936,128]{1,0:T(8,128)(2,1)S(1)}, bf16[1936,128]{1,0:T(8,128)(2,1)S(1)}, u32[]{:S(2)}, u32[]{:S(2)}) collective-permute-start(bf16[1936,128]{1,0:T(8,128)(2,1)S(1)} %fusion.1.refs_0_), channel_id=1, source_target_pairs={{0,16},{1,17},{2,18},{3,19},{4,20},{5,21},{6,22},{7,23},{8,24},{9,... | collective-permute-start | bytes 1486856 | tf_op jit(solution)/shard_map/ppermute | solution.py:21
  9.7 21.6 %collective-permute-start.2 = (bf16[1936,128]{1,0:T(8,128)(2,1)S(1)}, bf16[1936,128]{1,0:T(8,128)(2,1)S(1)}, u32[]{:S(2)}, u32[]{:S(2)}) collective-permute-start(bf16[1936,128]{1,0:T(8,128)(2,1)S(1)} %fusion.1.refs_0_), channel_id=1, source_target_pairs={{0,17},{1,16},{2,19},{3,18},{4,21},{5,20},{6,23},{7,22},{8,25},{9,... | collective-permute-start | bytes 1486856 | tf_op jit(solution)/shard_map/ppermute | solution.py:21
  17.2 14.1 %collective-permute-start.5 = (bf16[1936,128]{1,0:T(8,128)(2,1)S(1)}, bf16[1936,128]{1,0:T(8,128)(2,1)S(1)}, u32[]{:S(2)}, u32[]{:S(2)}) collective-permute-start(bf16[1936,128]{1,0:T(8,128)(2,1)S(1)} %collective-permute-done.3.refs_4_), channel_id=1, source_target_pairs={{2,4},{3,5},{4,2},{5,3},{10,12},{11,13},{12,10},{13,11},{18,20},{1... | collective-permute-start | bytes 1486856 | tf_op jit(solution)/shard_map/ppermute | solution.py:24
  17.9 18.9 %collective-permute-start.6 = (bf16[1936,128]{1,0:T(8,128)(2,1)S(1)}, bf16[1936,128]{1,0:T(8,128)(2,1)}, u32[]{:S(2)}, u32[]{:S(2)}) collective-permute-start(bf16[1936,128]{1,0:T(8,128)(2,1)S(1)} %collective-permute-done.4), channel_id=1, source_target_pairs={{2,0},{3,1},{4,6},{5,7},{10,8},{11,9},{12,14},{13,15},{18,16},{19,... | collective-permute-start | bytes 1486856 | tf_op jit(solution)/shard_map/ppermute | solution.py:27
  38.4 27.3 %copy-start.3 = (bf16[1936,128]{1,0:T(8,128)(2,1)}, bf16[1936,128]{1,0:T(8,128)(2,1)S(1)}, u32[]{:S(2)}) copy-start(bf16[1936,128]{1,0:T(8,128)(2,1)S(1)} %get-tuple-element.64.refs_5_) | copy-start | bytes 1486852
  38.4 27.1 %collective-permute-start.7 = (bf16[11616,128]{1,0:T(8,128)(2,1)S(1)}, bf16[11616,128]{1,0:T(8,128)(2,1)S(1)}, u32[]{:S(2)}, u32[]{:S(2)}) collective-permute-start(bf16[11616,128]{1,0:T(8,128)(2,1)S(1)} %get-tuple-element.63), channel_id=1, source_target_pairs={{0,8},{1,9},{2,10},{3,11},{4,12},{5,13},{6,14},{7,15},{8,0},{9,1},... | collective-permute-start | bytes 8921096 | tf_op jit(solution)/shard_map/ppermute | solution.py:21
  38.6 24.4 %collective-permute-start.8 = (bf16[3872,128]{1,0:T(8,128)(2,1)S(1)}, bf16[3872,128]{1,0:T(8,128)(2,1)S(1)}, u32[]{:S(2)}, u32[]{:S(2)}) collective-permute-start(bf16[3872,128]{1,0:T(8,128)(2,1)S(1)} %pad_maximum_fusion), channel_id=1, source_target_pairs={{0,1},{1,0},{2,3},{3,2},{4,5},{5,4},{6,7},{7,6},{8,9},{9,8},{10,11... | collective-permute-start | bytes 2973704 | tf_op jit(solution)/shard_map/ppermute | solution.py:21
  40.2 24.0 %collective-permute-start.9 = (bf16[3872,128]{1,0:T(8,128)(2,1)S(1)}, bf16[3872,128]{1,0:T(8,128)(2,1)S(1)}, u32[]{:S(2)}, u32[]{:S(2)}) collective-permute-start(bf16[3872,128]{1,0:T(8,128)(2,1)S(1)} %pad_maximum_fusion), channel_id=1, source_target_pairs={{0,16},{1,17},{2,18},{3,19},{4,20},{5,21},{6,22},{7,23},{8,24},{9,... | collective-permute-start | bytes 2973704 | tf_op jit(solution)/shard_map/ppermute | solution.py:21
  41.7 23.8 %collective-permute-start.11 = (bf16[3872,128]{1,0:T(8,128)(2,1)S(1)}, bf16[3872,128]{1,0:T(8,128)(2,1)S(1)}, u32[]{:S(2)}, u32[]{:S(2)}) collective-permute-start(bf16[3872,128]{1,0:T(8,128)(2,1)S(1)} %pad_maximum_fusion.1), channel_id=1, source_target_pairs={{0,2},{1,3},{2,0},{3,1},{4,6},{5,7},{6,4},{7,5},{8,10},{9,11},{10,... | collective-permute-start | bytes 2973704 | tf_op jit(solution)/shard_map/ppermute | solution.py:21
  41.8 0.7 collective-permute-start.10
  68.1 16.2 %collective-permute-start.12 = (bf16[13552,128]{1,0:T(8,128)(2,1)S(1)}, bf16[13552,128]{1,0:T(8,128)(2,1)S(1)}, u32[]{:S(2)}, u32[]{:S(2)}) collective-permute-start(bf16[13552,128]{1,0:T(8,128)(2,1)S(1)} %constant_dynamic-update-slice_fusion.6), channel_id=1, source_target_pairs={{0,8},{1,9},{2,10},{3,11},{4,12},{5,13},{6,14},{7,15},{8,0},{9,1},... | collective-permute-start | bytes 10407944 | tf_op jit(solution)/shard_map/ppermute | solution.py:21
  68.2 13.7 %collective-permute-start.13 = (bf16[1936,128]{1,0:T(8,128)(2,1)S(1)}, bf16[1936,128]{1,0:T(8,128)(2,1)S(1)}, u32[]{:S(2)}, u32[]{:S(2)}) collective-permute-start(bf16[1936,128]{1,0:T(8,128)(2,1)S(1)} %get-tuple-element.62.refs_7_), channel_id=1, source_target_pairs={{0,1},{1,0},{2,3},{3,2},{4,5},{5,4},{6,7},{7,6},{8,9},{9,8},{10,11... | collective-permute-start | bytes 1486856 | tf_op jit(solution)/shard_map/ppermute | solution.py:21
  68.8 13.4 %collective-permute-start.14 = (bf16[1936,128]{1,0:T(8,128)(2,1)S(1)}, bf16[1936,128]{1,0:T(8,128)(2,1)S(1)}, u32[]{:S(2)}, u32[]{:S(2)}) collective-permute-start(bf16[1936,128]{1,0:T(8,128)(2,1)S(1)} %get-tuple-element.62.refs_7_), channel_id=1, source_target_pairs={{0,16},{1,17},{2,18},{3,19},{4,20},{5,21},{6,22},{7,23},{8,24},{9,... | collective-permute-start | bytes 1486856 | tf_op jit(solution)/shard_map/ppermute | solution.py:21
  69.4 15.0 %collective-permute-start.15 = (bf16[1936,128]{1,0:T(8,128)(2,1)S(1)}, bf16[1936,128]{1,0:T(8,128)(2,1)S(1)}, u32[]{:S(2)}, u32[]{:S(2)}) collective-permute-start(bf16[1936,128]{1,0:T(8,128)(2,1)S(1)} %collective-permute-done.10.refs_11_), channel_id=1, source_target_pairs={{2,0},{3,1},{4,6},{5,7},{10,8},{11,9},{12,14},{13,15},{18,16},{19,... | collective-permute-start | bytes 1486856 | tf_op jit(solution)/shard_map/ppermute | solution.py:27
  86.1 9.7 %collective-permute-start.16 = (bf16[1936,128]{1,0:T(8,128)(2,1)S(1)}, bf16[1936,128]{1,0:T(8,128)(2,1)S(1)}, u32[]{:S(2)}, u32[]{:S(2)}) collective-permute-start(bf16[1936,128]{1,0:T(8,128)(2,1)S(1)} %collective-permute-done.13.refs_13_), channel_id=1, source_target_pairs={{0,8},{1,9},{2,10},{3,11},{4,12},{5,13},{6,14},{7,15},{8,0},{9,1},... | collective-permute-start | bytes 1486856 | tf_op jit(solution)/shard_map/ppermute | solution.py:21
  86.1 9.7 %collective-permute-start.18 = (bf16[976,128]{1,0:T(8,128)(2,1)S(1)}, bf16[976,128]{1,0:T(8,128)(2,1)S(1)}, u32[]{:S(2)}, u32[]{:S(2)}) collective-permute-start(bf16[976,128]{1,0:T(8,128)(2,1)S(1)} %slice.31), channel_id=1, source_target_pairs={{0,16},{1,17},{2,18},{3,19},{4,20},{5,21},{6,22},{7,23},{8,24},{9,... | collective-permute-start | bytes 749576 | tf_op jit(solution)/shard_map/ppermute | solution.py:21
  87.7 8.2 %collective-permute-start.17 = (bf16[960,128]{1,0:T(8,128)(2,1)S(1)}, bf16[960,128]{1,0:T(8,128)(2,1)S(1)}, u32[]{:S(2)}, u32[]{:S(2)}) collective-permute-start(bf16[960,128]{1,0:T(8,128)(2,1)S(1)} %slice.30), channel_id=1, source_target_pairs={{0,1},{1,0},{2,3},{3,2},{4,5},{5,4},{6,7},{7,6},{8,9},{9,8},{10,11... | collective-permute-start | bytes 737288 | tf_op jit(solution)/shard_map/ppermute | solution.py:21
  89.2 8.3 %collective-permute-start.19 = (bf16[1936,128]{1,0:T(8,128)(2,1)S(1)}, bf16[1936,128]{1,0:T(8,128)(2,1)S(1)}, u32[]{:S(2)}, u32[]{:S(2)}) collective-permute-start(bf16[1936,128]{1,0:T(8,128)(2,1)S(1)} %collective-permute-done.14.refs_15_), channel_id=1, source_target_pairs={{0,8},{1,9},{2,10},{3,11},{4,12},{5,13},{6,14},{7,15},{8,0},{9,1},... | collective-permute-start | bytes 1486856 | tf_op jit(solution)/shard_map/ppermute | solution.py:21
  89.2 8.3 %collective-permute-start.20 = (bf16[1936,128]{1,0:T(8,128)(2,1)S(1)}, bf16[1936,128]{1,0:T(8,128)(2,1)S(1)}, u32[]{:S(2)}, u32[]{:S(2)}) collective-permute-start(bf16[1936,128]{1,0:T(8,128)(2,1)S(1)} %collective-permute-done.15.refs_17_), channel_id=1, source_target_pairs={{0,8},{1,9},{2,10},{3,11},{4,12},{5,13},{6,14},{7,15},{8,0},{9,1},... | collective-permute-start | bytes 1486856 | tf_op jit(solution)/shard_map/ppermute | solution.py:21
  95.9 2.1 %collective-permute-start.21 = (bf16[1936,128]{1,0:T(8,128)(2,1)S(1)}, bf16[1936,128]{1,0:T(8,128)(2,1)}, u32[]{:S(2)}, u32[]{:S(2)}) collective-permute-start(bf16[1936,128]{1,0:T(8,128)(2,1)S(1)} %constant_dynamic-update-slice_fusion.11.refs_19_), channel_id=1, source_target_pairs={{0,8},{1,9},{2,10},{3,11},{4,12},{5,13},{6,14},{7,15},{8,0},{9,1},... | collective-permute-start | bytes 1486856 | tf_op jit(solution)/shard_map/ppermute | solution.py:21
  (17 other events, 144.9 us)

commit v7 on v3

v7 whole, which is shorter than its diff:
```python
import functools

import jax
import jax.numpy as jnp
from jax import lax
from jax.experimental import pallas as pl
from jax.experimental.pallas import tpu as pltpu
from jax.sharding import PartitionSpec as P

NOTE = 16
AXES = ("row", "col")


def cube(own, count, here, cut):
    x, z1, z2, z3, core, y = 1, 2, 4, 6, 8, 16
    full = own.shape[0]
    found = []

    def swap(value, mask):
        return lax.ppermute(value, AXES, [(i, i ^ mask) for i in range(count)])

    def whole(*masks):
        return [(mask, 0, full) for mask in masks]

    def cross(*items):
        arrays = [array for array, _ in items]
        batch = swap(jnp.concatenate(arrays, axis=0) if len(arrays) > 1 else arrays[0], core)
        found.extend(items)
        found.append((batch, [(mask | core, start, size) for _, parts in items for mask, start, size in parts]))
        return len(found) - 1

    def finish(spot, *arrays):
        batch, *arrays = lax.optimization_barrier((found[spot][0],) + arrays)
        found[spot] = (batch, found[spot][1])
        return arrays

    x0, y0, d0, f1, f3 = (swap(own, mask) for mask in (x, y, x | y, z1, z3))
    own, x0, y0, d0, f1, f3 = lax.optimization_barrier((own, x0, y0, d0, f1, f3))
    pair = jnp.concatenate([f1, f3], axis=0)
    xp, yp, f2, d2 = swap(pair, x), swap(pair, y), swap(f3, z1), swap(d0, z2)
    spot = cross(
        (own, whole(0)), (x0, whole(x)), (y0, whole(y)), (d0, whole(x | y)), (f1, whole(z1)), (f3, whole(z3))
    )
    xp, yp, f2, d2, d0 = finish(spot, xp, yp, f2, d2, d0)
    xl = swap(jnp.concatenate([f2, yp[full : full + cut]], axis=0), x)
    yl = swap(jnp.concatenate([f2, xp[full + cut :]], axis=0), y)
    d1 = swap(d0, z1)
    spot = cross(
        (f2, whole(z2)), (d2, whole(z2 | x | y)), (xp, whole(z1 | x, z3 | x)), (yp, whole(z1 | y, z3 | y))
    )
    xl, yl, d1 = finish(spot, xl, yl, d1)
    cross((xl, [(z2 | x, 0, full), (z3 | x | y, 0, cut)]))
    cross((yl, [(z2 | y, 0, full), (z3 | x | y, cut, full - cut)]))
    cross((d1, whole(z1 | x | y)))
    return found


def window(payload, need, cut):
    groups, width = lax.axis_size("row"), lax.axis_size("col")
    count = groups * width
    size = payload.shape[0]
    column = lax.axis_index("col")
    here = lax.axis_index("row") * width + column
    pieces, offsets = [], []
    if (groups, width) == (4, 8):
        for array, parts in cube(payload, count, here, cut):
            pieces.append((array, [(start, rows) for _, start, rows in parts]))
            for mask, _, _ in parts:
                offsets.append((((here ^ mask) - here + count // 2) % count - count // 2)[None])
    else:
        block = lax.all_gather(payload, "col", axis=0, tiled=True)
        pieces.append((block, [(0, size)] * width))
        offsets.append(jnp.arange(width, dtype=jnp.int32) - column)
        for hop in range(1, -(-need // width) + 1):
            part = min(width, need - (hop - 1) * width)
            up = [(g, (g + hop) % groups) for g in range(groups)]
            down = [(g, (g - hop) % groups) for g in range(groups)]
            steps = jnp.arange(part, dtype=jnp.int32) - column
            pieces.append((lax.ppermute(block[(width - part) * size :], "row", up), [(0, size)] * part))
            offsets.append(steps - (hop - 1) * width - part)
            pieces.append((lax.ppermute(block[: part * size], "row", down), [(0, size)] * part))
            offsets.append(steps + hop * width)
    offsets = jnp.concatenate(offsets).astype(jnp.int32)
    return pieces, jnp.where(jnp.abs(offsets) <= need, offsets + need, -1)


def purify(reach, edge, layout, place, *refs):
    count = len(layout)
    tables, (out, band, square, own, notes, keep, arrived, noted) = refs[:count], refs[count:]
    far = 2 * reach
    slots, wide = 2 * reach + 1, 4 * reach + 1
    pitch = slots + 2
    kind = band.dtype

    def span(first, n):
        first = first * edge
        return pl.ds(first if isinstance(first, int) else pl.multiple_of(first, edge), n * edge)

    base = 0
    for table, parts in zip(tables, layout):
        begin = 0
        for start, size in parts:
            k = place[base]
            body = min(size, slots * edge - start)

            @pl.when(k >= 0)
            def _(table=table, begin=begin, start=start, size=size, body=body, k=k):
                pltpu.make_async_copy(
                    table.at[pl.ds(begin, body)],
                    band.at[pl.ds(pl.multiple_of((k * pitch + 1) * edge + start, edge), body)],
                    arrived.at[k],
                ).start()
                if size > body:

                    @pl.when((k >= reach) & (k <= 3 * reach))
                    def _():
                        pltpu.make_async_copy(
                            table.at[pl.ds(begin + body, NOTE)], notes.at[k - reach], noted
                        ).start()

            begin += size
            base += 1

    def ready(k):
        body = pl.ds(0, slots * edge)
        pltpu.make_async_copy(tables[0].at[body], band.at[body], arrived.at[k]).wait()

    def clear(k, carry):
        zero = jnp.zeros((edge, edge), kind)
        band[span(k * pitch, 1), :] = zero
        band[span(k * pitch + slots + 1, 1), :] = zero
        return carry

    lax.fori_loop(0, 2 * far + 2, clear, 0)

    def clear_last(s, carry):
        band[span((2 * far + 1) * pitch + s, 1), :] = jnp.zeros((edge, edge), kind)
        return carry

    lax.fori_loop(1, slots + 1, clear_last, 0)

    def clear_square(r, carry):
        zero = jnp.zeros((edge, edge), kind)
        square[span(r, 1), pl.ds(0, edge)] = zero
        square[span(r, 1), pl.ds((wide + 1) * edge, edge)] = zero
        return carry

    lax.fori_loop(0, slots + 1, clear_square, 0)

    for r in range(slots):
        pltpu.make_async_copy(tables[0].at[pl.ds(0, NOTE)], notes.at[r], noted).wait()
    notes[slots] = jnp.zeros(notes.shape[1:], kind)
    spots = keep.shape[1]
    diagonal = lax.broadcasted_iota(jnp.int32, (spots, edge), 0) == lax.broadcasted_iota(jnp.int32, (spots, edge), 1)

    def spread(r, carry):
        line = notes[r].astype(jnp.float32)[:1]
        value = jnp.sum(jnp.where(diagonal, line, 0.0), axis=1, keepdims=True)
        keep[r] = jnp.broadcast_to(value, (spots, edge))
        return carry

    lax.fori_loop(0, slots + 1, spread, 0)

    for k in range(far):
        ready(k)

    def strip(k, first, n):
        return jnp.concatenate([band[span(k * pitch + first + s, 1), :] for s in range(n)], axis=1)

    def row_pair(pair, carry):
        r = 2 * pair
        ready(r + far)

        @pl.when(r + far + 1 <= 2 * far)
        def _():
            ready(r + far + 1)

        middle = jnp.where((r == reach) | (r + 1 == reach), 1, 0)
        for d in range(-far, far + 1, 2):
            low, high = max(-reach, d - reach), min(reach + 1, d + reach + 1)
            size = high - low + 1
            left = jnp.concatenate(
                [strip(r + reach, low + reach + 1, size), strip(r + reach + 1, low + reach, size)], axis=0
            )
            right = jnp.concatenate(
                [strip(r + reach + e, d - e + reach + 1, 2) for e in range(low, high + 1)], axis=0
            )
            product = jnp.dot(left, right, preferred_element_type=jnp.float32)
            for i in range(2):
                u = d + far - i
                mask = jnp.concatenate(
                    [keep[r + i, pl.ds(min(max(u + j, 0), wide - 1), 1), :] for j in range(2)], axis=1
                )
                kept = product[i * edge : (i + 1) * edge] * mask
                square[span(r + i, 1), pl.ds((u + 1) * edge, 2 * edge)] = kept.astype(kind)
                if i == reach % 2:
                    own[middle, :, pl.ds((u + 1) * edge, 2 * edge)] = kept
        return carry

    lax.fori_loop(0, (slots + 1) // 2, row_pair, 0)

    for c in range(-far, far + 1, 2):
        low, high = max(-reach, c - far), min(reach, c + far + 1)
        left = strip(far, low + reach + 1, high - low + 1)
        right = jnp.concatenate(
            [square[span(r + reach, 1), pl.ds((c - r + far + 1) * edge, 2 * edge)] for r in range(low, high + 1)],
            axis=0,
        )
        cube = jnp.dot(left, right, preferred_element_type=jnp.float32)
        for j in range(2):
            u = c + far + j
            if u < wide:
                kept = own[1, :, pl.ds((u + 1) * edge, edge)]
                value = 3.0 * kept - 2.0 * cube[:, j * edge : (j + 1) * edge]
                out[u] = (keep[reach, pl.ds(u, 1), :] * value).astype(out.dtype)


def pack(pattern, filter_mask, density, payload):
    slots, edge = density.shape[0], density.shape[1]
    for s in range(slots):
        scale = pattern[0, s].astype(jnp.float32)
        payload[s * edge : (s + 1) * edge] = (density[s].astype(jnp.float32) * scale).astype(payload.dtype)
    lane = lax.broadcasted_iota(jnp.int32, (NOTE, edge), 1)
    note = jnp.zeros((NOTE, edge), jnp.float32)
    for u in range(filter_mask.shape[1]):
        note = jnp.where(lane == u, filter_mask[0, u].astype(jnp.float32), note)
    payload[slots * edge :] = note.astype(payload.dtype)


def shards(density, pattern, filter_mask):
    slots, edge = density.shape[1], density.shape[2]
    wide = filter_mask.shape[1]
    reach = (slots - 1) // 2
    far = 2 * reach
    smem, vmem = pl.BlockSpec(memory_space=pltpu.SMEM), pl.BlockSpec(memory_space=pltpu.VMEM)
    payload = pl.pallas_call(
        pack,
        out_shape=jax.ShapeDtypeStruct((slots * edge + NOTE, edge), density.dtype),
        in_specs=[smem, smem, vmem],
        out_specs=vmem,
    )(pattern, filter_mask, density[0])
    pieces, place = window(payload, far, (slots + 1) // 2 * edge)
    tables = [array for array, _ in pieces]
    layout = [parts for _, parts in pieces]
    result = pl.pallas_call(
        functools.partial(purify, reach, edge, layout),
        out_shape=jax.ShapeDtypeStruct((wide, edge, edge), density.dtype),
        in_specs=[smem] + [pl.BlockSpec(memory_space=pl.ANY)] * len(tables),
        out_specs=vmem,
        scratch_shapes=[
            pltpu.VMEM(((2 * far + 2) * (slots + 2) * edge, edge), density.dtype),
            pltpu.VMEM(((slots + 1) * edge, (wide + 2) * edge), density.dtype),
            pltpu.VMEM((2, edge, (wide + 2) * edge), jnp.float32),
            pltpu.VMEM((slots + 1, NOTE, edge), density.dtype),
            pltpu.VMEM((slots + 1, -(-wide // 8) * 8, edge), jnp.float32),
            pltpu.SemaphoreType.DMA((2 * far + 1,)),
            pltpu.SemaphoreType.DMA,
        ],
        compiler_params=pltpu.CompilerParams(vmem_limit_bytes=56 * 2**20),
        cost_estimate=pl.CostEstimate(flops=17 * 10**9, bytes_accessed=15 * 2**20, transcendentals=0),
    )(place, *tables)
    return result[None]


def solution(mesh):
    in_specs = (P(AXES, None, None, None), P(AXES, None), P(AXES, None))
    out_specs = P(AXES, None, None, None)
    return jax.shard_map(shards, mesh=mesh, in_specs=in_specs, out_specs=out_specs, check_vma=False)
```

time: 142 us -> 135 us (0.951)
  waiting for transfers between devices: 80.4 us -> 64.2 us
  other arithmetic: 2.6 us -> 17.3 us
  starting transfers between devices: 24.2 us -> 16.6 us
  local copies, waits for them, and re-layouts: 3.64 us -> 5.28 us
    concatenate x1 -> x3, other arithmetic: 0.03 us -> 16.7 us  [the longest x1 16.6 us: cross(): jnp.concatenate(arrays, axis=0)]
    ppermute x39 -> x17, waiting for transfers between devices: 80.4 us -> 64.2 us  [swap(): return lax.ppermute(value, AXES, [(i, i ^ mask) for i in range(count)])]
    ppermute x39 -> x17, starting transfers between devices: 24.2 us -> 16.6 us  [swap(): return lax.ppermute(value, AXES, [(i, i ^ mask) for i in range(count)])]
    pallas_call x0 -> x1, Pallas kernels: none -> 1.92 us  [shards(): pl.pallas_call(pack, out_shape=jax.ShapeDtypeStruct((slots * edge + NOTE,...]
    unnamed x68 -> x35, local copies, waits for them, and re-layouts: 3.35 us -> 4.99 us
  transfers between devices with their start and end apart: 39 -> 17, of which waited for: 15 -> 10; matrix products, arithmetic and copies ran while one was open for 1% -> 1% of each run, Pallas kernels for 0% -> 0%
where the time goes in v7:
time: 135 us
  waiting for transfers between devices  64.2 us (48%)
  Pallas kernels  30.9 us (23%)
  other arithmetic  17.3 us (13%)
  starting transfers between devices  16.6 us (12%)
  local copies, waits for them, and re-layouts  5.28 us (4%)
    ppermute x17, waiting for transfers between devices, swap(): return lax.ppermute(value, AXES, [(i, i ^ mask) for i in range(count)])  64.2 us
    pallas_call x1, Pallas kernels, shards(): pl.pallas_call(functools.partial(purify, reach, edge, layout), out_shape=...  29 us
    concatenate x1, other arithmetic, cross(): jnp.concatenate(arrays, axis=0)  16.6 us
    ppermute x17, starting transfers between devices, swap(): return lax.ppermute(value, AXES, [(i, i ^ mask) for i in range(count)])  16.6 us
    unnamed x35, local copies, waits for them, and re-layouts  4.99 us
  transfers between devices with their start and end apart: 17, of which 10 were waited for; matrix products, arithmetic and copies ran while one was open for 1% of the time, Pallas kernels for 0%

profile of v7, /device:TPU:0, one launch (start us, length us, event | category | flops | bytes accessed | tf_op | source)
XLA Modules:
  0.0 134.9 jit_solution(17826554215436486854)
XLA Ops:
  0.0 1.9 %shard_map.37.refs_0_ = bf16[1936,128]{1,0:T(8,128)(2,1)} custom-call(s32[1,15]{1,0:T(1,128)} %pattern.1, s32[1,29]{1,0:T(1,128)} %filter_mask.1, bf16[15,128,128]{2,1,0:T(8,128)(2,1)} %bitcast.33), custom_call_target="tpu_custom_call" | custom-call | tf_op jit(solution)/shard_map/pallas_call | solution.py:236
  1.9 2.9 %collective-permute-start = (bf16[1936,128]{1,0:T(8,128)(2,1)}, bf16[1936,128]{1,0:T(8,128)(2,1)S(1)}, u32[]{:S(2)}, u32[]{:S(2)}) collective-permute-start(bf16[1936,128]{1,0:T(8,128)(2,1)} %shard_map.37.refs_0_), channel_id=1, source_target_pairs={{0,1},{1,0},{2,3},{3,2},{4,5},{5,4},{6,7},{7,6},{8,9},{9,8},{10,11... | collective-permute-start | bytes 1486856 | tf_op jit(solution)/shard_map/ppermute | solution.py:20
  4.9 1.5 %collective-permute-start.1 = (bf16[1936,128]{1,0:T(8,128)(2,1)}, bf16[1936,128]{1,0:T(8,128)(2,1)S(1)}, u32[]{:S(2)}, u32[]{:S(2)}) collective-permute-start(bf16[1936,128]{1,0:T(8,128)(2,1)} %shard_map.37.refs_0_), channel_id=1, source_target_pairs={{0,16},{1,17},{2,18},{3,19},{4,20},{5,21},{6,22},{7,23},{8,24},{9,... | collective-permute-start | bytes 1486856 | tf_op jit(solution)/shard_map/ppermute | solution.py:20
  6.4 2.1 %collective-permute-start.3 = (bf16[1936,128]{1,0:T(8,128)(2,1)}, bf16[1936,128]{1,0:T(8,128)(2,1)S(1)}, u32[]{:S(2)}, u32[]{:S(2)}) collective-permute-start(bf16[1936,128]{1,0:T(8,128)(2,1)} %shard_map.37.refs_0_), channel_id=1, source_target_pairs={{0,2},{1,3},{2,0},{3,1},{4,6},{5,7},{6,4},{7,5},{8,10},{9,11},{10,... | collective-permute-start | bytes 1486856 | tf_op jit(solution)/shard_map/ppermute | solution.py:20
  8.4 2.5 %collective-permute-start.4 = (bf16[1936,128]{1,0:T(8,128)(2,1)}, bf16[1936,128]{1,0:T(8,128)(2,1)S(1)}, u32[]{:S(2)}, u32[]{:S(2)}) collective-permute-start(bf16[1936,128]{1,0:T(8,128)(2,1)} %shard_map.37.refs_0_), channel_id=1, source_target_pairs={{0,6},{1,7},{2,4},{3,5},{4,2},{5,3},{6,0},{7,1},{8,14},{9,15},{10,... | collective-permute-start | bytes 1486856 | tf_op jit(solution)/shard_map/ppermute | solution.py:20
  10.9 6.3 %collective-permute-done.refs_1_ = bf16[1936,128]{1,0:T(8,128)(2,1)S(1)} collective-permute-done((bf16[1936,128]{1,0:T(8,128)(2,1)}, bf16[1936,128]{1,0:T(8,128)(2,1)S(1)}, u32[]{:S(2)}, u32[]{:S(2)}) %collective-permute-start) | collective-permute-done | bytes 495648 | tf_op jit(solution)/shard_map/ppermute | solution.py:20
  17.2 11.3 %collective-permute-done.1.refs_2_ = bf16[1936,128]{1,0:T(8,128)(2,1)S(1)} collective-permute-done((bf16[1936,128]{1,0:T(8,128)(2,1)}, bf16[1936,128]{1,0:T(8,128)(2,1)S(1)}, u32[]{:S(2)}, u32[]{:S(2)}) %collective-permute-start.1) | collective-permute-done | bytes 495648 | tf_op jit(solution)/shard_map/ppermute | solution.py:20
  28.5 3.5 %collective-permute-done.4.refs_5_ = bf16[1936,128]{1,0:T(8,128)(2,1)S(1)} collective-permute-done((bf16[1936,128]{1,0:T(8,128)(2,1)}, bf16[1936,128]{1,0:T(8,128)(2,1)S(1)}, u32[]{:S(2)}, u32[]{:S(2)}) %collective-permute-start.4) | collective-permute-done | bytes 495648 | tf_op jit(solution)/shard_map/ppermute | solution.py:20
  32.0 1.2 constant_dynamic-update-slice_fusion.5
  33.9 1.6 %collective-permute-start.6 = (bf16[3872,128]{1,0:T(8,128)(2,1)S(1)}, bf16[3872,128]{1,0:T(8,128)(2,1)S(1)}, u32[]{:S(2)}, u32[]{:S(2)}) collective-permute-start(bf16[3872,128]{1,0:T(8,128)(2,1)S(1)} %get-tuple-element.37), channel_id=1, source_target_pairs={{0,1},{1,0},{2,3},{3,2},{4,5},{5,4},{6,7},{7,6},{8,9},{9,8},{10,11... | collective-permute-start | bytes 2973704 | tf_op jit(solution)/shard_map/ppermute | solution.py:20
  35.4 1.5 %collective-permute-start.7 = (bf16[3872,128]{1,0:T(8,128)(2,1)S(1)}, bf16[3872,128]{1,0:T(8,128)(2,1)S(1)}, u32[]{:S(2)}, u32[]{:S(2)}) collective-permute-start(bf16[3872,128]{1,0:T(8,128)(2,1)S(1)} %get-tuple-element.37), channel_id=1, source_target_pairs={{0,16},{1,17},{2,18},{3,19},{4,20},{5,21},{6,22},{7,23},{8,24},{9,... | collective-permute-start | bytes 2973704 | tf_op jit(solution)/shard_map/ppermute | solution.py:20
  36.9 1.8 %collective-permute-start.9 = (bf16[1936,128]{1,0:T(8,128)(2,1)S(1)}, bf16[1936,128]{1,0:T(8,128)(2,1)S(1)}, u32[]{:S(2)}, u32[]{:S(2)}) collective-permute-start(bf16[1936,128]{1,0:T(8,128)(2,1)S(1)} %collective-permute-done.2.refs_3_), channel_id=1, source_target_pairs={{0,4},{1,5},{2,6},{3,7},{4,0},{5,1},{6,2},{7,3},{8,12},{9,13},{10,... | collective-permute-start | bytes 1486856 | tf_op jit(solution)/shard_map/ppermute | solution.py:20
  39.2 22.5 %collective-permute-done.9.refs_8_ = bf16[1936,128]{1,0:T(8,128)(2,1)S(1)} collective-permute-done((bf16[1936,128]{1,0:T(8,128)(2,1)S(1)}, bf16[1936,128]{1,0:T(8,128)(2,1)S(1)}, u32[]{:S(2)}, u32[]{:S(2)}) %collective-permute-start.9) | collective-permute-done | bytes 495648 | tf_op jit(solution)/shard_map/ppermute | solution.py:20
  62.0 16.6 %pad_maximum_fusion = bf16[11616,128]{1,0:T(8,128)(2,1)S(1)} fusion(bf16[3872,128]{1,0:T(8,128)(2,1)S(1)} %collective-permute-done.7.refs_10_, bf16[3872,128]{1,0:T(8,128)(2,1)S(1)} %collective-permute-done.6.refs_9_, bf16[1936,128]{1,0:T(8,128)(2,1)S(1)} %collective-permute-done.9.refs_8_, bf16[1936,128]{1,0:T(8,128)(2,1)S(1)} %collective-permute-done.8.refs_7_), kind=kLoop, calls=%fused_computation | loop fusion | flops 11894784 | bytes 5947392 | tf_op jit(solution)/shard_map/concatenate | solution.py:27
  78.9 0.6 collective-permute-start.11
  79.5 0.6 collective-permute-start.12
  80.6 12.8 %collective-permute-done.13.refs_16_ = bf16[1936,128]{1,0:T(8,128)(2,1)} collective-permute-done((bf16[1936,128]{1,0:T(8,128)(2,1)S(1)}, bf16[1936,128]{1,0:T(8,128)(2,1)}, u32[]{:S(2)}, u32[]{:S(2)}) %collective-permute-start.13) | collective-permute-done | bytes 495648 | tf_op jit(solution)/shard_map/ppermute | solution.py:20
  93.4 4.7 %collective-permute-done.12.refs_14_ = bf16[2848,128]{1,0:T(8,128)(2,1)S(1)} collective-permute-done((bf16[2848,128]{1,0:T(8,128)(2,1)S(1)}, bf16[2848,128]{1,0:T(8,128)(2,1)S(1)}, u32[]{:S(2)}, u32[]{:S(2)}) %collective-permute-start.12) | collective-permute-done | bytes 729120 | tf_op jit(solution)/shard_map/ppermute | solution.py:20
  98.3 1.7 %copy-done.9 = bf16[11616,128]{1,0:T(8,128)(2,1)} copy-done((bf16[11616,128]{1,0:T(8,128)(2,1)}, bf16[11616,128]{1,0:T(8,128)(2,1)S(1)}, u32[]{:S(2)}) %copy-start.9) | copy-done | bytes 2973720
  100.7 0.6 compare_select_fusion.place
  101.3 2.5 %collective-permute-done.16.refs_17_ = bf16[1936,128]{1,0:T(8,128)(2,1)S(1)} collective-permute-done((bf16[1936,128]{1,0:T(8,128)(2,1)}, bf16[1936,128]{1,0:T(8,128)(2,1)S(1)}, u32[]{:S(2)}, u32[]{:S(2)}) %collective-permute-start.16) | collective-permute-done | bytes 495648 | tf_op jit(solution)/shard_map/ppermute | solution.py:20
  104.0 0.6 copy-done.14
  104.8 0.9 copy-done.11
  105.7 29.0 %shard_map.38 = bf16[29,128,128]{2,1,0:T(8,128)(2,1)} custom-call(s32[34]{0:T(128)} %compare_select_fusion.place, bf16[1936,128]{1,0:T(8,128)(2,1)} %shard_map.37.refs_0_, bf16[1936,128]{1,0:T(8,128)(2,1)} %copy-done.3, bf16[1936,128]{1,0:T(8,128)(2,1)} %copy-done.4, bf16[1936,128]{1,0:T(8,128)(2,1)} %copy-done.5, bf16[1936,128]{1,0:T(8,128)(2,1)} %copy-done.6, ...), custom_call_target="tpu_custom_call" | custom-call | flops 16999999488 | bytes 15728640 | tf_op jit(solution)/shard_map/pallas_call | solution.py:245
  (55 shorter events, 3.3 us)
Async XLA Ops:
  1.9 15.3 %collective-permute-start = (bf16[1936,128]{1,0:T(8,128)(2,1)}, bf16[1936,128]{1,0:T(8,128)(2,1)S(1)}, u32[]{:S(2)}, u32[]{:S(2)}) collective-permute-start(bf16[1936,128]{1,0:T(8,128)(2,1)} %shard_map.37.refs_0_), channel_id=1, source_target_pairs={{0,1},{1,0},{2,3},{3,2},{4,5},{5,4},{6,7},{7,6},{8,9},{9,8},{10,11... | collective-permute-start | bytes 1486856 | tf_op jit(solution)/shard_map/ppermute | solution.py:20
  4.9 23.6 %collective-permute-start.1 = (bf16[1936,128]{1,0:T(8,128)(2,1)}, bf16[1936,128]{1,0:T(8,128)(2,1)S(1)}, u32[]{:S(2)}, u32[]{:S(2)}) collective-permute-start(bf16[1936,128]{1,0:T(8,128)(2,1)} %shard_map.37.refs_0_), channel_id=1, source_target_pairs={{0,16},{1,17},{2,18},{3,19},{4,20},{5,21},{6,22},{7,23},{8,24},{9,... | collective-permute-start | bytes 1486856 | tf_op jit(solution)/shard_map/ppermute | solution.py:20
  6.4 22.1 %collective-permute-start.2 = (bf16[1936,128]{1,0:T(8,128)(2,1)}, bf16[1936,128]{1,0:T(8,128)(2,1)S(1)}, u32[]{:S(2)}, u32[]{:S(2)}) collective-permute-start(bf16[1936,128]{1,0:T(8,128)(2,1)} %shard_map.37.refs_0_), channel_id=1, source_target_pairs={{0,17},{1,16},{2,19},{3,18},{4,21},{5,20},{6,23},{7,22},{8,25},{9,... | collective-permute-start | bytes 1486856 | tf_op jit(solution)/shard_map/ppermute | solution.py:20
  6.4 22.1 %collective-permute-start.3 = (bf16[1936,128]{1,0:T(8,128)(2,1)}, bf16[1936,128]{1,0:T(8,128)(2,1)S(1)}, u32[]{:S(2)}, u32[]{:S(2)}) collective-permute-start(bf16[1936,128]{1,0:T(8,128)(2,1)} %shard_map.37.refs_0_), channel_id=1, source_target_pairs={{0,2},{1,3},{2,0},{3,1},{4,6},{5,7},{6,4},{7,5},{8,10},{9,11},{10,... | collective-permute-start | bytes 1486856 | tf_op jit(solution)/shard_map/ppermute | solution.py:20
  8.4 23.6 %collective-permute-start.4 = (bf16[1936,128]{1,0:T(8,128)(2,1)}, bf16[1936,128]{1,0:T(8,128)(2,1)S(1)}, u32[]{:S(2)}, u32[]{:S(2)}) collective-permute-start(bf16[1936,128]{1,0:T(8,128)(2,1)} %shard_map.37.refs_0_), channel_id=1, source_target_pairs={{0,6},{1,7},{2,4},{3,5},{4,2},{5,3},{6,0},{7,1},{8,14},{9,15},{10,... | collective-permute-start | bytes 1486856 | tf_op jit(solution)/shard_map/ppermute | solution.py:20
  17.2 16.5 %copy-start.3 = (bf16[1936,128]{1,0:T(8,128)(2,1)}, bf16[1936,128]{1,0:T(8,128)(2,1)S(1)}, u32[]{:S(2)}) copy-start(bf16[1936,128]{1,0:T(8,128)(2,1)S(1)} %collective-permute-done.refs_1_) | copy-start | bytes 1486852
  28.5 51.6 %copy-start.5 = (bf16[1936,128]{1,0:T(8,128)(2,1)}, bf16[1936,128]{1,0:T(8,128)(2,1)S(1)}, u32[]{:S(2)}) copy-start(bf16[1936,128]{1,0:T(8,128)(2,1)S(1)} %collective-permute-done.2.refs_3_) | copy-start | bytes 1486852
  32.0 6.7 %copy-start.7 = (bf16[1936,128]{1,0:T(8,128)(2,1)}, bf16[1936,128]{1,0:T(8,128)(2,1)S(1)}, u32[]{:S(2)}) copy-start(bf16[1936,128]{1,0:T(8,128)(2,1)S(1)} %collective-permute-done.4.refs_5_) | copy-start | bytes 1486852
  33.8 28.2 %collective-permute-start.5 = (bf16[11616,128]{1,0:T(8,128)(2,1)S(1)}, bf16[11616,128]{1,0:T(8,128)(2,1)}, u32[]{:S(2)}, u32[]{:S(2)}) collective-permute-start(bf16[11616,128]{1,0:T(8,128)(2,1)S(1)} %get-tuple-element.38), channel_id=1, source_target_pairs={{0,8},{1,9},{2,10},{3,11},{4,12},{5,13},{6,14},{7,15},{8,0},{9,1},... | collective-permute-start | bytes 8921096 | tf_op jit(solution)/shard_map/ppermute | solution.py:20
  33.9 28.1 %collective-permute-start.6 = (bf16[3872,128]{1,0:T(8,128)(2,1)S(1)}, bf16[3872,128]{1,0:T(8,128)(2,1)S(1)}, u32[]{:S(2)}, u32[]{:S(2)}) collective-permute-start(bf16[3872,128]{1,0:T(8,128)(2,1)S(1)} %get-tuple-element.37), channel_id=1, source_target_pairs={{0,1},{1,0},{2,3},{3,2},{4,5},{5,4},{6,7},{7,6},{8,9},{9,8},{10,11... | collective-permute-start | bytes 2973704 | tf_op jit(solution)/shard_map/ppermute | solution.py:20
  35.4 26.6 %collective-permute-start.7 = (bf16[3872,128]{1,0:T(8,128)(2,1)S(1)}, bf16[3872,128]{1,0:T(8,128)(2,1)S(1)}, u32[]{:S(2)}, u32[]{:S(2)}) collective-permute-start(bf16[3872,128]{1,0:T(8,128)(2,1)S(1)} %get-tuple-element.37), channel_id=1, source_target_pairs={{0,16},{1,17},{2,18},{3,19},{4,20},{5,21},{6,22},{7,23},{8,24},{9,... | collective-permute-start | bytes 2973704 | tf_op jit(solution)/shard_map/ppermute | solution.py:20
  36.9 24.7 %collective-permute-start.9 = (bf16[1936,128]{1,0:T(8,128)(2,1)S(1)}, bf16[1936,128]{1,0:T(8,128)(2,1)S(1)}, u32[]{:S(2)}, u32[]{:S(2)}) collective-permute-start(bf16[1936,128]{1,0:T(8,128)(2,1)S(1)} %collective-permute-done.2.refs_3_), channel_id=1, source_target_pairs={{0,4},{1,5},{2,6},{3,7},{4,0},{5,1},{6,2},{7,3},{8,12},{9,13},{10,... | collective-permute-start | bytes 1486856 | tf_op jit(solution)/shard_map/ppermute | solution.py:20
  38.7 23.3 %collective-permute-start.8 = (bf16[1936,128]{1,0:T(8,128)(2,1)S(1)}, bf16[1936,128]{1,0:T(8,128)(2,1)S(1)}, u32[]{:S(2)}, u32[]{:S(2)}) collective-permute-start(bf16[1936,128]{1,0:T(8,128)(2,1)S(1)} %collective-permute-done.4.refs_5_), channel_id=1, source_target_pairs={{0,2},{1,3},{2,0},{3,1},{4,6},{5,7},{6,4},{7,5},{8,10},{9,11},{10,... | collective-permute-start | bytes 1486856 | tf_op jit(solution)/shard_map/ppermute | solution.py:20
  61.7 17.0 %copy-start.8 = (bf16[1936,128]{1,0:T(8,128)(2,1)}, bf16[1936,128]{1,0:T(8,128)(2,1)S(1)}, u32[]{:S(2)}) copy-start(bf16[1936,128]{1,0:T(8,128)(2,1)S(1)} %collective-permute-done.9.refs_8_) | copy-start | bytes 1486852
  62.0 17.5 %copy-start = (bf16[1936,128]{1,0:T(8,128)(2,1)}, bf16[1936,128]{1,0:T(8,128)(2,1)S(1)}, u32[]{:S(2)}) copy-start(bf16[1936,128]{1,0:T(8,128)(2,1)S(1)} %collective-permute-done.8.refs_7_) | copy-start | bytes 1486852
  62.0 16.8 %copy-start.2 = (bf16[3872,128]{1,0:T(8,128)(2,1)}, bf16[3872,128]{1,0:T(8,128)(2,1)S(1)}, u32[]{:S(2)}) copy-start(bf16[3872,128]{1,0:T(8,128)(2,1)S(1)} %collective-permute-done.6.refs_9_) | copy-start | bytes 2973700
  62.0 16.8 %copy-start.1 = (bf16[3872,128]{1,0:T(8,128)(2,1)}, bf16[3872,128]{1,0:T(8,128)(2,1)S(1)}, u32[]{:S(2)}) copy-start(bf16[3872,128]{1,0:T(8,128)(2,1)S(1)} %collective-permute-done.7.refs_10_) | copy-start | bytes 2973700
  78.7 19.6 %collective-permute-start.10 = (bf16[11616,128]{1,0:T(8,128)(2,1)S(1)}, bf16[11616,128]{1,0:T(8,128)(2,1)S(1)}, u32[]{:S(2)}, u32[]{:S(2)}) collective-permute-start(bf16[11616,128]{1,0:T(8,128)(2,1)S(1)} %pad_maximum_fusion), channel_id=1, source_target_pairs={{0,8},{1,9},{2,10},{3,11},{4,12},{5,13},{6,14},{7,15},{8,0},{9,1},... | collective-permute-start | bytes 8921096 | tf_op jit(solution)/shard_map/ppermute | solution.py:20
  78.9 19.4 %collective-permute-start.11 = (bf16[2960,128]{1,0:T(8,128)(2,1)S(1)}, bf16[2960,128]{1,0:T(8,128)(2,1)S(1)}, u32[]{:S(2)}, u32[]{:S(2)}) collective-permute-start(bf16[2960,128]{1,0:T(8,128)(2,1)S(1)} %pad_maximum_fusion.1), channel_id=1, source_target_pairs={{0,1},{1,0},{2,3},{3,2},{4,5},{5,4},{6,7},{7,6},{8,9},{9,8},{10,11... | collective-permute-start | bytes 2273288 | tf_op jit(solution)/shard_map/ppermute | solution.py:20
  79.5 18.5 %collective-permute-start.12 = (bf16[2848,128]{1,0:T(8,128)(2,1)S(1)}, bf16[2848,128]{1,0:T(8,128)(2,1)S(1)}, u32[]{:S(2)}, u32[]{:S(2)}) collective-permute-start(bf16[2848,128]{1,0:T(8,128)(2,1)S(1)} %pad_maximum_fusion.2), channel_id=1, source_target_pairs={{0,16},{1,17},{2,18},{3,19},{4,20},{5,21},{6,22},{7,23},{8,24},{9,... | collective-permute-start | bytes 2187272 | tf_op jit(solution)/shard_map/ppermute | solution.py:20
  80.1 13.2 %collective-permute-start.13 = (bf16[1936,128]{1,0:T(8,128)(2,1)S(1)}, bf16[1936,128]{1,0:T(8,128)(2,1)}, u32[]{:S(2)}, u32[]{:S(2)}) collective-permute-start(bf16[1936,128]{1,0:T(8,128)(2,1)S(1)} %collective-permute-done.2.refs_3_), channel_id=1, source_target_pairs={{0,2},{1,3},{2,0},{3,1},{4,6},{5,7},{6,4},{7,5},{8,10},{9,11},{10,... | collective-permute-start | bytes 1486856 | tf_op jit(solution)/shard_map/ppermute | solution.py:20
  99.9 4.0 %collective-permute-start.14 = (bf16[2960,128]{1,0:T(8,128)(2,1)S(1)}, bf16[2960,128]{1,0:T(8,128)(2,1)S(1)}, u32[]{:S(2)}, u32[]{:S(2)}) collective-permute-start(bf16[2960,128]{1,0:T(8,128)(2,1)S(1)} %collective-permute-done.11.refs_12_), channel_id=1, source_target_pairs={{0,8},{1,9},{2,10},{3,11},{4,12},{5,13},{6,14},{7,15},{8,0},{9,1},... | collective-permute-start | bytes 2273288 | tf_op jit(solution)/shard_map/ppermute | solution.py:20
  99.9 4.0 %collective-permute-start.15 = (bf16[2848,128]{1,0:T(8,128)(2,1)S(1)}, bf16[2848,128]{1,0:T(8,128)(2,1)S(1)}, u32[]{:S(2)}, u32[]{:S(2)}) collective-permute-start(bf16[2848,128]{1,0:T(8,128)(2,1)S(1)} %collective-permute-done.12.refs_14_), channel_id=1, source_target_pairs={{0,8},{1,9},{2,10},{3,11},{4,12},{5,13},{6,14},{7,15},{8,0},{9,1},... | collective-permute-start | bytes 2187272 | tf_op jit(solution)/shard_map/ppermute | solution.py:20
  100.5 3.4 %collective-permute-start.16 = (bf16[1936,128]{1,0:T(8,128)(2,1)}, bf16[1936,128]{1,0:T(8,128)(2,1)S(1)}, u32[]{:S(2)}, u32[]{:S(2)}) collective-permute-start(bf16[1936,128]{1,0:T(8,128)(2,1)} %collective-permute-done.13.refs_16_), channel_id=1, source_target_pairs={{0,8},{1,9},{2,10},{3,11},{4,12},{5,13},{6,14},{7,15},{8,0},{9,1},... | collective-permute-start | bytes 1486856 | tf_op jit(solution)/shard_map/ppermute | solution.py:20
  (8 other events, 26.4 us)

commit v8 on v7

--- a/solution.py
+++ b/solution.py
@@ -8,6 +8,7 @@
 from jax.sharding import PartitionSpec as P
 
 NOTE = 16
+QUAD = 4
 AXES = ("row", "col")
 
 
@@ -45,13 +46,12 @@
     xl = swap(jnp.concatenate([f2, yp[full : full + cut]], axis=0), x)
     yl = swap(jnp.concatenate([f2, xp[full + cut :]], axis=0), y)
     d1 = swap(d0, z1)
-    spot = cross(
-        (f2, whole(z2)), (d2, whole(z2 | x | y)), (xp, whole(z1 | x, z3 | x)), (yp, whole(z1 | y, z3 | y))
-    )
-    xl, yl, d1 = finish(spot, xl, yl, d1)
+    spots = [cross((xp, whole(z1 | x, z3 | x))), cross((yp, whole(z1 | y, z3 | y)))]
+    xl, yl, d1, f2, d2 = finish(spots[0], *finish(spots[1], xl, yl, d1, f2, d2))
     cross((xl, [(z2 | x, 0, full), (z3 | x | y, 0, cut)]))
     cross((yl, [(z2 | y, 0, full), (z3 | x | y, cut, full - cut)]))
-    cross((d1, whole(z1 | x | y)))
+    for item in ((f2, whole(z2)), (d2, whole(z2 | x | y)), (d1, whole(z1 | x | y))):
+        cross(item)
     return found
 
 
@@ -89,7 +89,7 @@
     tables, (out, band, square, own, notes, keep, arrived, noted) = refs[:count], refs[count:]
     far = 2 * reach
     slots, wide = 2 * reach + 1, 4 * reach + 1
-    pitch = slots + 2
+    pitch = slots
     kind = band.dtype
 
     def span(first, n):
@@ -107,7 +107,7 @@
             def _(table=table, begin=begin, start=start, size=size, body=body, k=k):
                 pltpu.make_async_copy(
                     table.at[pl.ds(begin, body)],
-                    band.at[pl.ds(pl.multiple_of((k * pitch + 1) * edge + start, edge), body)],
+                    band.at[pl.ds(pl.multiple_of(k * pitch * edge + start, edge), body)],
                     arrived.at[k],
                 ).start()
                 if size > body:
@@ -125,27 +125,13 @@
         body = pl.ds(0, slots * edge)
         pltpu.make_async_copy(tables[0].at[body], band.at[body], arrived.at[k]).wait()
 
-    def clear(k, carry):
-        zero = jnp.zeros((edge, edge), kind)
-        band[span(k * pitch, 1), :] = zero
-        band[span(k * pitch + slots + 1, 1), :] = zero
+    zero = jnp.zeros((edge, edge), kind)
+
+    def clear(s, carry):
+        band[span((2 * far + 1) * pitch + s, 1), :] = zero
         return carry
 
-    lax.fori_loop(0, 2 * far + 2, clear, 0)
-
-    def clear_last(s, carry):
-        band[span((2 * far + 1) * pitch + s, 1), :] = jnp.zeros((edge, edge), kind)
-        return carry
-
-    lax.fori_loop(1, slots + 1, clear_last, 0)
-
-    def clear_square(r, carry):
-        zero = jnp.zeros((edge, edge), kind)
-        square[span(r, 1), pl.ds(0, edge)] = zero
-        square[span(r, 1), pl.ds((wide + 1) * edge, edge)] = zero
-        return carry
-
-    lax.fori_loop(0, slots + 1, clear_square, 0)
+    lax.fori_loop(0, slots, clear, 0)
 
     for r in range(slots):
         pltpu.make_async_copy(tables[0].at[pl.ds(0, NOTE)], notes.at[r], noted).wait()
@@ -165,54 +151,60 @@
         ready(k)
 
     def strip(k, first, n):
-        return jnp.concatenate([band[span(k * pitch + first + s, 1), :] for s in range(n)], axis=1)
-
-    def row_pair(pair, carry):
-        r = 2 * pair
-        ready(r + far)
-
-        @pl.when(r + far + 1 <= 2 * far)
-        def _():
-            ready(r + far + 1)
-
-        middle = jnp.where((r == reach) | (r + 1 == reach), 1, 0)
-        for d in range(-far, far + 1, 2):
-            low, high = max(-reach, d - reach), min(reach + 1, d + reach + 1)
+        return jnp.concatenate(
+            [band[span(k * pitch + s, 1), :] if 0 <= s < slots else zero for s in range(first, first + n)], axis=1
+        )
+
+    def square_strip(r, first, n):
+        return jnp.concatenate(
+            [
+                square[r * edge : (r + 1) * edge, u * edge : (u + 1) * edge] if 0 <= u < wide else zero
+                for u in range(first, first + n)
+            ],
+            axis=1,
+        )
+
+    def row_quad(quad, carry):
+        r = QUAD * quad
+        for i in range(QUAD):
+            k = r + far + i
+
+            @pl.when(k <= 2 * far)
+            def _(k=k):
+                ready(k)
+
+        middle = jnp.where(quad == reach // QUAD, 1, 0)
+        for d in range(-far, far + QUAD, 2):
+            low, high = max(-reach, d - reach), min(reach + QUAD - 1, d + reach + 1)
             size = high - low + 1
-            left = jnp.concatenate(
-                [strip(r + reach, low + reach + 1, size), strip(r + reach + 1, low + reach, size)], axis=0
-            )
-            right = jnp.concatenate(
-                [strip(r + reach + e, d - e + reach + 1, 2) for e in range(low, high + 1)], axis=0
-            )
+            left = jnp.concatenate([strip(r + reach + i, low + reach - i, size) for i in range(QUAD)], axis=0)
+            right = jnp.concatenate([strip(r + reach + e, d - e + reach, 2) for e in range(low, high + 1)], axis=0)
             product = jnp.dot(left, right, preferred_element_type=jnp.float32)
-            for i in range(2):
-                u = d + far - i
-                mask = jnp.concatenate(
-                    [keep[r + i, pl.ds(min(max(u + j, 0), wide - 1), 1), :] for j in range(2)], axis=1
-                )
-                kept = product[i * edge : (i + 1) * edge] * mask
-                square[span(r + i, 1), pl.ds((u + 1) * edge, 2 * edge)] = kept.astype(kind)
-                if i == reach % 2:
-                    own[middle, :, pl.ds((u + 1) * edge, 2 * edge)] = kept
+            for i in range(QUAD):
+                for j in range(2):
+                    u = d + far - i + j
+                    if 0 <= u < wide:
+                        kept = product[i * edge : (i + 1) * edge, j * edge : (j + 1) * edge]
+                        kept = kept * keep[r + i, u : u + 1, :]
+                        square[span(r + i, 1), u * edge : (u + 1) * edge] = kept.astype(kind)
+                        if i == reach % QUAD:
+                            own[middle, :, u * edge : (u + 1) * edge] = kept
         return carry
 
-    lax.fori_loop(0, (slots + 1) // 2, row_pair, 0)
-
-    for c in range(-far, far + 1, 2):
-        low, high = max(-reach, c - far), min(reach, c + far + 1)
-        left = strip(far, low + reach + 1, high - low + 1)
+    lax.fori_loop(0, (slots + 1) // QUAD, row_quad, 0)
+
+    for c in range(-far, far + 1, QUAD):
+        low, high = max(-reach, c - far), min(reach, c + far + QUAD - 1)
+        left = strip(far, low + reach, high - low + 1)
         right = jnp.concatenate(
-            [square[span(r + reach, 1), pl.ds((c - r + far + 1) * edge, 2 * edge)] for r in range(low, high + 1)],
-            axis=0,
+            [square_strip(r + reach, c - r + far, QUAD) for r in range(low, high + 1)], axis=0
         )
         cube = jnp.dot(left, right, preferred_element_type=jnp.float32)
-        for j in range(2):
+        for j in range(QUAD):
             u = c + far + j
             if u < wide:
-                kept = own[1, :, pl.ds((u + 1) * edge, edge)]
-                value = 3.0 * kept - 2.0 * cube[:, j * edge : (j + 1) * edge]
-                out[u] = (keep[reach, pl.ds(u, 1), :] * value).astype(out.dtype)
+                value = 3.0 * own[1, :, u * edge : (u + 1) * edge] - 2.0 * cube[:, j * edge : (j + 1) * edge]
+                out[u] = (keep[reach, u : u + 1, :] * value).astype(out.dtype)
 
 
 def pack(pattern, filter_mask, density, payload):
@@ -248,15 +240,15 @@
         in_specs=[smem] + [pl.BlockSpec(memory_space=pl.ANY)] * len(tables),
         out_specs=vmem,
         scratch_shapes=[
-            pltpu.VMEM(((2 * far + 2) * (slots + 2) * edge, edge), density.dtype),
-            pltpu.VMEM(((slots + 1) * edge, (wide + 2) * edge), density.dtype),
-            pltpu.VMEM((2, edge, (wide + 2) * edge), jnp.float32),
+            pltpu.VMEM(((2 * far + 2) * slots * edge, edge), density.dtype),
+            pltpu.VMEM(((slots + 1) * edge, wide * edge), density.dtype),
+            pltpu.VMEM((2, edge, wide * edge), jnp.float32),
             pltpu.VMEM((slots + 1, NOTE, edge), density.dtype),
             pltpu.VMEM((slots + 1, -(-wide // 8) * 8, edge), jnp.float32),
             pltpu.SemaphoreType.DMA((2 * far + 1,)),
             pltpu.SemaphoreType.DMA,
         ],
-        compiler_params=pltpu.CompilerParams(vmem_limit_bytes=56 * 2**20),
+        compiler_params=pltpu.CompilerParams(vmem_limit_bytes=40 * 2**20),
         cost_estimate=pl.CostEstimate(flops=17 * 10**9, bytes_accessed=15 * 2**20, transcendentals=0),
     )(place, *tables)
     return result[None]

time: 135 us -> 127 us (0.941)
  other arithmetic: 17.3 us -> 0.1 us
  waiting for transfers between devices: 64.2 us -> 67.4 us
  local copies, waits for them, and re-layouts: 5.28 us -> 8.43 us
  Pallas kernels: 30.9 us -> 33.7 us
    concatenate x1 -> x0, other arithmetic: 16.6 us -> none  [cross(): jnp.concatenate(arrays, axis=0)]
    ppermute x17 -> x20, waiting for transfers between devices: 64.2 us -> 67.4 us  [swap(): return lax.ppermute(value, AXES, [(i, i ^ mask) for i in range(count)])]
    unnamed x35 -> x23, local copies, waits for them, and re-layouts: 4.99 us -> 8.15 us
    pallas_call x1, Pallas kernels: 29 us -> 31.8 us  [shards(): pl.pallas_call(functools.partial(purify, reach, edge, layout), out_shape=...]
    ppermute x17 -> x20, starting transfers between devices: 16.6 us -> 16.3 us  [swap(): return lax.ppermute(value, AXES, [(i, i ^ mask) for i in range(count)])]
  transfers between devices with their start and end apart: 17 -> 20, of which waited for: 10 -> 11; matrix products, arithmetic and copies ran while one was open for 1% -> 0% of each run, Pallas kernels for 0% -> 0%
where the time goes in v8:
time: 127 us; the launch traced here: 126 us
  waiting for transfers between devices  67.4 us (53%)
  Pallas kernels  33.7 us (27%)
  starting transfers between devices  16.3 us (13%)
  local copies, waits for them, and re-layouts  8.43 us (7%)
    ppermute x20, waiting for transfers between devices, swap(): return lax.ppermute(value, AXES, [(i, i ^ mask) for i in range(count)])  67.4 us
    pallas_call x1, Pallas kernels, shards(): pl.pallas_call(functools.partial(purify, reach, edge, layout), out_shape=...  31.8 us
    ppermute x20, starting transfers between devices, swap(): return lax.ppermute(value, AXES, [(i, i ^ mask) for i in range(count)])  16.3 us
    unnamed x23, local copies, waits for them, and re-layouts  8.15 us
  transfers between devices with their start and end apart: 20, of which 11 were waited for; matrix products, arithmetic and copies ran while one was open for 0% of the time, Pallas kernels for 0%

profile of v8, /device:TPU:0, one launch (start us, length us, event | category | flops | bytes accessed | tf_op | source)
XLA Modules:
  0.0 126.3 jit_solution(11840274517076843145)
XLA Ops:
  0.0 1.9 %shard_map.37.refs_0_ = bf16[1936,128]{1,0:T(8,128)(2,1)} custom-call(s32[1,15]{1,0:T(1,128)} %pattern.1, s32[1,29]{1,0:T(1,128)} %filter_mask.1, bf16[15,128,128]{2,1,0:T(8,128)(2,1)} %bitcast.33), custom_call_target="tpu_custom_call" | custom-call | tf_op jit(solution)/shard_map/pallas_call | solution.py:228
  1.9 5.0 %collective-permute-start.4 = (bf16[1936,128]{1,0:T(8,128)(2,1)}, bf16[1936,128]{1,0:T(8,128)(2,1)S(1)}, u32[]{:S(2)}, u32[]{:S(2)}) collective-permute-start(bf16[1936,128]{1,0:T(8,128)(2,1)} %shard_map.37.refs_0_), channel_id=1, source_target_pairs={{0,6},{1,7},{2,4},{3,5},{4,2},{5,3},{6,0},{7,1},{8,14},{9,15},{10,... | collective-permute-start | bytes 1486856 | tf_op jit(solution)/shard_map/ppermute | solution.py:21
  7.0 2.4 %collective-permute-start.2 = (bf16[1936,128]{1,0:T(8,128)(2,1)}, bf16[1936,128]{1,0:T(8,128)(2,1)S(1)}, u32[]{:S(2)}, u32[]{:S(2)}) collective-permute-start(bf16[1936,128]{1,0:T(8,128)(2,1)} %shard_map.37.refs_0_), channel_id=1, source_target_pairs={{0,17},{1,16},{2,19},{3,18},{4,21},{5,20},{6,23},{7,22},{8,25},{9,... | collective-permute-start | bytes 1486856 | tf_op jit(solution)/shard_map/ppermute | solution.py:21
  10.5 8.9 %collective-permute-done.4.refs_5_ = bf16[1936,128]{1,0:T(8,128)(2,1)S(1)} collective-permute-done((bf16[1936,128]{1,0:T(8,128)(2,1)}, bf16[1936,128]{1,0:T(8,128)(2,1)S(1)}, u32[]{:S(2)}, u32[]{:S(2)}) %collective-permute-start.4) | collective-permute-done | bytes 495648 | tf_op jit(solution)/shard_map/ppermute | solution.py:21
  19.4 9.8 %collective-permute-done.3.refs_4_ = bf16[1936,128]{1,0:T(8,128)(2,1)S(1)} collective-permute-done((bf16[1936,128]{1,0:T(8,128)(2,1)}, bf16[1936,128]{1,0:T(8,128)(2,1)S(1)}, u32[]{:S(2)}, u32[]{:S(2)}) %collective-permute-start.3) | collective-permute-done | bytes 495648 | tf_op jit(solution)/shard_map/ppermute | solution.py:21
  29.2 2.3 %collective-permute-done.1.refs_2_ = bf16[1936,128]{1,0:T(8,128)(2,1)S(1)} collective-permute-done((bf16[1936,128]{1,0:T(8,128)(2,1)}, bf16[1936,128]{1,0:T(8,128)(2,1)S(1)}, u32[]{:S(2)}, u32[]{:S(2)}) %collective-permute-start.1) | collective-permute-done | bytes 495648 | tf_op jit(solution)/shard_map/ppermute | solution.py:21
  31.6 1.1 constant_dynamic-update-slice_fusion.5
  33.2 1.5 %collective-permute-start.7 = (bf16[3872,128]{1,0:T(8,128)(2,1)S(1)}, bf16[3872,128]{1,0:T(8,128)(2,1)S(1)}, u32[]{:S(2)}, u32[]{:S(2)}) collective-permute-start(bf16[3872,128]{1,0:T(8,128)(2,1)S(1)} %get-tuple-element.53), channel_id=1, source_target_pairs={{0,16},{1,17},{2,18},{3,19},{4,20},{5,21},{6,22},{7,23},{8,24},{9,... | collective-permute-start | bytes 2973704 | tf_op jit(solution)/shard_map/ppermute | solution.py:21
  34.7 0.8 collective-permute-start.6
  35.5 1.7 %collective-permute-start.8 = (bf16[1936,128]{1,0:T(8,128)(2,1)S(1)}, bf16[1936,128]{1,0:T(8,128)(2,1)S(1)}, u32[]{:S(2)}, u32[]{:S(2)}) collective-permute-start(bf16[1936,128]{1,0:T(8,128)(2,1)S(1)} %collective-permute-done.4.refs_5_), channel_id=1, source_target_pairs={{0,2},{1,3},{2,0},{3,1},{4,6},{5,7},{6,4},{7,5},{8,10},{9,11},{10,... | collective-permute-start | bytes 1486856 | tf_op jit(solution)/shard_map/ppermute | solution.py:21
  37.2 19.7 %collective-permute-done.8.refs_15_ = bf16[1936,128]{1,0:T(8,128)(2,1)S(1)} collective-permute-done((bf16[1936,128]{1,0:T(8,128)(2,1)S(1)}, bf16[1936,128]{1,0:T(8,128)(2,1)S(1)}, u32[]{:S(2)}, u32[]{:S(2)}) %collective-permute-start.8) | collective-permute-done | bytes 495648 | tf_op jit(solution)/shard_map/ppermute | solution.py:21
  56.9 4.8 %collective-permute-done.9.refs_17_ = bf16[1936,128]{1,0:T(8,128)(2,1)} collective-permute-done((bf16[1936,128]{1,0:T(8,128)(2,1)S(1)}, bf16[1936,128]{1,0:T(8,128)(2,1)}, u32[]{:S(2)}, u32[]{:S(2)}) %collective-permute-start.9) | collective-permute-done | bytes 495648 | tf_op jit(solution)/shard_map/ppermute | solution.py:21
  62.5 1.3 %collective-permute-start.12 = (bf16[2960,128]{1,0:T(8,128)(2,1)S(1)}, bf16[2960,128]{1,0:T(8,128)(2,1)}, u32[]{:S(2)}, u32[]{:S(2)}) collective-permute-start(bf16[2960,128]{1,0:T(8,128)(2,1)S(1)} %pad_maximum_fusion), channel_id=1, source_target_pairs={{0,1},{1,0},{2,3},{3,2},{4,5},{5,4},{6,7},{7,6},{8,9},{9,8},{10,11... | collective-permute-start | bytes 2273288 | tf_op jit(solution)/shard_map/ppermute | solution.py:21
  64.5 12.8 %collective-permute-done.14.refs_19_ = bf16[1936,128]{1,0:T(8,128)(2,1)} collective-permute-done((bf16[1936,128]{1,0:T(8,128)(2,1)S(1)}, bf16[1936,128]{1,0:T(8,128)(2,1)}, u32[]{:S(2)}, u32[]{:S(2)}) %collective-permute-start.14) | collective-permute-done | bytes 495648 | tf_op jit(solution)/shard_map/ppermute | solution.py:21
  77.3 4.7 %collective-permute-done.13.refs_13_ = bf16[2848,128]{1,0:T(8,128)(2,1)} collective-permute-done((bf16[2848,128]{1,0:T(8,128)(2,1)S(1)}, bf16[2848,128]{1,0:T(8,128)(2,1)}, u32[]{:S(2)}, u32[]{:S(2)}) %collective-permute-start.13) | collective-permute-done | bytes 729120 | tf_op jit(solution)/shard_map/ppermute | solution.py:21
  82.0 1.0 copy-done.7
  83.0 1.0 copy-done.5
  85.3 2.4 %collective-permute-done.17.refs_16_ = bf16[1936,128]{1,0:T(8,128)(2,1)} collective-permute-done((bf16[1936,128]{1,0:T(8,128)(2,1)S(1)}, bf16[1936,128]{1,0:T(8,128)(2,1)}, u32[]{:S(2)}, u32[]{:S(2)}) %collective-permute-start.17) | collective-permute-done | bytes 495648 | tf_op jit(solution)/shard_map/ppermute | solution.py:21
  87.7 1.3 collective-permute-done.18.refs_18_
  89.7 1.2 copy-done.2
  90.9 1.2 copy-done.4
  92.1 1.2 copy-done.6
  93.3 1.2 copy-done.8
  94.5 31.8 %shard_map.38 = bf16[29,128,128]{2,1,0:T(8,128)(2,1)} custom-call(s32[34]{0:T(128)S(1)} %compare_select_fusion.place, bf16[1936,128]{1,0:T(8,128)(2,1)S(1)} %copy-done, bf16[1936,128]{1,0:T(8,128)(2,1)S(1)} %collective-permute-done.refs_1_, bf16[1936,128]{1,0:T(8,128)(2,1)S(1)} %collective-permute-done.1.refs_2_, ...), custom_call_target="tpu_custom_call" | custom-call | flops 16999999488 | bytes 15728640 | tf_op jit(solution)/shard_map/pallas_call | solution.py:237
  (48 shorter events, 5.0 us)
Async XLA Ops:
  1.9 17.5 %collective-permute-start.4 = (bf16[1936,128]{1,0:T(8,128)(2,1)}, bf16[1936,128]{1,0:T(8,128)(2,1)S(1)}, u32[]{:S(2)}, u32[]{:S(2)}) collective-permute-start(bf16[1936,128]{1,0:T(8,128)(2,1)} %shard_map.37.refs_0_), channel_id=1, source_target_pairs={{0,6},{1,7},{2,4},{3,5},{4,2},{5,3},{6,0},{7,1},{8,14},{9,15},{10,... | collective-permute-start | bytes 1486856 | tf_op jit(solution)/shard_map/ppermute | solution.py:21
  7.0 22.2 %collective-permute-start.3 = (bf16[1936,128]{1,0:T(8,128)(2,1)}, bf16[1936,128]{1,0:T(8,128)(2,1)S(1)}, u32[]{:S(2)}, u32[]{:S(2)}) collective-permute-start(bf16[1936,128]{1,0:T(8,128)(2,1)} %shard_map.37.refs_0_), channel_id=1, source_target_pairs={{0,2},{1,3},{2,0},{3,1},{4,6},{5,7},{6,4},{7,5},{8,10},{9,11},{10,... | collective-permute-start | bytes 1486856 | tf_op jit(solution)/shard_map/ppermute | solution.py:21
  7.0 22.2 %collective-permute-start.2 = (bf16[1936,128]{1,0:T(8,128)(2,1)}, bf16[1936,128]{1,0:T(8,128)(2,1)S(1)}, u32[]{:S(2)}, u32[]{:S(2)}) collective-permute-start(bf16[1936,128]{1,0:T(8,128)(2,1)} %shard_map.37.refs_0_), channel_id=1, source_target_pairs={{0,17},{1,16},{2,19},{3,18},{4,21},{5,20},{6,23},{7,22},{8,25},{9,... | collective-permute-start | bytes 1486856 | tf_op jit(solution)/shard_map/ppermute | solution.py:21
  9.4 22.1 %collective-permute-start.1 = (bf16[1936,128]{1,0:T(8,128)(2,1)}, bf16[1936,128]{1,0:T(8,128)(2,1)S(1)}, u32[]{:S(2)}, u32[]{:S(2)}) collective-permute-start(bf16[1936,128]{1,0:T(8,128)(2,1)} %shard_map.37.refs_0_), channel_id=1, source_target_pairs={{0,16},{1,17},{2,18},{3,19},{4,20},{5,21},{6,22},{7,23},{8,24},{9,... | collective-permute-start | bytes 1486856 | tf_op jit(solution)/shard_map/ppermute | solution.py:21
  9.9 21.6 %collective-permute-start = (bf16[1936,128]{1,0:T(8,128)(2,1)}, bf16[1936,128]{1,0:T(8,128)(2,1)S(1)}, u32[]{:S(2)}, u32[]{:S(2)}) collective-permute-start(bf16[1936,128]{1,0:T(8,128)(2,1)} %shard_map.37.refs_0_), channel_id=1, source_target_pairs={{0,1},{1,0},{2,3},{3,2},{4,5},{5,4},{6,7},{7,6},{8,9},{9,8},{10,11... | collective-permute-start | bytes 1486856 | tf_op jit(solution)/shard_map/ppermute | solution.py:21
  33.0 56.7 %copy-start = (bf16[1936,128]{1,0:T(8,128)(2,1)S(1)}, bf16[1936,128]{1,0:T(8,128)(2,1)}, u32[]{:S(2)}) copy-start(bf16[1936,128]{1,0:T(8,128)(2,1)} %shard_map.37.refs_0_) | copy-start | bytes 1486852
  33.1 28.6 %collective-permute-start.5 = (bf16[11616,128]{1,0:T(8,128)(2,1)S(1)}, bf16[11616,128]{1,0:T(8,128)(2,1)}, u32[]{:S(2)}, u32[]{:S(2)}) collective-permute-start(bf16[11616,128]{1,0:T(8,128)(2,1)S(1)} %get-tuple-element.54), channel_id=1, source_target_pairs={{0,8},{1,9},{2,10},{3,11},{4,12},{5,13},{6,14},{7,15},{8,0},{9,1},... | collective-permute-start | bytes 8921096 | tf_op jit(solution)/shard_map/ppermute | solution.py:21
  33.2 28.5 %collective-permute-start.7 = (bf16[3872,128]{1,0:T(8,128)(2,1)S(1)}, bf16[3872,128]{1,0:T(8,128)(2,1)S(1)}, u32[]{:S(2)}, u32[]{:S(2)}) collective-permute-start(bf16[3872,128]{1,0:T(8,128)(2,1)S(1)} %get-tuple-element.53), channel_id=1, source_target_pairs={{0,16},{1,17},{2,18},{3,19},{4,20},{5,21},{6,22},{7,23},{8,24},{9,... | collective-permute-start | bytes 2973704 | tf_op jit(solution)/shard_map/ppermute | solution.py:21
  34.7 27.0 %collective-permute-start.6 = (bf16[3872,128]{1,0:T(8,128)(2,1)S(1)}, bf16[3872,128]{1,0:T(8,128)(2,1)S(1)}, u32[]{:S(2)}, u32[]{:S(2)}) collective-permute-start(bf16[3872,128]{1,0:T(8,128)(2,1)S(1)} %get-tuple-element.53), channel_id=1, source_target_pairs={{0,1},{1,0},{2,3},{3,2},{4,5},{5,4},{6,7},{7,6},{8,9},{9,8},{10,11... | collective-permute-start | bytes 2973704 | tf_op jit(solution)/shard_map/ppermute | solution.py:21
  35.5 21.4 %collective-permute-start.8 = (bf16[1936,128]{1,0:T(8,128)(2,1)S(1)}, bf16[1936,128]{1,0:T(8,128)(2,1)S(1)}, u32[]{:S(2)}, u32[]{:S(2)}) collective-permute-start(bf16[1936,128]{1,0:T(8,128)(2,1)S(1)} %collective-permute-done.4.refs_5_), channel_id=1, source_target_pairs={{0,2},{1,3},{2,0},{3,1},{4,6},{5,7},{6,4},{7,5},{8,10},{9,11},{10,... | collective-permute-start | bytes 1486856 | tf_op jit(solution)/shard_map/ppermute | solution.py:21
  37.2 24.5 %collective-permute-start.9 = (bf16[1936,128]{1,0:T(8,128)(2,1)S(1)}, bf16[1936,128]{1,0:T(8,128)(2,1)}, u32[]{:S(2)}, u32[]{:S(2)}) collective-permute-start(bf16[1936,128]{1,0:T(8,128)(2,1)S(1)} %collective-permute-done.2.refs_3_), channel_id=1, source_target_pairs={{0,4},{1,5},{2,6},{3,7},{4,0},{5,1},{6,2},{7,3},{8,12},{9,13},{10,... | collective-permute-start | bytes 1486856 | tf_op jit(solution)/shard_map/ppermute | solution.py:21
  61.7 22.2 %copy-start.1 = (bf16[3872,128]{1,0:T(8,128)(2,1)}, bf16[3872,128]{1,0:T(8,128)(2,1)S(1)}, u32[]{:S(2)}) copy-start(bf16[3872,128]{1,0:T(8,128)(2,1)S(1)} %collective-permute-done.7.refs_9_) | copy-start | bytes 2973700
  61.7 22.7 %copy-start.3 = (bf16[3872,128]{1,0:T(8,128)(2,1)}, bf16[3872,128]{1,0:T(8,128)(2,1)S(1)}, u32[]{:S(2)}) copy-start(bf16[3872,128]{1,0:T(8,128)(2,1)S(1)} %collective-permute-done.6.refs_7_) | copy-start | bytes 2973700
  61.8 21.2 %collective-permute-start.10 = (bf16[3872,128]{1,0:T(8,128)(2,1)S(1)}, bf16[3872,128]{1,0:T(8,128)(2,1)S(1)}, u32[]{:S(2)}, u32[]{:S(2)}) collective-permute-start(bf16[3872,128]{1,0:T(8,128)(2,1)S(1)} %collective-permute-done.6.refs_7_), channel_id=1, source_target_pairs={{0,8},{1,9},{2,10},{3,11},{4,12},{5,13},{6,14},{7,15},{8,0},{9,1},... | collective-permute-start | bytes 2973704 | tf_op jit(solution)/shard_map/ppermute | solution.py:21
  61.9 20.1 %collective-permute-start.11 = (bf16[3872,128]{1,0:T(8,128)(2,1)S(1)}, bf16[3872,128]{1,0:T(8,128)(2,1)S(1)}, u32[]{:S(2)}, u32[]{:S(2)}) collective-permute-start(bf16[3872,128]{1,0:T(8,128)(2,1)S(1)} %collective-permute-done.7.refs_9_), channel_id=1, source_target_pairs={{0,8},{1,9},{2,10},{3,11},{4,12},{5,13},{6,14},{7,15},{8,0},{9,1},... | collective-permute-start | bytes 2973704 | tf_op jit(solution)/shard_map/ppermute | solution.py:21
  62.5 19.5 %collective-permute-start.12 = (bf16[2960,128]{1,0:T(8,128)(2,1)S(1)}, bf16[2960,128]{1,0:T(8,128)(2,1)}, u32[]{:S(2)}, u32[]{:S(2)}) collective-permute-start(bf16[2960,128]{1,0:T(8,128)(2,1)S(1)} %pad_maximum_fusion), channel_id=1, source_target_pairs={{0,1},{1,0},{2,3},{3,2},{4,5},{5,4},{6,7},{7,6},{8,9},{9,8},{10,11... | collective-permute-start | bytes 2273288 | tf_op jit(solution)/shard_map/ppermute | solution.py:21
  63.8 18.1 %collective-permute-start.13 = (bf16[2848,128]{1,0:T(8,128)(2,1)S(1)}, bf16[2848,128]{1,0:T(8,128)(2,1)}, u32[]{:S(2)}, u32[]{:S(2)}) collective-permute-start(bf16[2848,128]{1,0:T(8,128)(2,1)S(1)} %pad_maximum_fusion.1), channel_id=1, source_target_pairs={{0,16},{1,17},{2,18},{3,19},{4,20},{5,21},{6,22},{7,23},{8,24},{9,... | collective-permute-start | bytes 2187272 | tf_op jit(solution)/shard_map/ppermute | solution.py:21
  64.5 12.8 %collective-permute-start.14 = (bf16[1936,128]{1,0:T(8,128)(2,1)S(1)}, bf16[1936,128]{1,0:T(8,128)(2,1)}, u32[]{:S(2)}, u32[]{:S(2)}) collective-permute-start(bf16[1936,128]{1,0:T(8,128)(2,1)S(1)} %collective-permute-done.2.refs_3_), channel_id=1, source_target_pairs={{0,2},{1,3},{2,0},{3,1},{4,6},{5,7},{6,4},{7,5},{8,10},{9,11},{10,... | collective-permute-start | bytes 1486856 | tf_op jit(solution)/shard_map/ppermute | solution.py:21
  83.9 5.8 %collective-permute-start.15 = (bf16[2960,128]{1,0:T(8,128)(2,1)}, bf16[2960,128]{1,0:T(8,128)(2,1)}, u32[]{:S(2)}, u32[]{:S(2)}) collective-permute-start(bf16[2960,128]{1,0:T(8,128)(2,1)} %collective-permute-done.12.refs_11_), channel_id=1, source_target_pairs={{0,8},{1,9},{2,10},{3,11},{4,12},{5,13},{6,14},{7,15},{8,0},{9,1},... | collective-permute-start | bytes 2273288 | tf_op jit(solution)/shard_map/ppermute | solution.py:21
  83.9 5.8 %collective-permute-start.16 = (bf16[2848,128]{1,0:T(8,128)(2,1)}, bf16[2848,128]{1,0:T(8,128)(2,1)}, u32[]{:S(2)}, u32[]{:S(2)}) collective-permute-start(bf16[2848,128]{1,0:T(8,128)(2,1)} %collective-permute-done.13.refs_13_), channel_id=1, source_target_pairs={{0,8},{1,9},{2,10},{3,11},{4,12},{5,13},{6,14},{7,15},{8,0},{9,1},... | collective-permute-start | bytes 2187272 | tf_op jit(solution)/shard_map/ppermute | solution.py:21
  84.5 3.3 %collective-permute-start.17 = (bf16[1936,128]{1,0:T(8,128)(2,1)S(1)}, bf16[1936,128]{1,0:T(8,128)(2,1)}, u32[]{:S(2)}, u32[]{:S(2)}) collective-permute-start(bf16[1936,128]{1,0:T(8,128)(2,1)S(1)} %collective-permute-done.8.refs_15_), channel_id=1, source_target_pairs={{0,8},{1,9},{2,10},{3,11},{4,12},{5,13},{6,14},{7,15},{8,0},{9,1},... | collective-permute-start | bytes 1486856 | tf_op jit(solution)/shard_map/ppermute | solution.py:21
  84.5 4.5 %collective-permute-start.18 = (bf16[1936,128]{1,0:T(8,128)(2,1)}, bf16[1936,128]{1,0:T(8,128)(2,1)}, u32[]{:S(2)}, u32[]{:S(2)}) collective-permute-start(bf16[1936,128]{1,0:T(8,128)(2,1)} %collective-permute-done.9.refs_17_), channel_id=1, source_target_pairs={{0,8},{1,9},{2,10},{3,11},{4,12},{5,13},{6,14},{7,15},{8,0},{9,1},... | collective-permute-start | bytes 1486856 | tf_op jit(solution)/shard_map/ppermute | solution.py:21
  85.0 4.7 %collective-permute-start.19 = (bf16[1936,128]{1,0:T(8,128)(2,1)}, bf16[1936,128]{1,0:T(8,128)(2,1)}, u32[]{:S(2)}, u32[]{:S(2)}) collective-permute-start(bf16[1936,128]{1,0:T(8,128)(2,1)} %collective-permute-done.14.refs_19_), channel_id=1, source_target_pairs={{0,8},{1,9},{2,10},{3,11},{4,12},{5,13},{6,14},{7,15},{8,0},{9,1},... | collective-permute-start | bytes 1486856 | tf_op jit(solution)/shard_map/ppermute | solution.py:21
  89.7 1.2 copy-start.2
  (5 other events, 5.6 us)

commit v9 on v8

--- a/solution.py
+++ b/solution.py
@@ -2,17 +2,19 @@
 
 import jax
 import jax.numpy as jnp
+import numpy as np
 from jax import lax
 from jax.experimental import pallas as pl
 from jax.experimental.pallas import tpu as pltpu
 from jax.sharding import PartitionSpec as P
 
 NOTE = 16
-QUAD = 4
+GROUP = 2
+WIDTH = 4
 AXES = ("row", "col")
 
 
-def cube(own, count, here, cut):
+def cube(own, count, cut):
     x, z1, z2, z3, core, y = 1, 2, 4, 6, 8, 16
     full = own.shape[0]
     found = []
@@ -36,13 +38,12 @@
         return arrays
 
     x0, y0, d0, f1, f3 = (swap(own, mask) for mask in (x, y, x | y, z1, z3))
-    own, x0, y0, d0, f1, f3 = lax.optimization_barrier((own, x0, y0, d0, f1, f3))
     pair = jnp.concatenate([f1, f3], axis=0)
     xp, yp, f2, d2 = swap(pair, x), swap(pair, y), swap(f3, z1), swap(d0, z2)
     spot = cross(
         (own, whole(0)), (x0, whole(x)), (y0, whole(y)), (d0, whole(x | y)), (f1, whole(z1)), (f3, whole(z3))
     )
-    xp, yp, f2, d2, d0 = finish(spot, xp, yp, f2, d2, d0)
+    xp, yp, f2, d0 = finish(spot, xp, yp, f2, d0)
     xl = swap(jnp.concatenate([f2, yp[full : full + cut]], axis=0), x)
     yl = swap(jnp.concatenate([f2, xp[full + cut :]], axis=0), y)
     d1 = swap(d0, z1)
@@ -61,13 +62,14 @@
     size = payload.shape[0]
     column = lax.axis_index("col")
     here = lax.axis_index("row") * width + column
-    pieces, offsets = [], []
     if (groups, width) == (4, 8):
-        for array, parts in cube(payload, count, here, cut):
-            pieces.append((array, [(start, rows) for _, start, rows in parts]))
-            for mask, _, _ in parts:
-                offsets.append((((here ^ mask) - here + count // 2) % count - count // 2)[None])
+        found = cube(payload, count, cut)
+        pieces = [(array, [(start, rows) for _, start, rows in parts]) for array, parts in found]
+        masks = np.array([mask for _, parts in found for mask, _, _ in parts])
+        device = np.arange(count)[:, None]
+        offsets = jnp.asarray((((device ^ masks) - device + count // 2) % count - count // 2).astype(np.int32))[here]
     else:
+        pieces, offsets = [], []
         block = lax.all_gather(payload, "col", axis=0, tiled=True)
         pieces.append((block, [(0, size)] * width))
         offsets.append(jnp.arange(width, dtype=jnp.int32) - column)
@@ -80,7 +82,7 @@
             offsets.append(steps - (hop - 1) * width - part)
             pieces.append((lax.ppermute(block[: part * size], "row", down), [(0, size)] * part))
             offsets.append(steps + hop * width)
-    offsets = jnp.concatenate(offsets).astype(jnp.int32)
+        offsets = jnp.concatenate(offsets).astype(jnp.int32)
     return pieces, jnp.where(jnp.abs(offsets) <= need, offsets + need, -1)
 
 
@@ -164,43 +166,43 @@
             axis=1,
         )
 
-    def row_quad(quad, carry):
-        r = QUAD * quad
-        for i in range(QUAD):
+    def row_group(group, carry):
+        r = GROUP * group
+        for i in range(GROUP):
             k = r + far + i
 
             @pl.when(k <= 2 * far)
             def _(k=k):
                 ready(k)
 
-        middle = jnp.where(quad == reach // QUAD, 1, 0)
-        for d in range(-far, far + QUAD, 2):
-            low, high = max(-reach, d - reach), min(reach + QUAD - 1, d + reach + 1)
+        middle = jnp.where(group == reach // GROUP, 1, 0)
+        for d in range(-far, far + GROUP, 2):
+            low, high = max(-reach, d - reach), min(reach + GROUP - 1, d + reach + 1)
             size = high - low + 1
-            left = jnp.concatenate([strip(r + reach + i, low + reach - i, size) for i in range(QUAD)], axis=0)
+            left = jnp.concatenate([strip(r + reach + i, low + reach - i, size) for i in range(GROUP)], axis=0)
             right = jnp.concatenate([strip(r + reach + e, d - e + reach, 2) for e in range(low, high + 1)], axis=0)
             product = jnp.dot(left, right, preferred_element_type=jnp.float32)
-            for i in range(QUAD):
+            for i in range(GROUP):
                 for j in range(2):
                     u = d + far - i + j
                     if 0 <= u < wide:
                         kept = product[i * edge : (i + 1) * edge, j * edge : (j + 1) * edge]
                         kept = kept * keep[r + i, u : u + 1, :]
                         square[span(r + i, 1), u * edge : (u + 1) * edge] = kept.astype(kind)
-                        if i == reach % QUAD:
+                        if i == reach % GROUP:
                             own[middle, :, u * edge : (u + 1) * edge] = kept
         return carry
 
-    lax.fori_loop(0, (slots + 1) // QUAD, row_quad, 0)
-
-    for c in range(-far, far + 1, QUAD):
-        low, high = max(-reach, c - far), min(reach, c + far + QUAD - 1)
+    lax.fori_loop(0, (slots + 1) // GROUP, row_group, 0)
+
+    for c in range(-far, far + 1, WIDTH):
+        low, high = max(-reach, c - far), min(reach, c + far + WIDTH - 1)
         left = strip(far, low + reach, high - low + 1)
         right = jnp.concatenate(
-            [square_strip(r + reach, c - r + far, QUAD) for r in range(low, high + 1)], axis=0
+            [square_strip(r + reach, c - r + far, WIDTH) for r in range(low, high + 1)], axis=0
         )
         cube = jnp.dot(left, right, preferred_element_type=jnp.float32)
-        for j in range(QUAD):
+        for j in range(WIDTH):
             u = c + far + j
             if u < wide:
                 value = 3.0 * own[1, :, u * edge : (u + 1) * edge] - 2.0 * cube[:, j * edge : (j + 1) * edge]
@@ -248,7 +250,7 @@
             pltpu.SemaphoreType.DMA((2 * far + 1,)),
             pltpu.SemaphoreType.DMA,
         ],
-        compiler_params=pltpu.CompilerParams(vmem_limit_bytes=40 * 2**20),
+        compiler_params=pltpu.CompilerParams(vmem_limit_bytes=56 * 2**20),
         cost_estimate=pl.CostEstimate(flops=17 * 10**9, bytes_accessed=15 * 2**20, transcendentals=0),
     )(place, *tables)
     return result[None]

time: 127 us -> 113 us (0.89)
  waiting for transfers between devices: 67.4 us -> 59.3 us
  local copies, waits for them, and re-layouts: 8.43 us -> 3.87 us
  Pallas kernels: 33.7 us -> 30.9 us
  other arithmetic: 0.1 us -> 1.37 us
    ppermute x20, waiting for transfers between devices: 67.4 us -> 59.3 us  [swap(): return lax.ppermute(value, AXES, [(i, i ^ mask) for i in range(count)])]
    unnamed x23 -> x31, local copies, waits for them, and re-layouts: 8.15 us -> 3.7 us
    pallas_call x1, Pallas kernels: 31.8 us -> 29 us  [shards(): pl.pallas_call(functools.partial(purify, reach, edge, layout), out_shape=...]
  transfers between devices with their start and end apart: 20 -> 20, of which waited for: 11 -> 12; matrix products, arithmetic and copies ran while one was open for 0% -> 2% of each run, Pallas kernels for 0% -> 0%
where the time goes in v9:
time: 113 us
  waiting for transfers between devices  59.3 us (52%)
  Pallas kernels  30.9 us (27%)
  starting transfers between devices  17.3 us (15%)
  local copies, waits for them, and re-layouts  3.87 us (3%)
  other arithmetic  1.37 us (1%)
    ppermute x20, waiting for transfers between devices, swap(): return lax.ppermute(value, AXES, [(i, i ^ mask) for i in range(count)])  59.3 us
    pallas_call x1, Pallas kernels, shards(): pl.pallas_call(functools.partial(purify, reach, edge, layout), out_shape=...  29 us
    ppermute x20, starting transfers between devices, swap(): return lax.ppermute(value, AXES, [(i, i ^ mask) for i in range(count)])  17.3 us
    unnamed x31, local copies, waits for them, and re-layouts  3.7 us
  transfers between devices with their start and end apart: 20, of which 12 were waited for; matrix products, arithmetic and copies ran while one was open for 2% of the time, Pallas kernels for 0%

profile of v9, /device:TPU:0, one launch (start us, length us, event | category | flops | bytes accessed | tf_op | source)
XLA Modules:
  0.0 112.9 jit_solution(4125990910395729563)
XLA Ops:
  0.0 1.9 %shard_map.46.refs_0_ = bf16[1936,128]{1,0:T(8,128)(2,1)} custom-call(s32[1,15]{1,0:T(1,128)} %pattern.1, s32[1,29]{1,0:T(1,128)} %filter_mask.1, bf16[15,128,128]{2,1,0:T(8,128)(2,1)} %bitcast.4), custom_call_target="tpu_custom_call" | custom-call | tf_op jit(solution)/shard_map/pallas_call | solution.py:230
  1.9 2.9 %collective-permute-start = (bf16[1936,128]{1,0:T(8,128)(2,1)}, bf16[1936,128]{1,0:T(8,128)(2,1)S(1)}, u32[]{:S(2)}, u32[]{:S(2)}) collective-permute-start(bf16[1936,128]{1,0:T(8,128)(2,1)} %shard_map.46.refs_0_), channel_id=1, source_target_pairs={{0,1},{1,0},{2,3},{3,2},{4,5},{5,4},{6,7},{7,6},{8,9},{9,8},{10,11... | collective-permute-start | bytes 1486856 | tf_op jit(solution)/shard_map/ppermute | solution.py:23
  4.9 1.5 %collective-permute-start.1 = (bf16[1936,128]{1,0:T(8,128)(2,1)}, bf16[1936,128]{1,0:T(8,128)(2,1)S(1)}, u32[]{:S(2)}, u32[]{:S(2)}) collective-permute-start(bf16[1936,128]{1,0:T(8,128)(2,1)} %shard_map.46.refs_0_), channel_id=1, source_target_pairs={{0,16},{1,17},{2,18},{3,19},{4,20},{5,21},{6,22},{7,23},{8,24},{9,... | collective-permute-start | bytes 1486856 | tf_op jit(solution)/shard_map/ppermute | solution.py:23
  6.4 3.6 %collective-permute-start.4 = (bf16[1936,128]{1,0:T(8,128)(2,1)}, bf16[1936,128]{1,0:T(8,128)(2,1)S(1)}, u32[]{:S(2)}, u32[]{:S(2)}) collective-permute-start(bf16[1936,128]{1,0:T(8,128)(2,1)} %shard_map.46.refs_0_), channel_id=1, source_target_pairs={{0,6},{1,7},{2,4},{3,5},{4,2},{5,3},{6,0},{7,1},{8,14},{9,15},{10,... | collective-permute-start | bytes 1486856 | tf_op jit(solution)/shard_map/ppermute | solution.py:23
  10.5 1.1 constant_dynamic-update-slice_fusion.5
  11.6 5.6 %collective-permute-done.refs_1_ = bf16[1936,128]{1,0:T(8,128)(2,1)S(1)} collective-permute-done((bf16[1936,128]{1,0:T(8,128)(2,1)}, bf16[1936,128]{1,0:T(8,128)(2,1)S(1)}, u32[]{:S(2)}, u32[]{:S(2)}) %collective-permute-start) | collective-permute-done | bytes 495648 | tf_op jit(solution)/shard_map/ppermute | solution.py:23
  17.3 11.2 %collective-permute-done.1.refs_2_ = bf16[1936,128]{1,0:T(8,128)(2,1)S(1)} collective-permute-done((bf16[1936,128]{1,0:T(8,128)(2,1)}, bf16[1936,128]{1,0:T(8,128)(2,1)S(1)}, u32[]{:S(2)}, u32[]{:S(2)}) %collective-permute-start.1) | collective-permute-done | bytes 495648 | tf_op jit(solution)/shard_map/ppermute | solution.py:23
  28.6 3.1 %collective-permute-done.3.refs_4_ = bf16[1936,128]{1,0:T(8,128)(2,1)S(1)} collective-permute-done((bf16[1936,128]{1,0:T(8,128)(2,1)}, bf16[1936,128]{1,0:T(8,128)(2,1)S(1)}, u32[]{:S(2)}, u32[]{:S(2)}) %collective-permute-start.3) | collective-permute-done | bytes 495648 | tf_op jit(solution)/shard_map/ppermute | solution.py:23
  32.1 0.6 collective-permute-start.7
  33.2 1.7 %collective-permute-start.8 = (bf16[1936,128]{1,0:T(8,128)(2,1)S(1)}, bf16[1936,128]{1,0:T(8,128)(2,1)S(1)}, u32[]{:S(2)}, u32[]{:S(2)}) collective-permute-start(bf16[1936,128]{1,0:T(8,128)(2,1)S(1)} %collective-permute-done.4.refs_5_), channel_id=1, source_target_pairs={{0,2},{1,3},{2,0},{3,1},{4,6},{5,7},{6,4},{7,5},{8,10},{9,11},{10,... | collective-permute-start | bytes 1486856 | tf_op jit(solution)/shard_map/ppermute | solution.py:23
  35.4 19.3 %collective-permute-done.8.refs_15_ = bf16[1936,128]{1,0:T(8,128)(2,1)S(1)} collective-permute-done((bf16[1936,128]{1,0:T(8,128)(2,1)S(1)}, bf16[1936,128]{1,0:T(8,128)(2,1)S(1)}, u32[]{:S(2)}, u32[]{:S(2)}) %collective-permute-start.8) | collective-permute-done | bytes 495648 | tf_op jit(solution)/shard_map/ppermute | solution.py:23
  54.7 1.7 %collective-permute-done.7.refs_9_ = bf16[3872,128]{1,0:T(8,128)(2,1)S(1)} collective-permute-done((bf16[3872,128]{1,0:T(8,128)(2,1)S(1)}, bf16[3872,128]{1,0:T(8,128)(2,1)S(1)}, u32[]{:S(2)}, u32[]{:S(2)}) %collective-permute-start.7) | collective-permute-done | bytes 991264 | tf_op jit(solution)/shard_map/ppermute | solution.py:23
  56.8 0.6 collective-permute-start.10
  57.4 0.6 collective-permute-start.11
  58.1 1.6 %collective-permute-start.12 = (bf16[2848,128]{1,0:T(8,128)(2,1)S(1)}, bf16[2848,128]{1,0:T(8,128)(2,1)}, u32[]{:S(2)}, u32[]{:S(2)}) collective-permute-start(bf16[2848,128]{1,0:T(8,128)(2,1)S(1)} %pad_maximum_fusion.1), channel_id=1, source_target_pairs={{0,16},{1,17},{2,18},{3,19},{4,20},{5,21},{6,22},{7,23},{8,24},{9,... | collective-permute-start | bytes 2187272 | tf_op jit(solution)/shard_map/ppermute | solution.py:23
  59.6 1.7 %collective-permute-start.13 = (bf16[1936,128]{1,0:T(8,128)(2,1)S(1)}, bf16[1936,128]{1,0:T(8,128)(2,1)}, u32[]{:S(2)}, u32[]{:S(2)}) collective-permute-start(bf16[1936,128]{1,0:T(8,128)(2,1)S(1)} %collective-permute-done.2.refs_3_), channel_id=1, source_target_pairs={{0,2},{1,3},{2,0},{3,1},{4,6},{5,7},{6,4},{7,5},{8,10},{9,11},{10,... | collective-permute-start | bytes 1486856 | tf_op jit(solution)/shard_map/ppermute | solution.py:23
  61.3 11.1 %collective-permute-done.13.refs_19_ = bf16[1936,128]{1,0:T(8,128)(2,1)} collective-permute-done((bf16[1936,128]{1,0:T(8,128)(2,1)S(1)}, bf16[1936,128]{1,0:T(8,128)(2,1)}, u32[]{:S(2)}, u32[]{:S(2)}) %collective-permute-start.13) | collective-permute-done | bytes 495648 | tf_op jit(solution)/shard_map/ppermute | solution.py:23
  72.4 3.8 %collective-permute-done.12.refs_13_ = bf16[2848,128]{1,0:T(8,128)(2,1)} collective-permute-done((bf16[2848,128]{1,0:T(8,128)(2,1)S(1)}, bf16[2848,128]{1,0:T(8,128)(2,1)}, u32[]{:S(2)}, u32[]{:S(2)}) %collective-permute-start.12) | collective-permute-done | bytes 729120 | tf_op jit(solution)/shard_map/ppermute | solution.py:23
  77.8 1.3 %fusion.place = s32[34]{0:T(128)} fusion(s32[32,34]{1,0:T(8,128)} %constant.20.clone, s32[]{:T(128)S(6)} %select_n.9), kind=kLoop, calls=%fused_computation.11 | loop fusion | flops 136 | bytes 276 | tf_op jit(solution)/shard_map/jit(_where)/select_n | solution.py:86
  79.1 2.0 %collective-permute-done.17.refs_16_ = bf16[1936,128]{1,0:T(8,128)(2,1)} collective-permute-done((bf16[1936,128]{1,0:T(8,128)(2,1)S(1)}, bf16[1936,128]{1,0:T(8,128)(2,1)}, u32[]{:S(2)}, u32[]{:S(2)}) %collective-permute-start.17) | collective-permute-done | bytes 495648 | tf_op jit(solution)/shard_map/ppermute | solution.py:23
  81.3 0.8 collective-permute-done.19.refs_20_
  82.2 0.8 copy-done.12
  83.0 0.9 copy-done.11
  84.0 29.0 %shard_map.47 = bf16[29,128,128]{2,1,0:T(8,128)(2,1)} custom-call(s32[34]{0:T(128)} %fusion.place, bf16[1936,128]{1,0:T(8,128)(2,1)} %shard_map.46.refs_0_, bf16[1936,128]{1,0:T(8,128)(2,1)} %copy-done.1, bf16[1936,128]{1,0:T(8,128)(2,1)} %copy-done.2, bf16[1936,128]{1,0:T(8,128)(2,1)} %copy-done.5, bf16[1936,128]{1,0:T(8,128)(2,1)} %copy-done.4, ...), custom_call_target="tpu_custom_call" | custom-call | flops 16999999488 | bytes 15728640 | tf_op jit(solution)/shard_map/pallas_call | solution.py:239
  (55 shorter events, 4.3 us)
Async XLA Ops:
  1.9 15.3 %collective-permute-start = (bf16[1936,128]{1,0:T(8,128)(2,1)}, bf16[1936,128]{1,0:T(8,128)(2,1)S(1)}, u32[]{:S(2)}, u32[]{:S(2)}) collective-permute-start(bf16[1936,128]{1,0:T(8,128)(2,1)} %shard_map.46.refs_0_), channel_id=1, source_target_pairs={{0,1},{1,0},{2,3},{3,2},{4,5},{5,4},{6,7},{7,6},{8,9},{9,8},{10,11... | collective-permute-start | bytes 1486856 | tf_op jit(solution)/shard_map/ppermute | solution.py:23
  4.9 23.6 %collective-permute-start.1 = (bf16[1936,128]{1,0:T(8,128)(2,1)}, bf16[1936,128]{1,0:T(8,128)(2,1)S(1)}, u32[]{:S(2)}, u32[]{:S(2)}) collective-permute-start(bf16[1936,128]{1,0:T(8,128)(2,1)} %shard_map.46.refs_0_), channel_id=1, source_target_pairs={{0,16},{1,17},{2,18},{3,19},{4,20},{5,21},{6,22},{7,23},{8,24},{9,... | collective-permute-start | bytes 1486856 | tf_op jit(solution)/shard_map/ppermute | solution.py:23
  6.4 25.4 %collective-permute-start.4 = (bf16[1936,128]{1,0:T(8,128)(2,1)}, bf16[1936,128]{1,0:T(8,128)(2,1)S(1)}, u32[]{:S(2)}, u32[]{:S(2)}) collective-permute-start(bf16[1936,128]{1,0:T(8,128)(2,1)} %shard_map.46.refs_0_), channel_id=1, source_target_pairs={{0,6},{1,7},{2,4},{3,5},{4,2},{5,3},{6,0},{7,1},{8,14},{9,15},{10,... | collective-permute-start | bytes 1486856 | tf_op jit(solution)/shard_map/ppermute | solution.py:23
  10.0 21.7 %collective-permute-start.3 = (bf16[1936,128]{1,0:T(8,128)(2,1)}, bf16[1936,128]{1,0:T(8,128)(2,1)S(1)}, u32[]{:S(2)}, u32[]{:S(2)}) collective-permute-start(bf16[1936,128]{1,0:T(8,128)(2,1)} %shard_map.46.refs_0_), channel_id=1, source_target_pairs={{0,2},{1,3},{2,0},{3,1},{4,6},{5,7},{6,4},{7,5},{8,10},{9,11},{10,... | collective-permute-start | bytes 1486856 | tf_op jit(solution)/shard_map/ppermute | solution.py:23
  10.0 18.5 %collective-permute-start.2 = (bf16[1936,128]{1,0:T(8,128)(2,1)}, bf16[1936,128]{1,0:T(8,128)(2,1)S(1)}, u32[]{:S(2)}, u32[]{:S(2)}) collective-permute-start(bf16[1936,128]{1,0:T(8,128)(2,1)} %shard_map.46.refs_0_), channel_id=1, source_target_pairs={{0,17},{1,16},{2,19},{3,18},{4,21},{5,20},{6,23},{7,22},{8,25},{9,... | collective-permute-start | bytes 1486856 | tf_op jit(solution)/shard_map/ppermute | solution.py:23
  28.5 28.3 %copy-start.2 = (bf16[1936,128]{1,0:T(8,128)(2,1)}, bf16[1936,128]{1,0:T(8,128)(2,1)S(1)}, u32[]{:S(2)}) copy-start(bf16[1936,128]{1,0:T(8,128)(2,1)S(1)} %collective-permute-done.1.refs_2_) | copy-start | bytes 1486852
  28.6 31.1 %copy-start.5 = (bf16[1936,128]{1,0:T(8,128)(2,1)}, bf16[1936,128]{1,0:T(8,128)(2,1)S(1)}, u32[]{:S(2)}) copy-start(bf16[1936,128]{1,0:T(8,128)(2,1)S(1)} %collective-permute-done.2.refs_3_) | copy-start | bytes 1486852
  31.8 50.3 %copy-start.3 = (bf16[1936,128]{1,0:T(8,128)(2,1)}, bf16[1936,128]{1,0:T(8,128)(2,1)S(1)}, u32[]{:S(2)}) copy-start(bf16[1936,128]{1,0:T(8,128)(2,1)S(1)} %collective-permute-done.4.refs_5_) | copy-start | bytes 1486852
  32.0 24.7 %collective-permute-start.5 = (bf16[11616,128]{1,0:T(8,128)(2,1)S(1)}, bf16[11616,128]{1,0:T(8,128)(2,1)}, u32[]{:S(2)}, u32[]{:S(2)}) collective-permute-start(bf16[11616,128]{1,0:T(8,128)(2,1)S(1)} %get-tuple-element.40), channel_id=1, source_target_pairs={{0,8},{1,9},{2,10},{3,11},{4,12},{5,13},{6,14},{7,15},{8,0},{9,1},... | collective-permute-start | bytes 8921096 | tf_op jit(solution)/shard_map/ppermute | solution.py:23
  32.1 24.3 %collective-permute-start.7 = (bf16[3872,128]{1,0:T(8,128)(2,1)S(1)}, bf16[3872,128]{1,0:T(8,128)(2,1)S(1)}, u32[]{:S(2)}, u32[]{:S(2)}) collective-permute-start(bf16[3872,128]{1,0:T(8,128)(2,1)S(1)} %get-tuple-element.39), channel_id=1, source_target_pairs={{0,16},{1,17},{2,18},{3,19},{4,20},{5,21},{6,22},{7,23},{8,24},{9,... | collective-permute-start | bytes 2973704 | tf_op jit(solution)/shard_map/ppermute | solution.py:23
  32.6 24.0 %collective-permute-start.6 = (bf16[3872,128]{1,0:T(8,128)(2,1)S(1)}, bf16[3872,128]{1,0:T(8,128)(2,1)S(1)}, u32[]{:S(2)}, u32[]{:S(2)}) collective-permute-start(bf16[3872,128]{1,0:T(8,128)(2,1)S(1)} %get-tuple-element.39), channel_id=1, source_target_pairs={{0,1},{1,0},{2,3},{3,2},{4,5},{5,4},{6,7},{7,6},{8,9},{9,8},{10,11... | collective-permute-start | bytes 2973704 | tf_op jit(solution)/shard_map/ppermute | solution.py:23
  33.2 21.5 %collective-permute-start.8 = (bf16[1936,128]{1,0:T(8,128)(2,1)S(1)}, bf16[1936,128]{1,0:T(8,128)(2,1)S(1)}, u32[]{:S(2)}, u32[]{:S(2)}) collective-permute-start(bf16[1936,128]{1,0:T(8,128)(2,1)S(1)} %collective-permute-done.4.refs_5_), channel_id=1, source_target_pairs={{0,2},{1,3},{2,0},{3,1},{4,6},{5,7},{6,4},{7,5},{8,10},{9,11},{10,... | collective-permute-start | bytes 1486856 | tf_op jit(solution)/shard_map/ppermute | solution.py:23
  34.8 24.8 %collective-permute-start.14 = (bf16[1936,128]{1,0:T(8,128)(2,1)S(1)}, bf16[1936,128]{1,0:T(8,128)(2,1)}, u32[]{:S(2)}, u32[]{:S(2)}) collective-permute-start(bf16[1936,128]{1,0:T(8,128)(2,1)S(1)} %collective-permute-done.2.refs_3_), channel_id=1, source_target_pairs={{0,4},{1,5},{2,6},{3,7},{4,0},{5,1},{6,2},{7,3},{8,12},{9,13},{10,... | collective-permute-start | bytes 1486856 | tf_op jit(solution)/shard_map/ppermute | solution.py:23
  54.7 27.5 %copy-start = (bf16[1936,128]{1,0:T(8,128)(2,1)}, bf16[1936,128]{1,0:T(8,128)(2,1)S(1)}, u32[]{:S(2)}) copy-start(bf16[1936,128]{1,0:T(8,128)(2,1)S(1)} %collective-permute-done.8.refs_15_) | copy-start | bytes 1486852
  56.7 19.7 %collective-permute-start.9 = (bf16[3872,128]{1,0:T(8,128)(2,1)S(1)}, bf16[3872,128]{1,0:T(8,128)(2,1)S(1)}, u32[]{:S(2)}, u32[]{:S(2)}) collective-permute-start(bf16[3872,128]{1,0:T(8,128)(2,1)S(1)} %collective-permute-done.6.refs_7_), channel_id=1, source_target_pairs={{0,8},{1,9},{2,10},{3,11},{4,12},{5,13},{6,14},{7,15},{8,0},{9,1},... | collective-permute-start | bytes 2973704 | tf_op jit(solution)/shard_map/ppermute | solution.py:23
  56.8 19.5 %collective-permute-start.10 = (bf16[3872,128]{1,0:T(8,128)(2,1)S(1)}, bf16[3872,128]{1,0:T(8,128)(2,1)S(1)}, u32[]{:S(2)}, u32[]{:S(2)}) collective-permute-start(bf16[3872,128]{1,0:T(8,128)(2,1)S(1)} %collective-permute-done.7.refs_9_), channel_id=1, source_target_pairs={{0,8},{1,9},{2,10},{3,11},{4,12},{5,13},{6,14},{7,15},{8,0},{9,1},... | collective-permute-start | bytes 2973704 | tf_op jit(solution)/shard_map/ppermute | solution.py:23
  57.4 18.9 %collective-permute-start.11 = (bf16[2960,128]{1,0:T(8,128)(2,1)S(1)}, bf16[2960,128]{1,0:T(8,128)(2,1)S(1)}, u32[]{:S(2)}, u32[]{:S(2)}) collective-permute-start(bf16[2960,128]{1,0:T(8,128)(2,1)S(1)} %pad_maximum_fusion), channel_id=1, source_target_pairs={{0,1},{1,0},{2,3},{3,2},{4,5},{5,4},{6,7},{7,6},{8,9},{9,8},{10,11... | collective-permute-start | bytes 2273288 | tf_op jit(solution)/shard_map/ppermute | solution.py:23
  58.1 18.1 %collective-permute-start.12 = (bf16[2848,128]{1,0:T(8,128)(2,1)S(1)}, bf16[2848,128]{1,0:T(8,128)(2,1)}, u32[]{:S(2)}, u32[]{:S(2)}) collective-permute-start(bf16[2848,128]{1,0:T(8,128)(2,1)S(1)} %pad_maximum_fusion.1), channel_id=1, source_target_pairs={{0,16},{1,17},{2,18},{3,19},{4,20},{5,21},{6,22},{7,23},{8,24},{9,... | collective-permute-start | bytes 2187272 | tf_op jit(solution)/shard_map/ppermute | solution.py:23
  59.6 12.8 %collective-permute-start.13 = (bf16[1936,128]{1,0:T(8,128)(2,1)S(1)}, bf16[1936,128]{1,0:T(8,128)(2,1)}, u32[]{:S(2)}, u32[]{:S(2)}) collective-permute-start(bf16[1936,128]{1,0:T(8,128)(2,1)S(1)} %collective-permute-done.2.refs_3_), channel_id=1, source_target_pairs={{0,2},{1,3},{2,0},{3,1},{4,6},{5,7},{6,4},{7,5},{8,10},{9,11},{10,... | collective-permute-start | bytes 1486856 | tf_op jit(solution)/shard_map/ppermute | solution.py:23
  76.3 5.8 %collective-permute-start.15 = (bf16[2960,128]{1,0:T(8,128)(2,1)S(1)}, bf16[2960,128]{1,0:T(8,128)(2,1)S(1)}, u32[]{:S(2)}, u32[]{:S(2)}) collective-permute-start(bf16[2960,128]{1,0:T(8,128)(2,1)S(1)} %collective-permute-done.11.refs_11_), channel_id=1, source_target_pairs={{0,8},{1,9},{2,10},{3,11},{4,12},{5,13},{6,14},{7,15},{8,0},{9,1},... | collective-permute-start | bytes 2273288 | tf_op jit(solution)/shard_map/ppermute | solution.py:23
  76.4 5.7 %collective-permute-start.16 = (bf16[2848,128]{1,0:T(8,128)(2,1)}, bf16[2848,128]{1,0:T(8,128)(2,1)S(1)}, u32[]{:S(2)}, u32[]{:S(2)}) collective-permute-start(bf16[2848,128]{1,0:T(8,128)(2,1)} %collective-permute-done.12.refs_13_), channel_id=1, source_target_pairs={{0,8},{1,9},{2,10},{3,11},{4,12},{5,13},{6,14},{7,15},{8,0},{9,1},... | collective-permute-start | bytes 2187272 | tf_op jit(solution)/shard_map/ppermute | solution.py:23
  76.9 4.2 %collective-permute-start.17 = (bf16[1936,128]{1,0:T(8,128)(2,1)S(1)}, bf16[1936,128]{1,0:T(8,128)(2,1)}, u32[]{:S(2)}, u32[]{:S(2)}) collective-permute-start(bf16[1936,128]{1,0:T(8,128)(2,1)S(1)} %collective-permute-done.8.refs_15_), channel_id=1, source_target_pairs={{0,8},{1,9},{2,10},{3,11},{4,12},{5,13},{6,14},{7,15},{8,0},{9,1},... | collective-permute-start | bytes 1486856 | tf_op jit(solution)/shard_map/ppermute | solution.py:23
  77.3 4.0 %collective-permute-start.18 = (bf16[1936,128]{1,0:T(8,128)(2,1)}, bf16[1936,128]{1,0:T(8,128)(2,1)}, u32[]{:S(2)}, u32[]{:S(2)}) collective-permute-start(bf16[1936,128]{1,0:T(8,128)(2,1)} %collective-permute-done.14.refs_17_), channel_id=1, source_target_pairs={{0,8},{1,9},{2,10},{3,11},{4,12},{5,13},{6,14},{7,15},{8,0},{9,1},... | collective-permute-start | bytes 1486856 | tf_op jit(solution)/shard_map/ppermute | solution.py:23
  77.6 4.5 %collective-permute-start.19 = (bf16[1936,128]{1,0:T(8,128)(2,1)}, bf16[1936,128]{1,0:T(8,128)(2,1)}, u32[]{:S(2)}, u32[]{:S(2)}) collective-permute-start(bf16[1936,128]{1,0:T(8,128)(2,1)} %collective-permute-done.13.refs_19_), channel_id=1, source_target_pairs={{0,8},{1,9},{2,10},{3,11},{4,12},{5,13},{6,14},{7,15},{8,0},{9,1},... | collective-permute-start | bytes 1486856 | tf_op jit(solution)/shard_map/ppermute | solution.py:23
  (9 other events, 91.3 us)

commit v10 on v9

--- a/solution.py
+++ b/solution.py
@@ -88,73 +88,56 @@
 
 def purify(reach, edge, layout, place, *refs):
     count = len(layout)
-    tables, (out, band, square, own, notes, keep, arrived, noted) = refs[:count], refs[count:]
+    tables, (out, band, square, own, result, arrived, left_out) = refs[:count], refs[count:]
     far = 2 * reach
     slots, wide = 2 * reach + 1, 4 * reach + 1
-    pitch = slots
+    pitch = slots * edge + NOTE
     kind = band.dtype
-
-    def span(first, n):
-        first = first * edge
-        return pl.ds(first if isinstance(first, int) else pl.multiple_of(first, edge), n * edge)
 
     base = 0
     for table, parts in zip(tables, layout):
         begin = 0
         for start, size in parts:
             k = place[base]
-            body = min(size, slots * edge - start)
 
             @pl.when(k >= 0)
-            def _(table=table, begin=begin, start=start, size=size, body=body, k=k):
+            def _(table=table, begin=begin, start=start, size=size, k=k):
                 pltpu.make_async_copy(
-                    table.at[pl.ds(begin, body)],
-                    band.at[pl.ds(pl.multiple_of(k * pitch * edge + start, edge), body)],
+                    table.at[pl.ds(begin, size)],
+                    band.at[pl.ds(pl.multiple_of(k * pitch + start, NOTE), size)],
                     arrived.at[k],
                 ).start()
-                if size > body:
-
-                    @pl.when((k >= reach) & (k <= 3 * reach))
-                    def _():
-                        pltpu.make_async_copy(
-                            table.at[pl.ds(begin + body, NOTE)], notes.at[k - reach], noted
-                        ).start()
 
             begin += size
             base += 1
 
     def ready(k):
-        body = pl.ds(0, slots * edge)
-        pltpu.make_async_copy(tables[0].at[body], band.at[body], arrived.at[k]).wait()
+        row = pl.ds(0, pitch)
+        pltpu.make_async_copy(tables[0].at[row], band.at[row], arrived.at[k]).wait()
 
     zero = jnp.zeros((edge, edge), kind)
 
+    def block(k, s):
+        return band[pl.ds(pl.multiple_of(k * pitch + s * edge, NOTE), edge), :]
+
     def clear(s, carry):
-        band[span((2 * far + 1) * pitch + s, 1), :] = zero
+        band[pl.ds(pl.multiple_of((2 * far + 1) * pitch + s * edge, NOTE), edge), :] = zero
         return carry
 
     lax.fori_loop(0, slots, clear, 0)
-
-    for r in range(slots):
-        pltpu.make_async_copy(tables[0].at[pl.ds(0, NOTE)], notes.at[r], noted).wait()
-    notes[slots] = jnp.zeros(notes.shape[1:], kind)
-    spots = keep.shape[1]
+    band[(2 * far + 1) * pitch + slots * edge :, :] = jnp.zeros((NOTE, edge), kind)
+
+    spots = -(-wide // 8) * 8
     diagonal = lax.broadcasted_iota(jnp.int32, (spots, edge), 0) == lax.broadcasted_iota(jnp.int32, (spots, edge), 1)
 
-    def spread(r, carry):
-        line = notes[r].astype(jnp.float32)[:1]
+    def masks(k):
+        line = band[pl.ds(pl.multiple_of(k * pitch + slots * edge, NOTE), NOTE), :].astype(jnp.float32)[:1]
         value = jnp.sum(jnp.where(diagonal, line, 0.0), axis=1, keepdims=True)
-        keep[r] = jnp.broadcast_to(value, (spots, edge))
-        return carry
-
-    lax.fori_loop(0, slots + 1, spread, 0)
-
-    for k in range(far):
-        ready(k)
+        return jnp.broadcast_to(value, (spots, edge))
 
     def strip(k, first, n):
         return jnp.concatenate(
-            [band[span(k * pitch + s, 1), :] if 0 <= s < slots else zero for s in range(first, first + n)], axis=1
+            [block(k, s) if 0 <= s < slots else zero for s in range(first, first + n)], axis=1
         )
 
     def square_strip(r, first, n):
@@ -166,6 +149,9 @@
             axis=1,
         )
 
+    for k in range(far):
+        ready(k)
+
     def row_group(group, carry):
         r = GROUP * group
         for i in range(GROUP):
@@ -176,6 +162,7 @@
                 ready(k)
 
         middle = jnp.where(group == reach // GROUP, 1, 0)
+        keep = [masks(r + reach + i) for i in range(GROUP)]
         for d in range(-far, far + GROUP, 2):
             low, high = max(-reach, d - reach), min(reach + GROUP - 1, d + reach + 1)
             size = high - low + 1
@@ -187,14 +174,17 @@
                     u = d + far - i + j
                     if 0 <= u < wide:
                         kept = product[i * edge : (i + 1) * edge, j * edge : (j + 1) * edge]
-                        kept = kept * keep[r + i, u : u + 1, :]
-                        square[span(r + i, 1), u * edge : (u + 1) * edge] = kept.astype(kind)
+                        kept = kept * keep[i][u : u + 1, :]
+                        rows = pl.ds(pl.multiple_of((r + i) * edge, edge), edge)
+                        square[rows, u * edge : (u + 1) * edge] = kept.astype(kind)
                         if i == reach % GROUP:
                             own[middle, :, u * edge : (u + 1) * edge] = kept
         return carry
 
     lax.fori_loop(0, (slots + 1) // GROUP, row_group, 0)
 
+    keep = masks(far)
+    copies = []
     for c in range(-far, far + 1, WIDTH):
         low, high = max(-reach, c - far), min(reach, c + far + WIDTH - 1)
         left = strip(far, low + reach, high - low + 1)
@@ -202,11 +192,19 @@
             [square_strip(r + reach, c - r + far, WIDTH) for r in range(low, high + 1)], axis=0
         )
         cube = jnp.dot(left, right, preferred_element_type=jnp.float32)
-        for j in range(WIDTH):
-            u = c + far + j
-            if u < wide:
-                value = 3.0 * own[1, :, u * edge : (u + 1) * edge] - 2.0 * cube[:, j * edge : (j + 1) * edge]
-                out[u] = (keep[reach, u : u + 1, :] * value).astype(out.dtype)
+        first, last = c + far, min(c + far + WIDTH, wide)
+        for u in range(first, last):
+            j = u - first
+            value = 3.0 * own[1, :, u * edge : (u + 1) * edge] - 2.0 * cube[:, j * edge : (j + 1) * edge]
+            result[u] = (keep[u : u + 1, :] * value).astype(out.dtype)
+        copies.append(
+            pltpu.make_async_copy(
+                result.at[pl.ds(first, last - first)], out.at[pl.ds(first, last - first)], left_out.at[len(copies)]
+            )
+        )
+        copies[-1].start()
+    for copy in copies:
+        copy.wait()
 
 
 def pack(pattern, filter_mask, density, payload):
@@ -240,15 +238,14 @@
         functools.partial(purify, reach, edge, layout),
         out_shape=jax.ShapeDtypeStruct((wide, edge, edge), density.dtype),
         in_specs=[smem] + [pl.BlockSpec(memory_space=pl.ANY)] * len(tables),
-        out_specs=vmem,
+        out_specs=pl.BlockSpec(memory_space=pl.ANY),
         scratch_shapes=[
-            pltpu.VMEM(((2 * far + 2) * slots * edge, edge), density.dtype),
+            pltpu.VMEM(((2 * far + 2) * (slots * edge + NOTE), edge), density.dtype),
             pltpu.VMEM(((slots + 1) * edge, wide * edge), density.dtype),
             pltpu.VMEM((2, edge, wide * edge), jnp.float32),
-            pltpu.VMEM((slots + 1, NOTE, edge), density.dtype),
-            pltpu.VMEM((slots + 1, -(-wide // 8) * 8, edge), jnp.float32),
+            pltpu.VMEM((wide, edge, edge), density.dtype),
             pltpu.SemaphoreType.DMA((2 * far + 1,)),
-            pltpu.SemaphoreType.DMA,
+            pltpu.SemaphoreType.DMA((-(-wide // WIDTH),)),
         ],
         compiler_params=pltpu.CompilerParams(vmem_limit_bytes=56 * 2**20),
         cost_estimate=pl.CostEstimate(flops=17 * 10**9, bytes_accessed=15 * 2**20, transcendentals=0),

time: 113 us -> 112 us (level)
  no operation moved by 1% of the time
where the time goes in v10:
time: 112 us
  waiting for transfers between devices  59.3 us (53%)
  Pallas kernels  30.2 us (27%)
  starting transfers between devices  17.3 us (15%)
  local copies, waits for them, and re-layouts  3.87 us (3%)
  other arithmetic  1.37 us (1%)
    ppermute x20, waiting for transfers between devices, swap(): return lax.ppermute(value, AXES, [(i, i ^ mask) for i in range(count)])  59.3 us
    pallas_call x1, Pallas kernels, shards(): pl.pallas_call(functools.partial(purify, reach, edge, layout), out_shape=...  28.3 us
    ppermute x20, starting transfers between devices, swap(): return lax.ppermute(value, AXES, [(i, i ^ mask) for i in range(count)])  17.3 us
    unnamed x31, local copies, waits for them, and re-layouts  3.7 us
  transfers between devices with their start and end apart: 20, of which 12 were waited for; matrix products, arithmetic and copies ran while one was open for 2% of the time, Pallas kernels for 0%

profile of v10, /device:TPU:0, one launch (start us, length us, event | category | flops | bytes accessed | tf_op | source)
XLA Modules:
  0.0 112.2 jit_solution(4180814436107581066)
XLA Ops:
  0.0 1.9 %shard_map.46.refs_0_ = bf16[1936,128]{1,0:T(8,128)(2,1)} custom-call(s32[1,15]{1,0:T(1,128)} %pattern.1, s32[1,29]{1,0:T(1,128)} %filter_mask.1, bf16[15,128,128]{2,1,0:T(8,128)(2,1)} %bitcast.4), custom_call_target="tpu_custom_call" | custom-call | tf_op jit(solution)/shard_map/pallas_call | solution.py:228
  1.9 2.9 %collective-permute-start = (bf16[1936,128]{1,0:T(8,128)(2,1)}, bf16[1936,128]{1,0:T(8,128)(2,1)S(1)}, u32[]{:S(2)}, u32[]{:S(2)}) collective-permute-start(bf16[1936,128]{1,0:T(8,128)(2,1)} %shard_map.46.refs_0_), channel_id=1, source_target_pairs={{0,1},{1,0},{2,3},{3,2},{4,5},{5,4},{6,7},{7,6},{8,9},{9,8},{10,11... | collective-permute-start | bytes 1486856 | tf_op jit(solution)/shard_map/ppermute | solution.py:23
  4.9 1.5 %collective-permute-start.1 = (bf16[1936,128]{1,0:T(8,128)(2,1)}, bf16[1936,128]{1,0:T(8,128)(2,1)S(1)}, u32[]{:S(2)}, u32[]{:S(2)}) collective-permute-start(bf16[1936,128]{1,0:T(8,128)(2,1)} %shard_map.46.refs_0_), channel_id=1, source_target_pairs={{0,16},{1,17},{2,18},{3,19},{4,20},{5,21},{6,22},{7,23},{8,24},{9,... | collective-permute-start | bytes 1486856 | tf_op jit(solution)/shard_map/ppermute | solution.py:23
  6.4 3.6 %collective-permute-start.4 = (bf16[1936,128]{1,0:T(8,128)(2,1)}, bf16[1936,128]{1,0:T(8,128)(2,1)S(1)}, u32[]{:S(2)}, u32[]{:S(2)}) collective-permute-start(bf16[1936,128]{1,0:T(8,128)(2,1)} %shard_map.46.refs_0_), channel_id=1, source_target_pairs={{0,6},{1,7},{2,4},{3,5},{4,2},{5,3},{6,0},{7,1},{8,14},{9,15},{10,... | collective-permute-start | bytes 1486856 | tf_op jit(solution)/shard_map/ppermute | solution.py:23
  10.5 1.1 constant_dynamic-update-slice_fusion.5
  11.6 5.6 %collective-permute-done.refs_1_ = bf16[1936,128]{1,0:T(8,128)(2,1)S(1)} collective-permute-done((bf16[1936,128]{1,0:T(8,128)(2,1)}, bf16[1936,128]{1,0:T(8,128)(2,1)S(1)}, u32[]{:S(2)}, u32[]{:S(2)}) %collective-permute-start) | collective-permute-done | bytes 495648 | tf_op jit(solution)/shard_map/ppermute | solution.py:23
  17.3 11.2 %collective-permute-done.1.refs_2_ = bf16[1936,128]{1,0:T(8,128)(2,1)S(1)} collective-permute-done((bf16[1936,128]{1,0:T(8,128)(2,1)}, bf16[1936,128]{1,0:T(8,128)(2,1)S(1)}, u32[]{:S(2)}, u32[]{:S(2)}) %collective-permute-start.1) | collective-permute-done | bytes 495648 | tf_op jit(solution)/shard_map/ppermute | solution.py:23
  28.6 3.1 %collective-permute-done.3.refs_4_ = bf16[1936,128]{1,0:T(8,128)(2,1)S(1)} collective-permute-done((bf16[1936,128]{1,0:T(8,128)(2,1)}, bf16[1936,128]{1,0:T(8,128)(2,1)S(1)}, u32[]{:S(2)}, u32[]{:S(2)}) %collective-permute-start.3) | collective-permute-done | bytes 495648 | tf_op jit(solution)/shard_map/ppermute | solution.py:23
  32.1 0.6 collective-permute-start.7
  33.2 1.7 %collective-permute-start.8 = (bf16[1936,128]{1,0:T(8,128)(2,1)S(1)}, bf16[1936,128]{1,0:T(8,128)(2,1)S(1)}, u32[]{:S(2)}, u32[]{:S(2)}) collective-permute-start(bf16[1936,128]{1,0:T(8,128)(2,1)S(1)} %collective-permute-done.4.refs_5_), channel_id=1, source_target_pairs={{0,2},{1,3},{2,0},{3,1},{4,6},{5,7},{6,4},{7,5},{8,10},{9,11},{10,... | collective-permute-start | bytes 1486856 | tf_op jit(solution)/shard_map/ppermute | solution.py:23
  35.4 19.3 %collective-permute-done.8.refs_15_ = bf16[1936,128]{1,0:T(8,128)(2,1)S(1)} collective-permute-done((bf16[1936,128]{1,0:T(8,128)(2,1)S(1)}, bf16[1936,128]{1,0:T(8,128)(2,1)S(1)}, u32[]{:S(2)}, u32[]{:S(2)}) %collective-permute-start.8) | collective-permute-done | bytes 495648 | tf_op jit(solution)/shard_map/ppermute | solution.py:23
  54.7 1.7 %collective-permute-done.7.refs_9_ = bf16[3872,128]{1,0:T(8,128)(2,1)S(1)} collective-permute-done((bf16[3872,128]{1,0:T(8,128)(2,1)S(1)}, bf16[3872,128]{1,0:T(8,128)(2,1)S(1)}, u32[]{:S(2)}, u32[]{:S(2)}) %collective-permute-start.7) | collective-permute-done | bytes 991264 | tf_op jit(solution)/shard_map/ppermute | solution.py:23
  56.8 0.6 collective-permute-start.10
  57.4 0.6 collective-permute-start.11
  58.1 1.6 %collective-permute-start.12 = (bf16[2848,128]{1,0:T(8,128)(2,1)S(1)}, bf16[2848,128]{1,0:T(8,128)(2,1)}, u32[]{:S(2)}, u32[]{:S(2)}) collective-permute-start(bf16[2848,128]{1,0:T(8,128)(2,1)S(1)} %pad_maximum_fusion.1), channel_id=1, source_target_pairs={{0,16},{1,17},{2,18},{3,19},{4,20},{5,21},{6,22},{7,23},{8,24},{9,... | collective-permute-start | bytes 2187272 | tf_op jit(solution)/shard_map/ppermute | solution.py:23
  59.6 1.7 %collective-permute-start.13 = (bf16[1936,128]{1,0:T(8,128)(2,1)S(1)}, bf16[1936,128]{1,0:T(8,128)(2,1)}, u32[]{:S(2)}, u32[]{:S(2)}) collective-permute-start(bf16[1936,128]{1,0:T(8,128)(2,1)S(1)} %collective-permute-done.2.refs_3_), channel_id=1, source_target_pairs={{0,2},{1,3},{2,0},{3,1},{4,6},{5,7},{6,4},{7,5},{8,10},{9,11},{10,... | collective-permute-start | bytes 1486856 | tf_op jit(solution)/shard_map/ppermute | solution.py:23
  61.3 11.1 %collective-permute-done.13.refs_19_ = bf16[1936,128]{1,0:T(8,128)(2,1)} collective-permute-done((bf16[1936,128]{1,0:T(8,128)(2,1)S(1)}, bf16[1936,128]{1,0:T(8,128)(2,1)}, u32[]{:S(2)}, u32[]{:S(2)}) %collective-permute-start.13) | collective-permute-done | bytes 495648 | tf_op jit(solution)/shard_map/ppermute | solution.py:23
  72.4 3.8 %collective-permute-done.12.refs_13_ = bf16[2848,128]{1,0:T(8,128)(2,1)} collective-permute-done((bf16[2848,128]{1,0:T(8,128)(2,1)S(1)}, bf16[2848,128]{1,0:T(8,128)(2,1)}, u32[]{:S(2)}, u32[]{:S(2)}) %collective-permute-start.12) | collective-permute-done | bytes 729120 | tf_op jit(solution)/shard_map/ppermute | solution.py:23
  77.8 1.3 %fusion.place = s32[34]{0:T(128)} fusion(s32[32,34]{1,0:T(8,128)} %constant.20.clone, s32[]{:T(128)S(6)} %select_n.9), kind=kLoop, calls=%fused_computation.11 | loop fusion | flops 136 | bytes 276 | tf_op jit(solution)/shard_map/jit(_where)/select_n | solution.py:86
  79.1 2.0 %collective-permute-done.17.refs_16_ = bf16[1936,128]{1,0:T(8,128)(2,1)} collective-permute-done((bf16[1936,128]{1,0:T(8,128)(2,1)S(1)}, bf16[1936,128]{1,0:T(8,128)(2,1)}, u32[]{:S(2)}, u32[]{:S(2)}) %collective-permute-start.17) | collective-permute-done | bytes 495648 | tf_op jit(solution)/shard_map/ppermute | solution.py:23
  81.3 0.8 collective-permute-done.19.refs_20_
  82.2 0.8 copy-done.12
  83.0 0.9 copy-done.11
  84.0 28.3 %shard_map.47 = bf16[29,128,128]{2,1,0:T(8,128)(2,1)} custom-call(s32[34]{0:T(128)} %fusion.place, bf16[1936,128]{1,0:T(8,128)(2,1)} %shard_map.46.refs_0_, bf16[1936,128]{1,0:T(8,128)(2,1)} %copy-done.1, bf16[1936,128]{1,0:T(8,128)(2,1)} %copy-done.2, bf16[1936,128]{1,0:T(8,128)(2,1)} %copy-done.5, bf16[1936,128]{1,0:T(8,128)(2,1)} %copy-done.4, ...), custom_call_target="tpu_custom_call" | custom-call | flops 16999999488 | bytes 15728640 | tf_op jit(solution)/shard_map/pallas_call | solution.py:237
  (55 shorter events, 4.3 us)
Async XLA Ops:
  1.9 15.3 %collective-permute-start = (bf16[1936,128]{1,0:T(8,128)(2,1)}, bf16[1936,128]{1,0:T(8,128)(2,1)S(1)}, u32[]{:S(2)}, u32[]{:S(2)}) collective-permute-start(bf16[1936,128]{1,0:T(8,128)(2,1)} %shard_map.46.refs_0_), channel_id=1, source_target_pairs={{0,1},{1,0},{2,3},{3,2},{4,5},{5,4},{6,7},{7,6},{8,9},{9,8},{10,11... | collective-permute-start | bytes 1486856 | tf_op jit(solution)/shard_map/ppermute | solution.py:23
  4.9 23.6 %collective-permute-start.1 = (bf16[1936,128]{1,0:T(8,128)(2,1)}, bf16[1936,128]{1,0:T(8,128)(2,1)S(1)}, u32[]{:S(2)}, u32[]{:S(2)}) collective-permute-start(bf16[1936,128]{1,0:T(8,128)(2,1)} %shard_map.46.refs_0_), channel_id=1, source_target_pairs={{0,16},{1,17},{2,18},{3,19},{4,20},{5,21},{6,22},{7,23},{8,24},{9,... | collective-permute-start | bytes 1486856 | tf_op jit(solution)/shard_map/ppermute | solution.py:23
  6.4 25.4 %collective-permute-start.4 = (bf16[1936,128]{1,0:T(8,128)(2,1)}, bf16[1936,128]{1,0:T(8,128)(2,1)S(1)}, u32[]{:S(2)}, u32[]{:S(2)}) collective-permute-start(bf16[1936,128]{1,0:T(8,128)(2,1)} %shard_map.46.refs_0_), channel_id=1, source_target_pairs={{0,6},{1,7},{2,4},{3,5},{4,2},{5,3},{6,0},{7,1},{8,14},{9,15},{10,... | collective-permute-start | bytes 1486856 | tf_op jit(solution)/shard_map/ppermute | solution.py:23
  10.0 21.7 %collective-permute-start.3 = (bf16[1936,128]{1,0:T(8,128)(2,1)}, bf16[1936,128]{1,0:T(8,128)(2,1)S(1)}, u32[]{:S(2)}, u32[]{:S(2)}) collective-permute-start(bf16[1936,128]{1,0:T(8,128)(2,1)} %shard_map.46.refs_0_), channel_id=1, source_target_pairs={{0,2},{1,3},{2,0},{3,1},{4,6},{5,7},{6,4},{7,5},{8,10},{9,11},{10,... | collective-permute-start | bytes 1486856 | tf_op jit(solution)/shard_map/ppermute | solution.py:23
  10.0 18.5 %collective-permute-start.2 = (bf16[1936,128]{1,0:T(8,128)(2,1)}, bf16[1936,128]{1,0:T(8,128)(2,1)S(1)}, u32[]{:S(2)}, u32[]{:S(2)}) collective-permute-start(bf16[1936,128]{1,0:T(8,128)(2,1)} %shard_map.46.refs_0_), channel_id=1, source_target_pairs={{0,17},{1,16},{2,19},{3,18},{4,21},{5,20},{6,23},{7,22},{8,25},{9,... | collective-permute-start | bytes 1486856 | tf_op jit(solution)/shard_map/ppermute | solution.py:23
  28.5 28.3 %copy-start.2 = (bf16[1936,128]{1,0:T(8,128)(2,1)}, bf16[1936,128]{1,0:T(8,128)(2,1)S(1)}, u32[]{:S(2)}) copy-start(bf16[1936,128]{1,0:T(8,128)(2,1)S(1)} %collective-permute-done.1.refs_2_) | copy-start | bytes 1486852
  28.6 31.1 %copy-start.5 = (bf16[1936,128]{1,0:T(8,128)(2,1)}, bf16[1936,128]{1,0:T(8,128)(2,1)S(1)}, u32[]{:S(2)}) copy-start(bf16[1936,128]{1,0:T(8,128)(2,1)S(1)} %collective-permute-done.2.refs_3_) | copy-start | bytes 1486852
  31.8 50.3 %copy-start.3 = (bf16[1936,128]{1,0:T(8,128)(2,1)}, bf16[1936,128]{1,0:T(8,128)(2,1)S(1)}, u32[]{:S(2)}) copy-start(bf16[1936,128]{1,0:T(8,128)(2,1)S(1)} %collective-permute-done.4.refs_5_) | copy-start | bytes 1486852
  32.0 24.7 %collective-permute-start.5 = (bf16[11616,128]{1,0:T(8,128)(2,1)S(1)}, bf16[11616,128]{1,0:T(8,128)(2,1)}, u32[]{:S(2)}, u32[]{:S(2)}) collective-permute-start(bf16[11616,128]{1,0:T(8,128)(2,1)S(1)} %get-tuple-element.40), channel_id=1, source_target_pairs={{0,8},{1,9},{2,10},{3,11},{4,12},{5,13},{6,14},{7,15},{8,0},{9,1},... | collective-permute-start | bytes 8921096 | tf_op jit(solution)/shard_map/ppermute | solution.py:23
  32.1 24.3 %collective-permute-start.7 = (bf16[3872,128]{1,0:T(8,128)(2,1)S(1)}, bf16[3872,128]{1,0:T(8,128)(2,1)S(1)}, u32[]{:S(2)}, u32[]{:S(2)}) collective-permute-start(bf16[3872,128]{1,0:T(8,128)(2,1)S(1)} %get-tuple-element.39), channel_id=1, source_target_pairs={{0,16},{1,17},{2,18},{3,19},{4,20},{5,21},{6,22},{7,23},{8,24},{9,... | collective-permute-start | bytes 2973704 | tf_op jit(solution)/shard_map/ppermute | solution.py:23
  32.6 24.0 %collective-permute-start.6 = (bf16[3872,128]{1,0:T(8,128)(2,1)S(1)}, bf16[3872,128]{1,0:T(8,128)(2,1)S(1)}, u32[]{:S(2)}, u32[]{:S(2)}) collective-permute-start(bf16[3872,128]{1,0:T(8,128)(2,1)S(1)} %get-tuple-element.39), channel_id=1, source_target_pairs={{0,1},{1,0},{2,3},{3,2},{4,5},{5,4},{6,7},{7,6},{8,9},{9,8},{10,11... | collective-permute-start | bytes 2973704 | tf_op jit(solution)/shard_map/ppermute | solution.py:23
  33.2 21.5 %collective-permute-start.8 = (bf16[1936,128]{1,0:T(8,128)(2,1)S(1)}, bf16[1936,128]{1,0:T(8,128)(2,1)S(1)}, u32[]{:S(2)}, u32[]{:S(2)}) collective-permute-start(bf16[1936,128]{1,0:T(8,128)(2,1)S(1)} %collective-permute-done.4.refs_5_), channel_id=1, source_target_pairs={{0,2},{1,3},{2,0},{3,1},{4,6},{5,7},{6,4},{7,5},{8,10},{9,11},{10,... | collective-permute-start | bytes 1486856 | tf_op jit(solution)/shard_map/ppermute | solution.py:23
  34.8 24.8 %collective-permute-start.14 = (bf16[1936,128]{1,0:T(8,128)(2,1)S(1)}, bf16[1936,128]{1,0:T(8,128)(2,1)}, u32[]{:S(2)}, u32[]{:S(2)}) collective-permute-start(bf16[1936,128]{1,0:T(8,128)(2,1)S(1)} %collective-permute-done.2.refs_3_), channel_id=1, source_target_pairs={{0,4},{1,5},{2,6},{3,7},{4,0},{5,1},{6,2},{7,3},{8,12},{9,13},{10,... | collective-permute-start | bytes 1486856 | tf_op jit(solution)/shard_map/ppermute | solution.py:23
  54.7 27.5 %copy-start = (bf16[1936,128]{1,0:T(8,128)(2,1)}, bf16[1936,128]{1,0:T(8,128)(2,1)S(1)}, u32[]{:S(2)}) copy-start(bf16[1936,128]{1,0:T(8,128)(2,1)S(1)} %collective-permute-done.8.refs_15_) | copy-start | bytes 1486852
  56.7 19.7 %collective-permute-start.9 = (bf16[3872,128]{1,0:T(8,128)(2,1)S(1)}, bf16[3872,128]{1,0:T(8,128)(2,1)S(1)}, u32[]{:S(2)}, u32[]{:S(2)}) collective-permute-start(bf16[3872,128]{1,0:T(8,128)(2,1)S(1)} %collective-permute-done.6.refs_7_), channel_id=1, source_target_pairs={{0,8},{1,9},{2,10},{3,11},{4,12},{5,13},{6,14},{7,15},{8,0},{9,1},... | collective-permute-start | bytes 2973704 | tf_op jit(solution)/shard_map/ppermute | solution.py:23
  56.8 19.5 %collective-permute-start.10 = (bf16[3872,128]{1,0:T(8,128)(2,1)S(1)}, bf16[3872,128]{1,0:T(8,128)(2,1)S(1)}, u32[]{:S(2)}, u32[]{:S(2)}) collective-permute-start(bf16[3872,128]{1,0:T(8,128)(2,1)S(1)} %collective-permute-done.7.refs_9_), channel_id=1, source_target_pairs={{0,8},{1,9},{2,10},{3,11},{4,12},{5,13},{6,14},{7,15},{8,0},{9,1},... | collective-permute-start | bytes 2973704 | tf_op jit(solution)/shard_map/ppermute | solution.py:23
  57.4 18.9 %collective-permute-start.11 = (bf16[2960,128]{1,0:T(8,128)(2,1)S(1)}, bf16[2960,128]{1,0:T(8,128)(2,1)S(1)}, u32[]{:S(2)}, u32[]{:S(2)}) collective-permute-start(bf16[2960,128]{1,0:T(8,128)(2,1)S(1)} %pad_maximum_fusion), channel_id=1, source_target_pairs={{0,1},{1,0},{2,3},{3,2},{4,5},{5,4},{6,7},{7,6},{8,9},{9,8},{10,11... | collective-permute-start | bytes 2273288 | tf_op jit(solution)/shard_map/ppermute | solution.py:23
  58.1 18.1 %collective-permute-start.12 = (bf16[2848,128]{1,0:T(8,128)(2,1)S(1)}, bf16[2848,128]{1,0:T(8,128)(2,1)}, u32[]{:S(2)}, u32[]{:S(2)}) collective-permute-start(bf16[2848,128]{1,0:T(8,128)(2,1)S(1)} %pad_maximum_fusion.1), channel_id=1, source_target_pairs={{0,16},{1,17},{2,18},{3,19},{4,20},{5,21},{6,22},{7,23},{8,24},{9,... | collective-permute-start | bytes 2187272 | tf_op jit(solution)/shard_map/ppermute | solution.py:23
  59.6 12.8 %collective-permute-start.13 = (bf16[1936,128]{1,0:T(8,128)(2,1)S(1)}, bf16[1936,128]{1,0:T(8,128)(2,1)}, u32[]{:S(2)}, u32[]{:S(2)}) collective-permute-start(bf16[1936,128]{1,0:T(8,128)(2,1)S(1)} %collective-permute-done.2.refs_3_), channel_id=1, source_target_pairs={{0,2},{1,3},{2,0},{3,1},{4,6},{5,7},{6,4},{7,5},{8,10},{9,11},{10,... | collective-permute-start | bytes 1486856 | tf_op jit(solution)/shard_map/ppermute | solution.py:23
  76.3 5.8 %collective-permute-start.15 = (bf16[2960,128]{1,0:T(8,128)(2,1)S(1)}, bf16[2960,128]{1,0:T(8,128)(2,1)S(1)}, u32[]{:S(2)}, u32[]{:S(2)}) collective-permute-start(bf16[2960,128]{1,0:T(8,128)(2,1)S(1)} %collective-permute-done.11.refs_11_), channel_id=1, source_target_pairs={{0,8},{1,9},{2,10},{3,11},{4,12},{5,13},{6,14},{7,15},{8,0},{9,1},... | collective-permute-start | bytes 2273288 | tf_op jit(solution)/shard_map/ppermute | solution.py:23
  76.4 5.7 %collective-permute-start.16 = (bf16[2848,128]{1,0:T(8,128)(2,1)}, bf16[2848,128]{1,0:T(8,128)(2,1)S(1)}, u32[]{:S(2)}, u32[]{:S(2)}) collective-permute-start(bf16[2848,128]{1,0:T(8,128)(2,1)} %collective-permute-done.12.refs_13_), channel_id=1, source_target_pairs={{0,8},{1,9},{2,10},{3,11},{4,12},{5,13},{6,14},{7,15},{8,0},{9,1},... | collective-permute-start | bytes 2187272 | tf_op jit(solution)/shard_map/ppermute | solution.py:23
  76.9 4.2 %collective-permute-start.17 = (bf16[1936,128]{1,0:T(8,128)(2,1)S(1)}, bf16[1936,128]{1,0:T(8,128)(2,1)}, u32[]{:S(2)}, u32[]{:S(2)}) collective-permute-start(bf16[1936,128]{1,0:T(8,128)(2,1)S(1)} %collective-permute-done.8.refs_15_), channel_id=1, source_target_pairs={{0,8},{1,9},{2,10},{3,11},{4,12},{5,13},{6,14},{7,15},{8,0},{9,1},... | collective-permute-start | bytes 1486856 | tf_op jit(solution)/shard_map/ppermute | solution.py:23
  77.3 4.0 %collective-permute-start.18 = (bf16[1936,128]{1,0:T(8,128)(2,1)}, bf16[1936,128]{1,0:T(8,128)(2,1)}, u32[]{:S(2)}, u32[]{:S(2)}) collective-permute-start(bf16[1936,128]{1,0:T(8,128)(2,1)} %collective-permute-done.14.refs_17_), channel_id=1, source_target_pairs={{0,8},{1,9},{2,10},{3,11},{4,12},{5,13},{6,14},{7,15},{8,0},{9,1},... | collective-permute-start | bytes 1486856 | tf_op jit(solution)/shard_map/ppermute | solution.py:23
  77.6 4.5 %collective-permute-start.19 = (bf16[1936,128]{1,0:T(8,128)(2,1)}, bf16[1936,128]{1,0:T(8,128)(2,1)}, u32[]{:S(2)}, u32[]{:S(2)}) collective-permute-start(bf16[1936,128]{1,0:T(8,128)(2,1)} %collective-permute-done.13.refs_19_), channel_id=1, source_target_pairs={{0,8},{1,9},{2,10},{3,11},{4,12},{5,13},{6,14},{7,15},{8,0},{9,1},... | collective-permute-start | bytes 1486856 | tf_op jit(solution)/shard_map/ppermute | solution.py:23
  (9 other events, 91.3 us)

commit v11 on v10

--- a/solution.py
+++ b/solution.py
@@ -9,7 +9,7 @@
 from jax.sharding import PartitionSpec as P
 
 NOTE = 16
-GROUP = 2
+GROUP = 1
 WIDTH = 4
 AXES = ("row", "col")
 
@@ -181,7 +181,7 @@
                             own[middle, :, u * edge : (u + 1) * edge] = kept
         return carry
 
-    lax.fori_loop(0, (slots + 1) // GROUP, row_group, 0)
+    lax.fori_loop(0, -(-slots // GROUP), row_group, 0)
 
     keep = masks(far)
     copies = []
@@ -247,7 +247,7 @@
             pltpu.SemaphoreType.DMA((2 * far + 1,)),
             pltpu.SemaphoreType.DMA((-(-wide // WIDTH),)),
         ],
-        compiler_params=pltpu.CompilerParams(vmem_limit_bytes=56 * 2**20),
+        compiler_params=pltpu.CompilerParams(vmem_limit_bytes=36 * 2**20),
         cost_estimate=pl.CostEstimate(flops=17 * 10**9, bytes_accessed=15 * 2**20, transcendentals=0),
     )(place, *tables)
     return result[None]

time: 112 us -> 128 us (1.14)
  local copies, waits for them, and re-layouts: 3.87 us -> 11.9 us
  Pallas kernels: 30.2 us -> 36.9 us
    unnamed x31 -> x27, local copies, waits for them, and re-layouts: 3.7 us -> 11.7 us
    pallas_call x1, Pallas kernels: 28.3 us -> 35 us  [shards(): pl.pallas_call(functools.partial(purify, reach, edge, layout), out_shape=...]
where the time goes in v11:
time: 128 us; the launch traced here: 127 us
  waiting for transfers between devices  60.4 us (47%)
  Pallas kernels  36.9 us (29%)
  starting transfers between devices  17.4 us (14%)
  local copies, waits for them, and re-layouts  11.9 us (9%)
    ppermute x20, waiting for transfers between devices, swap(): return lax.ppermute(value, AXES, [(i, i ^ mask) for i in range(count)])  60.4 us
    pallas_call x1, Pallas kernels, shards(): pl.pallas_call(functools.partial(purify, reach, edge, layout), out_shape=...  35 us
    ppermute x20, starting transfers between devices, swap(): return lax.ppermute(value, AXES, [(i, i ^ mask) for i in range(count)])  17.4 us
    unnamed x27, local copies, waits for them, and re-layouts  11.7 us
  transfers between devices with their start and end apart: 20, of which 12 were waited for; matrix products, arithmetic and copies ran while one was open for 2% of the time, Pallas kernels for 0%

profile of v11, /device:TPU:0, one launch (start us, length us, event | category | flops | bytes accessed | tf_op | source)
XLA Modules:
  0.0 127.5 jit_solution(7722589770147854564)
XLA Ops:
  0.0 1.9 %shard_map.46.refs_0_ = bf16[1936,128]{1,0:T(8,128)(2,1)} custom-call(s32[1,15]{1,0:T(1,128)} %pattern.1, s32[1,29]{1,0:T(1,128)} %filter_mask.1, bf16[15,128,128]{2,1,0:T(8,128)(2,1)} %bitcast.4), custom_call_target="tpu_custom_call" | custom-call | tf_op jit(solution)/shard_map/pallas_call | solution.py:228
  1.9 2.9 %collective-permute-start = (bf16[1936,128]{1,0:T(8,128)(2,1)}, bf16[1936,128]{1,0:T(8,128)(2,1)S(1)}, u32[]{:S(2)}, u32[]{:S(2)}) collective-permute-start(bf16[1936,128]{1,0:T(8,128)(2,1)} %shard_map.46.refs_0_), channel_id=1, source_target_pairs={{0,1},{1,0},{2,3},{3,2},{4,5},{5,4},{6,7},{7,6},{8,9},{9,8},{10,11... | collective-permute-start | bytes 1486856 | tf_op jit(solution)/shard_map/ppermute | solution.py:23
  4.9 1.5 %collective-permute-start.1 = (bf16[1936,128]{1,0:T(8,128)(2,1)}, bf16[1936,128]{1,0:T(8,128)(2,1)S(1)}, u32[]{:S(2)}, u32[]{:S(2)}) collective-permute-start(bf16[1936,128]{1,0:T(8,128)(2,1)} %shard_map.46.refs_0_), channel_id=1, source_target_pairs={{0,16},{1,17},{2,18},{3,19},{4,20},{5,21},{6,22},{7,23},{8,24},{9,... | collective-permute-start | bytes 1486856 | tf_op jit(solution)/shard_map/ppermute | solution.py:23
  6.4 3.6 %collective-permute-start.4 = (bf16[1936,128]{1,0:T(8,128)(2,1)}, bf16[1936,128]{1,0:T(8,128)(2,1)S(1)}, u32[]{:S(2)}, u32[]{:S(2)}) collective-permute-start(bf16[1936,128]{1,0:T(8,128)(2,1)} %shard_map.46.refs_0_), channel_id=1, source_target_pairs={{0,6},{1,7},{2,4},{3,5},{4,2},{5,3},{6,0},{7,1},{8,14},{9,15},{10,... | collective-permute-start | bytes 1486856 | tf_op jit(solution)/shard_map/ppermute | solution.py:23
  10.5 1.1 constant_dynamic-update-slice_fusion.5
  11.6 5.6 %collective-permute-done.refs_1_ = bf16[1936,128]{1,0:T(8,128)(2,1)S(1)} collective-permute-done((bf16[1936,128]{1,0:T(8,128)(2,1)}, bf16[1936,128]{1,0:T(8,128)(2,1)S(1)}, u32[]{:S(2)}, u32[]{:S(2)}) %collective-permute-start) | collective-permute-done | bytes 495648 | tf_op jit(solution)/shard_map/ppermute | solution.py:23
  17.3 11.2 %collective-permute-done.1.refs_2_ = bf16[1936,128]{1,0:T(8,128)(2,1)S(1)} collective-permute-done((bf16[1936,128]{1,0:T(8,128)(2,1)}, bf16[1936,128]{1,0:T(8,128)(2,1)S(1)}, u32[]{:S(2)}, u32[]{:S(2)}) %collective-permute-start.1) | collective-permute-done | bytes 495648 | tf_op jit(solution)/shard_map/ppermute | solution.py:23
  28.6 3.1 %collective-permute-done.3.refs_4_ = bf16[1936,128]{1,0:T(8,128)(2,1)S(1)} collective-permute-done((bf16[1936,128]{1,0:T(8,128)(2,1)}, bf16[1936,128]{1,0:T(8,128)(2,1)S(1)}, u32[]{:S(2)}, u32[]{:S(2)}) %collective-permute-start.3) | collective-permute-done | bytes 495648 | tf_op jit(solution)/shard_map/ppermute | solution.py:23
  33.1 1.7 %collective-permute-start.8 = (bf16[1936,128]{1,0:T(8,128)(2,1)S(1)}, bf16[1936,128]{1,0:T(8,128)(2,1)S(1)}, u32[]{:S(2)}, u32[]{:S(2)}) collective-permute-start(bf16[1936,128]{1,0:T(8,128)(2,1)S(1)} %collective-permute-done.4.refs_5_), channel_id=1, source_target_pairs={{0,2},{1,3},{2,0},{3,1},{4,6},{5,7},{6,4},{7,5},{8,10},{9,11},{10,... | collective-permute-start | bytes 1486856 | tf_op jit(solution)/shard_map/ppermute | solution.py:23
  35.3 19.3 %collective-permute-done.8.refs_15_ = bf16[1936,128]{1,0:T(8,128)(2,1)S(1)} collective-permute-done((bf16[1936,128]{1,0:T(8,128)(2,1)S(1)}, bf16[1936,128]{1,0:T(8,128)(2,1)S(1)}, u32[]{:S(2)}, u32[]{:S(2)}) %collective-permute-start.8) | collective-permute-done | bytes 495648 | tf_op jit(solution)/shard_map/ppermute | solution.py:23
  54.6 1.7 %collective-permute-done.7.refs_9_ = bf16[3872,128]{1,0:T(8,128)(2,1)S(1)} collective-permute-done((bf16[3872,128]{1,0:T(8,128)(2,1)S(1)}, bf16[3872,128]{1,0:T(8,128)(2,1)S(1)}, u32[]{:S(2)}, u32[]{:S(2)}) %collective-permute-start.7) | collective-permute-done | bytes 991264 | tf_op jit(solution)/shard_map/ppermute | solution.py:23
  56.6 1.7 %copy-done.5 = bf16[11616,128]{1,0:T(8,128)(2,1)} copy-done((bf16[11616,128]{1,0:T(8,128)(2,1)}, bf16[11616,128]{1,0:T(8,128)(2,1)S(1)}, u32[]{:S(2)}) %copy-start.5) | copy-done | bytes 2973720
  59.7 1.5 %collective-permute-start.12 = (bf16[2848,128]{1,0:T(8,128)(2,1)S(1)}, bf16[2848,128]{1,0:T(8,128)(2,1)}, u32[]{:S(2)}, u32[]{:S(2)}) collective-permute-start(bf16[2848,128]{1,0:T(8,128)(2,1)S(1)} %pad_maximum_fusion.1), channel_id=1, source_target_pairs={{0,16},{1,17},{2,18},{3,19},{4,20},{5,21},{6,22},{7,23},{8,24},{9,... | collective-permute-start | bytes 2187272 | tf_op jit(solution)/shard_map/ppermute | solution.py:23
  61.2 1.7 %collective-permute-start.13 = (bf16[1936,128]{1,0:T(8,128)(2,1)S(1)}, bf16[1936,128]{1,0:T(8,128)(2,1)}, u32[]{:S(2)}, u32[]{:S(2)}) collective-permute-start(bf16[1936,128]{1,0:T(8,128)(2,1)S(1)} %collective-permute-done.2.refs_3_), channel_id=1, source_target_pairs={{0,2},{1,3},{2,0},{3,1},{4,6},{5,7},{6,4},{7,5},{8,10},{9,11},{10,... | collective-permute-start | bytes 1486856 | tf_op jit(solution)/shard_map/ppermute | solution.py:23
  62.9 11.1 %collective-permute-done.13.refs_19_ = bf16[1936,128]{1,0:T(8,128)(2,1)} collective-permute-done((bf16[1936,128]{1,0:T(8,128)(2,1)S(1)}, bf16[1936,128]{1,0:T(8,128)(2,1)}, u32[]{:S(2)}, u32[]{:S(2)}) %collective-permute-start.13) | collective-permute-done | bytes 495648 | tf_op jit(solution)/shard_map/ppermute | solution.py:23
  74.0 3.8 %collective-permute-done.12.refs_13_ = bf16[2848,128]{1,0:T(8,128)(2,1)} collective-permute-done((bf16[2848,128]{1,0:T(8,128)(2,1)S(1)}, bf16[2848,128]{1,0:T(8,128)(2,1)}, u32[]{:S(2)}, u32[]{:S(2)}) %collective-permute-start.12) | collective-permute-done | bytes 729120 | tf_op jit(solution)/shard_map/ppermute | solution.py:23
  81.8 2.0 %collective-permute-done.17.refs_16_ = bf16[1936,128]{1,0:T(8,128)(2,1)} collective-permute-done((bf16[1936,128]{1,0:T(8,128)(2,1)S(1)}, bf16[1936,128]{1,0:T(8,128)(2,1)}, u32[]{:S(2)}, u32[]{:S(2)}) %collective-permute-start.17) | collective-permute-done | bytes 495648 | tf_op jit(solution)/shard_map/ppermute | solution.py:23
  83.8 1.3 collective-permute-done.18.refs_18_
  85.8 1.2 copy-done.2
  87.0 1.2 copy-done.4
  88.2 1.8 %copy-done.6 = bf16[11616,128]{1,0:T(8,128)(2,1)S(1)} copy-done((bf16[11616,128]{1,0:T(8,128)(2,1)S(1)}, bf16[11616,128]{1,0:T(8,128)(2,1)}, u32[]{:S(2)}) %copy-start.6) | copy-done | bytes 2973720
  90.1 1.2 copy-done.8
  91.3 1.2 copy-done.10
  92.5 35.0 %shard_map.47 = bf16[29,128,128]{2,1,0:T(8,128)(2,1)} custom-call(s32[34]{0:T(128)S(1)} %fusion.place, bf16[1936,128]{1,0:T(8,128)(2,1)S(1)} %copy-done, bf16[1936,128]{1,0:T(8,128)(2,1)S(1)} %collective-permute-done.refs_1_, bf16[1936,128]{1,0:T(8,128)(2,1)S(1)} %collective-permute-done.1.refs_2_, bf16[1936,128]{1,0:T(8,128)(2,1)S(1)} %collective-permute-done.2.refs_3_, ...), custom_call_target="tpu_custom_call" | custom-call | flops 16999999488 | bytes 15728640 | tf_op jit(solution)/shard_map/pallas_call | solution.py:237
  (51 shorter events, 8.9 us)
Async XLA Ops:
  1.9 15.3 %collective-permute-start = (bf16[1936,128]{1,0:T(8,128)(2,1)}, bf16[1936,128]{1,0:T(8,128)(2,1)S(1)}, u32[]{:S(2)}, u32[]{:S(2)}) collective-permute-start(bf16[1936,128]{1,0:T(8,128)(2,1)} %shard_map.46.refs_0_), channel_id=1, source_target_pairs={{0,1},{1,0},{2,3},{3,2},{4,5},{5,4},{6,7},{7,6},{8,9},{9,8},{10,11... | collective-permute-start | bytes 1486856 | tf_op jit(solution)/shard_map/ppermute | solution.py:23
  4.9 23.6 %collective-permute-start.1 = (bf16[1936,128]{1,0:T(8,128)(2,1)}, bf16[1936,128]{1,0:T(8,128)(2,1)S(1)}, u32[]{:S(2)}, u32[]{:S(2)}) collective-permute-start(bf16[1936,128]{1,0:T(8,128)(2,1)} %shard_map.46.refs_0_), channel_id=1, source_target_pairs={{0,16},{1,17},{2,18},{3,19},{4,20},{5,21},{6,22},{7,23},{8,24},{9,... | collective-permute-start | bytes 1486856 | tf_op jit(solution)/shard_map/ppermute | solution.py:23
  6.4 25.4 %collective-permute-start.4 = (bf16[1936,128]{1,0:T(8,128)(2,1)}, bf16[1936,128]{1,0:T(8,128)(2,1)S(1)}, u32[]{:S(2)}, u32[]{:S(2)}) collective-permute-start(bf16[1936,128]{1,0:T(8,128)(2,1)} %shard_map.46.refs_0_), channel_id=1, source_target_pairs={{0,6},{1,7},{2,4},{3,5},{4,2},{5,3},{6,0},{7,1},{8,14},{9,15},{10,... | collective-permute-start | bytes 1486856 | tf_op jit(solution)/shard_map/ppermute | solution.py:23
  10.0 21.7 %collective-permute-start.3 = (bf16[1936,128]{1,0:T(8,128)(2,1)}, bf16[1936,128]{1,0:T(8,128)(2,1)S(1)}, u32[]{:S(2)}, u32[]{:S(2)}) collective-permute-start(bf16[1936,128]{1,0:T(8,128)(2,1)} %shard_map.46.refs_0_), channel_id=1, source_target_pairs={{0,2},{1,3},{2,0},{3,1},{4,6},{5,7},{6,4},{7,5},{8,10},{9,11},{10,... | collective-permute-start | bytes 1486856 | tf_op jit(solution)/shard_map/ppermute | solution.py:23
  10.0 18.5 %collective-permute-start.2 = (bf16[1936,128]{1,0:T(8,128)(2,1)}, bf16[1936,128]{1,0:T(8,128)(2,1)S(1)}, u32[]{:S(2)}, u32[]{:S(2)}) collective-permute-start(bf16[1936,128]{1,0:T(8,128)(2,1)} %shard_map.46.refs_0_), channel_id=1, source_target_pairs={{0,17},{1,16},{2,19},{3,18},{4,21},{5,20},{6,23},{7,22},{8,25},{9,... | collective-permute-start | bytes 1486856 | tf_op jit(solution)/shard_map/ppermute | solution.py:23
  31.8 54.0 %copy-start = (bf16[1936,128]{1,0:T(8,128)(2,1)S(1)}, bf16[1936,128]{1,0:T(8,128)(2,1)}, u32[]{:S(2)}) copy-start(bf16[1936,128]{1,0:T(8,128)(2,1)} %shard_map.46.refs_0_) | copy-start | bytes 1486852
  32.0 24.7 %collective-permute-start.5 = (bf16[11616,128]{1,0:T(8,128)(2,1)S(1)}, bf16[11616,128]{1,0:T(8,128)(2,1)S(1)}, u32[]{:S(2)}, u32[]{:S(2)}) collective-permute-start(bf16[11616,128]{1,0:T(8,128)(2,1)S(1)} %get-tuple-element.40), channel_id=1, source_target_pairs={{0,8},{1,9},{2,10},{3,11},{4,12},{5,13},{6,14},{7,15},{8,0},{9,1},... | collective-permute-start | bytes 8921096 | tf_op jit(solution)/shard_map/ppermute | solution.py:23
  32.0 24.3 %collective-permute-start.7 = (bf16[3872,128]{1,0:T(8,128)(2,1)S(1)}, bf16[3872,128]{1,0:T(8,128)(2,1)S(1)}, u32[]{:S(2)}, u32[]{:S(2)}) collective-permute-start(bf16[3872,128]{1,0:T(8,128)(2,1)S(1)} %get-tuple-element.39), channel_id=1, source_target_pairs={{0,16},{1,17},{2,18},{3,19},{4,20},{5,21},{6,22},{7,23},{8,24},{9,... | collective-permute-start | bytes 2973704 | tf_op jit(solution)/shard_map/ppermute | solution.py:23
  32.6 24.0 %collective-permute-start.6 = (bf16[3872,128]{1,0:T(8,128)(2,1)S(1)}, bf16[3872,128]{1,0:T(8,128)(2,1)S(1)}, u32[]{:S(2)}, u32[]{:S(2)}) collective-permute-start(bf16[3872,128]{1,0:T(8,128)(2,1)S(1)} %get-tuple-element.39), channel_id=1, source_target_pairs={{0,1},{1,0},{2,3},{3,2},{4,5},{5,4},{6,7},{7,6},{8,9},{9,8},{10,11... | collective-permute-start | bytes 2973704 | tf_op jit(solution)/shard_map/ppermute | solution.py:23
  33.1 21.5 %collective-permute-start.8 = (bf16[1936,128]{1,0:T(8,128)(2,1)S(1)}, bf16[1936,128]{1,0:T(8,128)(2,1)S(1)}, u32[]{:S(2)}, u32[]{:S(2)}) collective-permute-start(bf16[1936,128]{1,0:T(8,128)(2,1)S(1)} %collective-permute-done.4.refs_5_), channel_id=1, source_target_pairs={{0,2},{1,3},{2,0},{3,1},{4,6},{5,7},{6,4},{7,5},{8,10},{9,11},{10,... | collective-permute-start | bytes 1486856 | tf_op jit(solution)/shard_map/ppermute | solution.py:23
  34.8 26.4 %collective-permute-start.14 = (bf16[1936,128]{1,0:T(8,128)(2,1)S(1)}, bf16[1936,128]{1,0:T(8,128)(2,1)}, u32[]{:S(2)}, u32[]{:S(2)}) collective-permute-start(bf16[1936,128]{1,0:T(8,128)(2,1)S(1)} %collective-permute-done.2.refs_3_), channel_id=1, source_target_pairs={{0,4},{1,5},{2,6},{3,7},{4,0},{5,1},{6,2},{7,3},{8,12},{9,13},{10,... | collective-permute-start | bytes 1486856 | tf_op jit(solution)/shard_map/ppermute | solution.py:23
  56.4 23.7 %copy-start.1 = (bf16[3872,128]{1,0:T(8,128)(2,1)}, bf16[3872,128]{1,0:T(8,128)(2,1)S(1)}, u32[]{:S(2)}) copy-start(bf16[3872,128]{1,0:T(8,128)(2,1)S(1)} %collective-permute-done.7.refs_9_) | copy-start | bytes 2973700
  56.6 23.9 %copy-start.3 = (bf16[3872,128]{1,0:T(8,128)(2,1)}, bf16[3872,128]{1,0:T(8,128)(2,1)S(1)}, u32[]{:S(2)}) copy-start(bf16[3872,128]{1,0:T(8,128)(2,1)S(1)} %collective-permute-done.6.refs_7_) | copy-start | bytes 2973700
  58.3 20.7 %collective-permute-start.9 = (bf16[3872,128]{1,0:T(8,128)(2,1)S(1)}, bf16[3872,128]{1,0:T(8,128)(2,1)S(1)}, u32[]{:S(2)}, u32[]{:S(2)}) collective-permute-start(bf16[3872,128]{1,0:T(8,128)(2,1)S(1)} %collective-permute-done.6.refs_7_), channel_id=1, source_target_pairs={{0,8},{1,9},{2,10},{3,11},{4,12},{5,13},{6,14},{7,15},{8,0},{9,1},... | collective-permute-start | bytes 2973704 | tf_op jit(solution)/shard_map/ppermute | solution.py:23
  58.4 19.6 %collective-permute-start.10 = (bf16[3872,128]{1,0:T(8,128)(2,1)S(1)}, bf16[3872,128]{1,0:T(8,128)(2,1)S(1)}, u32[]{:S(2)}, u32[]{:S(2)}) collective-permute-start(bf16[3872,128]{1,0:T(8,128)(2,1)S(1)} %collective-permute-done.7.refs_9_), channel_id=1, source_target_pairs={{0,8},{1,9},{2,10},{3,11},{4,12},{5,13},{6,14},{7,15},{8,0},{9,1},... | collective-permute-start | bytes 2973704 | tf_op jit(solution)/shard_map/ppermute | solution.py:23
  59.0 19.0 %collective-permute-start.11 = (bf16[2960,128]{1,0:T(8,128)(2,1)S(1)}, bf16[2960,128]{1,0:T(8,128)(2,1)}, u32[]{:S(2)}, u32[]{:S(2)}) collective-permute-start(bf16[2960,128]{1,0:T(8,128)(2,1)S(1)} %pad_maximum_fusion), channel_id=1, source_target_pairs={{0,1},{1,0},{2,3},{3,2},{4,5},{5,4},{6,7},{7,6},{8,9},{9,8},{10,11... | collective-permute-start | bytes 2273288 | tf_op jit(solution)/shard_map/ppermute | solution.py:23
  59.7 18.1 %collective-permute-start.12 = (bf16[2848,128]{1,0:T(8,128)(2,1)S(1)}, bf16[2848,128]{1,0:T(8,128)(2,1)}, u32[]{:S(2)}, u32[]{:S(2)}) collective-permute-start(bf16[2848,128]{1,0:T(8,128)(2,1)S(1)} %pad_maximum_fusion.1), channel_id=1, source_target_pairs={{0,16},{1,17},{2,18},{3,19},{4,20},{5,21},{6,22},{7,23},{8,24},{9,... | collective-permute-start | bytes 2187272 | tf_op jit(solution)/shard_map/ppermute | solution.py:23
  61.2 12.8 %collective-permute-start.13 = (bf16[1936,128]{1,0:T(8,128)(2,1)S(1)}, bf16[1936,128]{1,0:T(8,128)(2,1)}, u32[]{:S(2)}, u32[]{:S(2)}) collective-permute-start(bf16[1936,128]{1,0:T(8,128)(2,1)S(1)} %collective-permute-done.2.refs_3_), channel_id=1, source_target_pairs={{0,2},{1,3},{2,0},{3,1},{4,6},{5,7},{6,4},{7,5},{8,10},{9,11},{10,... | collective-permute-start | bytes 1486856 | tf_op jit(solution)/shard_map/ppermute | solution.py:23
  80.0 5.8 %collective-permute-start.15 = (bf16[2960,128]{1,0:T(8,128)(2,1)}, bf16[2960,128]{1,0:T(8,128)(2,1)}, u32[]{:S(2)}, u32[]{:S(2)}) collective-permute-start(bf16[2960,128]{1,0:T(8,128)(2,1)} %collective-permute-done.11.refs_11_), channel_id=1, source_target_pairs={{0,8},{1,9},{2,10},{3,11},{4,12},{5,13},{6,14},{7,15},{8,0},{9,1},... | collective-permute-start | bytes 2273288 | tf_op jit(solution)/shard_map/ppermute | solution.py:23
  80.0 5.8 %collective-permute-start.16 = (bf16[2848,128]{1,0:T(8,128)(2,1)}, bf16[2848,128]{1,0:T(8,128)(2,1)}, u32[]{:S(2)}, u32[]{:S(2)}) collective-permute-start(bf16[2848,128]{1,0:T(8,128)(2,1)} %collective-permute-done.12.refs_13_), channel_id=1, source_target_pairs={{0,8},{1,9},{2,10},{3,11},{4,12},{5,13},{6,14},{7,15},{8,0},{9,1},... | collective-permute-start | bytes 2187272 | tf_op jit(solution)/shard_map/ppermute | solution.py:23
  80.5 3.3 %collective-permute-start.17 = (bf16[1936,128]{1,0:T(8,128)(2,1)S(1)}, bf16[1936,128]{1,0:T(8,128)(2,1)}, u32[]{:S(2)}, u32[]{:S(2)}) collective-permute-start(bf16[1936,128]{1,0:T(8,128)(2,1)S(1)} %collective-permute-done.8.refs_15_), channel_id=1, source_target_pairs={{0,8},{1,9},{2,10},{3,11},{4,12},{5,13},{6,14},{7,15},{8,0},{9,1},... | collective-permute-start | bytes 1486856 | tf_op jit(solution)/shard_map/ppermute | solution.py:23
  80.6 4.5 %collective-permute-start.18 = (bf16[1936,128]{1,0:T(8,128)(2,1)}, bf16[1936,128]{1,0:T(8,128)(2,1)}, u32[]{:S(2)}, u32[]{:S(2)}) collective-permute-start(bf16[1936,128]{1,0:T(8,128)(2,1)} %collective-permute-done.14.refs_17_), channel_id=1, source_target_pairs={{0,8},{1,9},{2,10},{3,11},{4,12},{5,13},{6,14},{7,15},{8,0},{9,1},... | collective-permute-start | bytes 1486856 | tf_op jit(solution)/shard_map/ppermute | solution.py:23
  81.1 4.7 %collective-permute-start.19 = (bf16[1936,128]{1,0:T(8,128)(2,1)}, bf16[1936,128]{1,0:T(8,128)(2,1)}, u32[]{:S(2)}, u32[]{:S(2)}) collective-permute-start(bf16[1936,128]{1,0:T(8,128)(2,1)} %collective-permute-done.13.refs_19_), channel_id=1, source_target_pairs={{0,8},{1,9},{2,10},{3,11},{4,12},{5,13},{6,14},{7,15},{8,0},{9,1},... | collective-permute-start | bytes 1486856 | tf_op jit(solution)/shard_map/ppermute | solution.py:23
  88.2 1.8 %copy-start.6 = (bf16[11616,128]{1,0:T(8,128)(2,1)S(1)}, bf16[11616,128]{1,0:T(8,128)(2,1)}, u32[]{:S(2)}) copy-start(bf16[11616,128]{1,0:T(8,128)(2,1)} %copy-done.5) | copy-start | bytes 8921092
  (7 other events, 8.5 us)

commit v12 on v10

--- a/solution.py
+++ b/solution.py
@@ -14,7 +14,7 @@
 AXES = ("row", "col")
 
 
-def cube(own, count, cut):
+def cube(own, count, cut, gather):
     x, z1, z2, z3, core, y = 1, 2, 4, 6, 8, 16
     full = own.shape[0]
     found = []
@@ -47,13 +47,16 @@
     xl = swap(jnp.concatenate([f2, yp[full : full + cut]], axis=0), x)
     yl = swap(jnp.concatenate([f2, xp[full + cut :]], axis=0), y)
     d1 = swap(d0, z1)
-    spots = [cross((xp, whole(z1 | x, z3 | x))), cross((yp, whole(z1 | y, z3 | y)))]
-    xl, yl, d1, f2, d2 = finish(spots[0], *finish(spots[1], xl, yl, d1, f2, d2))
+    cross((xp, whole(z1 | x, z3 | x)))
+    cross((yp, whole(z1 | y, z3 | y)))
+    band = gather(found + [(f2, whole(z2)), (d2, whole(z2 | x | y))])
+    band, xl, yl, d1, f2, d2 = lax.optimization_barrier((band, xl, yl, d1, f2, d2))
+    del found[:]
     cross((xl, [(z2 | x, 0, full), (z3 | x | y, 0, cut)]))
     cross((yl, [(z2 | y, 0, full), (z3 | x | y, cut, full - cut)]))
-    for item in ((f2, whole(z2)), (d2, whole(z2 | x | y)), (d1, whole(z1 | x | y))):
-        cross(item)
-    return found
+    for row, mask in ((f2, z2), (d2, z2 | x | y), (d1, z1 | x | y)):
+        cross((row, whole(mask)))
+    return band, [item for item in found if item[0] is not f2 and item[0] is not d2]
 
 
 def window(payload, need, cut):
@@ -62,70 +65,110 @@
     size = payload.shape[0]
     column = lax.axis_index("col")
     here = lax.axis_index("row") * width + column
+
+    def places(offsets):
+        return jnp.where(jnp.abs(offsets) <= need, offsets + need, -1)
+
     if (groups, width) == (4, 8):
-        found = cube(payload, count, cut)
-        pieces = [(array, [(start, rows) for _, start, rows in parts]) for array, parts in found]
-        masks = np.array([mask for _, parts in found for mask, _, _ in parts])
-        device = np.arange(count)[:, None]
-        offsets = jnp.asarray((((device ^ masks) - device + count // 2) % count - count // 2).astype(np.int32))[here]
-    else:
-        pieces, offsets = [], []
-        block = lax.all_gather(payload, "col", axis=0, tiled=True)
-        pieces.append((block, [(0, size)] * width))
-        offsets.append(jnp.arange(width, dtype=jnp.int32) - column)
-        for hop in range(1, -(-need // width) + 1):
-            part = min(width, need - (hop - 1) * width)
-            up = [(g, (g + hop) % groups) for g in range(groups)]
-            down = [(g, (g - hop) % groups) for g in range(groups)]
-            steps = jnp.arange(part, dtype=jnp.int32) - column
-            pieces.append((lax.ppermute(block[(width - part) * size :], "row", up), [(0, size)] * part))
-            offsets.append(steps - (hop - 1) * width - part)
-            pieces.append((lax.ppermute(block[: part * size], "row", down), [(0, size)] * part))
-            offsets.append(steps + hop * width)
-        offsets = jnp.concatenate(offsets).astype(jnp.int32)
-    return pieces, jnp.where(jnp.abs(offsets) <= need, offsets + need, -1)
+
+        def split(found):
+            masks = np.array([mask for _, parts in found for mask, _, _ in parts])
+            device = np.arange(count)[:, None]
+            offsets = ((device ^ masks) - device + count // 2) % count - count // 2
+            pieces = [(array, [(start, rows) for _, start, rows in parts]) for array, parts in found]
+            return pieces, places(jnp.asarray(offsets.astype(np.int32))[here])
+
+        band, late = cube(payload, count, cut, lambda found: assemble(*split(found), size, need))
+        return band, *split(late)
+    pieces, offsets = [], []
+    block = lax.all_gather(payload, "col", axis=0, tiled=True)
+    pieces.append((block, [(0, size)] * width))
+    offsets.append(jnp.arange(width, dtype=jnp.int32) - column)
+    for hop in range(1, -(-need // width) + 1):
+        part = min(width, need - (hop - 1) * width)
+        up = [(g, (g + hop) % groups) for g in range(groups)]
+        down = [(g, (g - hop) % groups) for g in range(groups)]
+        steps = jnp.arange(part, dtype=jnp.int32) - column
+        pieces.append((lax.ppermute(block[(width - part) * size :], "row", up), [(0, size)] * part))
+        offsets.append(steps - (hop - 1) * width - part)
+        pieces.append((lax.ppermute(block[: part * size], "row", down), [(0, size)] * part))
+        offsets.append(steps + hop * width)
+    band = assemble(pieces, places(jnp.concatenate(offsets).astype(jnp.int32)), size, need)
+    return band, [], jnp.zeros((1,), jnp.int32)
+
+
+def row_copies(layout, place, tables, band, arrived, pitch):
+    copies = []
+    for table, parts in zip(tables, layout):
+        begin = 0
+        for start, size in parts:
+            k = place[len(copies)]
+            copy = pltpu.make_async_copy(
+                table.at[pl.ds(begin, size)],
+                band.at[pl.ds(pl.multiple_of(jnp.maximum(k, 0) * pitch + start, NOTE), size)],
+                arrived.at[len(copies)],
+            )
+            copies.append((k, copy))
+            begin += size
+    for k, copy in copies:
+
+        @pl.when(k >= 0)
+        def _(copy=copy):
+            copy.start()
+
+    return copies
+
+
+def wait_all(copies):
+    for k, copy in copies:
+
+        @pl.when(k >= 0)
+        def _(copy=copy):
+            copy.wait()
+
+
+def assemble(pieces, place, pitch, need):
+    tables = [array for array, _ in pieces]
+    layout = [parts for _, parts in pieces]
+    kind, edge = tables[0].dtype, tables[0].shape[1]
+    rows = 2 * need + 2
+
+    def body(place, *refs):
+        band, arrived = refs[len(tables) :]
+        copies = row_copies(layout, place, refs[: len(tables)], band, arrived, pitch)
+
+        def clear(s, carry):
+            band[pl.ds(pl.multiple_of((rows - 1) * pitch + s * NOTE, NOTE), NOTE), :] = jnp.zeros((NOTE, edge), kind)
+            return carry
+
+        lax.fori_loop(0, pitch // NOTE, clear, 0)
+        wait_all(copies)
+
+    return pl.pallas_call(
+        body,
+        out_shape=pltpu.VMEM((rows * pitch, edge), kind),
+        in_specs=[pl.BlockSpec(memory_space=pltpu.SMEM)] + [pl.BlockSpec(memory_space=pl.ANY)] * len(tables),
+        out_specs=pl.BlockSpec(memory_space=pltpu.VMEM),
+        scratch_shapes=[pltpu.SemaphoreType.DMA((sum(len(parts) for parts in layout),))],
+        compiler_params=pltpu.CompilerParams(vmem_limit_bytes=2 * 2**20),
+        cost_estimate=pl.CostEstimate(flops=0, bytes_accessed=rows * pitch * edge * 4, transcendentals=0),
+    )(place, *tables)
 
 
 def purify(reach, edge, layout, place, *refs):
     count = len(layout)
-    tables, (out, band, square, own, result, arrived, left_out) = refs[:count], refs[count:]
+    tables, (_, band, out, square, own, result, arrived, left_out) = refs[:count], refs[count:]
     far = 2 * reach
     slots, wide = 2 * reach + 1, 4 * reach + 1
     pitch = slots * edge + NOTE
     kind = band.dtype
-
-    base = 0
-    for table, parts in zip(tables, layout):
-        begin = 0
-        for start, size in parts:
-            k = place[base]
-
-            @pl.when(k >= 0)
-            def _(table=table, begin=begin, start=start, size=size, k=k):
-                pltpu.make_async_copy(
-                    table.at[pl.ds(begin, size)],
-                    band.at[pl.ds(pl.multiple_of(k * pitch + start, NOTE), size)],
-                    arrived.at[k],
-                ).start()
-
-            begin += size
-            base += 1
-
-    def ready(k):
-        row = pl.ds(0, pitch)
-        pltpu.make_async_copy(tables[0].at[row], band.at[row], arrived.at[k]).wait()
+    copies = row_copies(layout, place, tables, band, arrived, pitch)
+    wait_all(copies)
 
     zero = jnp.zeros((edge, edge), kind)
 
     def block(k, s):
         return band[pl.ds(pl.multiple_of(k * pitch + s * edge, NOTE), edge), :]
-
-    def clear(s, carry):
-        band[pl.ds(pl.multiple_of((2 * far + 1) * pitch + s * edge, NOTE), edge), :] = zero
-        return carry
-
-    lax.fori_loop(0, slots, clear, 0)
-    band[(2 * far + 1) * pitch + slots * edge :, :] = jnp.zeros((NOTE, edge), kind)
 
     spots = -(-wide // 8) * 8
     diagonal = lax.broadcasted_iota(jnp.int32, (spots, edge), 0) == lax.broadcasted_iota(jnp.int32, (spots, edge), 1)
@@ -149,18 +192,8 @@
             axis=1,
         )
 
-    for k in range(far):
-        ready(k)
-
     def row_group(group, carry):
         r = GROUP * group
-        for i in range(GROUP):
-            k = r + far + i
-
-            @pl.when(k <= 2 * far)
-            def _(k=k):
-                ready(k)
-
         middle = jnp.where(group == reach // GROUP, 1, 0)
         keep = [masks(r + reach + i) for i in range(GROUP)]
         for d in range(-far, far + GROUP, 2):
@@ -230,26 +263,28 @@
         out_shape=jax.ShapeDtypeStruct((slots * edge + NOTE, edge), density.dtype),
         in_specs=[smem, smem, vmem],
         out_specs=vmem,
+        compiler_params=pltpu.CompilerParams(vmem_limit_bytes=4 * 2**20),
     )(pattern, filter_mask, density[0])
-    pieces, place = window(payload, far, (slots + 1) // 2 * edge)
+    band, pieces, place = window(payload, far, (slots + 1) // 2 * edge)
     tables = [array for array, _ in pieces]
     layout = [parts for _, parts in pieces]
-    result = pl.pallas_call(
+    anywhere = pl.BlockSpec(memory_space=pl.ANY)
+    _, result = pl.pallas_call(
         functools.partial(purify, reach, edge, layout),
-        out_shape=jax.ShapeDtypeStruct((wide, edge, edge), density.dtype),
-        in_specs=[smem] + [pl.BlockSpec(memory_space=pl.ANY)] * len(tables),
-        out_specs=pl.BlockSpec(memory_space=pl.ANY),
+        out_shape=[pltpu.VMEM(band.shape, band.dtype), jax.ShapeDtypeStruct((wide, edge, edge), density.dtype)],
+        in_specs=[smem] + [anywhere] * len(tables) + [vmem],
+        out_specs=[vmem, anywhere],
+        input_output_aliases={1 + len(tables): 0},
         scratch_shapes=[
-            pltpu.VMEM(((2 * far + 2) * (slots * edge + NOTE), edge), density.dtype),
             pltpu.VMEM(((slots + 1) * edge, wide * edge), density.dtype),
             pltpu.VMEM((2, edge, wide * edge), jnp.float32),
             pltpu.VMEM((wide, edge, edge), density.dtype),
-            pltpu.SemaphoreType.DMA((2 * far + 1,)),
+            pltpu.SemaphoreType.DMA((max(1, sum(len(parts) for parts in layout)),)),
             pltpu.SemaphoreType.DMA((-(-wide // WIDTH),)),
         ],
-        compiler_params=pltpu.CompilerParams(vmem_limit_bytes=56 * 2**20),
+        compiler_params=pltpu.CompilerParams(vmem_limit_bytes=24 * 2**20),
         cost_estimate=pl.CostEstimate(flops=17 * 10**9, bytes_accessed=15 * 2**20, transcendentals=0),
-    )(place, *tables)
+    )(place, *tables, band)
     return result[None]
 
 

time: 112 us -> 114 us (1.018)
  waiting for transfers between devices: 59.3 us -> 51.8 us
  local copies, waits for them, and re-layouts: 3.87 us -> 8.16 us
  Pallas kernels: 30.2 us -> 33.3 us
  other arithmetic: 1.37 us -> 3.29 us
    ppermute x20, waiting for transfers between devices: 59.3 us -> 51.8 us  [swap(): return lax.ppermute(value, AXES, [(i, i ^ mask) for i in range(count)])]
    pallas_call x0 -> x1, Pallas kernels: none -> 6.69 us  [assemble(): pl.pallas_call(body, out_shape=pltpu.VMEM((rows * pitch, edge), kind), in...]
    unnamed x31 -> x15, local copies, waits for them, and re-layouts: 3.7 us -> 6.1 us
    pallas_call x1, Pallas kernels: 28.3 us -> 26 us  [shards(): pl.pallas_call(functools.partial(purify, reach, edge, layout), out_shape=...]
    pallas_call x1, Pallas kernels: 1.94 us -> 0.64 us  [shards(): pl.pallas_call(pack, out_shape=jax.ShapeDtypeStruct((slots * edge + NOTE,...]
  transfers between devices with their start and end apart: 20 -> 20, of which waited for: 12 -> 11; matrix products, arithmetic and copies ran while one was open for 2% -> 5% of each run, Pallas kernels for 0% -> 6%
where the time goes in v12:
time: 114 us
  waiting for transfers between devices  51.8 us (45%)
  Pallas kernels  33.3 us (29%)
  starting transfers between devices  17.4 us (15%)
  local copies, waits for them, and re-layouts  8.16 us (7%)
  other arithmetic  3.29 us (3%)
    ppermute x20, waiting for transfers between devices, swap(): return lax.ppermute(value, AXES, [(i, i ^ mask) for i in range(count)])  51.8 us
    pallas_call x1, Pallas kernels, shards(): pl.pallas_call(functools.partial(purify, reach, edge, layout), out_shape=...  26 us
    ppermute x20, starting transfers between devices, swap(): return lax.ppermute(value, AXES, [(i, i ^ mask) for i in range(count)])  17.4 us
    pallas_call x1, Pallas kernels, assemble(): pl.pallas_call(body, out_shape=pltpu.VMEM((rows * pitch, edge), kind), in...  6.69 us
    unnamed x15, local copies, waits for them, and re-layouts  6.1 us
  transfers between devices with their start and end apart: 20, of which 11 were waited for; matrix products, arithmetic and copies ran while one was open for 5% of the time, Pallas kernels for 6%

profile of v12, /device:TPU:0, one launch (start us, length us, event | category | flops | bytes accessed | tf_op | source)
XLA Modules:
  0.0 114.1 jit_solution(17278102716879124857)
XLA Ops:
  0.0 1.0 copy-done.2
  3.0 3.0 %collective-permute-start = (bf16[1936,128]{1,0:T(8,128)(2,1)S(1)}, bf16[1936,128]{1,0:T(8,128)(2,1)S(1)}, u32[]{:S(2)}, u32[]{:S(2)}) collective-permute-start(bf16[1936,128]{1,0:T(8,128)(2,1)S(1)} %shard_map.55.refs_0_), channel_id=1, source_target_pairs={{0,1},{1,0},{2,3},{3,2},{4,5},{5,4},{6,7},{7,6},{8,9},{9,8},{10,11... | collective-permute-start | bytes 1486856 | tf_op jit(solution)/shard_map/ppermute | solution.py:23
  6.0 1.5 %collective-permute-start.1 = (bf16[1936,128]{1,0:T(8,128)(2,1)S(1)}, bf16[1936,128]{1,0:T(8,128)(2,1)S(1)}, u32[]{:S(2)}, u32[]{:S(2)}) collective-permute-start(bf16[1936,128]{1,0:T(8,128)(2,1)S(1)} %shard_map.55.refs_0_), channel_id=1, source_target_pairs={{0,16},{1,17},{2,18},{3,19},{4,20},{5,21},{6,22},{7,23},{8,24},{9,... | collective-permute-start | bytes 1486856 | tf_op jit(solution)/shard_map/ppermute | solution.py:23
  7.5 3.6 %collective-permute-start.4 = (bf16[1936,128]{1,0:T(8,128)(2,1)S(1)}, bf16[1936,128]{1,0:T(8,128)(2,1)S(1)}, u32[]{:S(2)}, u32[]{:S(2)}) collective-permute-start(bf16[1936,128]{1,0:T(8,128)(2,1)S(1)} %shard_map.55.refs_0_), channel_id=1, source_target_pairs={{0,6},{1,7},{2,4},{3,5},{4,2},{5,3},{6,0},{7,1},{8,14},{9,15},{10,... | collective-permute-start | bytes 1486856 | tf_op jit(solution)/shard_map/ppermute | solution.py:23
  11.6 6.5 %collective-permute-done.refs_1_ = bf16[1936,128]{1,0:T(8,128)(2,1)S(1)} collective-permute-done((bf16[1936,128]{1,0:T(8,128)(2,1)S(1)}, bf16[1936,128]{1,0:T(8,128)(2,1)S(1)}, u32[]{:S(2)}, u32[]{:S(2)}) %collective-permute-start) | collective-permute-done | bytes 495648 | tf_op jit(solution)/shard_map/ppermute | solution.py:23
  18.2 11.2 %collective-permute-done.1.refs_2_ = bf16[1936,128]{1,0:T(8,128)(2,1)S(1)} collective-permute-done((bf16[1936,128]{1,0:T(8,128)(2,1)S(1)}, bf16[1936,128]{1,0:T(8,128)(2,1)S(1)}, u32[]{:S(2)}, u32[]{:S(2)}) %collective-permute-start.1) | collective-permute-done | bytes 495648 | tf_op jit(solution)/shard_map/ppermute | solution.py:23
  29.5 3.0 %collective-permute-done.3.refs_4_ = bf16[1936,128]{1,0:T(8,128)(2,1)S(1)} collective-permute-done((bf16[1936,128]{1,0:T(8,128)(2,1)S(1)}, bf16[1936,128]{1,0:T(8,128)(2,1)S(1)}, u32[]{:S(2)}, u32[]{:S(2)}) %collective-permute-start.3) | collective-permute-done | bytes 495648 | tf_op jit(solution)/shard_map/ppermute | solution.py:23
  34.0 1.7 %collective-permute-start.8 = (bf16[1936,128]{1,0:T(8,128)(2,1)S(1)}, bf16[1936,128]{1,0:T(8,128)(2,1)S(1)}, u32[]{:S(2)}, u32[]{:S(2)}) collective-permute-start(bf16[1936,128]{1,0:T(8,128)(2,1)S(1)} %collective-permute-done.4.refs_5_), channel_id=1, source_target_pairs={{0,2},{1,3},{2,0},{3,1},{4,6},{5,7},{6,4},{7,5},{8,10},{9,11},{10,... | collective-permute-start | bytes 1486856 | tf_op jit(solution)/shard_map/ppermute | solution.py:23
  36.2 19.3 %collective-permute-done.8.refs_11_ = bf16[1936,128]{1,0:T(8,128)(2,1)S(1)} collective-permute-done((bf16[1936,128]{1,0:T(8,128)(2,1)S(1)}, bf16[1936,128]{1,0:T(8,128)(2,1)S(1)}, u32[]{:S(2)}, u32[]{:S(2)}) %collective-permute-start.8) | collective-permute-done | bytes 495648 | tf_op jit(solution)/shard_map/ppermute | solution.py:23
  55.5 1.9 %collective-permute-done.7.refs_9_ = bf16[3872,128]{1,0:T(8,128)(2,1)} collective-permute-done((bf16[3872,128]{1,0:T(8,128)(2,1)S(1)}, bf16[3872,128]{1,0:T(8,128)(2,1)}, u32[]{:S(2)}, u32[]{:S(2)}) %collective-permute-start.7) | collective-permute-done | bytes 991264 | tf_op jit(solution)/shard_map/ppermute | solution.py:23
  57.6 1.6 %copy-done = bf16[11616,128]{1,0:T(8,128)(2,1)} copy-done((bf16[11616,128]{1,0:T(8,128)(2,1)}, bf16[11616,128]{1,0:T(8,128)(2,1)S(1)}, u32[]{:S(2)}) %copy-start) | copy-done | bytes 2973720
  59.2 1.0 slice.7
  60.2 1.0 slice.6
  61.8 0.9 pad_maximum_fusion
  63.2 1.0 pad_maximum_fusion.1
  64.2 1.5 %collective-permute-start.13 = (bf16[2848,128]{1,0:T(8,128)(2,1)}, bf16[2848,128]{1,0:T(8,128)(2,1)}, u32[]{:S(2)}, u32[]{:S(2)}) collective-permute-start(bf16[2848,128]{1,0:T(8,128)(2,1)} %pad_maximum_fusion.1), channel_id=1, source_target_pairs={{0,16},{1,17},{2,18},{3,19},{4,20},{5,21},{6,22},{7,23},{8,24},{9,... | collective-permute-start | bytes 2187272 | tf_op jit(solution)/shard_map/ppermute | solution.py:23
  65.7 1.7 %collective-permute-start.14 = (bf16[1936,128]{1,0:T(8,128)(2,1)S(1)}, bf16[1936,128]{1,0:T(8,128)(2,1)}, u32[]{:S(2)}, u32[]{:S(2)}) collective-permute-start(bf16[1936,128]{1,0:T(8,128)(2,1)S(1)} %collective-permute-done.2.refs_3_), channel_id=1, source_target_pairs={{0,2},{1,3},{2,0},{3,1},{4,6},{5,7},{6,4},{7,5},{8,10},{9,11},{10,... | collective-permute-start | bytes 1486856 | tf_op jit(solution)/shard_map/ppermute | solution.py:23
  68.1 1.8 %copy-done.1 = bf16[11616,128]{1,0:T(8,128)(2,1)S(1)} copy-done((bf16[11616,128]{1,0:T(8,128)(2,1)S(1)}, bf16[11616,128]{1,0:T(8,128)(2,1)}, u32[]{:S(2)}) %copy-start.1) | copy-done | bytes 2973720
  70.0 6.7 %shard_map.56.refs_8_ = bf16[58080,128]{1,0:T(8,128)(2,1)S(1)} custom-call(s32[22]{0:T(128)S(1)} %fusion.1.place, bf16[1936,128]{1,0:T(8,128)(2,1)S(1)} %shard_map.55.refs_0_, bf16[1936,128]{1,0:T(8,128)(2,1)S(1)} %collective-permute-done.refs_1_, bf16[1936,128]{1,0:T(8,128)(2,1)S(1)} %collective-permute-done.1.refs_2_, ...), custom_call_target="tpu_custom_call" | custom-call | bytes 29736960 | tf_op jit(solution)/shard_map/pallas_call | solution.py:147
  76.7 1.8 %collective-permute-done.14.refs_6_ = bf16[1936,128]{1,0:T(8,128)(2,1)} collective-permute-done((bf16[1936,128]{1,0:T(8,128)(2,1)S(1)}, bf16[1936,128]{1,0:T(8,128)(2,1)}, u32[]{:S(2)}, u32[]{:S(2)}) %collective-permute-start.14) | collective-permute-done | bytes 495648 | tf_op jit(solution)/shard_map/ppermute | solution.py:23
  78.5 4.0 %collective-permute-done.13.refs_2_ = bf16[2848,128]{1,0:T(8,128)(2,1)} collective-permute-done((bf16[2848,128]{1,0:T(8,128)(2,1)}, bf16[2848,128]{1,0:T(8,128)(2,1)}, u32[]{:S(2)}, u32[]{:S(2)}) %collective-permute-start.13) | collective-permute-done | bytes 729120 | tf_op jit(solution)/shard_map/ppermute | solution.py:23
  84.2 1.9 %collective-permute-done.17.refs_4_ = bf16[1936,128]{1,0:T(8,128)(2,1)S(1)} collective-permute-done((bf16[1936,128]{1,0:T(8,128)(2,1)S(1)}, bf16[1936,128]{1,0:T(8,128)(2,1)S(1)}, u32[]{:S(2)}, u32[]{:S(2)}) %collective-permute-start.17) | collective-permute-done | bytes 495648 | tf_op jit(solution)/shard_map/ppermute | solution.py:23
  86.1 1.3 %collective-permute-done.18.refs_5_ = bf16[1936,128]{1,0:T(8,128)(2,1)S(1)} collective-permute-done((bf16[1936,128]{1,0:T(8,128)(2,1)}, bf16[1936,128]{1,0:T(8,128)(2,1)S(1)}, u32[]{:S(2)}, u32[]{:S(2)}) %collective-permute-start.18) | collective-permute-done | bytes 495648 | tf_op jit(solution)/shard_map/ppermute | solution.py:23
  88.1 26.0 %shard_map.57 = (bf16[58080,128]{1,0:T(8,128)(2,1)S(1)}, bf16[29,128,128]{2,1,0:T(8,128)(2,1)}) custom-call(s32[12]{0:T(128)S(1)} %fusion.place, bf16[2960,128]{1,0:T(8,128)(2,1)} %collective-permute-done.12.refs_0_, bf16[2960,128]{1,0:T(8,128)(2,1)S(1)} %collective-permute-done.15.refs_1_, ...), custom_call_target="tpu_custom_call", output_to_operand_aliasing={{0}: (9, {})} | custom-call | flops 16999999488 | bytes 15728640 | tf_op jit(solution)/shard_map/pallas_call | solution.py:272
  (41 shorter events, 9.1 us)
Async XLA Ops:
  0.0 1.0 copy-start.2
  1.0 0.7 copy-start.3
  3.0 15.1 %collective-permute-start = (bf16[1936,128]{1,0:T(8,128)(2,1)S(1)}, bf16[1936,128]{1,0:T(8,128)(2,1)S(1)}, u32[]{:S(2)}, u32[]{:S(2)}) collective-permute-start(bf16[1936,128]{1,0:T(8,128)(2,1)S(1)} %shard_map.55.refs_0_), channel_id=1, source_target_pairs={{0,1},{1,0},{2,3},{3,2},{4,5},{5,4},{6,7},{7,6},{8,9},{9,8},{10,11... | collective-permute-start | bytes 1486856 | tf_op jit(solution)/shard_map/ppermute | solution.py:23
  6.0 23.4 %collective-permute-start.1 = (bf16[1936,128]{1,0:T(8,128)(2,1)S(1)}, bf16[1936,128]{1,0:T(8,128)(2,1)S(1)}, u32[]{:S(2)}, u32[]{:S(2)}) collective-permute-start(bf16[1936,128]{1,0:T(8,128)(2,1)S(1)} %shard_map.55.refs_0_), channel_id=1, source_target_pairs={{0,16},{1,17},{2,18},{3,19},{4,20},{5,21},{6,22},{7,23},{8,24},{9,... | collective-permute-start | bytes 1486856 | tf_op jit(solution)/shard_map/ppermute | solution.py:23
  7.5 25.2 %collective-permute-start.4 = (bf16[1936,128]{1,0:T(8,128)(2,1)S(1)}, bf16[1936,128]{1,0:T(8,128)(2,1)S(1)}, u32[]{:S(2)}, u32[]{:S(2)}) collective-permute-start(bf16[1936,128]{1,0:T(8,128)(2,1)S(1)} %shard_map.55.refs_0_), channel_id=1, source_target_pairs={{0,6},{1,7},{2,4},{3,5},{4,2},{5,3},{6,0},{7,1},{8,14},{9,15},{10,... | collective-permute-start | bytes 1486856 | tf_op jit(solution)/shard_map/ppermute | solution.py:23
  11.1 21.5 %collective-permute-start.3 = (bf16[1936,128]{1,0:T(8,128)(2,1)S(1)}, bf16[1936,128]{1,0:T(8,128)(2,1)S(1)}, u32[]{:S(2)}, u32[]{:S(2)}) collective-permute-start(bf16[1936,128]{1,0:T(8,128)(2,1)S(1)} %shard_map.55.refs_0_), channel_id=1, source_target_pairs={{0,2},{1,3},{2,0},{3,1},{4,6},{5,7},{6,4},{7,5},{8,10},{9,11},{10,... | collective-permute-start | bytes 1486856 | tf_op jit(solution)/shard_map/ppermute | solution.py:23
  11.1 18.3 %collective-permute-start.2 = (bf16[1936,128]{1,0:T(8,128)(2,1)S(1)}, bf16[1936,128]{1,0:T(8,128)(2,1)S(1)}, u32[]{:S(2)}, u32[]{:S(2)}) collective-permute-start(bf16[1936,128]{1,0:T(8,128)(2,1)S(1)} %shard_map.55.refs_0_), channel_id=1, source_target_pairs={{0,17},{1,16},{2,19},{3,18},{4,21},{5,20},{6,23},{7,22},{8,25},{9,... | collective-permute-start | bytes 1486856 | tf_op jit(solution)/shard_map/ppermute | solution.py:23
  32.8 24.8 %collective-permute-start.5 = (bf16[11616,128]{1,0:T(8,128)(2,1)S(1)}, bf16[11616,128]{1,0:T(8,128)(2,1)S(1)}, u32[]{:S(2)}, u32[]{:S(2)}) collective-permute-start(bf16[11616,128]{1,0:T(8,128)(2,1)S(1)} %get-tuple-element.30), channel_id=1, source_target_pairs={{0,8},{1,9},{2,10},{3,11},{4,12},{5,13},{6,14},{7,15},{8,0},{9,1},... | collective-permute-start | bytes 8921096 | tf_op jit(solution)/shard_map/ppermute | solution.py:23
  32.9 24.4 %collective-permute-start.7 = (bf16[3872,128]{1,0:T(8,128)(2,1)S(1)}, bf16[3872,128]{1,0:T(8,128)(2,1)}, u32[]{:S(2)}, u32[]{:S(2)}) collective-permute-start(bf16[3872,128]{1,0:T(8,128)(2,1)S(1)} %get-tuple-element.29), channel_id=1, source_target_pairs={{0,16},{1,17},{2,18},{3,19},{4,20},{5,21},{6,22},{7,23},{8,24},{9,... | collective-permute-start | bytes 2973704 | tf_op jit(solution)/shard_map/ppermute | solution.py:23
  33.5 24.1 %collective-permute-start.6 = (bf16[3872,128]{1,0:T(8,128)(2,1)S(1)}, bf16[3872,128]{1,0:T(8,128)(2,1)}, u32[]{:S(2)}, u32[]{:S(2)}) collective-permute-start(bf16[3872,128]{1,0:T(8,128)(2,1)S(1)} %get-tuple-element.29), channel_id=1, source_target_pairs={{0,1},{1,0},{2,3},{3,2},{4,5},{5,4},{6,7},{7,6},{8,9},{9,8},{10,11... | collective-permute-start | bytes 2973704 | tf_op jit(solution)/shard_map/ppermute | solution.py:23
  34.0 21.5 %collective-permute-start.8 = (bf16[1936,128]{1,0:T(8,128)(2,1)S(1)}, bf16[1936,128]{1,0:T(8,128)(2,1)S(1)}, u32[]{:S(2)}, u32[]{:S(2)}) collective-permute-start(bf16[1936,128]{1,0:T(8,128)(2,1)S(1)} %collective-permute-done.4.refs_5_), channel_id=1, source_target_pairs={{0,2},{1,3},{2,0},{3,1},{4,6},{5,7},{6,4},{7,5},{8,10},{9,11},{10,... | collective-permute-start | bytes 1486856 | tf_op jit(solution)/shard_map/ppermute | solution.py:23
  35.7 30.0 %collective-permute-start.11 = (bf16[1936,128]{1,0:T(8,128)(2,1)S(1)}, bf16[1936,128]{1,0:T(8,128)(2,1)}, u32[]{:S(2)}, u32[]{:S(2)}) collective-permute-start(bf16[1936,128]{1,0:T(8,128)(2,1)S(1)} %collective-permute-done.2.refs_3_), channel_id=1, source_target_pairs={{0,4},{1,5},{2,6},{3,7},{4,0},{5,1},{6,2},{7,3},{8,12},{9,13},{10,... | collective-permute-start | bytes 1486856 | tf_op jit(solution)/shard_map/ppermute | solution.py:23
  57.6 1.6 %copy-start = (bf16[11616,128]{1,0:T(8,128)(2,1)}, bf16[11616,128]{1,0:T(8,128)(2,1)S(1)}, u32[]{:S(2)}) copy-start(bf16[11616,128]{1,0:T(8,128)(2,1)S(1)} %collective-permute-done.5.refs_6_) | copy-start | bytes 8921092
  60.2 8.0 %collective-permute-start.9 = (bf16[3872,128]{1,0:T(8,128)(2,1)}, bf16[3872,128]{1,0:T(8,128)(2,1)}, u32[]{:S(2)}, u32[]{:S(2)}) collective-permute-start(bf16[3872,128]{1,0:T(8,128)(2,1)} %collective-permute-done.6.refs_7_), channel_id=1, source_target_pairs={{0,8},{1,9},{2,10},{3,11},{4,12},{5,13},{6,14},{7,15},{8,0},{9,1},... | collective-permute-start | bytes 2973704 | tf_op jit(solution)/shard_map/ppermute | solution.py:23
  61.2 6.9 %collective-permute-start.10 = (bf16[3872,128]{1,0:T(8,128)(2,1)}, bf16[3872,128]{1,0:T(8,128)(2,1)}, u32[]{:S(2)}, u32[]{:S(2)}) collective-permute-start(bf16[3872,128]{1,0:T(8,128)(2,1)} %collective-permute-done.7.refs_9_), channel_id=1, source_target_pairs={{0,8},{1,9},{2,10},{3,11},{4,12},{5,13},{6,14},{7,15},{8,0},{9,1},... | collective-permute-start | bytes 2973704 | tf_op jit(solution)/shard_map/ppermute | solution.py:23
  62.7 19.8 %collective-permute-start.12 = (bf16[2960,128]{1,0:T(8,128)(2,1)}, bf16[2960,128]{1,0:T(8,128)(2,1)}, u32[]{:S(2)}, u32[]{:S(2)}) collective-permute-start(bf16[2960,128]{1,0:T(8,128)(2,1)} %pad_maximum_fusion), channel_id=1, source_target_pairs={{0,1},{1,0},{2,3},{3,2},{4,5},{5,4},{6,7},{7,6},{8,9},{9,8},{10,11... | collective-permute-start | bytes 2273288 | tf_op jit(solution)/shard_map/ppermute | solution.py:23
  64.2 18.3 %collective-permute-start.13 = (bf16[2848,128]{1,0:T(8,128)(2,1)}, bf16[2848,128]{1,0:T(8,128)(2,1)}, u32[]{:S(2)}, u32[]{:S(2)}) collective-permute-start(bf16[2848,128]{1,0:T(8,128)(2,1)} %pad_maximum_fusion.1), channel_id=1, source_target_pairs={{0,16},{1,17},{2,18},{3,19},{4,20},{5,21},{6,22},{7,23},{8,24},{9,... | collective-permute-start | bytes 2187272 | tf_op jit(solution)/shard_map/ppermute | solution.py:23
  65.7 12.8 %collective-permute-start.14 = (bf16[1936,128]{1,0:T(8,128)(2,1)S(1)}, bf16[1936,128]{1,0:T(8,128)(2,1)}, u32[]{:S(2)}, u32[]{:S(2)}) collective-permute-start(bf16[1936,128]{1,0:T(8,128)(2,1)S(1)} %collective-permute-done.2.refs_3_), channel_id=1, source_target_pairs={{0,2},{1,3},{2,0},{3,1},{4,6},{5,7},{6,4},{7,5},{8,10},{9,11},{10,... | collective-permute-start | bytes 1486856 | tf_op jit(solution)/shard_map/ppermute | solution.py:23
  68.1 1.8 %copy-start.1 = (bf16[11616,128]{1,0:T(8,128)(2,1)S(1)}, bf16[11616,128]{1,0:T(8,128)(2,1)}, u32[]{:S(2)}) copy-start(bf16[11616,128]{1,0:T(8,128)(2,1)} %copy-done) | copy-start | bytes 8921092
  82.5 5.6 %collective-permute-start.15 = (bf16[2960,128]{1,0:T(8,128)(2,1)}, bf16[2960,128]{1,0:T(8,128)(2,1)S(1)}, u32[]{:S(2)}, u32[]{:S(2)}) collective-permute-start(bf16[2960,128]{1,0:T(8,128)(2,1)} %collective-permute-done.12.refs_0_), channel_id=1, source_target_pairs={{0,8},{1,9},{2,10},{3,11},{4,12},{5,13},{6,14},{7,15},{8,0},{9,1},... | collective-permute-start | bytes 2273288 | tf_op jit(solution)/shard_map/ppermute | solution.py:23
  82.5 5.6 %collective-permute-start.16 = (bf16[2848,128]{1,0:T(8,128)(2,1)}, bf16[2848,128]{1,0:T(8,128)(2,1)S(1)}, u32[]{:S(2)}, u32[]{:S(2)}) collective-permute-start(bf16[2848,128]{1,0:T(8,128)(2,1)} %collective-permute-done.13.refs_2_), channel_id=1, source_target_pairs={{0,8},{1,9},{2,10},{3,11},{4,12},{5,13},{6,14},{7,15},{8,0},{9,1},... | collective-permute-start | bytes 2187272 | tf_op jit(solution)/shard_map/ppermute | solution.py:23
  83.0 3.2 %collective-permute-start.17 = (bf16[1936,128]{1,0:T(8,128)(2,1)S(1)}, bf16[1936,128]{1,0:T(8,128)(2,1)S(1)}, u32[]{:S(2)}, u32[]{:S(2)}) collective-permute-start(bf16[1936,128]{1,0:T(8,128)(2,1)S(1)} %collective-permute-done.8.refs_11_), channel_id=1, source_target_pairs={{0,8},{1,9},{2,10},{3,11},{4,12},{5,13},{6,14},{7,15},{8,0},{9,1},... | collective-permute-start | bytes 1486856 | tf_op jit(solution)/shard_map/ppermute | solution.py:23
  83.0 4.4 %collective-permute-start.18 = (bf16[1936,128]{1,0:T(8,128)(2,1)}, bf16[1936,128]{1,0:T(8,128)(2,1)S(1)}, u32[]{:S(2)}, u32[]{:S(2)}) collective-permute-start(bf16[1936,128]{1,0:T(8,128)(2,1)} %collective-permute-done.11.refs_12_), channel_id=1, source_target_pairs={{0,8},{1,9},{2,10},{3,11},{4,12},{5,13},{6,14},{7,15},{8,0},{9,1},... | collective-permute-start | bytes 1486856 | tf_op jit(solution)/shard_map/ppermute | solution.py:23
  83.5 4.6 %collective-permute-start.19 = (bf16[1936,128]{1,0:T(8,128)(2,1)}, bf16[1936,128]{1,0:T(8,128)(2,1)S(1)}, u32[]{:S(2)}, u32[]{:S(2)}) collective-permute-start(bf16[1936,128]{1,0:T(8,128)(2,1)} %collective-permute-done.14.refs_6_), channel_id=1, source_target_pairs={{0,8},{1,9},{2,10},{3,11},{4,12},{5,13},{6,14},{7,15},{8,0},{9,1},... | collective-permute-start | bytes 1486856 | tf_op jit(solution)/shard_map/ppermute | solution.py:23
  (1 other events, 0.7 us)

commit v13 on v12

--- a/solution.py
+++ b/solution.py
@@ -2,7 +2,6 @@
 
 import jax
 import jax.numpy as jnp
-import numpy as np
 from jax import lax
 from jax.experimental import pallas as pl
 from jax.experimental.pallas import tpu as pltpu
@@ -63,56 +62,57 @@
     groups, width = lax.axis_size("row"), lax.axis_size("col")
     count = groups * width
     size = payload.shape[0]
-    column = lax.axis_index("col")
-    here = lax.axis_index("row") * width + column
-
-    def places(offsets):
-        return jnp.where(jnp.abs(offsets) <= need, offsets + need, -1)
+
+    def flipped(mask):
+        def offset():
+            here = lax.axis_index("row") * width + lax.axis_index("col")
+            return (((here ^ mask) - here + count // 2) & (count - 1)) - count // 2
+
+        return offset
+
+    def shifted(place):
+        return lambda: place - lax.axis_index("col")
 
     if (groups, width) == (4, 8):
 
-        def split(found):
-            masks = np.array([mask for _, parts in found for mask, _, _ in parts])
-            device = np.arange(count)[:, None]
-            offsets = ((device ^ masks) - device + count // 2) % count - count // 2
-            pieces = [(array, [(start, rows) for _, start, rows in parts]) for array, parts in found]
-            return pieces, places(jnp.asarray(offsets.astype(np.int32))[here])
-
-        band, late = cube(payload, count, cut, lambda found: assemble(*split(found), size, need))
-        return band, *split(late)
-    pieces, offsets = [], []
+        def pieces(found):
+            return [(array, [(start, rows, flipped(mask)) for mask, start, rows in parts]) for array, parts in found]
+
+        band, late = cube(payload, count, cut, lambda found: assemble(pieces(found), size, need))
+        return band, pieces(late)
+
+    def piece(array, first):
+        return array, [(0, size, shifted(first + j)) for j in range(array.shape[0] // size)]
+
     block = lax.all_gather(payload, "col", axis=0, tiled=True)
-    pieces.append((block, [(0, size)] * width))
-    offsets.append(jnp.arange(width, dtype=jnp.int32) - column)
+    pieces = [piece(block, 0)]
     for hop in range(1, -(-need // width) + 1):
         part = min(width, need - (hop - 1) * width)
         up = [(g, (g + hop) % groups) for g in range(groups)]
         down = [(g, (g - hop) % groups) for g in range(groups)]
-        steps = jnp.arange(part, dtype=jnp.int32) - column
-        pieces.append((lax.ppermute(block[(width - part) * size :], "row", up), [(0, size)] * part))
-        offsets.append(steps - (hop - 1) * width - part)
-        pieces.append((lax.ppermute(block[: part * size], "row", down), [(0, size)] * part))
-        offsets.append(steps + hop * width)
-    band = assemble(pieces, places(jnp.concatenate(offsets).astype(jnp.int32)), size, need)
-    return band, [], jnp.zeros((1,), jnp.int32)
-
-
-def row_copies(layout, place, tables, band, arrived, pitch):
+        pieces.append(piece(lax.ppermute(block[(width - part) * size :], "row", up), (1 - hop) * width - part))
+        pieces.append(piece(lax.ppermute(block[: part * size], "row", down), hop * width))
+    return assemble(pieces, size, need), []
+
+
+def row_copies(layout, need, tables, band, arrived, pitch):
     copies = []
     for table, parts in zip(tables, layout):
         begin = 0
-        for start, size in parts:
-            k = place[len(copies)]
+        for start, size, offset in parts:
+            k = offset() + need
+            wanted = (k >= 0) & (k <= 2 * need)
+            row = jnp.where(wanted, k, 0)
             copy = pltpu.make_async_copy(
                 table.at[pl.ds(begin, size)],
-                band.at[pl.ds(pl.multiple_of(jnp.maximum(k, 0) * pitch + start, NOTE), size)],
+                band.at[pl.ds(pl.multiple_of(row * pitch + start, NOTE), size)],
                 arrived.at[len(copies)],
             )
-            copies.append((k, copy))
+            copies.append((wanted, copy))
             begin += size
-    for k, copy in copies:
-
-        @pl.when(k >= 0)
+    for wanted, copy in copies:
+
+        @pl.when(wanted)
         def _(copy=copy):
             copy.start()
 
@@ -120,22 +120,22 @@
 
 
 def wait_all(copies):
-    for k, copy in copies:
-
-        @pl.when(k >= 0)
+    for wanted, copy in copies:
+
+        @pl.when(wanted)
         def _(copy=copy):
             copy.wait()
 
 
-def assemble(pieces, place, pitch, need):
+def assemble(pieces, pitch, need):
     tables = [array for array, _ in pieces]
     layout = [parts for _, parts in pieces]
     kind, edge = tables[0].dtype, tables[0].shape[1]
     rows = 2 * need + 2
 
-    def body(place, *refs):
+    def body(*refs):
         band, arrived = refs[len(tables) :]
-        copies = row_copies(layout, place, refs[: len(tables)], band, arrived, pitch)
+        copies = row_copies(layout, need, refs[: len(tables)], band, arrived, pitch)
 
         def clear(s, carry):
             band[pl.ds(pl.multiple_of((rows - 1) * pitch + s * NOTE, NOTE), NOTE), :] = jnp.zeros((NOTE, edge), kind)
@@ -147,22 +147,22 @@
     return pl.pallas_call(
         body,
         out_shape=pltpu.VMEM((rows * pitch, edge), kind),
-        in_specs=[pl.BlockSpec(memory_space=pltpu.SMEM)] + [pl.BlockSpec(memory_space=pl.ANY)] * len(tables),
+        in_specs=[pl.BlockSpec(memory_space=pl.ANY)] * len(tables),
         out_specs=pl.BlockSpec(memory_space=pltpu.VMEM),
         scratch_shapes=[pltpu.SemaphoreType.DMA((sum(len(parts) for parts in layout),))],
         compiler_params=pltpu.CompilerParams(vmem_limit_bytes=2 * 2**20),
         cost_estimate=pl.CostEstimate(flops=0, bytes_accessed=rows * pitch * edge * 4, transcendentals=0),
-    )(place, *tables)
-
-
-def purify(reach, edge, layout, place, *refs):
+    )(*tables)
+
+
+def purify(reach, edge, layout, *refs):
     count = len(layout)
     tables, (_, band, out, square, own, result, arrived, left_out) = refs[:count], refs[count:]
     far = 2 * reach
     slots, wide = 2 * reach + 1, 4 * reach + 1
     pitch = slots * edge + NOTE
     kind = band.dtype
-    copies = row_copies(layout, place, tables, band, arrived, pitch)
+    copies = row_copies(layout, far, tables, band, arrived, pitch)
     wait_all(copies)
 
     zero = jnp.zeros((edge, edge), kind)
@@ -265,16 +265,16 @@
         out_specs=vmem,
         compiler_params=pltpu.CompilerParams(vmem_limit_bytes=4 * 2**20),
     )(pattern, filter_mask, density[0])
-    band, pieces, place = window(payload, far, (slots + 1) // 2 * edge)
+    band, pieces = window(payload, far, (slots + 1) // 2 * edge)
     tables = [array for array, _ in pieces]
     layout = [parts for _, parts in pieces]
     anywhere = pl.BlockSpec(memory_space=pl.ANY)
     _, result = pl.pallas_call(
         functools.partial(purify, reach, edge, layout),
         out_shape=[pltpu.VMEM(band.shape, band.dtype), jax.ShapeDtypeStruct((wide, edge, edge), density.dtype)],
-        in_specs=[smem] + [anywhere] * len(tables) + [vmem],
+        in_specs=[anywhere] * len(tables) + [vmem],
         out_specs=[vmem, anywhere],
-        input_output_aliases={1 + len(tables): 0},
+        input_output_aliases={len(tables): 0},
         scratch_shapes=[
             pltpu.VMEM(((slots + 1) * edge, wide * edge), density.dtype),
             pltpu.VMEM((2, edge, wide * edge), jnp.float32),
@@ -284,7 +284,7 @@
         ],
         compiler_params=pltpu.CompilerParams(vmem_limit_bytes=24 * 2**20),
         cost_estimate=pl.CostEstimate(flops=17 * 10**9, bytes_accessed=15 * 2**20, transcendentals=0),
-    )(place, *tables, band)
+    )(*tables, band)
     return result[None]
 
 

time: 114 us -> 109 us (0.956)
  local copies, waits for them, and re-layouts: 8.16 us -> 2.83 us
  other arithmetic: 3.29 us -> 0.1 us
  waiting for transfers between devices: 51.8 us -> 53.3 us
  Pallas kernels: 33.3 us -> 34.7 us
    unnamed x15 -> x11, local copies, waits for them, and re-layouts: 6.1 us -> 2.67 us
    ppermute x20, waiting for transfers between devices: 51.8 us -> 53.3 us  [swap(): return lax.ppermute(value, AXES, [(i, i ^ mask) for i in range(count)])]
    select_n x2 -> x0, other arithmetic: 1.39 us -> none  [places(): return jnp.where(jnp.abs(offsets) <= need, offsets + need, -1)]
    pallas_call x1, Pallas kernels: 6.69 us -> 8.02 us  [assemble(): pl.pallas_call(body, out_shape=pltpu.VMEM((rows * pitch, edge), kind), in...]
  transfers between devices with their start and end apart: 20 -> 20, of which waited for: 11 -> 12; matrix products, arithmetic and copies ran while one was open for 5% -> 0% of each run, Pallas kernels for 6% -> 7%
where the time goes in v13:
time: 109 us
  waiting for transfers between devices  53.3 us (49%)
  Pallas kernels  34.7 us (32%)
  starting transfers between devices  17.5 us (16%)
  local copies, waits for them, and re-layouts  2.83 us (3%)
    ppermute x20, waiting for transfers between devices, swap(): return lax.ppermute(value, AXES, [(i, i ^ mask) for i in range(count)])  53.3 us
    pallas_call x1, Pallas kernels, shards(): pl.pallas_call(functools.partial(purify, reach, edge, layout), out_shape=...  26.1 us
    ppermute x20, starting transfers between devices, swap(): return lax.ppermute(value, AXES, [(i, i ^ mask) for i in range(count)])  17.5 us
    pallas_call x1, Pallas kernels, assemble(): pl.pallas_call(body, out_shape=pltpu.VMEM((rows * pitch, edge), kind), in...  8.02 us
    unnamed x11, local copies, waits for them, and re-layouts  2.67 us
  transfers between devices with their start and end apart: 20, of which 12 were waited for; matrix products, arithmetic and copies ran while one was open for 0% of the time, Pallas kernels for 7%

profile of v13, /device:TPU:0, one launch (start us, length us, event | category | flops | bytes accessed | tf_op | source)
XLA Modules:
  0.0 108.6 jit_solution(10416154258037124322)
XLA Ops:
  0.0 1.0 copy-done
  1.0 0.7 copy-done.1
  1.7 0.7 copy-done.2
  2.3 0.6 shard_map.37.refs_0_
  3.0 3.0 %collective-permute-start = (bf16[1936,128]{1,0:T(8,128)(2,1)S(1)}, bf16[1936,128]{1,0:T(8,128)(2,1)S(1)}, u32[]{:S(2)}, u32[]{:S(2)}) collective-permute-start(bf16[1936,128]{1,0:T(8,128)(2,1)S(1)} %shard_map.37.refs_0_), channel_id=1, source_target_pairs={{0,1},{1,0},{2,3},{3,2},{4,5},{5,4},{6,7},{7,6},{8,9},{9,8},{10,11... | collective-permute-start | bytes 1486856 | tf_op jit(solution)/shard_map/ppermute | solution.py:22
  6.0 1.5 %collective-permute-start.1 = (bf16[1936,128]{1,0:T(8,128)(2,1)S(1)}, bf16[1936,128]{1,0:T(8,128)(2,1)S(1)}, u32[]{:S(2)}, u32[]{:S(2)}) collective-permute-start(bf16[1936,128]{1,0:T(8,128)(2,1)S(1)} %shard_map.37.refs_0_), channel_id=1, source_target_pairs={{0,16},{1,17},{2,18},{3,19},{4,20},{5,21},{6,22},{7,23},{8,24},{9,... | collective-permute-start | bytes 1486856 | tf_op jit(solution)/shard_map/ppermute | solution.py:22
  7.5 3.6 %collective-permute-start.4 = (bf16[1936,128]{1,0:T(8,128)(2,1)S(1)}, bf16[1936,128]{1,0:T(8,128)(2,1)S(1)}, u32[]{:S(2)}, u32[]{:S(2)}) collective-permute-start(bf16[1936,128]{1,0:T(8,128)(2,1)S(1)} %shard_map.37.refs_0_), channel_id=1, source_target_pairs={{0,6},{1,7},{2,4},{3,5},{4,2},{5,3},{6,0},{7,1},{8,14},{9,15},{10,... | collective-permute-start | bytes 1486856 | tf_op jit(solution)/shard_map/ppermute | solution.py:22
  11.6 6.5 %collective-permute-done.refs_1_ = bf16[1936,128]{1,0:T(8,128)(2,1)S(1)} collective-permute-done((bf16[1936,128]{1,0:T(8,128)(2,1)S(1)}, bf16[1936,128]{1,0:T(8,128)(2,1)S(1)}, u32[]{:S(2)}, u32[]{:S(2)}) %collective-permute-start) | collective-permute-done | bytes 495648 | tf_op jit(solution)/shard_map/ppermute | solution.py:22
  18.2 11.2 %collective-permute-done.1.refs_2_ = bf16[1936,128]{1,0:T(8,128)(2,1)S(1)} collective-permute-done((bf16[1936,128]{1,0:T(8,128)(2,1)S(1)}, bf16[1936,128]{1,0:T(8,128)(2,1)S(1)}, u32[]{:S(2)}, u32[]{:S(2)}) %collective-permute-start.1) | collective-permute-done | bytes 495648 | tf_op jit(solution)/shard_map/ppermute | solution.py:22
  29.5 3.0 %collective-permute-done.3.refs_4_ = bf16[1936,128]{1,0:T(8,128)(2,1)S(1)} collective-permute-done((bf16[1936,128]{1,0:T(8,128)(2,1)S(1)}, bf16[1936,128]{1,0:T(8,128)(2,1)S(1)}, u32[]{:S(2)}, u32[]{:S(2)}) %collective-permute-start.3) | collective-permute-done | bytes 495648 | tf_op jit(solution)/shard_map/ppermute | solution.py:22
  32.9 0.6 collective-permute-start.7
  34.0 1.7 %collective-permute-start.8 = (bf16[1936,128]{1,0:T(8,128)(2,1)S(1)}, bf16[1936,128]{1,0:T(8,128)(2,1)S(1)}, u32[]{:S(2)}, u32[]{:S(2)}) collective-permute-start(bf16[1936,128]{1,0:T(8,128)(2,1)S(1)} %collective-permute-done.4.refs_5_), channel_id=1, source_target_pairs={{0,2},{1,3},{2,0},{3,1},{4,6},{5,7},{6,4},{7,5},{8,10},{9,11},{10,... | collective-permute-start | bytes 1486856 | tf_op jit(solution)/shard_map/ppermute | solution.py:22
  36.2 19.3 %collective-permute-done.8.refs_11_ = bf16[1936,128]{1,0:T(8,128)(2,1)S(1)} collective-permute-done((bf16[1936,128]{1,0:T(8,128)(2,1)S(1)}, bf16[1936,128]{1,0:T(8,128)(2,1)S(1)}, u32[]{:S(2)}, u32[]{:S(2)}) %collective-permute-start.8) | collective-permute-done | bytes 495648 | tf_op jit(solution)/shard_map/ppermute | solution.py:22
  55.5 1.8 %collective-permute-done.7.refs_9_ = bf16[3872,128]{1,0:T(8,128)(2,1)S(1)} collective-permute-done((bf16[3872,128]{1,0:T(8,128)(2,1)S(1)}, bf16[3872,128]{1,0:T(8,128)(2,1)S(1)}, u32[]{:S(2)}, u32[]{:S(2)}) %collective-permute-start.7) | collective-permute-done | bytes 991264 | tf_op jit(solution)/shard_map/ppermute | solution.py:22
  58.2 0.6 collective-permute-start.12
  58.9 1.6 %collective-permute-start.13 = (bf16[2848,128]{1,0:T(8,128)(2,1)S(1)}, bf16[2848,128]{1,0:T(8,128)(2,1)S(1)}, u32[]{:S(2)}, u32[]{:S(2)}) collective-permute-start(bf16[2848,128]{1,0:T(8,128)(2,1)S(1)} %pad_maximum_fusion.1), channel_id=1, source_target_pairs={{0,16},{1,17},{2,18},{3,19},{4,20},{5,21},{6,22},{7,23},{8,24},{9,... | collective-permute-start | bytes 2187272 | tf_op jit(solution)/shard_map/ppermute | solution.py:22
  60.5 1.7 %collective-permute-start.14 = (bf16[1936,128]{1,0:T(8,128)(2,1)S(1)}, bf16[1936,128]{1,0:T(8,128)(2,1)S(1)}, u32[]{:S(2)}, u32[]{:S(2)}) collective-permute-start(bf16[1936,128]{1,0:T(8,128)(2,1)S(1)} %collective-permute-done.2.refs_3_), channel_id=1, source_target_pairs={{0,2},{1,3},{2,0},{3,1},{4,6},{5,7},{6,4},{7,5},{8,10},{9,11},{10,... | collective-permute-start | bytes 1486856 | tf_op jit(solution)/shard_map/ppermute | solution.py:22
  62.2 8.0 %shard_map.38.refs_8_ = bf16[58080,128]{1,0:T(8,128)(2,1)S(1)} custom-call(bf16[1936,128]{1,0:T(8,128)(2,1)S(1)} %shard_map.37.refs_0_, bf16[1936,128]{1,0:T(8,128)(2,1)S(1)} %collective-permute-done.refs_1_, bf16[1936,128]{1,0:T(8,128)(2,1)S(1)} %collective-permute-done.1.refs_2_, bf16[1936,128]{1,0:T(8,128)(2,1)S(1)} %collective-permute-done.2.refs_3_, ...), custom_call_target="tpu_custom_call" | custom-call | bytes 29736960 | tf_op jit(solution)/shard_map/pallas_call | solution.py:147
  70.2 3.0 %collective-permute-done.14.refs_6_ = bf16[1936,128]{1,0:T(8,128)(2,1)S(1)} collective-permute-done((bf16[1936,128]{1,0:T(8,128)(2,1)S(1)}, bf16[1936,128]{1,0:T(8,128)(2,1)S(1)}, u32[]{:S(2)}, u32[]{:S(2)}) %collective-permute-start.14) | collective-permute-done | bytes 495648 | tf_op jit(solution)/shard_map/ppermute | solution.py:22
  73.1 3.8 %collective-permute-done.13.refs_2_ = bf16[2848,128]{1,0:T(8,128)(2,1)S(1)} collective-permute-done((bf16[2848,128]{1,0:T(8,128)(2,1)S(1)}, bf16[2848,128]{1,0:T(8,128)(2,1)S(1)}, u32[]{:S(2)}, u32[]{:S(2)}) %collective-permute-start.13) | collective-permute-done | bytes 729120 | tf_op jit(solution)/shard_map/ppermute | solution.py:22
  78.2 3.0 %collective-permute-done.17.refs_4_ = bf16[1936,128]{1,0:T(8,128)(2,1)S(1)} collective-permute-done((bf16[1936,128]{1,0:T(8,128)(2,1)S(1)}, bf16[1936,128]{1,0:T(8,128)(2,1)S(1)}, u32[]{:S(2)}, u32[]{:S(2)}) %collective-permute-start.17) | collective-permute-done | bytes 495648 | tf_op jit(solution)/shard_map/ppermute | solution.py:22
  81.1 0.7 collective-permute-done.18.refs_5_
  81.9 0.7 collective-permute-done.19.refs_7_
  82.6 26.1 %shard_map.39 = (bf16[58080,128]{1,0:T(8,128)(2,1)S(1)}, bf16[29,128,128]{2,1,0:T(8,128)(2,1)}) custom-call(bf16[2960,128]{1,0:T(8,128)(2,1)S(1)} %collective-permute-done.12.refs_0_, bf16[2960,128]{1,0:T(8,128)(2,1)S(1)} %collective-permute-done.15.refs_1_, bf16[2848,128]{1,0:T(8,128)(2,1)S(1)} %collective-permute-done.13.refs_2_, ...), custom_call_target="tpu_custom_call", output_to_operand_aliasing={{0}: (8, {})} | custom-call | flops 16999999488 | bytes 15728640 | tf_op jit(solution)/shard_map/pallas_call | solution.py:272
  (35 shorter events, 4.4 us)
Async XLA Ops:
  0.0 1.0 copy-start
  1.0 0.7 copy-start.1
  1.7 0.7 copy-start.2
  3.0 15.1 %collective-permute-start = (bf16[1936,128]{1,0:T(8,128)(2,1)S(1)}, bf16[1936,128]{1,0:T(8,128)(2,1)S(1)}, u32[]{:S(2)}, u32[]{:S(2)}) collective-permute-start(bf16[1936,128]{1,0:T(8,128)(2,1)S(1)} %shard_map.37.refs_0_), channel_id=1, source_target_pairs={{0,1},{1,0},{2,3},{3,2},{4,5},{5,4},{6,7},{7,6},{8,9},{9,8},{10,11... | collective-permute-start | bytes 1486856 | tf_op jit(solution)/shard_map/ppermute | solution.py:22
  6.0 23.4 %collective-permute-start.1 = (bf16[1936,128]{1,0:T(8,128)(2,1)S(1)}, bf16[1936,128]{1,0:T(8,128)(2,1)S(1)}, u32[]{:S(2)}, u32[]{:S(2)}) collective-permute-start(bf16[1936,128]{1,0:T(8,128)(2,1)S(1)} %shard_map.37.refs_0_), channel_id=1, source_target_pairs={{0,16},{1,17},{2,18},{3,19},{4,20},{5,21},{6,22},{7,23},{8,24},{9,... | collective-permute-start | bytes 1486856 | tf_op jit(solution)/shard_map/ppermute | solution.py:22
  7.5 25.2 %collective-permute-start.4 = (bf16[1936,128]{1,0:T(8,128)(2,1)S(1)}, bf16[1936,128]{1,0:T(8,128)(2,1)S(1)}, u32[]{:S(2)}, u32[]{:S(2)}) collective-permute-start(bf16[1936,128]{1,0:T(8,128)(2,1)S(1)} %shard_map.37.refs_0_), channel_id=1, source_target_pairs={{0,6},{1,7},{2,4},{3,5},{4,2},{5,3},{6,0},{7,1},{8,14},{9,15},{10,... | collective-permute-start | bytes 1486856 | tf_op jit(solution)/shard_map/ppermute | solution.py:22
  11.1 21.5 %collective-permute-start.3 = (bf16[1936,128]{1,0:T(8,128)(2,1)S(1)}, bf16[1936,128]{1,0:T(8,128)(2,1)S(1)}, u32[]{:S(2)}, u32[]{:S(2)}) collective-permute-start(bf16[1936,128]{1,0:T(8,128)(2,1)S(1)} %shard_map.37.refs_0_), channel_id=1, source_target_pairs={{0,2},{1,3},{2,0},{3,1},{4,6},{5,7},{6,4},{7,5},{8,10},{9,11},{10,... | collective-permute-start | bytes 1486856 | tf_op jit(solution)/shard_map/ppermute | solution.py:22
  11.1 18.3 %collective-permute-start.2 = (bf16[1936,128]{1,0:T(8,128)(2,1)S(1)}, bf16[1936,128]{1,0:T(8,128)(2,1)S(1)}, u32[]{:S(2)}, u32[]{:S(2)}) collective-permute-start(bf16[1936,128]{1,0:T(8,128)(2,1)S(1)} %shard_map.37.refs_0_), channel_id=1, source_target_pairs={{0,17},{1,16},{2,19},{3,18},{4,21},{5,20},{6,23},{7,22},{8,25},{9,... | collective-permute-start | bytes 1486856 | tf_op jit(solution)/shard_map/ppermute | solution.py:22
  32.8 24.7 %collective-permute-start.5 = (bf16[11616,128]{1,0:T(8,128)(2,1)S(1)}, bf16[11616,128]{1,0:T(8,128)(2,1)S(1)}, u32[]{:S(2)}, u32[]{:S(2)}) collective-permute-start(bf16[11616,128]{1,0:T(8,128)(2,1)S(1)} %get-tuple-element.30), channel_id=1, source_target_pairs={{0,8},{1,9},{2,10},{3,11},{4,12},{5,13},{6,14},{7,15},{8,0},{9,1},... | collective-permute-start | bytes 8921096 | tf_op jit(solution)/shard_map/ppermute | solution.py:22
  32.9 24.3 %collective-permute-start.7 = (bf16[3872,128]{1,0:T(8,128)(2,1)S(1)}, bf16[3872,128]{1,0:T(8,128)(2,1)S(1)}, u32[]{:S(2)}, u32[]{:S(2)}) collective-permute-start(bf16[3872,128]{1,0:T(8,128)(2,1)S(1)} %get-tuple-element.29), channel_id=1, source_target_pairs={{0,16},{1,17},{2,18},{3,19},{4,20},{5,21},{6,22},{7,23},{8,24},{9,... | collective-permute-start | bytes 2973704 | tf_op jit(solution)/shard_map/ppermute | solution.py:22
  33.5 24.0 %collective-permute-start.6 = (bf16[3872,128]{1,0:T(8,128)(2,1)S(1)}, bf16[3872,128]{1,0:T(8,128)(2,1)S(1)}, u32[]{:S(2)}, u32[]{:S(2)}) collective-permute-start(bf16[3872,128]{1,0:T(8,128)(2,1)S(1)} %get-tuple-element.29), channel_id=1, source_target_pairs={{0,1},{1,0},{2,3},{3,2},{4,5},{5,4},{6,7},{7,6},{8,9},{9,8},{10,11... | collective-permute-start | bytes 2973704 | tf_op jit(solution)/shard_map/ppermute | solution.py:22
  34.0 21.5 %collective-permute-start.8 = (bf16[1936,128]{1,0:T(8,128)(2,1)S(1)}, bf16[1936,128]{1,0:T(8,128)(2,1)S(1)}, u32[]{:S(2)}, u32[]{:S(2)}) collective-permute-start(bf16[1936,128]{1,0:T(8,128)(2,1)S(1)} %collective-permute-done.4.refs_5_), channel_id=1, source_target_pairs={{0,2},{1,3},{2,0},{3,1},{4,6},{5,7},{6,4},{7,5},{8,10},{9,11},{10,... | collective-permute-start | bytes 1486856 | tf_op jit(solution)/shard_map/ppermute | solution.py:22
  35.7 24.8 %collective-permute-start.11 = (bf16[1936,128]{1,0:T(8,128)(2,1)S(1)}, bf16[1936,128]{1,0:T(8,128)(2,1)S(1)}, u32[]{:S(2)}, u32[]{:S(2)}) collective-permute-start(bf16[1936,128]{1,0:T(8,128)(2,1)S(1)} %collective-permute-done.2.refs_3_), channel_id=1, source_target_pairs={{0,4},{1,5},{2,6},{3,7},{4,0},{5,1},{6,2},{7,3},{8,12},{9,13},{10,... | collective-permute-start | bytes 1486856 | tf_op jit(solution)/shard_map/ppermute | solution.py:22
  57.5 4.6 %collective-permute-start.9 = (bf16[3872,128]{1,0:T(8,128)(2,1)S(1)}, bf16[3872,128]{1,0:T(8,128)(2,1)S(1)}, u32[]{:S(2)}, u32[]{:S(2)}) collective-permute-start(bf16[3872,128]{1,0:T(8,128)(2,1)S(1)} %collective-permute-done.6.refs_7_), channel_id=1, source_target_pairs={{0,8},{1,9},{2,10},{3,11},{4,12},{5,13},{6,14},{7,15},{8,0},{9,1},... | collective-permute-start | bytes 2973704 | tf_op jit(solution)/shard_map/ppermute | solution.py:22
  57.6 4.5 %collective-permute-start.10 = (bf16[3872,128]{1,0:T(8,128)(2,1)S(1)}, bf16[3872,128]{1,0:T(8,128)(2,1)S(1)}, u32[]{:S(2)}, u32[]{:S(2)}) collective-permute-start(bf16[3872,128]{1,0:T(8,128)(2,1)S(1)} %collective-permute-done.7.refs_9_), channel_id=1, source_target_pairs={{0,8},{1,9},{2,10},{3,11},{4,12},{5,13},{6,14},{7,15},{8,0},{9,1},... | collective-permute-start | bytes 2973704 | tf_op jit(solution)/shard_map/ppermute | solution.py:22
  58.2 18.9 %collective-permute-start.12 = (bf16[2960,128]{1,0:T(8,128)(2,1)S(1)}, bf16[2960,128]{1,0:T(8,128)(2,1)S(1)}, u32[]{:S(2)}, u32[]{:S(2)}) collective-permute-start(bf16[2960,128]{1,0:T(8,128)(2,1)S(1)} %pad_maximum_fusion), channel_id=1, source_target_pairs={{0,1},{1,0},{2,3},{3,2},{4,5},{5,4},{6,7},{7,6},{8,9},{9,8},{10,11... | collective-permute-start | bytes 2273288 | tf_op jit(solution)/shard_map/ppermute | solution.py:22
  58.9 18.0 %collective-permute-start.13 = (bf16[2848,128]{1,0:T(8,128)(2,1)S(1)}, bf16[2848,128]{1,0:T(8,128)(2,1)S(1)}, u32[]{:S(2)}, u32[]{:S(2)}) collective-permute-start(bf16[2848,128]{1,0:T(8,128)(2,1)S(1)} %pad_maximum_fusion.1), channel_id=1, source_target_pairs={{0,16},{1,17},{2,18},{3,19},{4,20},{5,21},{6,22},{7,23},{8,24},{9,... | collective-permute-start | bytes 2187272 | tf_op jit(solution)/shard_map/ppermute | solution.py:22
  60.5 12.7 %collective-permute-start.14 = (bf16[1936,128]{1,0:T(8,128)(2,1)S(1)}, bf16[1936,128]{1,0:T(8,128)(2,1)S(1)}, u32[]{:S(2)}, u32[]{:S(2)}) collective-permute-start(bf16[1936,128]{1,0:T(8,128)(2,1)S(1)} %collective-permute-done.2.refs_3_), channel_id=1, source_target_pairs={{0,2},{1,3},{2,0},{3,1},{4,6},{5,7},{6,4},{7,5},{8,10},{9,11},{10,... | collective-permute-start | bytes 1486856 | tf_op jit(solution)/shard_map/ppermute | solution.py:22
  77.1 5.4 %collective-permute-start.15 = (bf16[2960,128]{1,0:T(8,128)(2,1)S(1)}, bf16[2960,128]{1,0:T(8,128)(2,1)S(1)}, u32[]{:S(2)}, u32[]{:S(2)}) collective-permute-start(bf16[2960,128]{1,0:T(8,128)(2,1)S(1)} %collective-permute-done.12.refs_0_), channel_id=1, source_target_pairs={{0,8},{1,9},{2,10},{3,11},{4,12},{5,13},{6,14},{7,15},{8,0},{9,1},... | collective-permute-start | bytes 2273288 | tf_op jit(solution)/shard_map/ppermute | solution.py:22
  77.2 5.4 %collective-permute-start.16 = (bf16[2848,128]{1,0:T(8,128)(2,1)S(1)}, bf16[2848,128]{1,0:T(8,128)(2,1)S(1)}, u32[]{:S(2)}, u32[]{:S(2)}) collective-permute-start(bf16[2848,128]{1,0:T(8,128)(2,1)S(1)} %collective-permute-done.13.refs_2_), channel_id=1, source_target_pairs={{0,8},{1,9},{2,10},{3,11},{4,12},{5,13},{6,14},{7,15},{8,0},{9,1},... | collective-permute-start | bytes 2187272 | tf_op jit(solution)/shard_map/ppermute | solution.py:22
  77.7 3.5 %collective-permute-start.17 = (bf16[1936,128]{1,0:T(8,128)(2,1)S(1)}, bf16[1936,128]{1,0:T(8,128)(2,1)S(1)}, u32[]{:S(2)}, u32[]{:S(2)}) collective-permute-start(bf16[1936,128]{1,0:T(8,128)(2,1)S(1)} %collective-permute-done.8.refs_11_), channel_id=1, source_target_pairs={{0,8},{1,9},{2,10},{3,11},{4,12},{5,13},{6,14},{7,15},{8,0},{9,1},... | collective-permute-start | bytes 1486856 | tf_op jit(solution)/shard_map/ppermute | solution.py:22
  77.7 4.2 %collective-permute-start.18 = (bf16[1936,128]{1,0:T(8,128)(2,1)S(1)}, bf16[1936,128]{1,0:T(8,128)(2,1)S(1)}, u32[]{:S(2)}, u32[]{:S(2)}) collective-permute-start(bf16[1936,128]{1,0:T(8,128)(2,1)S(1)} %collective-permute-done.11.refs_12_), channel_id=1, source_target_pairs={{0,8},{1,9},{2,10},{3,11},{4,12},{5,13},{6,14},{7,15},{8,0},{9,1},... | collective-permute-start | bytes 1486856 | tf_op jit(solution)/shard_map/ppermute | solution.py:22
  78.2 4.4 %collective-permute-start.19 = (bf16[1936,128]{1,0:T(8,128)(2,1)S(1)}, bf16[1936,128]{1,0:T(8,128)(2,1)S(1)}, u32[]{:S(2)}, u32[]{:S(2)}) collective-permute-start(bf16[1936,128]{1,0:T(8,128)(2,1)S(1)} %collective-permute-done.14.refs_6_), channel_id=1, source_target_pairs={{0,8},{1,9},{2,10},{3,11},{4,12},{5,13},{6,14},{7,15},{8,0},{9,1},... | collective-permute-start | bytes 1486856 | tf_op jit(solution)/shard_map/ppermute | solution.py:22

commit v14 on v13

--- a/solution.py
+++ b/solution.py
@@ -10,6 +10,7 @@
 NOTE = 16
 GROUP = 2
 WIDTH = 4
+PIECES = 3
 AXES = ("row", "col")
 
 
@@ -131,17 +132,11 @@
     tables = [array for array, _ in pieces]
     layout = [parts for _, parts in pieces]
     kind, edge = tables[0].dtype, tables[0].shape[1]
-    rows = 2 * need + 2
+    rows = 2 * need + 1
 
     def body(*refs):
         band, arrived = refs[len(tables) :]
         copies = row_copies(layout, need, refs[: len(tables)], band, arrived, pitch)
-
-        def clear(s, carry):
-            band[pl.ds(pl.multiple_of((rows - 1) * pitch + s * NOTE, NOTE), NOTE), :] = jnp.zeros((NOTE, edge), kind)
-            return carry
-
-        lax.fori_loop(0, pitch // NOTE, clear, 0)
         wait_all(copies)
 
     return pl.pallas_call(
@@ -167,14 +162,17 @@
 
     zero = jnp.zeros((edge, edge), kind)
 
+    def from_row(first, n):
+        return pl.ds(first if isinstance(first, int) else pl.multiple_of(first, NOTE), n)
+
     def block(k, s):
-        return band[pl.ds(pl.multiple_of(k * pitch + s * edge, NOTE), edge), :]
+        return band[from_row(k * pitch + s * edge, edge), :]
 
     spots = -(-wide // 8) * 8
     diagonal = lax.broadcasted_iota(jnp.int32, (spots, edge), 0) == lax.broadcasted_iota(jnp.int32, (spots, edge), 1)
 
     def masks(k):
-        line = band[pl.ds(pl.multiple_of(k * pitch + slots * edge, NOTE), NOTE), :].astype(jnp.float32)[:1]
+        line = band[from_row(k * pitch + slots * edge, NOTE), :].astype(jnp.float32)[:1]
         value = jnp.sum(jnp.where(diagonal, line, 0.0), axis=1, keepdims=True)
         return jnp.broadcast_to(value, (spots, edge))
 
@@ -192,29 +190,32 @@
             axis=1,
         )
 
-    def row_group(group, carry):
-        r = GROUP * group
-        middle = jnp.where(group == reach // GROUP, 1, 0)
-        keep = [masks(r + reach + i) for i in range(GROUP)]
-        for d in range(-far, far + GROUP, 2):
-            low, high = max(-reach, d - reach), min(reach + GROUP - 1, d + reach + 1)
+    def square_rows(r, n, slot, own_row, offsets):
+        keep = [masks(r + reach + i) for i in range(n)]
+        for d in offsets:
+            low, high = max(-reach, d - reach), min(reach + n - 1, d + reach + 1)
             size = high - low + 1
-            left = jnp.concatenate([strip(r + reach + i, low + reach - i, size) for i in range(GROUP)], axis=0)
+            left = jnp.concatenate([strip(r + reach + i, low + reach - i, size) for i in range(n)], axis=0)
             right = jnp.concatenate([strip(r + reach + e, d - e + reach, 2) for e in range(low, high + 1)], axis=0)
             product = jnp.dot(left, right, preferred_element_type=jnp.float32)
-            for i in range(GROUP):
+            for i in range(n):
                 for j in range(2):
                     u = d + far - i + j
                     if 0 <= u < wide:
                         kept = product[i * edge : (i + 1) * edge, j * edge : (j + 1) * edge]
                         kept = kept * keep[i][u : u + 1, :]
-                        rows = pl.ds(pl.multiple_of((r + i) * edge, edge), edge)
-                        square[rows, u * edge : (u + 1) * edge] = kept.astype(kind)
-                        if i == reach % GROUP:
-                            own[middle, :, u * edge : (u + 1) * edge] = kept
+                        square[from_row((r + i) * edge, edge), u * edge : (u + 1) * edge] = kept.astype(kind)
+                        if i == own_row:
+                            own[slot, :, u * edge : (u + 1) * edge] = kept
+
+    def row_group(group, carry):
+        slot = jnp.where(group == reach // GROUP, 1, 0)
+        square_rows(GROUP * group, GROUP, slot, reach % GROUP, range(-far, far + GROUP, 2))
         return carry
 
-    lax.fori_loop(0, (slots + 1) // GROUP, row_group, 0)
+    lax.fori_loop(0, slots // GROUP, row_group, 0)
+    for r in range(slots // GROUP * GROUP, slots):
+        square_rows(r, 1, 0, None, range(-far, far + reach - r + 1, 2))
 
     keep = masks(far)
     copies = []
@@ -240,16 +241,30 @@
         copy.wait()
 
 
-def pack(pattern, filter_mask, density, payload):
+def pack(pattern, filter_mask, density, payload, blocks, packed, arrived, left):
     slots, edge = density.shape[0], density.shape[1]
-    for s in range(slots):
-        scale = pattern[0, s].astype(jnp.float32)
-        payload[s * edge : (s + 1) * edge] = (density[s].astype(jnp.float32) * scale).astype(payload.dtype)
+    bounds = [slots * part // PIECES for part in range(PIECES + 1)]
+    fetches, stores = [], []
+    for part in range(PIECES):
+        held = pl.ds(bounds[part], bounds[part + 1] - bounds[part])
+        fetches.append(pltpu.make_async_copy(density.at[held], blocks.at[held], arrived.at[part]))
+        fetches[-1].start()
     lane = lax.broadcasted_iota(jnp.int32, (NOTE, edge), 1)
     note = jnp.zeros((NOTE, edge), jnp.float32)
     for u in range(filter_mask.shape[1]):
         note = jnp.where(lane == u, filter_mask[0, u].astype(jnp.float32), note)
-    payload[slots * edge :] = note.astype(payload.dtype)
+    packed[slots * edge :] = note.astype(packed.dtype)
+    for part in range(PIECES):
+        fetches[part].wait()
+        for s in range(bounds[part], bounds[part + 1]):
+            scale = pattern[0, s].astype(jnp.float32)
+            packed[s * edge : (s + 1) * edge] = (blocks[s].astype(jnp.float32) * scale).astype(packed.dtype)
+        end = bounds[part + 1] * edge + (NOTE if part == PIECES - 1 else 0)
+        held = pl.ds(bounds[part] * edge, end - bounds[part] * edge)
+        stores.append(pltpu.make_async_copy(packed.at[held], payload.at[held], left.at[part]))
+        stores[-1].start()
+    for store in stores:
+        store.wait()
 
 
 def shards(density, pattern, filter_mask):
@@ -258,17 +273,23 @@
     reach = (slots - 1) // 2
     far = 2 * reach
     smem, vmem = pl.BlockSpec(memory_space=pltpu.SMEM), pl.BlockSpec(memory_space=pltpu.VMEM)
+    anywhere = pl.BlockSpec(memory_space=pl.ANY)
     payload = pl.pallas_call(
         pack,
         out_shape=jax.ShapeDtypeStruct((slots * edge + NOTE, edge), density.dtype),
-        in_specs=[smem, smem, vmem],
-        out_specs=vmem,
-        compiler_params=pltpu.CompilerParams(vmem_limit_bytes=4 * 2**20),
+        in_specs=[smem, smem, anywhere],
+        out_specs=anywhere,
+        scratch_shapes=[
+            pltpu.VMEM((slots, edge, edge), density.dtype),
+            pltpu.VMEM((slots * edge + NOTE, edge), density.dtype),
+            pltpu.SemaphoreType.DMA((PIECES,)),
+            pltpu.SemaphoreType.DMA((PIECES,)),
+        ],
+        compiler_params=pltpu.CompilerParams(vmem_limit_bytes=60 * 2**20),
     )(pattern, filter_mask, density[0])
     band, pieces = window(payload, far, (slots + 1) // 2 * edge)
     tables = [array for array, _ in pieces]
     layout = [parts for _, parts in pieces]
-    anywhere = pl.BlockSpec(memory_space=pl.ANY)
     _, result = pl.pallas_call(
         functools.partial(purify, reach, edge, layout),
         out_shape=[pltpu.VMEM(band.shape, band.dtype), jax.ShapeDtypeStruct((wide, edge, edge), density.dtype)],
@@ -276,7 +297,7 @@
         out_specs=[vmem, anywhere],
         input_output_aliases={len(tables): 0},
         scratch_shapes=[
-            pltpu.VMEM(((slots + 1) * edge, wide * edge), density.dtype),
+            pltpu.VMEM((slots * edge, wide * edge), density.dtype),
             pltpu.VMEM((2, edge, wide * edge), jnp.float32),
             pltpu.VMEM((wide, edge, edge), density.dtype),
             pltpu.SemaphoreType.DMA((max(1, sum(len(parts) for parts in layout)),)),

time: 109 us -> 107 us (0.982)
  local copies, waits for them, and re-layouts: 2.83 us -> 1.56 us
    pallas_call x1, Pallas kernels: 0.64 us -> 2.49 us  [shards(): pl.pallas_call(pack, out_shape=jax.ShapeDtypeStruct((slots * edge + NOTE,...]
    pallas_call x1, Pallas kernels: 26.1 us -> 24.7 us  [shards(): pl.pallas_call(functools.partial(purify, reach, edge, layout), out_shape=...]
    unnamed x11 -> x7, local copies, waits for them, and re-layouts: 2.67 us -> 1.4 us
  transfers between devices with their start and end apart: 20 -> 20, of which waited for: 12 -> 12; matrix products, arithmetic and copies ran while one was open for 0% -> 1% of each run, Pallas kernels for 7% -> 7%
where the time goes in v14:
time: 107 us
  waiting for transfers between devices  53.1 us (50%)
  Pallas kernels  34.6 us (32%)
  starting transfers between devices  17.5 us (16%)
  local copies, waits for them, and re-layouts  1.56 us (1%)
    ppermute x20, waiting for transfers between devices, swap(): return lax.ppermute(value, AXES, [(i, i ^ mask) for i in range(count)])  53.1 us
    pallas_call x1, Pallas kernels, shards(): pl.pallas_call(functools.partial(purify, reach, edge, layout), out_shape=...  24.7 us
    ppermute x20, starting transfers between devices, swap(): return lax.ppermute(value, AXES, [(i, i ^ mask) for i in range(count)])  17.5 us
    pallas_call x1, Pallas kernels, assemble(): pl.pallas_call(body, out_shape=pltpu.VMEM((rows * pitch, edge), kind), in...  7.47 us
    pallas_call x1, Pallas kernels, shards(): pl.pallas_call(pack, out_shape=jax.ShapeDtypeStruct((slots * edge + NOTE,...  2.49 us
  transfers between devices with their start and end apart: 20, of which 12 were waited for; matrix products, arithmetic and copies ran while one was open for 1% of the time, Pallas kernels for 7%

profile of v14, /device:TPU:0, one launch (start us, length us, event | category | flops | bytes accessed | tf_op | source)
XLA Modules:
  0.0 107.0 jit_solution(5846268775015368069)
XLA Ops:
  0.0 2.5 %shard_map.37.refs_0_ = bf16[1936,128]{1,0:T(8,128)(2,1)} custom-call(s32[1,15]{1,0:T(1,128)} %pattern.1, s32[1,29]{1,0:T(1,128)} %filter_mask.1, bf16[15,128,128]{2,1,0:T(8,128)(2,1)} %bitcast.2), custom_call_target="tpu_custom_call" | custom-call | tf_op jit(solution)/shard_map/pallas_call | solution.py:277
  2.5 3.0 %collective-permute-start = (bf16[1936,128]{1,0:T(8,128)(2,1)}, bf16[1936,128]{1,0:T(8,128)(2,1)S(1)}, u32[]{:S(2)}, u32[]{:S(2)}) collective-permute-start(bf16[1936,128]{1,0:T(8,128)(2,1)} %shard_map.37.refs_0_), channel_id=1, source_target_pairs={{0,1},{1,0},{2,3},{3,2},{4,5},{5,4},{6,7},{7,6},{8,9},{9,8},{10,11... | collective-permute-start | bytes 1486856 | tf_op jit(solution)/shard_map/ppermute | solution.py:23
  5.5 1.5 %collective-permute-start.1 = (bf16[1936,128]{1,0:T(8,128)(2,1)}, bf16[1936,128]{1,0:T(8,128)(2,1)S(1)}, u32[]{:S(2)}, u32[]{:S(2)}) collective-permute-start(bf16[1936,128]{1,0:T(8,128)(2,1)} %shard_map.37.refs_0_), channel_id=1, source_target_pairs={{0,16},{1,17},{2,18},{3,19},{4,20},{5,21},{6,22},{7,23},{8,24},{9,... | collective-permute-start | bytes 1486856 | tf_op jit(solution)/shard_map/ppermute | solution.py:23
  7.0 3.6 %collective-permute-start.4 = (bf16[1936,128]{1,0:T(8,128)(2,1)}, bf16[1936,128]{1,0:T(8,128)(2,1)S(1)}, u32[]{:S(2)}, u32[]{:S(2)}) collective-permute-start(bf16[1936,128]{1,0:T(8,128)(2,1)} %shard_map.37.refs_0_), channel_id=1, source_target_pairs={{0,6},{1,7},{2,4},{3,5},{4,2},{5,3},{6,0},{7,1},{8,14},{9,15},{10,... | collective-permute-start | bytes 1486856 | tf_op jit(solution)/shard_map/ppermute | solution.py:23
  11.1 1.1 %constant_dynamic-update-slice_fusion.5 = bf16[11616,128]{1,0:T(8,128)(2,1)S(1)} fusion(bf16[1936,128]{1,0:T(8,128)(2,1)} %shard_map.37.refs_0_), kind=kLoop, calls=%fused_computation.7 | loop fusion | bytes 991232
  12.2 5.6 %collective-permute-done.refs_1_ = bf16[1936,128]{1,0:T(8,128)(2,1)S(1)} collective-permute-done((bf16[1936,128]{1,0:T(8,128)(2,1)}, bf16[1936,128]{1,0:T(8,128)(2,1)S(1)}, u32[]{:S(2)}, u32[]{:S(2)}) %collective-permute-start) | collective-permute-done | bytes 495648 | tf_op jit(solution)/shard_map/ppermute | solution.py:23
  17.9 11.2 %collective-permute-done.1.refs_2_ = bf16[1936,128]{1,0:T(8,128)(2,1)S(1)} collective-permute-done((bf16[1936,128]{1,0:T(8,128)(2,1)}, bf16[1936,128]{1,0:T(8,128)(2,1)S(1)}, u32[]{:S(2)}, u32[]{:S(2)}) %collective-permute-start.1) | collective-permute-done | bytes 495648 | tf_op jit(solution)/shard_map/ppermute | solution.py:23
  29.3 3.1 %collective-permute-done.3.refs_4_ = bf16[1936,128]{1,0:T(8,128)(2,1)S(1)} collective-permute-done((bf16[1936,128]{1,0:T(8,128)(2,1)}, bf16[1936,128]{1,0:T(8,128)(2,1)S(1)}, u32[]{:S(2)}, u32[]{:S(2)}) %collective-permute-start.3) | collective-permute-done | bytes 495648 | tf_op jit(solution)/shard_map/ppermute | solution.py:23
  32.7 0.6 collective-permute-start.7
  33.3 0.5 collective-permute-start.6
  33.8 1.7 %collective-permute-start.8 = (bf16[1936,128]{1,0:T(8,128)(2,1)S(1)}, bf16[1936,128]{1,0:T(8,128)(2,1)S(1)}, u32[]{:S(2)}, u32[]{:S(2)}) collective-permute-start(bf16[1936,128]{1,0:T(8,128)(2,1)S(1)} %collective-permute-done.4.refs_5_), channel_id=1, source_target_pairs={{0,2},{1,3},{2,0},{3,1},{4,6},{5,7},{6,4},{7,5},{8,10},{9,11},{10,... | collective-permute-start | bytes 1486856 | tf_op jit(solution)/shard_map/ppermute | solution.py:23
  36.0 19.3 %collective-permute-done.8.refs_11_ = bf16[1936,128]{1,0:T(8,128)(2,1)S(1)} collective-permute-done((bf16[1936,128]{1,0:T(8,128)(2,1)S(1)}, bf16[1936,128]{1,0:T(8,128)(2,1)S(1)}, u32[]{:S(2)}, u32[]{:S(2)}) %collective-permute-start.8) | collective-permute-done | bytes 495648 | tf_op jit(solution)/shard_map/ppermute | solution.py:23
  55.3 1.7 %collective-permute-done.7.refs_9_ = bf16[3872,128]{1,0:T(8,128)(2,1)S(1)} collective-permute-done((bf16[3872,128]{1,0:T(8,128)(2,1)S(1)}, bf16[3872,128]{1,0:T(8,128)(2,1)S(1)}, u32[]{:S(2)}, u32[]{:S(2)}) %collective-permute-start.7) | collective-permute-done | bytes 991264 | tf_op jit(solution)/shard_map/ppermute | solution.py:23
  57.4 0.6 collective-permute-start.10
  58.0 0.6 collective-permute-start.12
  58.6 1.6 %collective-permute-start.13 = (bf16[2848,128]{1,0:T(8,128)(2,1)S(1)}, bf16[2848,128]{1,0:T(8,128)(2,1)S(1)}, u32[]{:S(2)}, u32[]{:S(2)}) collective-permute-start(bf16[2848,128]{1,0:T(8,128)(2,1)S(1)} %pad_maximum_fusion.1), channel_id=1, source_target_pairs={{0,16},{1,17},{2,18},{3,19},{4,20},{5,21},{6,22},{7,23},{8,24},{9,... | collective-permute-start | bytes 2187272 | tf_op jit(solution)/shard_map/ppermute | solution.py:23
  60.2 1.7 %collective-permute-start.14 = (bf16[1936,128]{1,0:T(8,128)(2,1)S(1)}, bf16[1936,128]{1,0:T(8,128)(2,1)S(1)}, u32[]{:S(2)}, u32[]{:S(2)}) collective-permute-start(bf16[1936,128]{1,0:T(8,128)(2,1)S(1)} %collective-permute-done.2.refs_3_), channel_id=1, source_target_pairs={{0,2},{1,3},{2,0},{3,1},{4,6},{5,7},{6,4},{7,5},{8,10},{9,11},{10,... | collective-permute-start | bytes 1486856 | tf_op jit(solution)/shard_map/ppermute | solution.py:23
  61.9 7.5 %shard_map.38.refs_8_ = bf16[56144,128]{1,0:T(8,128)(2,1)S(1)} custom-call(bf16[1936,128]{1,0:T(8,128)(2,1)S(1)} %copy-done, bf16[1936,128]{1,0:T(8,128)(2,1)S(1)} %collective-permute-done.refs_1_, bf16[1936,128]{1,0:T(8,128)(2,1)S(1)} %collective-permute-done.1.refs_2_, bf16[1936,128]{1,0:T(8,128)(2,1)S(1)} %collective-permute-done.2.refs_3_, ...), custom_call_target="tpu_custom_call" | custom-call | bytes 28745728 | tf_op jit(solution)/shard_map/pallas_call | solution.py:142
  69.4 3.5 %collective-permute-done.14.refs_6_ = bf16[1936,128]{1,0:T(8,128)(2,1)S(1)} collective-permute-done((bf16[1936,128]{1,0:T(8,128)(2,1)S(1)}, bf16[1936,128]{1,0:T(8,128)(2,1)S(1)}, u32[]{:S(2)}, u32[]{:S(2)}) %collective-permute-start.14) | collective-permute-done | bytes 495648 | tf_op jit(solution)/shard_map/ppermute | solution.py:23
  72.9 3.8 %collective-permute-done.13.refs_2_ = bf16[2848,128]{1,0:T(8,128)(2,1)S(1)} collective-permute-done((bf16[2848,128]{1,0:T(8,128)(2,1)S(1)}, bf16[2848,128]{1,0:T(8,128)(2,1)S(1)}, u32[]{:S(2)}, u32[]{:S(2)}) %collective-permute-start.13) | collective-permute-done | bytes 729120 | tf_op jit(solution)/shard_map/ppermute | solution.py:23
  77.9 3.0 %collective-permute-done.17.refs_4_ = bf16[1936,128]{1,0:T(8,128)(2,1)S(1)} collective-permute-done((bf16[1936,128]{1,0:T(8,128)(2,1)S(1)}, bf16[1936,128]{1,0:T(8,128)(2,1)S(1)}, u32[]{:S(2)}, u32[]{:S(2)}) %collective-permute-start.17) | collective-permute-done | bytes 495648 | tf_op jit(solution)/shard_map/ppermute | solution.py:23
  80.9 0.7 collective-permute-done.18.refs_5_
  81.6 0.7 collective-permute-done.19.refs_7_
  82.3 24.7 %shard_map.39 = (bf16[56144,128]{1,0:T(8,128)(2,1)S(1)}, bf16[29,128,128]{2,1,0:T(8,128)(2,1)}) custom-call(bf16[2960,128]{1,0:T(8,128)(2,1)S(1)} %collective-permute-done.12.refs_0_, bf16[2960,128]{1,0:T(8,128)(2,1)S(1)} %collective-permute-done.15.refs_1_, bf16[2848,128]{1,0:T(8,128)(2,1)S(1)} %collective-permute-done.13.refs_2_, ...), custom_call_target="tpu_custom_call", output_to_operand_aliasing={{0}: (8, {})} | custom-call | flops 16999999488 | bytes 15728640 | tf_op jit(solution)/shard_map/pallas_call | solution.py:293
  (31 shorter events, 3.2 us)
Async XLA Ops:
  2.5 15.4 %collective-permute-start = (bf16[1936,128]{1,0:T(8,128)(2,1)}, bf16[1936,128]{1,0:T(8,128)(2,1)S(1)}, u32[]{:S(2)}, u32[]{:S(2)}) collective-permute-start(bf16[1936,128]{1,0:T(8,128)(2,1)} %shard_map.37.refs_0_), channel_id=1, source_target_pairs={{0,1},{1,0},{2,3},{3,2},{4,5},{5,4},{6,7},{7,6},{8,9},{9,8},{10,11... | collective-permute-start | bytes 1486856 | tf_op jit(solution)/shard_map/ppermute | solution.py:23
  5.5 23.6 %collective-permute-start.1 = (bf16[1936,128]{1,0:T(8,128)(2,1)}, bf16[1936,128]{1,0:T(8,128)(2,1)S(1)}, u32[]{:S(2)}, u32[]{:S(2)}) collective-permute-start(bf16[1936,128]{1,0:T(8,128)(2,1)} %shard_map.37.refs_0_), channel_id=1, source_target_pairs={{0,16},{1,17},{2,18},{3,19},{4,20},{5,21},{6,22},{7,23},{8,24},{9,... | collective-permute-start | bytes 1486856 | tf_op jit(solution)/shard_map/ppermute | solution.py:23
  7.0 25.4 %collective-permute-start.4 = (bf16[1936,128]{1,0:T(8,128)(2,1)}, bf16[1936,128]{1,0:T(8,128)(2,1)S(1)}, u32[]{:S(2)}, u32[]{:S(2)}) collective-permute-start(bf16[1936,128]{1,0:T(8,128)(2,1)} %shard_map.37.refs_0_), channel_id=1, source_target_pairs={{0,6},{1,7},{2,4},{3,5},{4,2},{5,3},{6,0},{7,1},{8,14},{9,15},{10,... | collective-permute-start | bytes 1486856 | tf_op jit(solution)/shard_map/ppermute | solution.py:23
  10.6 21.7 %collective-permute-start.3 = (bf16[1936,128]{1,0:T(8,128)(2,1)}, bf16[1936,128]{1,0:T(8,128)(2,1)S(1)}, u32[]{:S(2)}, u32[]{:S(2)}) collective-permute-start(bf16[1936,128]{1,0:T(8,128)(2,1)} %shard_map.37.refs_0_), channel_id=1, source_target_pairs={{0,2},{1,3},{2,0},{3,1},{4,6},{5,7},{6,4},{7,5},{8,10},{9,11},{10,... | collective-permute-start | bytes 1486856 | tf_op jit(solution)/shard_map/ppermute | solution.py:23
  10.6 18.5 %collective-permute-start.2 = (bf16[1936,128]{1,0:T(8,128)(2,1)}, bf16[1936,128]{1,0:T(8,128)(2,1)S(1)}, u32[]{:S(2)}, u32[]{:S(2)}) collective-permute-start(bf16[1936,128]{1,0:T(8,128)(2,1)} %shard_map.37.refs_0_), channel_id=1, source_target_pairs={{0,17},{1,16},{2,19},{3,18},{4,21},{5,20},{6,23},{7,22},{8,25},{9,... | collective-permute-start | bytes 1486856 | tf_op jit(solution)/shard_map/ppermute | solution.py:23
  32.4 29.5 %copy-start = (bf16[1936,128]{1,0:T(8,128)(2,1)S(1)}, bf16[1936,128]{1,0:T(8,128)(2,1)}, u32[]{:S(2)}) copy-start(bf16[1936,128]{1,0:T(8,128)(2,1)} %shard_map.37.refs_0_) | copy-start | bytes 1486852
  32.6 24.7 %collective-permute-start.5 = (bf16[11616,128]{1,0:T(8,128)(2,1)S(1)}, bf16[11616,128]{1,0:T(8,128)(2,1)S(1)}, u32[]{:S(2)}, u32[]{:S(2)}) collective-permute-start(bf16[11616,128]{1,0:T(8,128)(2,1)S(1)} %get-tuple-element.30), channel_id=1, source_target_pairs={{0,8},{1,9},{2,10},{3,11},{4,12},{5,13},{6,14},{7,15},{8,0},{9,1},... | collective-permute-start | bytes 8921096 | tf_op jit(solution)/shard_map/ppermute | solution.py:23
  32.7 24.3 %collective-permute-start.7 = (bf16[3872,128]{1,0:T(8,128)(2,1)S(1)}, bf16[3872,128]{1,0:T(8,128)(2,1)S(1)}, u32[]{:S(2)}, u32[]{:S(2)}) collective-permute-start(bf16[3872,128]{1,0:T(8,128)(2,1)S(1)} %get-tuple-element.29), channel_id=1, source_target_pairs={{0,16},{1,17},{2,18},{3,19},{4,20},{5,21},{6,22},{7,23},{8,24},{9,... | collective-permute-start | bytes 2973704 | tf_op jit(solution)/shard_map/ppermute | solution.py:23
  33.3 24.0 %collective-permute-start.6 = (bf16[3872,128]{1,0:T(8,128)(2,1)S(1)}, bf16[3872,128]{1,0:T(8,128)(2,1)S(1)}, u32[]{:S(2)}, u32[]{:S(2)}) collective-permute-start(bf16[3872,128]{1,0:T(8,128)(2,1)S(1)} %get-tuple-element.29), channel_id=1, source_target_pairs={{0,1},{1,0},{2,3},{3,2},{4,5},{5,4},{6,7},{7,6},{8,9},{9,8},{10,11... | collective-permute-start | bytes 2973704 | tf_op jit(solution)/shard_map/ppermute | solution.py:23
  33.8 21.5 %collective-permute-start.8 = (bf16[1936,128]{1,0:T(8,128)(2,1)S(1)}, bf16[1936,128]{1,0:T(8,128)(2,1)S(1)}, u32[]{:S(2)}, u32[]{:S(2)}) collective-permute-start(bf16[1936,128]{1,0:T(8,128)(2,1)S(1)} %collective-permute-done.4.refs_5_), channel_id=1, source_target_pairs={{0,2},{1,3},{2,0},{3,1},{4,6},{5,7},{6,4},{7,5},{8,10},{9,11},{10,... | collective-permute-start | bytes 1486856 | tf_op jit(solution)/shard_map/ppermute | solution.py:23
  35.4 24.8 %collective-permute-start.11 = (bf16[1936,128]{1,0:T(8,128)(2,1)S(1)}, bf16[1936,128]{1,0:T(8,128)(2,1)S(1)}, u32[]{:S(2)}, u32[]{:S(2)}) collective-permute-start(bf16[1936,128]{1,0:T(8,128)(2,1)S(1)} %collective-permute-done.2.refs_3_), channel_id=1, source_target_pairs={{0,4},{1,5},{2,6},{3,7},{4,0},{5,1},{6,2},{7,3},{8,12},{9,13},{10,... | collective-permute-start | bytes 1486856 | tf_op jit(solution)/shard_map/ppermute | solution.py:23
  57.3 4.6 %collective-permute-start.9 = (bf16[3872,128]{1,0:T(8,128)(2,1)S(1)}, bf16[3872,128]{1,0:T(8,128)(2,1)S(1)}, u32[]{:S(2)}, u32[]{:S(2)}) collective-permute-start(bf16[3872,128]{1,0:T(8,128)(2,1)S(1)} %collective-permute-done.6.refs_7_), channel_id=1, source_target_pairs={{0,8},{1,9},{2,10},{3,11},{4,12},{5,13},{6,14},{7,15},{8,0},{9,1},... | collective-permute-start | bytes 2973704 | tf_op jit(solution)/shard_map/ppermute | solution.py:23
  57.4 4.5 %collective-permute-start.10 = (bf16[3872,128]{1,0:T(8,128)(2,1)S(1)}, bf16[3872,128]{1,0:T(8,128)(2,1)S(1)}, u32[]{:S(2)}, u32[]{:S(2)}) collective-permute-start(bf16[3872,128]{1,0:T(8,128)(2,1)S(1)} %collective-permute-done.7.refs_9_), channel_id=1, source_target_pairs={{0,8},{1,9},{2,10},{3,11},{4,12},{5,13},{6,14},{7,15},{8,0},{9,1},... | collective-permute-start | bytes 2973704 | tf_op jit(solution)/shard_map/ppermute | solution.py:23
  58.0 18.9 %collective-permute-start.12 = (bf16[2960,128]{1,0:T(8,128)(2,1)S(1)}, bf16[2960,128]{1,0:T(8,128)(2,1)S(1)}, u32[]{:S(2)}, u32[]{:S(2)}) collective-permute-start(bf16[2960,128]{1,0:T(8,128)(2,1)S(1)} %pad_maximum_fusion), channel_id=1, source_target_pairs={{0,1},{1,0},{2,3},{3,2},{4,5},{5,4},{6,7},{7,6},{8,9},{9,8},{10,11... | collective-permute-start | bytes 2273288 | tf_op jit(solution)/shard_map/ppermute | solution.py:23
  58.6 18.0 %collective-permute-start.13 = (bf16[2848,128]{1,0:T(8,128)(2,1)S(1)}, bf16[2848,128]{1,0:T(8,128)(2,1)S(1)}, u32[]{:S(2)}, u32[]{:S(2)}) collective-permute-start(bf16[2848,128]{1,0:T(8,128)(2,1)S(1)} %pad_maximum_fusion.1), channel_id=1, source_target_pairs={{0,16},{1,17},{2,18},{3,19},{4,20},{5,21},{6,22},{7,23},{8,24},{9,... | collective-permute-start | bytes 2187272 | tf_op jit(solution)/shard_map/ppermute | solution.py:23
  60.2 12.7 %collective-permute-start.14 = (bf16[1936,128]{1,0:T(8,128)(2,1)S(1)}, bf16[1936,128]{1,0:T(8,128)(2,1)S(1)}, u32[]{:S(2)}, u32[]{:S(2)}) collective-permute-start(bf16[1936,128]{1,0:T(8,128)(2,1)S(1)} %collective-permute-done.2.refs_3_), channel_id=1, source_target_pairs={{0,2},{1,3},{2,0},{3,1},{4,6},{5,7},{6,4},{7,5},{8,10},{9,11},{10,... | collective-permute-start | bytes 1486856 | tf_op jit(solution)/shard_map/ppermute | solution.py:23
  76.9 5.4 %collective-permute-start.15 = (bf16[2960,128]{1,0:T(8,128)(2,1)S(1)}, bf16[2960,128]{1,0:T(8,128)(2,1)S(1)}, u32[]{:S(2)}, u32[]{:S(2)}) collective-permute-start(bf16[2960,128]{1,0:T(8,128)(2,1)S(1)} %collective-permute-done.12.refs_0_), channel_id=1, source_target_pairs={{0,8},{1,9},{2,10},{3,11},{4,12},{5,13},{6,14},{7,15},{8,0},{9,1},... | collective-permute-start | bytes 2273288 | tf_op jit(solution)/shard_map/ppermute | solution.py:23
  76.9 5.4 %collective-permute-start.16 = (bf16[2848,128]{1,0:T(8,128)(2,1)S(1)}, bf16[2848,128]{1,0:T(8,128)(2,1)S(1)}, u32[]{:S(2)}, u32[]{:S(2)}) collective-permute-start(bf16[2848,128]{1,0:T(8,128)(2,1)S(1)} %collective-permute-done.13.refs_2_), channel_id=1, source_target_pairs={{0,8},{1,9},{2,10},{3,11},{4,12},{5,13},{6,14},{7,15},{8,0},{9,1},... | collective-permute-start | bytes 2187272 | tf_op jit(solution)/shard_map/ppermute | solution.py:23
  77.4 3.5 %collective-permute-start.17 = (bf16[1936,128]{1,0:T(8,128)(2,1)S(1)}, bf16[1936,128]{1,0:T(8,128)(2,1)S(1)}, u32[]{:S(2)}, u32[]{:S(2)}) collective-permute-start(bf16[1936,128]{1,0:T(8,128)(2,1)S(1)} %collective-permute-done.8.refs_11_), channel_id=1, source_target_pairs={{0,8},{1,9},{2,10},{3,11},{4,12},{5,13},{6,14},{7,15},{8,0},{9,1},... | collective-permute-start | bytes 1486856 | tf_op jit(solution)/shard_map/ppermute | solution.py:23
  77.4 4.2 %collective-permute-start.18 = (bf16[1936,128]{1,0:T(8,128)(2,1)S(1)}, bf16[1936,128]{1,0:T(8,128)(2,1)S(1)}, u32[]{:S(2)}, u32[]{:S(2)}) collective-permute-start(bf16[1936,128]{1,0:T(8,128)(2,1)S(1)} %collective-permute-done.11.refs_12_), channel_id=1, source_target_pairs={{0,8},{1,9},{2,10},{3,11},{4,12},{5,13},{6,14},{7,15},{8,0},{9,1},... | collective-permute-start | bytes 1486856 | tf_op jit(solution)/shard_map/ppermute | solution.py:23
  77.9 4.4 %collective-permute-start.19 = (bf16[1936,128]{1,0:T(8,128)(2,1)S(1)}, bf16[1936,128]{1,0:T(8,128)(2,1)S(1)}, u32[]{:S(2)}, u32[]{:S(2)}) collective-permute-start(bf16[1936,128]{1,0:T(8,128)(2,1)S(1)} %collective-permute-done.14.refs_6_), channel_id=1, source_target_pairs={{0,8},{1,9},{2,10},{3,11},{4,12},{5,13},{6,14},{7,15},{8,0},{9,1},... | collective-permute-start | bytes 1486856 | tf_op jit(solution)/shard_map/ppermute | solution.py:23

commit v15 on v14

--- a/solution.py
+++ b/solution.py
@@ -10,7 +10,6 @@
 NOTE = 16
 GROUP = 2
 WIDTH = 4
-PIECES = 3
 AXES = ("row", "col")
 
 
@@ -49,14 +48,14 @@
     d1 = swap(d0, z1)
     cross((xp, whole(z1 | x, z3 | x)))
     cross((yp, whole(z1 | y, z3 | y)))
-    band = gather(found + [(f2, whole(z2)), (d2, whole(z2 | x | y))])
+    band = gather(None, found + [(f2, whole(z2)), (d2, whole(z2 | x | y))])
     band, xl, yl, d1, f2, d2 = lax.optimization_barrier((band, xl, yl, d1, f2, d2))
     del found[:]
     cross((xl, [(z2 | x, 0, full), (z3 | x | y, 0, cut)]))
     cross((yl, [(z2 | y, 0, full), (z3 | x | y, cut, full - cut)]))
     for row, mask in ((f2, z2), (d2, z2 | x | y), (d1, z1 | x | y)):
         cross((row, whole(mask)))
-    return band, [item for item in found if item[0] is not f2 and item[0] is not d2]
+    return gather(band, [item for item in found if any(item[0] is late for late in (xl, yl, d1))]), found[1::2]
 
 
 def window(payload, need, cut):
@@ -79,7 +78,10 @@
         def pieces(found):
             return [(array, [(start, rows, flipped(mask)) for mask, start, rows in parts]) for array, parts in found]
 
-        band, late = cube(payload, count, cut, lambda found: assemble(pieces(found), size, need))
+        def gather(band, found):
+            return assemble(pieces(found), size, need, band)
+
+        band, late = cube(payload, count, cut, gather)
         return band, pieces(late)
 
     def piece(array, first):
@@ -109,9 +111,9 @@
                 band.at[pl.ds(pl.multiple_of(row * pitch + start, NOTE), size)],
                 arrived.at[len(copies)],
             )
-            copies.append((wanted, copy))
+            copies.append((wanted, row, copy))
             begin += size
-    for wanted, copy in copies:
+    for wanted, _, copy in copies:
 
         @pl.when(wanted)
         def _(copy=copy):
@@ -121,33 +123,38 @@
 
 
 def wait_all(copies):
-    for wanted, copy in copies:
+    for wanted, _, copy in copies:
 
         @pl.when(wanted)
         def _(copy=copy):
             copy.wait()
 
 
-def assemble(pieces, pitch, need):
+def assemble(pieces, pitch, need, band=None):
     tables = [array for array, _ in pieces]
     layout = [parts for _, parts in pieces]
     kind, edge = tables[0].dtype, tables[0].shape[1]
     rows = 2 * need + 1
 
+    vmem = pl.BlockSpec(memory_space=pltpu.VMEM)
+    given = [] if band is None else [band]
+
     def body(*refs):
-        band, arrived = refs[len(tables) :]
-        copies = row_copies(layout, need, refs[: len(tables)], band, arrived, pitch)
-        wait_all(copies)
+        band, arrived = refs[-2:]
+        wait_all(row_copies(layout, need, refs[: len(tables)], band, arrived, pitch))
 
     return pl.pallas_call(
         body,
         out_shape=pltpu.VMEM((rows * pitch, edge), kind),
-        in_specs=[pl.BlockSpec(memory_space=pl.ANY)] * len(tables),
-        out_specs=pl.BlockSpec(memory_space=pltpu.VMEM),
+        in_specs=[pl.BlockSpec(memory_space=pl.ANY)] * len(tables) + [vmem] * len(given),
+        out_specs=vmem,
+        input_output_aliases={len(tables): 0} if given else {},
         scratch_shapes=[pltpu.SemaphoreType.DMA((sum(len(parts) for parts in layout),))],
         compiler_params=pltpu.CompilerParams(vmem_limit_bytes=2 * 2**20),
-        cost_estimate=pl.CostEstimate(flops=0, bytes_accessed=rows * pitch * edge * 4, transcendentals=0),
-    )(*tables)
+        cost_estimate=pl.CostEstimate(
+            flops=0, bytes_accessed=sum(table.size for table in tables) * 4, transcendentals=0
+        ),
+    )(*tables, *given)
 
 
 def purify(reach, edge, layout, *refs):
@@ -157,8 +164,7 @@
     slots, wide = 2 * reach + 1, 4 * reach + 1
     pitch = slots * edge + NOTE
     kind = band.dtype
-    copies = row_copies(layout, far, tables, band, arrived, pitch)
-    wait_all(copies)
+    late = row_copies(layout, far, tables, band, arrived, pitch)
 
     zero = jnp.zeros((edge, edge), kind)
 
@@ -208,7 +214,12 @@
                         if i == own_row:
                             own[slot, :, u * edge : (u + 1) * edge] = kept
 
+    def first_user(row):
+        return jnp.minimum(lax.div(jnp.maximum(row - far, 0), GROUP), slots // GROUP - 1)
+
     def row_group(group, carry):
+        needed = [(first_user(row) == group) & wanted for wanted, row, _ in late]
+        wait_all([(now, row, copy) for now, (_, row, copy) in zip(needed, late)])
         slot = jnp.where(group == reach // GROUP, 1, 0)
         square_rows(GROUP * group, GROUP, slot, reach % GROUP, range(-far, far + GROUP, 2))
         return carry
@@ -241,30 +252,16 @@
         copy.wait()
 
 
-def pack(pattern, filter_mask, density, payload, blocks, packed, arrived, left):
+def pack(pattern, filter_mask, density, payload):
     slots, edge = density.shape[0], density.shape[1]
-    bounds = [slots * part // PIECES for part in range(PIECES + 1)]
-    fetches, stores = [], []
-    for part in range(PIECES):
-        held = pl.ds(bounds[part], bounds[part + 1] - bounds[part])
-        fetches.append(pltpu.make_async_copy(density.at[held], blocks.at[held], arrived.at[part]))
-        fetches[-1].start()
+    for s in range(slots):
+        scale = pattern[0, s].astype(jnp.float32)
+        payload[s * edge : (s + 1) * edge] = (density[s].astype(jnp.float32) * scale).astype(payload.dtype)
     lane = lax.broadcasted_iota(jnp.int32, (NOTE, edge), 1)
     note = jnp.zeros((NOTE, edge), jnp.float32)
     for u in range(filter_mask.shape[1]):
         note = jnp.where(lane == u, filter_mask[0, u].astype(jnp.float32), note)
-    packed[slots * edge :] = note.astype(packed.dtype)
-    for part in range(PIECES):
-        fetches[part].wait()
-        for s in range(bounds[part], bounds[part + 1]):
-            scale = pattern[0, s].astype(jnp.float32)
-            packed[s * edge : (s + 1) * edge] = (blocks[s].astype(jnp.float32) * scale).astype(packed.dtype)
-        end = bounds[part + 1] * edge + (NOTE if part == PIECES - 1 else 0)
-        held = pl.ds(bounds[part] * edge, end - bounds[part] * edge)
-        stores.append(pltpu.make_async_copy(packed.at[held], payload.at[held], left.at[part]))
-        stores[-1].start()
-    for store in stores:
-        store.wait()
+    payload[slots * edge :] = note.astype(payload.dtype)
 
 
 def shards(density, pattern, filter_mask):
@@ -277,14 +274,8 @@
     payload = pl.pallas_call(
         pack,
         out_shape=jax.ShapeDtypeStruct((slots * edge + NOTE, edge), density.dtype),
-        in_specs=[smem, smem, anywhere],
-        out_specs=anywhere,
-        scratch_shapes=[
-            pltpu.VMEM((slots, edge, edge), density.dtype),
-            pltpu.VMEM((slots * edge + NOTE, edge), density.dtype),
-            pltpu.SemaphoreType.DMA((PIECES,)),
-            pltpu.SemaphoreType.DMA((PIECES,)),
-        ],
+        in_specs=[smem, smem, vmem],
+        out_specs=vmem,
         compiler_params=pltpu.CompilerParams(vmem_limit_bytes=60 * 2**20),
     )(pattern, filter_mask, density[0])
     band, pieces = window(payload, far, (slots + 1) // 2 * edge)

time: 107 us -> 108 us (level)
  waiting for transfers between devices: 53.1 us -> 54.2 us
    pallas_call x1, Pallas kernels: 24.7 us -> 23.2 us  [shards(): pl.pallas_call(functools.partial(purify, reach, edge, layout), out_shape=...]
    pallas_call x1 -> x2, Pallas kernels: 7.47 us -> 8.71 us  [assemble(): pl.pallas_call(body, out_shape=pltpu.VMEM((rows * pitch, edge), kind), in...]
    ppermute x20, waiting for transfers between devices: 53.1 us -> 54.2 us  [swap(): return lax.ppermute(value, AXES, [(i, i ^ mask) for i in range(count)])]
  transfers between devices with their start and end apart: 20 -> 20, of which waited for: 12 -> 12; matrix products, arithmetic and copies ran while one was open for 1% -> 1% of each run, Pallas kernels for 7% -> 8%
where the time goes in v15:
time: 108 us; the launch traced here: 107 us
  waiting for transfers between devices  54.2 us (50%)
  Pallas kernels  33.9 us (31%)
  starting transfers between devices  17.5 us (16%)
  local copies, waits for them, and re-layouts  1.56 us (1%)
    ppermute x20, waiting for transfers between devices, swap(): return lax.ppermute(value, AXES, [(i, i ^ mask) for i in range(count)])  54.2 us
    pallas_call x1, Pallas kernels, shards(): pl.pallas_call(functools.partial(purify, reach, edge, layout), out_shape=...  23.2 us
    ppermute x20, starting transfers between devices, swap(): return lax.ppermute(value, AXES, [(i, i ^ mask) for i in range(count)])  17.5 us
    pallas_call x2, Pallas kernels, assemble(): pl.pallas_call(body, out_shape=pltpu.VMEM((rows * pitch, edge), kind), in...  8.71 us
  transfers between devices with their start and end apart: 20, of which 12 were waited for; matrix products, arithmetic and copies ran while one was open for 1% of the time, Pallas kernels for 8%

profile of v15, /device:TPU:0, one launch (start us, length us, event | category | flops | bytes accessed | tf_op | source)
XLA Modules:
  0.0 107.4 jit_solution(11464933363932188106)
XLA Ops:
  0.0 1.9 %shard_map.37.refs_0_ = bf16[1936,128]{1,0:T(8,128)(2,1)} custom-call(s32[1,15]{1,0:T(1,128)} %pattern.1, s32[1,29]{1,0:T(1,128)} %filter_mask.1, bf16[15,128,128]{2,1,0:T(8,128)(2,1)} %bitcast.2), custom_call_target="tpu_custom_call" | custom-call | tf_op jit(solution)/shard_map/pallas_call | solution.py:274
  1.9 2.9 %collective-permute-start = (bf16[1936,128]{1,0:T(8,128)(2,1)}, bf16[1936,128]{1,0:T(8,128)(2,1)S(1)}, u32[]{:S(2)}, u32[]{:S(2)}) collective-permute-start(bf16[1936,128]{1,0:T(8,128)(2,1)} %shard_map.37.refs_0_), channel_id=1, source_target_pairs={{0,1},{1,0},{2,3},{3,2},{4,5},{5,4},{6,7},{7,6},{8,9},{9,8},{10,11... | collective-permute-start | bytes 1486856 | tf_op jit(solution)/shard_map/ppermute | solution.py:22
  4.9 1.5 %collective-permute-start.1 = (bf16[1936,128]{1,0:T(8,128)(2,1)}, bf16[1936,128]{1,0:T(8,128)(2,1)S(1)}, u32[]{:S(2)}, u32[]{:S(2)}) collective-permute-start(bf16[1936,128]{1,0:T(8,128)(2,1)} %shard_map.37.refs_0_), channel_id=1, source_target_pairs={{0,16},{1,17},{2,18},{3,19},{4,20},{5,21},{6,22},{7,23},{8,24},{9,... | collective-permute-start | bytes 1486856 | tf_op jit(solution)/shard_map/ppermute | solution.py:22
  6.4 2.1 %collective-permute-start.3 = (bf16[1936,128]{1,0:T(8,128)(2,1)}, bf16[1936,128]{1,0:T(8,128)(2,1)S(1)}, u32[]{:S(2)}, u32[]{:S(2)}) collective-permute-start(bf16[1936,128]{1,0:T(8,128)(2,1)} %shard_map.37.refs_0_), channel_id=1, source_target_pairs={{0,2},{1,3},{2,0},{3,1},{4,6},{5,7},{6,4},{7,5},{8,10},{9,11},{10,... | collective-permute-start | bytes 1486856 | tf_op jit(solution)/shard_map/ppermute | solution.py:22
  8.4 2.5 %collective-permute-start.4 = (bf16[1936,128]{1,0:T(8,128)(2,1)}, bf16[1936,128]{1,0:T(8,128)(2,1)S(1)}, u32[]{:S(2)}, u32[]{:S(2)}) collective-permute-start(bf16[1936,128]{1,0:T(8,128)(2,1)} %shard_map.37.refs_0_), channel_id=1, source_target_pairs={{0,6},{1,7},{2,4},{3,5},{4,2},{5,3},{6,0},{7,1},{8,14},{9,15},{10,... | collective-permute-start | bytes 1486856 | tf_op jit(solution)/shard_map/ppermute | solution.py:22
  10.9 1.1 %constant_dynamic-update-slice_fusion.5 = bf16[11616,128]{1,0:T(8,128)(2,1)S(1)} fusion(bf16[1936,128]{1,0:T(8,128)(2,1)} %shard_map.37.refs_0_), kind=kLoop, calls=%fused_computation.7 | loop fusion | bytes 991232
  12.0 5.2 %collective-permute-done.refs_1_ = bf16[1936,128]{1,0:T(8,128)(2,1)S(1)} collective-permute-done((bf16[1936,128]{1,0:T(8,128)(2,1)}, bf16[1936,128]{1,0:T(8,128)(2,1)S(1)}, u32[]{:S(2)}, u32[]{:S(2)}) %collective-permute-start) | collective-permute-done | bytes 495648 | tf_op jit(solution)/shard_map/ppermute | solution.py:22
  17.3 11.2 %collective-permute-done.1.refs_2_ = bf16[1936,128]{1,0:T(8,128)(2,1)S(1)} collective-permute-done((bf16[1936,128]{1,0:T(8,128)(2,1)}, bf16[1936,128]{1,0:T(8,128)(2,1)S(1)}, u32[]{:S(2)}, u32[]{:S(2)}) %collective-permute-start.1) | collective-permute-done | bytes 495648 | tf_op jit(solution)/shard_map/ppermute | solution.py:22
  28.7 3.3 %collective-permute-done.4.refs_5_ = bf16[1936,128]{1,0:T(8,128)(2,1)S(1)} collective-permute-done((bf16[1936,128]{1,0:T(8,128)(2,1)}, bf16[1936,128]{1,0:T(8,128)(2,1)S(1)}, u32[]{:S(2)}, u32[]{:S(2)}) %collective-permute-start.4) | collective-permute-done | bytes 495648 | tf_op jit(solution)/shard_map/ppermute | solution.py:22
  32.2 1.6 %collective-permute-start.6 = (bf16[3872,128]{1,0:T(8,128)(2,1)S(1)}, bf16[3872,128]{1,0:T(8,128)(2,1)S(1)}, u32[]{:S(2)}, u32[]{:S(2)}) collective-permute-start(bf16[3872,128]{1,0:T(8,128)(2,1)S(1)} %get-tuple-element.29), channel_id=1, source_target_pairs={{0,1},{1,0},{2,3},{3,2},{4,5},{5,4},{6,7},{7,6},{8,9},{9,8},{10,11... | collective-permute-start | bytes 2973704 | tf_op jit(solution)/shard_map/ppermute | solution.py:22
  33.8 1.5 %collective-permute-start.7 = (bf16[3872,128]{1,0:T(8,128)(2,1)S(1)}, bf16[3872,128]{1,0:T(8,128)(2,1)S(1)}, u32[]{:S(2)}, u32[]{:S(2)}) collective-permute-start(bf16[3872,128]{1,0:T(8,128)(2,1)S(1)} %get-tuple-element.29), channel_id=1, source_target_pairs={{0,16},{1,17},{2,18},{3,19},{4,20},{5,21},{6,22},{7,23},{8,24},{9,... | collective-permute-start | bytes 2973704 | tf_op jit(solution)/shard_map/ppermute | solution.py:22
  35.3 0.6 collective-permute-start.8
  35.9 1.6 %collective-permute-start.11 = (bf16[1936,128]{1,0:T(8,128)(2,1)S(1)}, bf16[1936,128]{1,0:T(8,128)(2,1)S(1)}, u32[]{:S(2)}, u32[]{:S(2)}) collective-permute-start(bf16[1936,128]{1,0:T(8,128)(2,1)S(1)} %collective-permute-done.2.refs_3_), channel_id=1, source_target_pairs={{0,4},{1,5},{2,6},{3,7},{4,0},{5,1},{6,2},{7,3},{8,12},{9,13},{10,... | collective-permute-start | bytes 1486856 | tf_op jit(solution)/shard_map/ppermute | solution.py:22
  37.5 21.6 %collective-permute-done.8.refs_11_ = bf16[1936,128]{1,0:T(8,128)(2,1)S(1)} collective-permute-done((bf16[1936,128]{1,0:T(8,128)(2,1)S(1)}, bf16[1936,128]{1,0:T(8,128)(2,1)S(1)}, u32[]{:S(2)}, u32[]{:S(2)}) %collective-permute-start.8) | collective-permute-done | bytes 495648 | tf_op jit(solution)/shard_map/ppermute | solution.py:22
  59.8 0.6 collective-permute-start.12
  61.7 1.4 %collective-permute-done.9.refs_8_ = bf16[3872,128]{1,0:T(8,128)(2,1)S(1)} collective-permute-done((bf16[3872,128]{1,0:T(8,128)(2,1)S(1)}, bf16[3872,128]{1,0:T(8,128)(2,1)S(1)}, u32[]{:S(2)}, u32[]{:S(2)}) %collective-permute-start.9) | collective-permute-done | bytes 991264 | tf_op jit(solution)/shard_map/ppermute | solution.py:22
  63.1 7.4 %shard_map.38.refs_3_ = bf16[56144,128]{1,0:T(8,128)(2,1)S(1)} custom-call(bf16[1936,128]{1,0:T(8,128)(2,1)S(1)} %copy-done, bf16[1936,128]{1,0:T(8,128)(2,1)S(1)} %collective-permute-done.refs_1_, bf16[1936,128]{1,0:T(8,128)(2,1)S(1)} %collective-permute-done.1.refs_2_, bf16[1936,128]{1,0:T(8,128)(2,1)S(1)} %collective-permute-done.2.refs_3_, ...), custom_call_target="tpu_custom_call" | custom-call | bytes 21807104 | tf_op jit(solution)/shard_map/pallas_call | solution.py:146
  70.5 3.2 %collective-permute-done.14.refs_2_ = bf16[1936,128]{1,0:T(8,128)(2,1)S(1)} collective-permute-done((bf16[1936,128]{1,0:T(8,128)(2,1)S(1)}, bf16[1936,128]{1,0:T(8,128)(2,1)S(1)}, u32[]{:S(2)}, u32[]{:S(2)}) %collective-permute-start.14) | collective-permute-done | bytes 495648 | tf_op jit(solution)/shard_map/ppermute | solution.py:22
  73.7 4.8 %collective-permute-done.13.refs_1_ = bf16[2848,128]{1,0:T(8,128)(2,1)S(1)} collective-permute-done((bf16[2848,128]{1,0:T(8,128)(2,1)S(1)}, bf16[2848,128]{1,0:T(8,128)(2,1)S(1)}, u32[]{:S(2)}, u32[]{:S(2)}) %collective-permute-start.13) | collective-permute-done | bytes 729120 | tf_op jit(solution)/shard_map/ppermute | solution.py:22
  79.7 1.3 %shard_map.39.refs_5_ = bf16[56144,128]{1,0:T(8,128)(2,1)S(1)} custom-call(bf16[2960,128]{1,0:T(8,128)(2,1)S(1)} %collective-permute-done.12.refs_0_, bf16[2848,128]{1,0:T(8,128)(2,1)S(1)} %collective-permute-done.13.refs_1_, bf16[1936,128]{1,0:T(8,128)(2,1)S(1)} %collective-permute-done.14.refs_2_, ...), custom_call_target="tpu_custom_call", output_to_operand_aliasing={{}: (3, {})} | custom-call | bytes 3964928 | tf_op jit(solution)/shard_map/pallas_call | solution.py:146
  81.1 1.6 %collective-permute-done.17.refs_2_ = bf16[1936,128]{1,0:T(8,128)(2,1)S(1)} collective-permute-done((bf16[1936,128]{1,0:T(8,128)(2,1)S(1)}, bf16[1936,128]{1,0:T(8,128)(2,1)S(1)}, u32[]{:S(2)}, u32[]{:S(2)}) %collective-permute-start.17) | collective-permute-done | bytes 495648 | tf_op jit(solution)/shard_map/ppermute | solution.py:22
  82.7 0.7 collective-permute-done.18.refs_3_
  83.4 0.7 collective-permute-done.19.refs_4_
  84.1 23.2 %shard_map.40 = (bf16[56144,128]{1,0:T(8,128)(2,1)S(1)}, bf16[29,128,128]{2,1,0:T(8,128)(2,1)}) custom-call(bf16[2960,128]{1,0:T(8,128)(2,1)S(1)} %collective-permute-done.15.refs_0_, bf16[2848,128]{1,0:T(8,128)(2,1)S(1)} %collective-permute-done.16.refs_1_, bf16[1936,128]{1,0:T(8,128)(2,1)S(1)} %collective-permute-done.17.refs_2_, ...), custom_call_target="tpu_custom_call", output_to_operand_aliasing={{0}: (5, {})} | custom-call | flops 16999999488 | bytes 15728640 | tf_op jit(solution)/shard_map/pallas_call | solution.py:284
  (32 shorter events, 3.8 us)
Async XLA Ops:
  1.9 15.3 %collective-permute-start = (bf16[1936,128]{1,0:T(8,128)(2,1)}, bf16[1936,128]{1,0:T(8,128)(2,1)S(1)}, u32[]{:S(2)}, u32[]{:S(2)}) collective-permute-start(bf16[1936,128]{1,0:T(8,128)(2,1)} %shard_map.37.refs_0_), channel_id=1, source_target_pairs={{0,1},{1,0},{2,3},{3,2},{4,5},{5,4},{6,7},{7,6},{8,9},{9,8},{10,11... | collective-permute-start | bytes 1486856 | tf_op jit(solution)/shard_map/ppermute | solution.py:22
  4.9 23.6 %collective-permute-start.1 = (bf16[1936,128]{1,0:T(8,128)(2,1)}, bf16[1936,128]{1,0:T(8,128)(2,1)S(1)}, u32[]{:S(2)}, u32[]{:S(2)}) collective-permute-start(bf16[1936,128]{1,0:T(8,128)(2,1)} %shard_map.37.refs_0_), channel_id=1, source_target_pairs={{0,16},{1,17},{2,18},{3,19},{4,20},{5,21},{6,22},{7,23},{8,24},{9,... | collective-permute-start | bytes 1486856 | tf_op jit(solution)/shard_map/ppermute | solution.py:22
  6.4 22.2 %collective-permute-start.2 = (bf16[1936,128]{1,0:T(8,128)(2,1)}, bf16[1936,128]{1,0:T(8,128)(2,1)S(1)}, u32[]{:S(2)}, u32[]{:S(2)}) collective-permute-start(bf16[1936,128]{1,0:T(8,128)(2,1)} %shard_map.37.refs_0_), channel_id=1, source_target_pairs={{0,17},{1,16},{2,19},{3,18},{4,21},{5,20},{6,23},{7,22},{8,25},{9,... | collective-permute-start | bytes 1486856 | tf_op jit(solution)/shard_map/ppermute | solution.py:22
  6.4 22.2 %collective-permute-start.3 = (bf16[1936,128]{1,0:T(8,128)(2,1)}, bf16[1936,128]{1,0:T(8,128)(2,1)S(1)}, u32[]{:S(2)}, u32[]{:S(2)}) collective-permute-start(bf16[1936,128]{1,0:T(8,128)(2,1)} %shard_map.37.refs_0_), channel_id=1, source_target_pairs={{0,2},{1,3},{2,0},{3,1},{4,6},{5,7},{6,4},{7,5},{8,10},{9,11},{10,... | collective-permute-start | bytes 1486856 | tf_op jit(solution)/shard_map/ppermute | solution.py:22
  8.4 23.6 %collective-permute-start.4 = (bf16[1936,128]{1,0:T(8,128)(2,1)}, bf16[1936,128]{1,0:T(8,128)(2,1)S(1)}, u32[]{:S(2)}, u32[]{:S(2)}) collective-permute-start(bf16[1936,128]{1,0:T(8,128)(2,1)} %shard_map.37.refs_0_), channel_id=1, source_target_pairs={{0,6},{1,7},{2,4},{3,5},{4,2},{5,3},{6,0},{7,1},{8,14},{9,15},{10,... | collective-permute-start | bytes 1486856 | tf_op jit(solution)/shard_map/ppermute | solution.py:22
  28.7 34.4 %copy-start = (bf16[1936,128]{1,0:T(8,128)(2,1)S(1)}, bf16[1936,128]{1,0:T(8,128)(2,1)}, u32[]{:S(2)}) copy-start(bf16[1936,128]{1,0:T(8,128)(2,1)} %shard_map.37.refs_0_) | copy-start | bytes 1486852
  32.2 26.9 %collective-permute-start.5 = (bf16[11616,128]{1,0:T(8,128)(2,1)S(1)}, bf16[11616,128]{1,0:T(8,128)(2,1)S(1)}, u32[]{:S(2)}, u32[]{:S(2)}) collective-permute-start(bf16[11616,128]{1,0:T(8,128)(2,1)S(1)} %get-tuple-element.30), channel_id=1, source_target_pairs={{0,8},{1,9},{2,10},{3,11},{4,12},{5,13},{6,14},{7,15},{8,0},{9,1},... | collective-permute-start | bytes 8921096 | tf_op jit(solution)/shard_map/ppermute | solution.py:22
  32.2 26.8 %collective-permute-start.6 = (bf16[3872,128]{1,0:T(8,128)(2,1)S(1)}, bf16[3872,128]{1,0:T(8,128)(2,1)S(1)}, u32[]{:S(2)}, u32[]{:S(2)}) collective-permute-start(bf16[3872,128]{1,0:T(8,128)(2,1)S(1)} %get-tuple-element.29), channel_id=1, source_target_pairs={{0,1},{1,0},{2,3},{3,2},{4,5},{5,4},{6,7},{7,6},{8,9},{9,8},{10,11... | collective-permute-start | bytes 2973704 | tf_op jit(solution)/shard_map/ppermute | solution.py:22
  33.8 25.2 %collective-permute-start.7 = (bf16[3872,128]{1,0:T(8,128)(2,1)S(1)}, bf16[3872,128]{1,0:T(8,128)(2,1)S(1)}, u32[]{:S(2)}, u32[]{:S(2)}) collective-permute-start(bf16[3872,128]{1,0:T(8,128)(2,1)S(1)} %get-tuple-element.29), channel_id=1, source_target_pairs={{0,16},{1,17},{2,18},{3,19},{4,20},{5,21},{6,22},{7,23},{8,24},{9,... | collective-permute-start | bytes 2973704 | tf_op jit(solution)/shard_map/ppermute | solution.py:22
  35.3 23.7 %collective-permute-start.8 = (bf16[1936,128]{1,0:T(8,128)(2,1)S(1)}, bf16[1936,128]{1,0:T(8,128)(2,1)S(1)}, u32[]{:S(2)}, u32[]{:S(2)}) collective-permute-start(bf16[1936,128]{1,0:T(8,128)(2,1)S(1)} %collective-permute-done.4.refs_5_), channel_id=1, source_target_pairs={{0,2},{1,3},{2,0},{3,1},{4,6},{5,7},{6,4},{7,5},{8,10},{9,11},{10,... | collective-permute-start | bytes 1486856 | tf_op jit(solution)/shard_map/ppermute | solution.py:22
  35.9 25.1 %collective-permute-start.11 = (bf16[1936,128]{1,0:T(8,128)(2,1)S(1)}, bf16[1936,128]{1,0:T(8,128)(2,1)S(1)}, u32[]{:S(2)}, u32[]{:S(2)}) collective-permute-start(bf16[1936,128]{1,0:T(8,128)(2,1)S(1)} %collective-permute-done.2.refs_3_), channel_id=1, source_target_pairs={{0,4},{1,5},{2,6},{3,7},{4,0},{5,1},{6,2},{7,3},{8,12},{9,13},{10,... | collective-permute-start | bytes 1486856 | tf_op jit(solution)/shard_map/ppermute | solution.py:22
  59.1 2.6 %collective-permute-start.10 = (bf16[3872,128]{1,0:T(8,128)(2,1)S(1)}, bf16[3872,128]{1,0:T(8,128)(2,1)S(1)}, u32[]{:S(2)}, u32[]{:S(2)}) collective-permute-start(bf16[3872,128]{1,0:T(8,128)(2,1)S(1)} %collective-permute-done.7.refs_9_), channel_id=1, source_target_pairs={{0,8},{1,9},{2,10},{3,11},{4,12},{5,13},{6,14},{7,15},{8,0},{9,1},... | collective-permute-start | bytes 2973704 | tf_op jit(solution)/shard_map/ppermute | solution.py:22
  59.2 4.0 %collective-permute-start.9 = (bf16[3872,128]{1,0:T(8,128)(2,1)S(1)}, bf16[3872,128]{1,0:T(8,128)(2,1)S(1)}, u32[]{:S(2)}, u32[]{:S(2)}) collective-permute-start(bf16[3872,128]{1,0:T(8,128)(2,1)S(1)} %collective-permute-done.6.refs_7_), channel_id=1, source_target_pairs={{0,8},{1,9},{2,10},{3,11},{4,12},{5,13},{6,14},{7,15},{8,0},{9,1},... | collective-permute-start | bytes 2973704 | tf_op jit(solution)/shard_map/ppermute | solution.py:22
  59.8 18.9 %collective-permute-start.12 = (bf16[2960,128]{1,0:T(8,128)(2,1)S(1)}, bf16[2960,128]{1,0:T(8,128)(2,1)S(1)}, u32[]{:S(2)}, u32[]{:S(2)}) collective-permute-start(bf16[2960,128]{1,0:T(8,128)(2,1)S(1)} %pad_maximum_fusion), channel_id=1, source_target_pairs={{0,1},{1,0},{2,3},{3,2},{4,5},{5,4},{6,7},{7,6},{8,9},{9,8},{10,11... | collective-permute-start | bytes 2273288 | tf_op jit(solution)/shard_map/ppermute | solution.py:22
  60.4 18.0 %collective-permute-start.13 = (bf16[2848,128]{1,0:T(8,128)(2,1)S(1)}, bf16[2848,128]{1,0:T(8,128)(2,1)S(1)}, u32[]{:S(2)}, u32[]{:S(2)}) collective-permute-start(bf16[2848,128]{1,0:T(8,128)(2,1)S(1)} %pad_maximum_fusion.1), channel_id=1, source_target_pairs={{0,16},{1,17},{2,18},{3,19},{4,20},{5,21},{6,22},{7,23},{8,24},{9,... | collective-permute-start | bytes 2187272 | tf_op jit(solution)/shard_map/ppermute | solution.py:22
  61.0 12.7 %collective-permute-start.14 = (bf16[1936,128]{1,0:T(8,128)(2,1)S(1)}, bf16[1936,128]{1,0:T(8,128)(2,1)S(1)}, u32[]{:S(2)}, u32[]{:S(2)}) collective-permute-start(bf16[1936,128]{1,0:T(8,128)(2,1)S(1)} %collective-permute-done.2.refs_3_), channel_id=1, source_target_pairs={{0,2},{1,3},{2,0},{3,1},{4,6},{5,7},{6,4},{7,5},{8,10},{9,11},{10,... | collective-permute-start | bytes 1486856 | tf_op jit(solution)/shard_map/ppermute | solution.py:22
  78.7 5.4 %collective-permute-start.15 = (bf16[2960,128]{1,0:T(8,128)(2,1)S(1)}, bf16[2960,128]{1,0:T(8,128)(2,1)S(1)}, u32[]{:S(2)}, u32[]{:S(2)}) collective-permute-start(bf16[2960,128]{1,0:T(8,128)(2,1)S(1)} %collective-permute-done.12.refs_0_), channel_id=1, source_target_pairs={{0,8},{1,9},{2,10},{3,11},{4,12},{5,13},{6,14},{7,15},{8,0},{9,1},... | collective-permute-start | bytes 2273288 | tf_op jit(solution)/shard_map/ppermute | solution.py:22
  78.7 5.4 %collective-permute-start.16 = (bf16[2848,128]{1,0:T(8,128)(2,1)S(1)}, bf16[2848,128]{1,0:T(8,128)(2,1)S(1)}, u32[]{:S(2)}, u32[]{:S(2)}) collective-permute-start(bf16[2848,128]{1,0:T(8,128)(2,1)S(1)} %collective-permute-done.13.refs_1_), channel_id=1, source_target_pairs={{0,8},{1,9},{2,10},{3,11},{4,12},{5,13},{6,14},{7,15},{8,0},{9,1},... | collective-permute-start | bytes 2187272 | tf_op jit(solution)/shard_map/ppermute | solution.py:22
  79.2 3.5 %collective-permute-start.17 = (bf16[1936,128]{1,0:T(8,128)(2,1)S(1)}, bf16[1936,128]{1,0:T(8,128)(2,1)S(1)}, u32[]{:S(2)}, u32[]{:S(2)}) collective-permute-start(bf16[1936,128]{1,0:T(8,128)(2,1)S(1)} %collective-permute-done.8.refs_11_), channel_id=1, source_target_pairs={{0,8},{1,9},{2,10},{3,11},{4,12},{5,13},{6,14},{7,15},{8,0},{9,1},... | collective-permute-start | bytes 1486856 | tf_op jit(solution)/shard_map/ppermute | solution.py:22
  79.2 4.2 %collective-permute-start.18 = (bf16[1936,128]{1,0:T(8,128)(2,1)S(1)}, bf16[1936,128]{1,0:T(8,128)(2,1)S(1)}, u32[]{:S(2)}, u32[]{:S(2)}) collective-permute-start(bf16[1936,128]{1,0:T(8,128)(2,1)S(1)} %collective-permute-done.11.refs_12_), channel_id=1, source_target_pairs={{0,8},{1,9},{2,10},{3,11},{4,12},{5,13},{6,14},{7,15},{8,0},{9,1},... | collective-permute-start | bytes 1486856 | tf_op jit(solution)/shard_map/ppermute | solution.py:22
  79.7 4.4 %collective-permute-start.19 = (bf16[1936,128]{1,0:T(8,128)(2,1)S(1)}, bf16[1936,128]{1,0:T(8,128)(2,1)S(1)}, u32[]{:S(2)}, u32[]{:S(2)}) collective-permute-start(bf16[1936,128]{1,0:T(8,128)(2,1)S(1)} %collective-permute-done.14.refs_2_), channel_id=1, source_target_pairs={{0,8},{1,9},{2,10},{3,11},{4,12},{5,13},{6,14},{7,15},{8,0},{9,1},... | collective-permute-start | bytes 1486856 | tf_op jit(solution)/shard_map/ppermute | solution.py:22

commit v16 on v15

--- a/solution.py
+++ b/solution.py
@@ -42,7 +42,7 @@
     spot = cross(
         (own, whole(0)), (x0, whole(x)), (y0, whole(y)), (d0, whole(x | y)), (f1, whole(z1)), (f3, whole(z3))
     )
-    xp, yp, f2, d0 = finish(spot, xp, yp, f2, d0)
+    yp, xp, f2, d0 = finish(spot, yp, xp, f2, d0)
     xl = swap(jnp.concatenate([f2, yp[full : full + cut]], axis=0), x)
     yl = swap(jnp.concatenate([f2, xp[full + cut :]], axis=0), y)
     d1 = swap(d0, z1)

time: 108 us -> 108 us (level)
  no operation moved by 1% of the time
where the time goes in v16:
time: 108 us; the launch traced here: 107 us
  waiting for transfers between devices  54.3 us (50%)
  Pallas kernels  33.9 us (31%)
  starting transfers between devices  17.5 us (16%)
  local copies, waits for them, and re-layouts  1.56 us (1%)
    ppermute x20, waiting for transfers between devices, swap(): return lax.ppermute(value, AXES, [(i, i ^ mask) for i in range(count)])  54.3 us
    pallas_call x1, Pallas kernels, shards(): pl.pallas_call(functools.partial(purify, reach, edge, layout), out_shape=...  23.2 us
    ppermute x20, starting transfers between devices, swap(): return lax.ppermute(value, AXES, [(i, i ^ mask) for i in range(count)])  17.5 us
    pallas_call x2, Pallas kernels, assemble(): pl.pallas_call(body, out_shape=pltpu.VMEM((rows * pitch, edge), kind), in...  8.71 us
  transfers between devices with their start and end apart: 20, of which 12 were waited for; matrix products, arithmetic and copies ran while one was open for 1% of the time, Pallas kernels for 8%

profile of v16, /device:TPU:0, one launch (start us, length us, event | category | flops | bytes accessed | tf_op | source)
XLA Modules:
  0.0 107.4 jit_solution(18357695845836204095)
XLA Ops:
  0.0 1.9 %shard_map.37.refs_0_ = bf16[1936,128]{1,0:T(8,128)(2,1)} custom-call(s32[1,15]{1,0:T(1,128)} %pattern.1, s32[1,29]{1,0:T(1,128)} %filter_mask.1, bf16[15,128,128]{2,1,0:T(8,128)(2,1)} %bitcast.2), custom_call_target="tpu_custom_call" | custom-call | tf_op jit(solution)/shard_map/pallas_call | solution.py:274
  1.9 2.9 %collective-permute-start = (bf16[1936,128]{1,0:T(8,128)(2,1)}, bf16[1936,128]{1,0:T(8,128)(2,1)S(1)}, u32[]{:S(2)}, u32[]{:S(2)}) collective-permute-start(bf16[1936,128]{1,0:T(8,128)(2,1)} %shard_map.37.refs_0_), channel_id=1, source_target_pairs={{0,1},{1,0},{2,3},{3,2},{4,5},{5,4},{6,7},{7,6},{8,9},{9,8},{10,11... | collective-permute-start | bytes 1486856 | tf_op jit(solution)/shard_map/ppermute | solution.py:22
  4.9 1.5 %collective-permute-start.1 = (bf16[1936,128]{1,0:T(8,128)(2,1)}, bf16[1936,128]{1,0:T(8,128)(2,1)S(1)}, u32[]{:S(2)}, u32[]{:S(2)}) collective-permute-start(bf16[1936,128]{1,0:T(8,128)(2,1)} %shard_map.37.refs_0_), channel_id=1, source_target_pairs={{0,16},{1,17},{2,18},{3,19},{4,20},{5,21},{6,22},{7,23},{8,24},{9,... | collective-permute-start | bytes 1486856 | tf_op jit(solution)/shard_map/ppermute | solution.py:22
  6.4 2.1 %collective-permute-start.3 = (bf16[1936,128]{1,0:T(8,128)(2,1)}, bf16[1936,128]{1,0:T(8,128)(2,1)S(1)}, u32[]{:S(2)}, u32[]{:S(2)}) collective-permute-start(bf16[1936,128]{1,0:T(8,128)(2,1)} %shard_map.37.refs_0_), channel_id=1, source_target_pairs={{0,2},{1,3},{2,0},{3,1},{4,6},{5,7},{6,4},{7,5},{8,10},{9,11},{10,... | collective-permute-start | bytes 1486856 | tf_op jit(solution)/shard_map/ppermute | solution.py:22
  8.4 2.5 %collective-permute-start.4 = (bf16[1936,128]{1,0:T(8,128)(2,1)}, bf16[1936,128]{1,0:T(8,128)(2,1)S(1)}, u32[]{:S(2)}, u32[]{:S(2)}) collective-permute-start(bf16[1936,128]{1,0:T(8,128)(2,1)} %shard_map.37.refs_0_), channel_id=1, source_target_pairs={{0,6},{1,7},{2,4},{3,5},{4,2},{5,3},{6,0},{7,1},{8,14},{9,15},{10,... | collective-permute-start | bytes 1486856 | tf_op jit(solution)/shard_map/ppermute | solution.py:22
  10.9 1.1 %constant_dynamic-update-slice_fusion.5 = bf16[11616,128]{1,0:T(8,128)(2,1)S(1)} fusion(bf16[1936,128]{1,0:T(8,128)(2,1)} %shard_map.37.refs_0_), kind=kLoop, calls=%fused_computation.7 | loop fusion | bytes 991232
  12.0 5.2 %collective-permute-done.refs_1_ = bf16[1936,128]{1,0:T(8,128)(2,1)S(1)} collective-permute-done((bf16[1936,128]{1,0:T(8,128)(2,1)}, bf16[1936,128]{1,0:T(8,128)(2,1)S(1)}, u32[]{:S(2)}, u32[]{:S(2)}) %collective-permute-start) | collective-permute-done | bytes 495648 | tf_op jit(solution)/shard_map/ppermute | solution.py:22
  17.3 11.2 %collective-permute-done.1.refs_2_ = bf16[1936,128]{1,0:T(8,128)(2,1)S(1)} collective-permute-done((bf16[1936,128]{1,0:T(8,128)(2,1)}, bf16[1936,128]{1,0:T(8,128)(2,1)S(1)}, u32[]{:S(2)}, u32[]{:S(2)}) %collective-permute-start.1) | collective-permute-done | bytes 495648 | tf_op jit(solution)/shard_map/ppermute | solution.py:22
  28.7 3.3 %collective-permute-done.4.refs_5_ = bf16[1936,128]{1,0:T(8,128)(2,1)S(1)} collective-permute-done((bf16[1936,128]{1,0:T(8,128)(2,1)}, bf16[1936,128]{1,0:T(8,128)(2,1)S(1)}, u32[]{:S(2)}, u32[]{:S(2)}) %collective-permute-start.4) | collective-permute-done | bytes 495648 | tf_op jit(solution)/shard_map/ppermute | solution.py:22
  32.2 1.6 %collective-permute-start.6 = (bf16[3872,128]{1,0:T(8,128)(2,1)S(1)}, bf16[3872,128]{1,0:T(8,128)(2,1)S(1)}, u32[]{:S(2)}, u32[]{:S(2)}) collective-permute-start(bf16[3872,128]{1,0:T(8,128)(2,1)S(1)} %get-tuple-element.29), channel_id=1, source_target_pairs={{0,16},{1,17},{2,18},{3,19},{4,20},{5,21},{6,22},{7,23},{8,24},{9,... | collective-permute-start | bytes 2973704 | tf_op jit(solution)/shard_map/ppermute | solution.py:22
  33.8 1.5 %collective-permute-start.7 = (bf16[3872,128]{1,0:T(8,128)(2,1)S(1)}, bf16[3872,128]{1,0:T(8,128)(2,1)S(1)}, u32[]{:S(2)}, u32[]{:S(2)}) collective-permute-start(bf16[3872,128]{1,0:T(8,128)(2,1)S(1)} %get-tuple-element.29), channel_id=1, source_target_pairs={{0,1},{1,0},{2,3},{3,2},{4,5},{5,4},{6,7},{7,6},{8,9},{9,8},{10,11... | collective-permute-start | bytes 2973704 | tf_op jit(solution)/shard_map/ppermute | solution.py:22
  35.3 0.6 collective-permute-start.8
  35.9 1.6 %collective-permute-start.11 = (bf16[1936,128]{1,0:T(8,128)(2,1)S(1)}, bf16[1936,128]{1,0:T(8,128)(2,1)S(1)}, u32[]{:S(2)}, u32[]{:S(2)}) collective-permute-start(bf16[1936,128]{1,0:T(8,128)(2,1)S(1)} %collective-permute-done.2.refs_3_), channel_id=1, source_target_pairs={{0,4},{1,5},{2,6},{3,7},{4,0},{5,1},{6,2},{7,3},{8,12},{9,13},{10,... | collective-permute-start | bytes 1486856 | tf_op jit(solution)/shard_map/ppermute | solution.py:22
  37.5 21.6 %collective-permute-done.8.refs_11_ = bf16[1936,128]{1,0:T(8,128)(2,1)S(1)} collective-permute-done((bf16[1936,128]{1,0:T(8,128)(2,1)S(1)}, bf16[1936,128]{1,0:T(8,128)(2,1)S(1)}, u32[]{:S(2)}, u32[]{:S(2)}) %collective-permute-start.8) | collective-permute-done | bytes 495648 | tf_op jit(solution)/shard_map/ppermute | solution.py:22
  59.8 0.6 collective-permute-start.12
  61.7 1.4 %collective-permute-done.9.refs_8_ = bf16[3872,128]{1,0:T(8,128)(2,1)S(1)} collective-permute-done((bf16[3872,128]{1,0:T(8,128)(2,1)S(1)}, bf16[3872,128]{1,0:T(8,128)(2,1)S(1)}, u32[]{:S(2)}, u32[]{:S(2)}) %collective-permute-start.9) | collective-permute-done | bytes 991264 | tf_op jit(solution)/shard_map/ppermute | solution.py:22
  63.1 7.4 %shard_map.38.refs_3_ = bf16[56144,128]{1,0:T(8,128)(2,1)S(1)} custom-call(bf16[1936,128]{1,0:T(8,128)(2,1)S(1)} %copy-done, bf16[1936,128]{1,0:T(8,128)(2,1)S(1)} %collective-permute-done.refs_1_, bf16[1936,128]{1,0:T(8,128)(2,1)S(1)} %collective-permute-done.1.refs_2_, bf16[1936,128]{1,0:T(8,128)(2,1)S(1)} %collective-permute-done.2.refs_3_, ...), custom_call_target="tpu_custom_call" | custom-call | bytes 21807104 | tf_op jit(solution)/shard_map/pallas_call | solution.py:146
  70.5 3.2 %collective-permute-done.14.refs_2_ = bf16[1936,128]{1,0:T(8,128)(2,1)S(1)} collective-permute-done((bf16[1936,128]{1,0:T(8,128)(2,1)S(1)}, bf16[1936,128]{1,0:T(8,128)(2,1)S(1)}, u32[]{:S(2)}, u32[]{:S(2)}) %collective-permute-start.14) | collective-permute-done | bytes 495648 | tf_op jit(solution)/shard_map/ppermute | solution.py:22
  73.7 4.8 %collective-permute-done.13.refs_1_ = bf16[2848,128]{1,0:T(8,128)(2,1)S(1)} collective-permute-done((bf16[2848,128]{1,0:T(8,128)(2,1)S(1)}, bf16[2848,128]{1,0:T(8,128)(2,1)S(1)}, u32[]{:S(2)}, u32[]{:S(2)}) %collective-permute-start.13) | collective-permute-done | bytes 729120 | tf_op jit(solution)/shard_map/ppermute | solution.py:22
  79.7 1.3 %shard_map.39.refs_5_ = bf16[56144,128]{1,0:T(8,128)(2,1)S(1)} custom-call(bf16[2960,128]{1,0:T(8,128)(2,1)S(1)} %collective-permute-done.12.refs_0_, bf16[2848,128]{1,0:T(8,128)(2,1)S(1)} %collective-permute-done.13.refs_1_, bf16[1936,128]{1,0:T(8,128)(2,1)S(1)} %collective-permute-done.14.refs_2_, ...), custom_call_target="tpu_custom_call", output_to_operand_aliasing={{}: (3, {})} | custom-call | bytes 3964928 | tf_op jit(solution)/shard_map/pallas_call | solution.py:146
  81.1 1.6 %collective-permute-done.17.refs_2_ = bf16[1936,128]{1,0:T(8,128)(2,1)S(1)} collective-permute-done((bf16[1936,128]{1,0:T(8,128)(2,1)S(1)}, bf16[1936,128]{1,0:T(8,128)(2,1)S(1)}, u32[]{:S(2)}, u32[]{:S(2)}) %collective-permute-start.17) | collective-permute-done | bytes 495648 | tf_op jit(solution)/shard_map/ppermute | solution.py:22
  82.7 0.7 collective-permute-done.18.refs_3_
  83.4 0.7 collective-permute-done.19.refs_4_
  84.1 23.2 %shard_map.40 = (bf16[56144,128]{1,0:T(8,128)(2,1)S(1)}, bf16[29,128,128]{2,1,0:T(8,128)(2,1)}) custom-call(bf16[2960,128]{1,0:T(8,128)(2,1)S(1)} %collective-permute-done.15.refs_0_, bf16[2848,128]{1,0:T(8,128)(2,1)S(1)} %collective-permute-done.16.refs_1_, bf16[1936,128]{1,0:T(8,128)(2,1)S(1)} %collective-permute-done.17.refs_2_, ...), custom_call_target="tpu_custom_call", output_to_operand_aliasing={{0}: (5, {})} | custom-call | flops 16999999488 | bytes 15728640 | tf_op jit(solution)/shard_map/pallas_call | solution.py:284
  (32 shorter events, 3.8 us)
Async XLA Ops:
  1.9 15.3 %collective-permute-start = (bf16[1936,128]{1,0:T(8,128)(2,1)}, bf16[1936,128]{1,0:T(8,128)(2,1)S(1)}, u32[]{:S(2)}, u32[]{:S(2)}) collective-permute-start(bf16[1936,128]{1,0:T(8,128)(2,1)} %shard_map.37.refs_0_), channel_id=1, source_target_pairs={{0,1},{1,0},{2,3},{3,2},{4,5},{5,4},{6,7},{7,6},{8,9},{9,8},{10,11... | collective-permute-start | bytes 1486856 | tf_op jit(solution)/shard_map/ppermute | solution.py:22
  4.9 23.6 %collective-permute-start.1 = (bf16[1936,128]{1,0:T(8,128)(2,1)}, bf16[1936,128]{1,0:T(8,128)(2,1)S(1)}, u32[]{:S(2)}, u32[]{:S(2)}) collective-permute-start(bf16[1936,128]{1,0:T(8,128)(2,1)} %shard_map.37.refs_0_), channel_id=1, source_target_pairs={{0,16},{1,17},{2,18},{3,19},{4,20},{5,21},{6,22},{7,23},{8,24},{9,... | collective-permute-start | bytes 1486856 | tf_op jit(solution)/shard_map/ppermute | solution.py:22
  6.4 22.2 %collective-permute-start.2 = (bf16[1936,128]{1,0:T(8,128)(2,1)}, bf16[1936,128]{1,0:T(8,128)(2,1)S(1)}, u32[]{:S(2)}, u32[]{:S(2)}) collective-permute-start(bf16[1936,128]{1,0:T(8,128)(2,1)} %shard_map.37.refs_0_), channel_id=1, source_target_pairs={{0,17},{1,16},{2,19},{3,18},{4,21},{5,20},{6,23},{7,22},{8,25},{9,... | collective-permute-start | bytes 1486856 | tf_op jit(solution)/shard_map/ppermute | solution.py:22
  6.4 22.2 %collective-permute-start.3 = (bf16[1936,128]{1,0:T(8,128)(2,1)}, bf16[1936,128]{1,0:T(8,128)(2,1)S(1)}, u32[]{:S(2)}, u32[]{:S(2)}) collective-permute-start(bf16[1936,128]{1,0:T(8,128)(2,1)} %shard_map.37.refs_0_), channel_id=1, source_target_pairs={{0,2},{1,3},{2,0},{3,1},{4,6},{5,7},{6,4},{7,5},{8,10},{9,11},{10,... | collective-permute-start | bytes 1486856 | tf_op jit(solution)/shard_map/ppermute | solution.py:22
  8.4 23.6 %collective-permute-start.4 = (bf16[1936,128]{1,0:T(8,128)(2,1)}, bf16[1936,128]{1,0:T(8,128)(2,1)S(1)}, u32[]{:S(2)}, u32[]{:S(2)}) collective-permute-start(bf16[1936,128]{1,0:T(8,128)(2,1)} %shard_map.37.refs_0_), channel_id=1, source_target_pairs={{0,6},{1,7},{2,4},{3,5},{4,2},{5,3},{6,0},{7,1},{8,14},{9,15},{10,... | collective-permute-start | bytes 1486856 | tf_op jit(solution)/shard_map/ppermute | solution.py:22
  28.7 34.4 %copy-start = (bf16[1936,128]{1,0:T(8,128)(2,1)S(1)}, bf16[1936,128]{1,0:T(8,128)(2,1)}, u32[]{:S(2)}) copy-start(bf16[1936,128]{1,0:T(8,128)(2,1)} %shard_map.37.refs_0_) | copy-start | bytes 1486852
  32.2 26.9 %collective-permute-start.5 = (bf16[11616,128]{1,0:T(8,128)(2,1)S(1)}, bf16[11616,128]{1,0:T(8,128)(2,1)S(1)}, u32[]{:S(2)}, u32[]{:S(2)}) collective-permute-start(bf16[11616,128]{1,0:T(8,128)(2,1)S(1)} %get-tuple-element.30), channel_id=1, source_target_pairs={{0,8},{1,9},{2,10},{3,11},{4,12},{5,13},{6,14},{7,15},{8,0},{9,1},... | collective-permute-start | bytes 8921096 | tf_op jit(solution)/shard_map/ppermute | solution.py:22
  32.2 26.8 %collective-permute-start.6 = (bf16[3872,128]{1,0:T(8,128)(2,1)S(1)}, bf16[3872,128]{1,0:T(8,128)(2,1)S(1)}, u32[]{:S(2)}, u32[]{:S(2)}) collective-permute-start(bf16[3872,128]{1,0:T(8,128)(2,1)S(1)} %get-tuple-element.29), channel_id=1, source_target_pairs={{0,16},{1,17},{2,18},{3,19},{4,20},{5,21},{6,22},{7,23},{8,24},{9,... | collective-permute-start | bytes 2973704 | tf_op jit(solution)/shard_map/ppermute | solution.py:22
  33.8 25.2 %collective-permute-start.7 = (bf16[3872,128]{1,0:T(8,128)(2,1)S(1)}, bf16[3872,128]{1,0:T(8,128)(2,1)S(1)}, u32[]{:S(2)}, u32[]{:S(2)}) collective-permute-start(bf16[3872,128]{1,0:T(8,128)(2,1)S(1)} %get-tuple-element.29), channel_id=1, source_target_pairs={{0,1},{1,0},{2,3},{3,2},{4,5},{5,4},{6,7},{7,6},{8,9},{9,8},{10,11... | collective-permute-start | bytes 2973704 | tf_op jit(solution)/shard_map/ppermute | solution.py:22
  35.3 23.7 %collective-permute-start.8 = (bf16[1936,128]{1,0:T(8,128)(2,1)S(1)}, bf16[1936,128]{1,0:T(8,128)(2,1)S(1)}, u32[]{:S(2)}, u32[]{:S(2)}) collective-permute-start(bf16[1936,128]{1,0:T(8,128)(2,1)S(1)} %collective-permute-done.4.refs_5_), channel_id=1, source_target_pairs={{0,2},{1,3},{2,0},{3,1},{4,6},{5,7},{6,4},{7,5},{8,10},{9,11},{10,... | collective-permute-start | bytes 1486856 | tf_op jit(solution)/shard_map/ppermute | solution.py:22
  35.9 25.1 %collective-permute-start.11 = (bf16[1936,128]{1,0:T(8,128)(2,1)S(1)}, bf16[1936,128]{1,0:T(8,128)(2,1)S(1)}, u32[]{:S(2)}, u32[]{:S(2)}) collective-permute-start(bf16[1936,128]{1,0:T(8,128)(2,1)S(1)} %collective-permute-done.2.refs_3_), channel_id=1, source_target_pairs={{0,4},{1,5},{2,6},{3,7},{4,0},{5,1},{6,2},{7,3},{8,12},{9,13},{10,... | collective-permute-start | bytes 1486856 | tf_op jit(solution)/shard_map/ppermute | solution.py:22
  59.1 2.6 %collective-permute-start.10 = (bf16[3872,128]{1,0:T(8,128)(2,1)S(1)}, bf16[3872,128]{1,0:T(8,128)(2,1)S(1)}, u32[]{:S(2)}, u32[]{:S(2)}) collective-permute-start(bf16[3872,128]{1,0:T(8,128)(2,1)S(1)} %collective-permute-done.6.refs_9_), channel_id=1, source_target_pairs={{0,8},{1,9},{2,10},{3,11},{4,12},{5,13},{6,14},{7,15},{8,0},{9,1},... | collective-permute-start | bytes 2973704 | tf_op jit(solution)/shard_map/ppermute | solution.py:22
  59.2 4.0 %collective-permute-start.9 = (bf16[3872,128]{1,0:T(8,128)(2,1)S(1)}, bf16[3872,128]{1,0:T(8,128)(2,1)S(1)}, u32[]{:S(2)}, u32[]{:S(2)}) collective-permute-start(bf16[3872,128]{1,0:T(8,128)(2,1)S(1)} %collective-permute-done.7.refs_7_), channel_id=1, source_target_pairs={{0,8},{1,9},{2,10},{3,11},{4,12},{5,13},{6,14},{7,15},{8,0},{9,1},... | collective-permute-start | bytes 2973704 | tf_op jit(solution)/shard_map/ppermute | solution.py:22
  59.8 18.9 %collective-permute-start.12 = (bf16[2960,128]{1,0:T(8,128)(2,1)S(1)}, bf16[2960,128]{1,0:T(8,128)(2,1)S(1)}, u32[]{:S(2)}, u32[]{:S(2)}) collective-permute-start(bf16[2960,128]{1,0:T(8,128)(2,1)S(1)} %pad_maximum_fusion), channel_id=1, source_target_pairs={{0,1},{1,0},{2,3},{3,2},{4,5},{5,4},{6,7},{7,6},{8,9},{9,8},{10,11... | collective-permute-start | bytes 2273288 | tf_op jit(solution)/shard_map/ppermute | solution.py:22
  60.4 18.0 %collective-permute-start.13 = (bf16[2848,128]{1,0:T(8,128)(2,1)S(1)}, bf16[2848,128]{1,0:T(8,128)(2,1)S(1)}, u32[]{:S(2)}, u32[]{:S(2)}) collective-permute-start(bf16[2848,128]{1,0:T(8,128)(2,1)S(1)} %pad_maximum_fusion.1), channel_id=1, source_target_pairs={{0,16},{1,17},{2,18},{3,19},{4,20},{5,21},{6,22},{7,23},{8,24},{9,... | collective-permute-start | bytes 2187272 | tf_op jit(solution)/shard_map/ppermute | solution.py:22
  61.0 12.7 %collective-permute-start.14 = (bf16[1936,128]{1,0:T(8,128)(2,1)S(1)}, bf16[1936,128]{1,0:T(8,128)(2,1)S(1)}, u32[]{:S(2)}, u32[]{:S(2)}) collective-permute-start(bf16[1936,128]{1,0:T(8,128)(2,1)S(1)} %collective-permute-done.2.refs_3_), channel_id=1, source_target_pairs={{0,2},{1,3},{2,0},{3,1},{4,6},{5,7},{6,4},{7,5},{8,10},{9,11},{10,... | collective-permute-start | bytes 1486856 | tf_op jit(solution)/shard_map/ppermute | solution.py:22
  78.7 5.4 %collective-permute-start.15 = (bf16[2960,128]{1,0:T(8,128)(2,1)S(1)}, bf16[2960,128]{1,0:T(8,128)(2,1)S(1)}, u32[]{:S(2)}, u32[]{:S(2)}) collective-permute-start(bf16[2960,128]{1,0:T(8,128)(2,1)S(1)} %collective-permute-done.12.refs_0_), channel_id=1, source_target_pairs={{0,8},{1,9},{2,10},{3,11},{4,12},{5,13},{6,14},{7,15},{8,0},{9,1},... | collective-permute-start | bytes 2273288 | tf_op jit(solution)/shard_map/ppermute | solution.py:22
  78.7 5.4 %collective-permute-start.16 = (bf16[2848,128]{1,0:T(8,128)(2,1)S(1)}, bf16[2848,128]{1,0:T(8,128)(2,1)S(1)}, u32[]{:S(2)}, u32[]{:S(2)}) collective-permute-start(bf16[2848,128]{1,0:T(8,128)(2,1)S(1)} %collective-permute-done.13.refs_1_), channel_id=1, source_target_pairs={{0,8},{1,9},{2,10},{3,11},{4,12},{5,13},{6,14},{7,15},{8,0},{9,1},... | collective-permute-start | bytes 2187272 | tf_op jit(solution)/shard_map/ppermute | solution.py:22
  79.2 3.5 %collective-permute-start.17 = (bf16[1936,128]{1,0:T(8,128)(2,1)S(1)}, bf16[1936,128]{1,0:T(8,128)(2,1)S(1)}, u32[]{:S(2)}, u32[]{:S(2)}) collective-permute-start(bf16[1936,128]{1,0:T(8,128)(2,1)S(1)} %collective-permute-done.8.refs_11_), channel_id=1, source_target_pairs={{0,8},{1,9},{2,10},{3,11},{4,12},{5,13},{6,14},{7,15},{8,0},{9,1},... | collective-permute-start | bytes 1486856 | tf_op jit(solution)/shard_map/ppermute | solution.py:22
  79.2 4.2 %collective-permute-start.18 = (bf16[1936,128]{1,0:T(8,128)(2,1)S(1)}, bf16[1936,128]{1,0:T(8,128)(2,1)S(1)}, u32[]{:S(2)}, u32[]{:S(2)}) collective-permute-start(bf16[1936,128]{1,0:T(8,128)(2,1)S(1)} %collective-permute-done.11.refs_12_), channel_id=1, source_target_pairs={{0,8},{1,9},{2,10},{3,11},{4,12},{5,13},{6,14},{7,15},{8,0},{9,1},... | collective-permute-start | bytes 1486856 | tf_op jit(solution)/shard_map/ppermute | solution.py:22
  79.7 4.4 %collective-permute-start.19 = (bf16[1936,128]{1,0:T(8,128)(2,1)S(1)}, bf16[1936,128]{1,0:T(8,128)(2,1)S(1)}, u32[]{:S(2)}, u32[]{:S(2)}) collective-permute-start(bf16[1936,128]{1,0:T(8,128)(2,1)S(1)} %collective-permute-done.14.refs_2_), channel_id=1, source_target_pairs={{0,8},{1,9},{2,10},{3,11},{4,12},{5,13},{6,14},{7,15},{8,0},{9,1},... | collective-permute-start | bytes 1486856 | tf_op jit(solution)/shard_map/ppermute | solution.py:22

commit v17 on v16

--- a/solution.py
+++ b/solution.py
@@ -37,17 +37,17 @@
         return arrays
 
     x0, y0, d0, f1, f3 = (swap(own, mask) for mask in (x, y, x | y, z1, z3))
-    pair = jnp.concatenate([f1, f3], axis=0)
+    pair = jnp.concatenate([f3, f1], axis=0)
     xp, yp, f2, d2 = swap(pair, x), swap(pair, y), swap(f3, z1), swap(d0, z2)
     spot = cross(
-        (own, whole(0)), (x0, whole(x)), (y0, whole(y)), (d0, whole(x | y)), (f1, whole(z1)), (f3, whole(z3))
+        (own, whole(0)), (x0, whole(x)), (y0, whole(y)), (f3, whole(z3)), (f1, whole(z1)), (d0, whole(x | y))
     )
     yp, xp, f2, d0 = finish(spot, yp, xp, f2, d0)
-    xl = swap(jnp.concatenate([f2, yp[full : full + cut]], axis=0), x)
-    yl = swap(jnp.concatenate([f2, xp[full + cut :]], axis=0), y)
+    xl = swap(jnp.concatenate([f2, yp[:cut]], axis=0), x)
+    yl = swap(jnp.concatenate([f2, xp[cut:full]], axis=0), y)
     d1 = swap(d0, z1)
-    cross((xp, whole(z1 | x, z3 | x)))
-    cross((yp, whole(z1 | y, z3 | y)))
+    cross((xp, whole(z3 | x, z1 | x)))
+    cross((yp, whole(z3 | y, z1 | y)))
     band = gather(None, found + [(f2, whole(z2)), (d2, whole(z2 | x | y))])
     band, xl, yl, d1, f2, d2 = lax.optimization_barrier((band, xl, yl, d1, f2, d2))
     del found[:]

time: 108 us -> 105 us (0.972)
  waiting for transfers between devices: 54.3 us -> 51.8 us
    ppermute x20, waiting for transfers between devices: 54.3 us -> 51.8 us  [swap(): return lax.ppermute(value, AXES, [(i, i ^ mask) for i in range(count)])]
  transfers between devices with their start and end apart: 20 -> 20, of which waited for: 12 -> 12; matrix products, arithmetic and copies ran while one was open for 1% -> 2% of each run, Pallas kernels for 8% -> 8%
where the time goes in v17:
time: 105 us
  waiting for transfers between devices  51.8 us (49%)
  Pallas kernels  33.9 us (32%)
  starting transfers between devices  17.4 us (17%)
  local copies, waits for them, and re-layouts  1.56 us (1%)
    ppermute x20, waiting for transfers between devices, swap(): return lax.ppermute(value, AXES, [(i, i ^ mask) for i in range(count)])  51.8 us
    pallas_call x1, Pallas kernels, shards(): pl.pallas_call(functools.partial(purify, reach, edge, layout), out_shape=...  23.2 us
    ppermute x20, starting transfers between devices, swap(): return lax.ppermute(value, AXES, [(i, i ^ mask) for i in range(count)])  17.4 us
    pallas_call x2, Pallas kernels, assemble(): pl.pallas_call(body, out_shape=pltpu.VMEM((rows * pitch, edge), kind), in...  8.74 us
  transfers between devices with their start and end apart: 20, of which 12 were waited for; matrix products, arithmetic and copies ran while one was open for 2% of the time, Pallas kernels for 8%

profile of v17, /device:TPU:0, one launch (start us, length us, event | category | flops | bytes accessed | tf_op | source)
XLA Modules:
  0.0 104.9 jit_solution(10872754590633801404)
XLA Ops:
  0.0 1.9 %shard_map.37.refs_0_ = bf16[1936,128]{1,0:T(8,128)(2,1)} custom-call(s32[1,15]{1,0:T(1,128)} %pattern.1, s32[1,29]{1,0:T(1,128)} %filter_mask.1, bf16[15,128,128]{2,1,0:T(8,128)(2,1)} %bitcast.2), custom_call_target="tpu_custom_call" | custom-call | tf_op jit(solution)/shard_map/pallas_call | solution.py:274
  1.9 2.9 %collective-permute-start = (bf16[1936,128]{1,0:T(8,128)(2,1)}, bf16[1936,128]{1,0:T(8,128)(2,1)S(1)}, u32[]{:S(2)}, u32[]{:S(2)}) collective-permute-start(bf16[1936,128]{1,0:T(8,128)(2,1)} %shard_map.37.refs_0_), channel_id=1, source_target_pairs={{0,1},{1,0},{2,3},{3,2},{4,5},{5,4},{6,7},{7,6},{8,9},{9,8},{10,11... | collective-permute-start | bytes 1486856 | tf_op jit(solution)/shard_map/ppermute | solution.py:22
  4.9 1.5 %collective-permute-start.1 = (bf16[1936,128]{1,0:T(8,128)(2,1)}, bf16[1936,128]{1,0:T(8,128)(2,1)S(1)}, u32[]{:S(2)}, u32[]{:S(2)}) collective-permute-start(bf16[1936,128]{1,0:T(8,128)(2,1)} %shard_map.37.refs_0_), channel_id=1, source_target_pairs={{0,16},{1,17},{2,18},{3,19},{4,20},{5,21},{6,22},{7,23},{8,24},{9,... | collective-permute-start | bytes 1486856 | tf_op jit(solution)/shard_map/ppermute | solution.py:22
  6.4 3.6 %collective-permute-start.2 = (bf16[1936,128]{1,0:T(8,128)(2,1)}, bf16[1936,128]{1,0:T(8,128)(2,1)S(1)}, u32[]{:S(2)}, u32[]{:S(2)}) collective-permute-start(bf16[1936,128]{1,0:T(8,128)(2,1)} %shard_map.37.refs_0_), channel_id=1, source_target_pairs={{0,6},{1,7},{2,4},{3,5},{4,2},{5,3},{6,0},{7,1},{8,14},{9,15},{10,... | collective-permute-start | bytes 1486856 | tf_op jit(solution)/shard_map/ppermute | solution.py:22
  10.5 1.1 %constant_dynamic-update-slice_fusion.5 = bf16[11616,128]{1,0:T(8,128)(2,1)S(1)} fusion(bf16[1936,128]{1,0:T(8,128)(2,1)} %shard_map.37.refs_0_), kind=kLoop, calls=%fused_computation.7 | loop fusion | bytes 991232
  11.6 5.6 %collective-permute-done.refs_1_ = bf16[1936,128]{1,0:T(8,128)(2,1)S(1)} collective-permute-done((bf16[1936,128]{1,0:T(8,128)(2,1)}, bf16[1936,128]{1,0:T(8,128)(2,1)S(1)}, u32[]{:S(2)}, u32[]{:S(2)}) %collective-permute-start) | collective-permute-done | bytes 495648 | tf_op jit(solution)/shard_map/ppermute | solution.py:22
  17.3 11.2 %collective-permute-done.1.refs_2_ = bf16[1936,128]{1,0:T(8,128)(2,1)S(1)} collective-permute-done((bf16[1936,128]{1,0:T(8,128)(2,1)}, bf16[1936,128]{1,0:T(8,128)(2,1)S(1)}, u32[]{:S(2)}, u32[]{:S(2)}) %collective-permute-start.1) | collective-permute-done | bytes 495648 | tf_op jit(solution)/shard_map/ppermute | solution.py:22
  28.6 3.0 %collective-permute-done.3.refs_4_ = bf16[1936,128]{1,0:T(8,128)(2,1)S(1)} collective-permute-done((bf16[1936,128]{1,0:T(8,128)(2,1)}, bf16[1936,128]{1,0:T(8,128)(2,1)S(1)}, u32[]{:S(2)}, u32[]{:S(2)}) %collective-permute-start.3) | collective-permute-done | bytes 495648 | tf_op jit(solution)/shard_map/ppermute | solution.py:22
  32.0 0.6 collective-permute-start.6
  33.1 1.7 %collective-permute-start.8 = (bf16[1936,128]{1,0:T(8,128)(2,1)S(1)}, bf16[1936,128]{1,0:T(8,128)(2,1)S(1)}, u32[]{:S(2)}, u32[]{:S(2)}) collective-permute-start(bf16[1936,128]{1,0:T(8,128)(2,1)S(1)} %collective-permute-done.2.refs_3_), channel_id=1, source_target_pairs={{0,2},{1,3},{2,0},{3,1},{4,6},{5,7},{6,4},{7,5},{8,10},{9,11},{10,... | collective-permute-start | bytes 1486856 | tf_op jit(solution)/shard_map/ppermute | solution.py:22
  35.3 19.5 %collective-permute-done.8.refs_11_ = bf16[1936,128]{1,0:T(8,128)(2,1)S(1)} collective-permute-done((bf16[1936,128]{1,0:T(8,128)(2,1)S(1)}, bf16[1936,128]{1,0:T(8,128)(2,1)S(1)}, u32[]{:S(2)}, u32[]{:S(2)}) %collective-permute-start.8) | collective-permute-done | bytes 495648 | tf_op jit(solution)/shard_map/ppermute | solution.py:22
  54.8 1.6 %collective-permute-done.6.refs_9_ = bf16[3872,128]{1,0:T(8,128)(2,1)S(1)} collective-permute-done((bf16[3872,128]{1,0:T(8,128)(2,1)S(1)}, bf16[3872,128]{1,0:T(8,128)(2,1)S(1)}, u32[]{:S(2)}, u32[]{:S(2)}) %collective-permute-start.6) | collective-permute-done | bytes 991264 | tf_op jit(solution)/shard_map/ppermute | solution.py:22
  56.7 0.6 collective-permute-start.9
  57.3 0.6 collective-permute-start.12
  58.0 1.6 %collective-permute-start.13 = (bf16[2848,128]{1,0:T(8,128)(2,1)S(1)}, bf16[2848,128]{1,0:T(8,128)(2,1)S(1)}, u32[]{:S(2)}, u32[]{:S(2)}) collective-permute-start(bf16[2848,128]{1,0:T(8,128)(2,1)S(1)} %pad_maximum_fusion.1), channel_id=1, source_target_pairs={{0,16},{1,17},{2,18},{3,19},{4,20},{5,21},{6,22},{7,23},{8,24},{9,... | collective-permute-start | bytes 2187272 | tf_op jit(solution)/shard_map/ppermute | solution.py:22
  59.5 1.7 %collective-permute-start.14 = (bf16[1936,128]{1,0:T(8,128)(2,1)S(1)}, bf16[1936,128]{1,0:T(8,128)(2,1)S(1)}, u32[]{:S(2)}, u32[]{:S(2)}) collective-permute-start(bf16[1936,128]{1,0:T(8,128)(2,1)S(1)} %collective-permute-done.4.refs_5_), channel_id=1, source_target_pairs={{0,2},{1,3},{2,0},{3,1},{4,6},{5,7},{6,4},{7,5},{8,10},{9,11},{10,... | collective-permute-start | bytes 1486856 | tf_op jit(solution)/shard_map/ppermute | solution.py:22
  61.2 7.4 %shard_map.38.refs_3_ = bf16[56144,128]{1,0:T(8,128)(2,1)S(1)} custom-call(bf16[1936,128]{1,0:T(8,128)(2,1)S(1)} %copy-done, bf16[1936,128]{1,0:T(8,128)(2,1)S(1)} %collective-permute-done.refs_1_, bf16[1936,128]{1,0:T(8,128)(2,1)S(1)} %collective-permute-done.1.refs_2_, bf16[1936,128]{1,0:T(8,128)(2,1)S(1)} %collective-permute-done.2.refs_3_, ...), custom_call_target="tpu_custom_call" | custom-call | bytes 21807104 | tf_op jit(solution)/shard_map/pallas_call | solution.py:146
  68.6 3.6 %collective-permute-done.14.refs_2_ = bf16[1936,128]{1,0:T(8,128)(2,1)S(1)} collective-permute-done((bf16[1936,128]{1,0:T(8,128)(2,1)S(1)}, bf16[1936,128]{1,0:T(8,128)(2,1)S(1)}, u32[]{:S(2)}, u32[]{:S(2)}) %collective-permute-start.14) | collective-permute-done | bytes 495648 | tf_op jit(solution)/shard_map/ppermute | solution.py:22
  72.2 3.8 %collective-permute-done.13.refs_1_ = bf16[2848,128]{1,0:T(8,128)(2,1)S(1)} collective-permute-done((bf16[2848,128]{1,0:T(8,128)(2,1)S(1)}, bf16[2848,128]{1,0:T(8,128)(2,1)S(1)}, u32[]{:S(2)}, u32[]{:S(2)}) %collective-permute-start.13) | collective-permute-done | bytes 729120 | tf_op jit(solution)/shard_map/ppermute | solution.py:22
  77.2 1.3 %shard_map.39.refs_5_ = bf16[56144,128]{1,0:T(8,128)(2,1)S(1)} custom-call(bf16[2960,128]{1,0:T(8,128)(2,1)S(1)} %collective-permute-done.12.refs_0_, bf16[2848,128]{1,0:T(8,128)(2,1)S(1)} %collective-permute-done.13.refs_1_, bf16[1936,128]{1,0:T(8,128)(2,1)S(1)} %collective-permute-done.14.refs_2_, ...), custom_call_target="tpu_custom_call", output_to_operand_aliasing={{}: (3, {})} | custom-call | bytes 3964928 | tf_op jit(solution)/shard_map/pallas_call | solution.py:146
  78.6 1.6 %collective-permute-done.17.refs_2_ = bf16[1936,128]{1,0:T(8,128)(2,1)S(1)} collective-permute-done((bf16[1936,128]{1,0:T(8,128)(2,1)S(1)}, bf16[1936,128]{1,0:T(8,128)(2,1)S(1)}, u32[]{:S(2)}, u32[]{:S(2)}) %collective-permute-start.17) | collective-permute-done | bytes 495648 | tf_op jit(solution)/shard_map/ppermute | solution.py:22
  80.2 0.7 collective-permute-done.18.refs_3_
  80.9 0.7 collective-permute-done.19.refs_4_
  81.6 23.2 %shard_map.40 = (bf16[56144,128]{1,0:T(8,128)(2,1)S(1)}, bf16[29,128,128]{2,1,0:T(8,128)(2,1)}) custom-call(bf16[2960,128]{1,0:T(8,128)(2,1)S(1)} %collective-permute-done.15.refs_0_, bf16[2848,128]{1,0:T(8,128)(2,1)S(1)} %collective-permute-done.16.refs_1_, bf16[1936,128]{1,0:T(8,128)(2,1)S(1)} %collective-permute-done.17.refs_2_, ...), custom_call_target="tpu_custom_call", output_to_operand_aliasing={{0}: (5, {})} | custom-call | flops 16999999488 | bytes 15728640 | tf_op jit(solution)/shard_map/pallas_call | solution.py:284
  (32 shorter events, 3.8 us)
Async XLA Ops:
  1.9 15.3 %collective-permute-start = (bf16[1936,128]{1,0:T(8,128)(2,1)}, bf16[1936,128]{1,0:T(8,128)(2,1)S(1)}, u32[]{:S(2)}, u32[]{:S(2)}) collective-permute-start(bf16[1936,128]{1,0:T(8,128)(2,1)} %shard_map.37.refs_0_), channel_id=1, source_target_pairs={{0,1},{1,0},{2,3},{3,2},{4,5},{5,4},{6,7},{7,6},{8,9},{9,8},{10,11... | collective-permute-start | bytes 1486856 | tf_op jit(solution)/shard_map/ppermute | solution.py:22
  4.9 23.6 %collective-permute-start.1 = (bf16[1936,128]{1,0:T(8,128)(2,1)}, bf16[1936,128]{1,0:T(8,128)(2,1)S(1)}, u32[]{:S(2)}, u32[]{:S(2)}) collective-permute-start(bf16[1936,128]{1,0:T(8,128)(2,1)} %shard_map.37.refs_0_), channel_id=1, source_target_pairs={{0,16},{1,17},{2,18},{3,19},{4,20},{5,21},{6,22},{7,23},{8,24},{9,... | collective-permute-start | bytes 1486856 | tf_op jit(solution)/shard_map/ppermute | solution.py:22
  6.4 22.2 %collective-permute-start.2 = (bf16[1936,128]{1,0:T(8,128)(2,1)}, bf16[1936,128]{1,0:T(8,128)(2,1)S(1)}, u32[]{:S(2)}, u32[]{:S(2)}) collective-permute-start(bf16[1936,128]{1,0:T(8,128)(2,1)} %shard_map.37.refs_0_), channel_id=1, source_target_pairs={{0,6},{1,7},{2,4},{3,5},{4,2},{5,3},{6,0},{7,1},{8,14},{9,15},{10,... | collective-permute-start | bytes 1486856 | tf_op jit(solution)/shard_map/ppermute | solution.py:22
  10.0 21.7 %collective-permute-start.3 = (bf16[1936,128]{1,0:T(8,128)(2,1)}, bf16[1936,128]{1,0:T(8,128)(2,1)S(1)}, u32[]{:S(2)}, u32[]{:S(2)}) collective-permute-start(bf16[1936,128]{1,0:T(8,128)(2,1)} %shard_map.37.refs_0_), channel_id=1, source_target_pairs={{0,2},{1,3},{2,0},{3,1},{4,6},{5,7},{6,4},{7,5},{8,10},{9,11},{10,... | collective-permute-start | bytes 1486856 | tf_op jit(solution)/shard_map/ppermute | solution.py:22
  10.0 21.8 %collective-permute-start.4 = (bf16[1936,128]{1,0:T(8,128)(2,1)}, bf16[1936,128]{1,0:T(8,128)(2,1)S(1)}, u32[]{:S(2)}, u32[]{:S(2)}) collective-permute-start(bf16[1936,128]{1,0:T(8,128)(2,1)} %shard_map.37.refs_0_), channel_id=1, source_target_pairs={{0,17},{1,16},{2,19},{3,18},{4,21},{5,20},{6,23},{7,22},{8,25},{9,... | collective-permute-start | bytes 1486856 | tf_op jit(solution)/shard_map/ppermute | solution.py:22
  31.7 29.5 %copy-start = (bf16[1936,128]{1,0:T(8,128)(2,1)S(1)}, bf16[1936,128]{1,0:T(8,128)(2,1)}, u32[]{:S(2)}) copy-start(bf16[1936,128]{1,0:T(8,128)(2,1)} %shard_map.37.refs_0_) | copy-start | bytes 1486852
  31.9 24.7 %collective-permute-start.5 = (bf16[11616,128]{1,0:T(8,128)(2,1)S(1)}, bf16[11616,128]{1,0:T(8,128)(2,1)S(1)}, u32[]{:S(2)}, u32[]{:S(2)}) collective-permute-start(bf16[11616,128]{1,0:T(8,128)(2,1)S(1)} %constant_dynamic-update-slice_fusion), channel_id=1, source_target_pairs={{0,8},{1,9},{2,10},{3,11},{4,12},{5,13},{6,14},{7,15},{8,0},{9,1},... | collective-permute-start | bytes 8921096 | tf_op jit(solution)/shard_map/ppermute | solution.py:22
  32.0 24.3 %collective-permute-start.6 = (bf16[3872,128]{1,0:T(8,128)(2,1)S(1)}, bf16[3872,128]{1,0:T(8,128)(2,1)S(1)}, u32[]{:S(2)}, u32[]{:S(2)}) collective-permute-start(bf16[3872,128]{1,0:T(8,128)(2,1)S(1)} %get-tuple-element.29), channel_id=1, source_target_pairs={{0,16},{1,17},{2,18},{3,19},{4,20},{5,21},{6,22},{7,23},{8,24},{9,... | collective-permute-start | bytes 2973704 | tf_op jit(solution)/shard_map/ppermute | solution.py:22
  32.6 24.0 %collective-permute-start.7 = (bf16[3872,128]{1,0:T(8,128)(2,1)S(1)}, bf16[3872,128]{1,0:T(8,128)(2,1)S(1)}, u32[]{:S(2)}, u32[]{:S(2)}) collective-permute-start(bf16[3872,128]{1,0:T(8,128)(2,1)S(1)} %get-tuple-element.29), channel_id=1, source_target_pairs={{0,1},{1,0},{2,3},{3,2},{4,5},{5,4},{6,7},{7,6},{8,9},{9,8},{10,11... | collective-permute-start | bytes 2973704 | tf_op jit(solution)/shard_map/ppermute | solution.py:22
  33.1 21.7 %collective-permute-start.8 = (bf16[1936,128]{1,0:T(8,128)(2,1)S(1)}, bf16[1936,128]{1,0:T(8,128)(2,1)S(1)}, u32[]{:S(2)}, u32[]{:S(2)}) collective-permute-start(bf16[1936,128]{1,0:T(8,128)(2,1)S(1)} %collective-permute-done.2.refs_3_), channel_id=1, source_target_pairs={{0,2},{1,3},{2,0},{3,1},{4,6},{5,7},{6,4},{7,5},{8,10},{9,11},{10,... | collective-permute-start | bytes 1486856 | tf_op jit(solution)/shard_map/ppermute | solution.py:22
  34.8 24.8 %collective-permute-start.11 = (bf16[1936,128]{1,0:T(8,128)(2,1)S(1)}, bf16[1936,128]{1,0:T(8,128)(2,1)S(1)}, u32[]{:S(2)}, u32[]{:S(2)}) collective-permute-start(bf16[1936,128]{1,0:T(8,128)(2,1)S(1)} %collective-permute-done.4.refs_5_), channel_id=1, source_target_pairs={{0,4},{1,5},{2,6},{3,7},{4,0},{5,1},{6,2},{7,3},{8,12},{9,13},{10,... | collective-permute-start | bytes 1486856 | tf_op jit(solution)/shard_map/ppermute | solution.py:22
  56.6 4.6 %collective-permute-start.10 = (bf16[3872,128]{1,0:T(8,128)(2,1)S(1)}, bf16[3872,128]{1,0:T(8,128)(2,1)S(1)}, u32[]{:S(2)}, u32[]{:S(2)}) collective-permute-start(bf16[3872,128]{1,0:T(8,128)(2,1)S(1)} %collective-permute-done.6.refs_9_), channel_id=1, source_target_pairs={{0,8},{1,9},{2,10},{3,11},{4,12},{5,13},{6,14},{7,15},{8,0},{9,1},... | collective-permute-start | bytes 2973704 | tf_op jit(solution)/shard_map/ppermute | solution.py:22
  56.7 4.5 %collective-permute-start.9 = (bf16[3872,128]{1,0:T(8,128)(2,1)S(1)}, bf16[3872,128]{1,0:T(8,128)(2,1)S(1)}, u32[]{:S(2)}, u32[]{:S(2)}) collective-permute-start(bf16[3872,128]{1,0:T(8,128)(2,1)S(1)} %collective-permute-done.7.refs_7_), channel_id=1, source_target_pairs={{0,8},{1,9},{2,10},{3,11},{4,12},{5,13},{6,14},{7,15},{8,0},{9,1},... | collective-permute-start | bytes 2973704 | tf_op jit(solution)/shard_map/ppermute | solution.py:22
  57.3 18.9 %collective-permute-start.12 = (bf16[2960,128]{1,0:T(8,128)(2,1)S(1)}, bf16[2960,128]{1,0:T(8,128)(2,1)S(1)}, u32[]{:S(2)}, u32[]{:S(2)}) collective-permute-start(bf16[2960,128]{1,0:T(8,128)(2,1)S(1)} %pad_maximum_fusion), channel_id=1, source_target_pairs={{0,1},{1,0},{2,3},{3,2},{4,5},{5,4},{6,7},{7,6},{8,9},{9,8},{10,11... | collective-permute-start | bytes 2273288 | tf_op jit(solution)/shard_map/ppermute | solution.py:22
  58.0 18.0 %collective-permute-start.13 = (bf16[2848,128]{1,0:T(8,128)(2,1)S(1)}, bf16[2848,128]{1,0:T(8,128)(2,1)S(1)}, u32[]{:S(2)}, u32[]{:S(2)}) collective-permute-start(bf16[2848,128]{1,0:T(8,128)(2,1)S(1)} %pad_maximum_fusion.1), channel_id=1, source_target_pairs={{0,16},{1,17},{2,18},{3,19},{4,20},{5,21},{6,22},{7,23},{8,24},{9,... | collective-permute-start | bytes 2187272 | tf_op jit(solution)/shard_map/ppermute | solution.py:22
  59.5 12.7 %collective-permute-start.14 = (bf16[1936,128]{1,0:T(8,128)(2,1)S(1)}, bf16[1936,128]{1,0:T(8,128)(2,1)S(1)}, u32[]{:S(2)}, u32[]{:S(2)}) collective-permute-start(bf16[1936,128]{1,0:T(8,128)(2,1)S(1)} %collective-permute-done.4.refs_5_), channel_id=1, source_target_pairs={{0,2},{1,3},{2,0},{3,1},{4,6},{5,7},{6,4},{7,5},{8,10},{9,11},{10,... | collective-permute-start | bytes 1486856 | tf_op jit(solution)/shard_map/ppermute | solution.py:22
  76.2 5.4 %collective-permute-start.15 = (bf16[2960,128]{1,0:T(8,128)(2,1)S(1)}, bf16[2960,128]{1,0:T(8,128)(2,1)S(1)}, u32[]{:S(2)}, u32[]{:S(2)}) collective-permute-start(bf16[2960,128]{1,0:T(8,128)(2,1)S(1)} %collective-permute-done.12.refs_0_), channel_id=1, source_target_pairs={{0,8},{1,9},{2,10},{3,11},{4,12},{5,13},{6,14},{7,15},{8,0},{9,1},... | collective-permute-start | bytes 2273288 | tf_op jit(solution)/shard_map/ppermute | solution.py:22
  76.2 5.4 %collective-permute-start.16 = (bf16[2848,128]{1,0:T(8,128)(2,1)S(1)}, bf16[2848,128]{1,0:T(8,128)(2,1)S(1)}, u32[]{:S(2)}, u32[]{:S(2)}) collective-permute-start(bf16[2848,128]{1,0:T(8,128)(2,1)S(1)} %collective-permute-done.13.refs_1_), channel_id=1, source_target_pairs={{0,8},{1,9},{2,10},{3,11},{4,12},{5,13},{6,14},{7,15},{8,0},{9,1},... | collective-permute-start | bytes 2187272 | tf_op jit(solution)/shard_map/ppermute | solution.py:22
  76.7 3.5 %collective-permute-start.17 = (bf16[1936,128]{1,0:T(8,128)(2,1)S(1)}, bf16[1936,128]{1,0:T(8,128)(2,1)S(1)}, u32[]{:S(2)}, u32[]{:S(2)}) collective-permute-start(bf16[1936,128]{1,0:T(8,128)(2,1)S(1)} %collective-permute-done.8.refs_11_), channel_id=1, source_target_pairs={{0,8},{1,9},{2,10},{3,11},{4,12},{5,13},{6,14},{7,15},{8,0},{9,1},... | collective-permute-start | bytes 1486856 | tf_op jit(solution)/shard_map/ppermute | solution.py:22
  76.7 4.2 %collective-permute-start.18 = (bf16[1936,128]{1,0:T(8,128)(2,1)S(1)}, bf16[1936,128]{1,0:T(8,128)(2,1)S(1)}, u32[]{:S(2)}, u32[]{:S(2)}) collective-permute-start(bf16[1936,128]{1,0:T(8,128)(2,1)S(1)} %collective-permute-done.11.refs_12_), channel_id=1, source_target_pairs={{0,8},{1,9},{2,10},{3,11},{4,12},{5,13},{6,14},{7,15},{8,0},{9,1},... | collective-permute-start | bytes 1486856 | tf_op jit(solution)/shard_map/ppermute | solution.py:22
  77.2 4.4 %collective-permute-start.19 = (bf16[1936,128]{1,0:T(8,128)(2,1)S(1)}, bf16[1936,128]{1,0:T(8,128)(2,1)S(1)}, u32[]{:S(2)}, u32[]{:S(2)}) collective-permute-start(bf16[1936,128]{1,0:T(8,128)(2,1)S(1)} %collective-permute-done.14.refs_2_), channel_id=1, source_target_pairs={{0,8},{1,9},{2,10},{3,11},{4,12},{5,13},{6,14},{7,15},{8,0},{9,1},... | collective-permute-start | bytes 1486856 | tf_op jit(solution)/shard_map/ppermute | solution.py:22

commit v18 on v17

--- a/solution.py
+++ b/solution.py
@@ -8,7 +8,7 @@
 from jax.sharding import PartitionSpec as P
 
 NOTE = 16
-GROUP = 2
+GROUP = 4
 WIDTH = 4
 AXES = ("row", "col")
 
@@ -225,8 +225,8 @@
         return carry
 
     lax.fori_loop(0, slots // GROUP, row_group, 0)
-    for r in range(slots // GROUP * GROUP, slots):
-        square_rows(r, 1, 0, None, range(-far, far + reach - r + 1, 2))
+    r = slots // GROUP * GROUP
+    square_rows(r, slots - r, 0, None, range(-far, far + reach - r + 1, 2))
 
     keep = masks(far)
     copies = []

time: 105 us -> 106 us (level)
  no operation moved by 1% of the time
where the time goes in v18:
time: 106 us
  waiting for transfers between devices  51.8 us (49%)
  Pallas kernels  34.4 us (32%)
  starting transfers between devices  17.4 us (16%)
  local copies, waits for them, and re-layouts  1.56 us (1%)
    ppermute x20, waiting for transfers between devices, swap(): return lax.ppermute(value, AXES, [(i, i ^ mask) for i in range(count)])  51.8 us
    pallas_call x1, Pallas kernels, shards(): pl.pallas_call(functools.partial(purify, reach, edge, layout), out_shape=...  23.7 us
    ppermute x20, starting transfers between devices, swap(): return lax.ppermute(value, AXES, [(i, i ^ mask) for i in range(count)])  17.4 us
    pallas_call x2, Pallas kernels, assemble(): pl.pallas_call(body, out_shape=pltpu.VMEM((rows * pitch, edge), kind), in...  8.74 us
  transfers between devices with their start and end apart: 20, of which 12 were waited for; matrix products, arithmetic and copies ran while one was open for 2% of the time, Pallas kernels for 8%

profile of v18, /device:TPU:0, one launch (start us, length us, event | category | flops | bytes accessed | tf_op | source)
XLA Modules:
  0.0 105.5 jit_solution(12865681209250884451)
XLA Ops:
  0.0 1.9 %shard_map.37.refs_0_ = bf16[1936,128]{1,0:T(8,128)(2,1)} custom-call(s32[1,15]{1,0:T(1,128)} %pattern.1, s32[1,29]{1,0:T(1,128)} %filter_mask.1, bf16[15,128,128]{2,1,0:T(8,128)(2,1)} %bitcast.2), custom_call_target="tpu_custom_call" | custom-call | tf_op jit(solution)/shard_map/pallas_call | solution.py:274
  1.9 2.9 %collective-permute-start = (bf16[1936,128]{1,0:T(8,128)(2,1)}, bf16[1936,128]{1,0:T(8,128)(2,1)S(1)}, u32[]{:S(2)}, u32[]{:S(2)}) collective-permute-start(bf16[1936,128]{1,0:T(8,128)(2,1)} %shard_map.37.refs_0_), channel_id=1, source_target_pairs={{0,1},{1,0},{2,3},{3,2},{4,5},{5,4},{6,7},{7,6},{8,9},{9,8},{10,11... | collective-permute-start | bytes 1486856 | tf_op jit(solution)/shard_map/ppermute | solution.py:22
  4.9 1.5 %collective-permute-start.1 = (bf16[1936,128]{1,0:T(8,128)(2,1)}, bf16[1936,128]{1,0:T(8,128)(2,1)S(1)}, u32[]{:S(2)}, u32[]{:S(2)}) collective-permute-start(bf16[1936,128]{1,0:T(8,128)(2,1)} %shard_map.37.refs_0_), channel_id=1, source_target_pairs={{0,16},{1,17},{2,18},{3,19},{4,20},{5,21},{6,22},{7,23},{8,24},{9,... | collective-permute-start | bytes 1486856 | tf_op jit(solution)/shard_map/ppermute | solution.py:22
  6.4 3.6 %collective-permute-start.2 = (bf16[1936,128]{1,0:T(8,128)(2,1)}, bf16[1936,128]{1,0:T(8,128)(2,1)S(1)}, u32[]{:S(2)}, u32[]{:S(2)}) collective-permute-start(bf16[1936,128]{1,0:T(8,128)(2,1)} %shard_map.37.refs_0_), channel_id=1, source_target_pairs={{0,6},{1,7},{2,4},{3,5},{4,2},{5,3},{6,0},{7,1},{8,14},{9,15},{10,... | collective-permute-start | bytes 1486856 | tf_op jit(solution)/shard_map/ppermute | solution.py:22
  10.5 1.1 %constant_dynamic-update-slice_fusion.5 = bf16[11616,128]{1,0:T(8,128)(2,1)S(1)} fusion(bf16[1936,128]{1,0:T(8,128)(2,1)} %shard_map.37.refs_0_), kind=kLoop, calls=%fused_computation.7 | loop fusion | bytes 991232
  11.6 5.6 %collective-permute-done.refs_1_ = bf16[1936,128]{1,0:T(8,128)(2,1)S(1)} collective-permute-done((bf16[1936,128]{1,0:T(8,128)(2,1)}, bf16[1936,128]{1,0:T(8,128)(2,1)S(1)}, u32[]{:S(2)}, u32[]{:S(2)}) %collective-permute-start) | collective-permute-done | bytes 495648 | tf_op jit(solution)/shard_map/ppermute | solution.py:22
  17.3 11.2 %collective-permute-done.1.refs_2_ = bf16[1936,128]{1,0:T(8,128)(2,1)S(1)} collective-permute-done((bf16[1936,128]{1,0:T(8,128)(2,1)}, bf16[1936,128]{1,0:T(8,128)(2,1)S(1)}, u32[]{:S(2)}, u32[]{:S(2)}) %collective-permute-start.1) | collective-permute-done | bytes 495648 | tf_op jit(solution)/shard_map/ppermute | solution.py:22
  28.6 3.0 %collective-permute-done.3.refs_4_ = bf16[1936,128]{1,0:T(8,128)(2,1)S(1)} collective-permute-done((bf16[1936,128]{1,0:T(8,128)(2,1)}, bf16[1936,128]{1,0:T(8,128)(2,1)S(1)}, u32[]{:S(2)}, u32[]{:S(2)}) %collective-permute-start.3) | collective-permute-done | bytes 495648 | tf_op jit(solution)/shard_map/ppermute | solution.py:22
  32.0 0.6 collective-permute-start.6
  33.1 1.7 %collective-permute-start.8 = (bf16[1936,128]{1,0:T(8,128)(2,1)S(1)}, bf16[1936,128]{1,0:T(8,128)(2,1)S(1)}, u32[]{:S(2)}, u32[]{:S(2)}) collective-permute-start(bf16[1936,128]{1,0:T(8,128)(2,1)S(1)} %collective-permute-done.2.refs_3_), channel_id=1, source_target_pairs={{0,2},{1,3},{2,0},{3,1},{4,6},{5,7},{6,4},{7,5},{8,10},{9,11},{10,... | collective-permute-start | bytes 1486856 | tf_op jit(solution)/shard_map/ppermute | solution.py:22
  35.3 19.5 %collective-permute-done.8.refs_11_ = bf16[1936,128]{1,0:T(8,128)(2,1)S(1)} collective-permute-done((bf16[1936,128]{1,0:T(8,128)(2,1)S(1)}, bf16[1936,128]{1,0:T(8,128)(2,1)S(1)}, u32[]{:S(2)}, u32[]{:S(2)}) %collective-permute-start.8) | collective-permute-done | bytes 495648 | tf_op jit(solution)/shard_map/ppermute | solution.py:22
  54.8 1.6 %collective-permute-done.6.refs_9_ = bf16[3872,128]{1,0:T(8,128)(2,1)S(1)} collective-permute-done((bf16[3872,128]{1,0:T(8,128)(2,1)S(1)}, bf16[3872,128]{1,0:T(8,128)(2,1)S(1)}, u32[]{:S(2)}, u32[]{:S(2)}) %collective-permute-start.6) | collective-permute-done | bytes 991264 | tf_op jit(solution)/shard_map/ppermute | solution.py:22
  56.7 0.6 collective-permute-start.9
  57.3 0.6 collective-permute-start.12
  58.0 1.6 %collective-permute-start.13 = (bf16[2848,128]{1,0:T(8,128)(2,1)S(1)}, bf16[2848,128]{1,0:T(8,128)(2,1)S(1)}, u32[]{:S(2)}, u32[]{:S(2)}) collective-permute-start(bf16[2848,128]{1,0:T(8,128)(2,1)S(1)} %pad_maximum_fusion.1), channel_id=1, source_target_pairs={{0,16},{1,17},{2,18},{3,19},{4,20},{5,21},{6,22},{7,23},{8,24},{9,... | collective-permute-start | bytes 2187272 | tf_op jit(solution)/shard_map/ppermute | solution.py:22
  59.5 1.7 %collective-permute-start.14 = (bf16[1936,128]{1,0:T(8,128)(2,1)S(1)}, bf16[1936,128]{1,0:T(8,128)(2,1)S(1)}, u32[]{:S(2)}, u32[]{:S(2)}) collective-permute-start(bf16[1936,128]{1,0:T(8,128)(2,1)S(1)} %collective-permute-done.4.refs_5_), channel_id=1, source_target_pairs={{0,2},{1,3},{2,0},{3,1},{4,6},{5,7},{6,4},{7,5},{8,10},{9,11},{10,... | collective-permute-start | bytes 1486856 | tf_op jit(solution)/shard_map/ppermute | solution.py:22
  61.2 7.4 %shard_map.38.refs_3_ = bf16[56144,128]{1,0:T(8,128)(2,1)S(1)} custom-call(bf16[1936,128]{1,0:T(8,128)(2,1)S(1)} %copy-done, bf16[1936,128]{1,0:T(8,128)(2,1)S(1)} %collective-permute-done.refs_1_, bf16[1936,128]{1,0:T(8,128)(2,1)S(1)} %collective-permute-done.1.refs_2_, bf16[1936,128]{1,0:T(8,128)(2,1)S(1)} %collective-permute-done.2.refs_3_, ...), custom_call_target="tpu_custom_call" | custom-call | bytes 21807104 | tf_op jit(solution)/shard_map/pallas_call | solution.py:146
  68.6 3.6 %collective-permute-done.14.refs_2_ = bf16[1936,128]{1,0:T(8,128)(2,1)S(1)} collective-permute-done((bf16[1936,128]{1,0:T(8,128)(2,1)S(1)}, bf16[1936,128]{1,0:T(8,128)(2,1)S(1)}, u32[]{:S(2)}, u32[]{:S(2)}) %collective-permute-start.14) | collective-permute-done | bytes 495648 | tf_op jit(solution)/shard_map/ppermute | solution.py:22
  72.2 3.8 %collective-permute-done.13.refs_1_ = bf16[2848,128]{1,0:T(8,128)(2,1)S(1)} collective-permute-done((bf16[2848,128]{1,0:T(8,128)(2,1)S(1)}, bf16[2848,128]{1,0:T(8,128)(2,1)S(1)}, u32[]{:S(2)}, u32[]{:S(2)}) %collective-permute-start.13) | collective-permute-done | bytes 729120 | tf_op jit(solution)/shard_map/ppermute | solution.py:22
  77.2 1.3 %shard_map.39.refs_5_ = bf16[56144,128]{1,0:T(8,128)(2,1)S(1)} custom-call(bf16[2960,128]{1,0:T(8,128)(2,1)S(1)} %collective-permute-done.12.refs_0_, bf16[2848,128]{1,0:T(8,128)(2,1)S(1)} %collective-permute-done.13.refs_1_, bf16[1936,128]{1,0:T(8,128)(2,1)S(1)} %collective-permute-done.14.refs_2_, ...), custom_call_target="tpu_custom_call", output_to_operand_aliasing={{}: (3, {})} | custom-call | bytes 3964928 | tf_op jit(solution)/shard_map/pallas_call | solution.py:146
  78.6 1.6 %collective-permute-done.17.refs_2_ = bf16[1936,128]{1,0:T(8,128)(2,1)S(1)} collective-permute-done((bf16[1936,128]{1,0:T(8,128)(2,1)S(1)}, bf16[1936,128]{1,0:T(8,128)(2,1)S(1)}, u32[]{:S(2)}, u32[]{:S(2)}) %collective-permute-start.17) | collective-permute-done | bytes 495648 | tf_op jit(solution)/shard_map/ppermute | solution.py:22
  80.2 0.7 collective-permute-done.18.refs_3_
  80.9 0.7 collective-permute-done.19.refs_4_
  81.6 23.7 %shard_map.40 = (bf16[56144,128]{1,0:T(8,128)(2,1)S(1)}, bf16[29,128,128]{2,1,0:T(8,128)(2,1)}) custom-call(bf16[2960,128]{1,0:T(8,128)(2,1)S(1)} %collective-permute-done.15.refs_0_, bf16[2848,128]{1,0:T(8,128)(2,1)S(1)} %collective-permute-done.16.refs_1_, bf16[1936,128]{1,0:T(8,128)(2,1)S(1)} %collective-permute-done.17.refs_2_, ...), custom_call_target="tpu_custom_call", output_to_operand_aliasing={{0}: (5, {})} | custom-call | flops 16999999488 | bytes 15728640 | tf_op jit(solution)/shard_map/pallas_call | solution.py:284
  (32 shorter events, 3.8 us)
Async XLA Ops:
  1.9 15.3 %collective-permute-start = (bf16[1936,128]{1,0:T(8,128)(2,1)}, bf16[1936,128]{1,0:T(8,128)(2,1)S(1)}, u32[]{:S(2)}, u32[]{:S(2)}) collective-permute-start(bf16[1936,128]{1,0:T(8,128)(2,1)} %shard_map.37.refs_0_), channel_id=1, source_target_pairs={{0,1},{1,0},{2,3},{3,2},{4,5},{5,4},{6,7},{7,6},{8,9},{9,8},{10,11... | collective-permute-start | bytes 1486856 | tf_op jit(solution)/shard_map/ppermute | solution.py:22
  4.9 23.6 %collective-permute-start.1 = (bf16[1936,128]{1,0:T(8,128)(2,1)}, bf16[1936,128]{1,0:T(8,128)(2,1)S(1)}, u32[]{:S(2)}, u32[]{:S(2)}) collective-permute-start(bf16[1936,128]{1,0:T(8,128)(2,1)} %shard_map.37.refs_0_), channel_id=1, source_target_pairs={{0,16},{1,17},{2,18},{3,19},{4,20},{5,21},{6,22},{7,23},{8,24},{9,... | collective-permute-start | bytes 1486856 | tf_op jit(solution)/shard_map/ppermute | solution.py:22
  6.4 22.2 %collective-permute-start.2 = (bf16[1936,128]{1,0:T(8,128)(2,1)}, bf16[1936,128]{1,0:T(8,128)(2,1)S(1)}, u32[]{:S(2)}, u32[]{:S(2)}) collective-permute-start(bf16[1936,128]{1,0:T(8,128)(2,1)} %shard_map.37.refs_0_), channel_id=1, source_target_pairs={{0,6},{1,7},{2,4},{3,5},{4,2},{5,3},{6,0},{7,1},{8,14},{9,15},{10,... | collective-permute-start | bytes 1486856 | tf_op jit(solution)/shard_map/ppermute | solution.py:22
  10.0 21.7 %collective-permute-start.3 = (bf16[1936,128]{1,0:T(8,128)(2,1)}, bf16[1936,128]{1,0:T(8,128)(2,1)S(1)}, u32[]{:S(2)}, u32[]{:S(2)}) collective-permute-start(bf16[1936,128]{1,0:T(8,128)(2,1)} %shard_map.37.refs_0_), channel_id=1, source_target_pairs={{0,2},{1,3},{2,0},{3,1},{4,6},{5,7},{6,4},{7,5},{8,10},{9,11},{10,... | collective-permute-start | bytes 1486856 | tf_op jit(solution)/shard_map/ppermute | solution.py:22
  10.0 21.8 %collective-permute-start.4 = (bf16[1936,128]{1,0:T(8,128)(2,1)}, bf16[1936,128]{1,0:T(8,128)(2,1)S(1)}, u32[]{:S(2)}, u32[]{:S(2)}) collective-permute-start(bf16[1936,128]{1,0:T(8,128)(2,1)} %shard_map.37.refs_0_), channel_id=1, source_target_pairs={{0,17},{1,16},{2,19},{3,18},{4,21},{5,20},{6,23},{7,22},{8,25},{9,... | collective-permute-start | bytes 1486856 | tf_op jit(solution)/shard_map/ppermute | solution.py:22
  31.7 29.5 %copy-start = (bf16[1936,128]{1,0:T(8,128)(2,1)S(1)}, bf16[1936,128]{1,0:T(8,128)(2,1)}, u32[]{:S(2)}) copy-start(bf16[1936,128]{1,0:T(8,128)(2,1)} %shard_map.37.refs_0_) | copy-start | bytes 1486852
  31.9 24.7 %collective-permute-start.5 = (bf16[11616,128]{1,0:T(8,128)(2,1)S(1)}, bf16[11616,128]{1,0:T(8,128)(2,1)S(1)}, u32[]{:S(2)}, u32[]{:S(2)}) collective-permute-start(bf16[11616,128]{1,0:T(8,128)(2,1)S(1)} %constant_dynamic-update-slice_fusion), channel_id=1, source_target_pairs={{0,8},{1,9},{2,10},{3,11},{4,12},{5,13},{6,14},{7,15},{8,0},{9,1},... | collective-permute-start | bytes 8921096 | tf_op jit(solution)/shard_map/ppermute | solution.py:22
  32.0 24.3 %collective-permute-start.6 = (bf16[3872,128]{1,0:T(8,128)(2,1)S(1)}, bf16[3872,128]{1,0:T(8,128)(2,1)S(1)}, u32[]{:S(2)}, u32[]{:S(2)}) collective-permute-start(bf16[3872,128]{1,0:T(8,128)(2,1)S(1)} %get-tuple-element.29), channel_id=1, source_target_pairs={{0,16},{1,17},{2,18},{3,19},{4,20},{5,21},{6,22},{7,23},{8,24},{9,... | collective-permute-start | bytes 2973704 | tf_op jit(solution)/shard_map/ppermute | solution.py:22
  32.6 24.0 %collective-permute-start.7 = (bf16[3872,128]{1,0:T(8,128)(2,1)S(1)}, bf16[3872,128]{1,0:T(8,128)(2,1)S(1)}, u32[]{:S(2)}, u32[]{:S(2)}) collective-permute-start(bf16[3872,128]{1,0:T(8,128)(2,1)S(1)} %get-tuple-element.29), channel_id=1, source_target_pairs={{0,1},{1,0},{2,3},{3,2},{4,5},{5,4},{6,7},{7,6},{8,9},{9,8},{10,11... | collective-permute-start | bytes 2973704 | tf_op jit(solution)/shard_map/ppermute | solution.py:22
  33.1 21.7 %collective-permute-start.8 = (bf16[1936,128]{1,0:T(8,128)(2,1)S(1)}, bf16[1936,128]{1,0:T(8,128)(2,1)S(1)}, u32[]{:S(2)}, u32[]{:S(2)}) collective-permute-start(bf16[1936,128]{1,0:T(8,128)(2,1)S(1)} %collective-permute-done.2.refs_3_), channel_id=1, source_target_pairs={{0,2},{1,3},{2,0},{3,1},{4,6},{5,7},{6,4},{7,5},{8,10},{9,11},{10,... | collective-permute-start | bytes 1486856 | tf_op jit(solution)/shard_map/ppermute | solution.py:22
  34.8 24.8 %collective-permute-start.11 = (bf16[1936,128]{1,0:T(8,128)(2,1)S(1)}, bf16[1936,128]{1,0:T(8,128)(2,1)S(1)}, u32[]{:S(2)}, u32[]{:S(2)}) collective-permute-start(bf16[1936,128]{1,0:T(8,128)(2,1)S(1)} %collective-permute-done.4.refs_5_), channel_id=1, source_target_pairs={{0,4},{1,5},{2,6},{3,7},{4,0},{5,1},{6,2},{7,3},{8,12},{9,13},{10,... | collective-permute-start | bytes 1486856 | tf_op jit(solution)/shard_map/ppermute | solution.py:22
  56.6 4.6 %collective-permute-start.10 = (bf16[3872,128]{1,0:T(8,128)(2,1)S(1)}, bf16[3872,128]{1,0:T(8,128)(2,1)S(1)}, u32[]{:S(2)}, u32[]{:S(2)}) collective-permute-start(bf16[3872,128]{1,0:T(8,128)(2,1)S(1)} %collective-permute-done.6.refs_9_), channel_id=1, source_target_pairs={{0,8},{1,9},{2,10},{3,11},{4,12},{5,13},{6,14},{7,15},{8,0},{9,1},... | collective-permute-start | bytes 2973704 | tf_op jit(solution)/shard_map/ppermute | solution.py:22
  56.7 4.5 %collective-permute-start.9 = (bf16[3872,128]{1,0:T(8,128)(2,1)S(1)}, bf16[3872,128]{1,0:T(8,128)(2,1)S(1)}, u32[]{:S(2)}, u32[]{:S(2)}) collective-permute-start(bf16[3872,128]{1,0:T(8,128)(2,1)S(1)} %collective-permute-done.7.refs_7_), channel_id=1, source_target_pairs={{0,8},{1,9},{2,10},{3,11},{4,12},{5,13},{6,14},{7,15},{8,0},{9,1},... | collective-permute-start | bytes 2973704 | tf_op jit(solution)/shard_map/ppermute | solution.py:22
  57.3 18.9 %collective-permute-start.12 = (bf16[2960,128]{1,0:T(8,128)(2,1)S(1)}, bf16[2960,128]{1,0:T(8,128)(2,1)S(1)}, u32[]{:S(2)}, u32[]{:S(2)}) collective-permute-start(bf16[2960,128]{1,0:T(8,128)(2,1)S(1)} %pad_maximum_fusion), channel_id=1, source_target_pairs={{0,1},{1,0},{2,3},{3,2},{4,5},{5,4},{6,7},{7,6},{8,9},{9,8},{10,11... | collective-permute-start | bytes 2273288 | tf_op jit(solution)/shard_map/ppermute | solution.py:22
  58.0 18.0 %collective-permute-start.13 = (bf16[2848,128]{1,0:T(8,128)(2,1)S(1)}, bf16[2848,128]{1,0:T(8,128)(2,1)S(1)}, u32[]{:S(2)}, u32[]{:S(2)}) collective-permute-start(bf16[2848,128]{1,0:T(8,128)(2,1)S(1)} %pad_maximum_fusion.1), channel_id=1, source_target_pairs={{0,16},{1,17},{2,18},{3,19},{4,20},{5,21},{6,22},{7,23},{8,24},{9,... | collective-permute-start | bytes 2187272 | tf_op jit(solution)/shard_map/ppermute | solution.py:22
  59.5 12.7 %collective-permute-start.14 = (bf16[1936,128]{1,0:T(8,128)(2,1)S(1)}, bf16[1936,128]{1,0:T(8,128)(2,1)S(1)}, u32[]{:S(2)}, u32[]{:S(2)}) collective-permute-start(bf16[1936,128]{1,0:T(8,128)(2,1)S(1)} %collective-permute-done.4.refs_5_), channel_id=1, source_target_pairs={{0,2},{1,3},{2,0},{3,1},{4,6},{5,7},{6,4},{7,5},{8,10},{9,11},{10,... | collective-permute-start | bytes 1486856 | tf_op jit(solution)/shard_map/ppermute | solution.py:22
  76.2 5.4 %collective-permute-start.15 = (bf16[2960,128]{1,0:T(8,128)(2,1)S(1)}, bf16[2960,128]{1,0:T(8,128)(2,1)S(1)}, u32[]{:S(2)}, u32[]{:S(2)}) collective-permute-start(bf16[2960,128]{1,0:T(8,128)(2,1)S(1)} %collective-permute-done.12.refs_0_), channel_id=1, source_target_pairs={{0,8},{1,9},{2,10},{3,11},{4,12},{5,13},{6,14},{7,15},{8,0},{9,1},... | collective-permute-start | bytes 2273288 | tf_op jit(solution)/shard_map/ppermute | solution.py:22
  76.2 5.4 %collective-permute-start.16 = (bf16[2848,128]{1,0:T(8,128)(2,1)S(1)}, bf16[2848,128]{1,0:T(8,128)(2,1)S(1)}, u32[]{:S(2)}, u32[]{:S(2)}) collective-permute-start(bf16[2848,128]{1,0:T(8,128)(2,1)S(1)} %collective-permute-done.13.refs_1_), channel_id=1, source_target_pairs={{0,8},{1,9},{2,10},{3,11},{4,12},{5,13},{6,14},{7,15},{8,0},{9,1},... | collective-permute-start | bytes 2187272 | tf_op jit(solution)/shard_map/ppermute | solution.py:22
  76.7 3.5 %collective-permute-start.17 = (bf16[1936,128]{1,0:T(8,128)(2,1)S(1)}, bf16[1936,128]{1,0:T(8,128)(2,1)S(1)}, u32[]{:S(2)}, u32[]{:S(2)}) collective-permute-start(bf16[1936,128]{1,0:T(8,128)(2,1)S(1)} %collective-permute-done.8.refs_11_), channel_id=1, source_target_pairs={{0,8},{1,9},{2,10},{3,11},{4,12},{5,13},{6,14},{7,15},{8,0},{9,1},... | collective-permute-start | bytes 1486856 | tf_op jit(solution)/shard_map/ppermute | solution.py:22
  76.7 4.2 %collective-permute-start.18 = (bf16[1936,128]{1,0:T(8,128)(2,1)S(1)}, bf16[1936,128]{1,0:T(8,128)(2,1)S(1)}, u32[]{:S(2)}, u32[]{:S(2)}) collective-permute-start(bf16[1936,128]{1,0:T(8,128)(2,1)S(1)} %collective-permute-done.11.refs_12_), channel_id=1, source_target_pairs={{0,8},{1,9},{2,10},{3,11},{4,12},{5,13},{6,14},{7,15},{8,0},{9,1},... | collective-permute-start | bytes 1486856 | tf_op jit(solution)/shard_map/ppermute | solution.py:22
  77.2 4.4 %collective-permute-start.19 = (bf16[1936,128]{1,0:T(8,128)(2,1)S(1)}, bf16[1936,128]{1,0:T(8,128)(2,1)S(1)}, u32[]{:S(2)}, u32[]{:S(2)}) collective-permute-start(bf16[1936,128]{1,0:T(8,128)(2,1)S(1)} %collective-permute-done.14.refs_2_), channel_id=1, source_target_pairs={{0,8},{1,9},{2,10},{3,11},{4,12},{5,13},{6,14},{7,15},{8,0},{9,1},... | collective-permute-start | bytes 1486856 | tf_op jit(solution)/shard_map/ppermute | solution.py:22

commit v19 on v17

--- a/solution.py
+++ b/solution.py
@@ -199,13 +199,13 @@
     def square_rows(r, n, slot, own_row, offsets):
         keep = [masks(r + reach + i) for i in range(n)]
         for d in offsets:
-            low, high = max(-reach, d - reach), min(reach + n - 1, d + reach + 1)
+            low, high = max(-reach, d - reach), min(reach + n - 1, d + reach + WIDTH - 1)
             size = high - low + 1
             left = jnp.concatenate([strip(r + reach + i, low + reach - i, size) for i in range(n)], axis=0)
-            right = jnp.concatenate([strip(r + reach + e, d - e + reach, 2) for e in range(low, high + 1)], axis=0)
+            right = jnp.concatenate([strip(r + reach + e, d - e + reach, WIDTH) for e in range(low, high + 1)], axis=0)
             product = jnp.dot(left, right, preferred_element_type=jnp.float32)
             for i in range(n):
-                for j in range(2):
+                for j in range(WIDTH):
                     u = d + far - i + j
                     if 0 <= u < wide:
                         kept = product[i * edge : (i + 1) * edge, j * edge : (j + 1) * edge]
@@ -221,12 +221,12 @@
         needed = [(first_user(row) == group) & wanted for wanted, row, _ in late]
         wait_all([(now, row, copy) for now, (_, row, copy) in zip(needed, late)])
         slot = jnp.where(group == reach // GROUP, 1, 0)
-        square_rows(GROUP * group, GROUP, slot, reach % GROUP, range(-far, far + GROUP, 2))
+        square_rows(GROUP * group, GROUP, slot, reach % GROUP, range(-far, far + GROUP, WIDTH))
         return carry
 
     lax.fori_loop(0, slots // GROUP, row_group, 0)
     for r in range(slots // GROUP * GROUP, slots):
-        square_rows(r, 1, 0, None, range(-far, far + reach - r + 1, 2))
+        square_rows(r, 1, 0, None, range(-far, far + reach - r + 1, WIDTH))
 
     keep = masks(far)
     copies = []

time: 105 us -> 107 us (1.019)
  Pallas kernels: 33.9 us -> 35.5 us
    pallas_call x1, Pallas kernels: 23.2 us -> 24.8 us  [shards(): pl.pallas_call(functools.partial(purify, reach, edge, layout), out_shape=...]
  transfers between devices with their start and end apart: 20 -> 20, of which waited for: 12 -> 12; matrix products, arithmetic and copies ran while one was open for 2% -> 1% of each run, Pallas kernels for 8% -> 8%
where the time goes in v19:
time: 107 us; the launch traced here: 106 us
  waiting for transfers between devices  51.8 us (48%)
  Pallas kernels  35.5 us (33%)
  starting transfers between devices  17.4 us (16%)
  local copies, waits for them, and re-layouts  1.56 us (1%)
    ppermute x20, waiting for transfers between devices, swap(): return lax.ppermute(value, AXES, [(i, i ^ mask) for i in range(count)])  51.8 us
    pallas_call x1, Pallas kernels, shards(): pl.pallas_call(functools.partial(purify, reach, edge, layout), out_shape=...  24.8 us
    ppermute x20, starting transfers between devices, swap(): return lax.ppermute(value, AXES, [(i, i ^ mask) for i in range(count)])  17.4 us
    pallas_call x2, Pallas kernels, assemble(): pl.pallas_call(body, out_shape=pltpu.VMEM((rows * pitch, edge), kind), in...  8.74 us
  transfers between devices with their start and end apart: 20, of which 12 were waited for; matrix products, arithmetic and copies ran while one was open for 1% of the time, Pallas kernels for 8%

profile of v19, /device:TPU:0, one launch (start us, length us, event | category | flops | bytes accessed | tf_op | source)
XLA Modules:
  0.0 106.5 jit_solution(7285186742566058284)
XLA Ops:
  0.0 1.9 %shard_map.37.refs_0_ = bf16[1936,128]{1,0:T(8,128)(2,1)} custom-call(s32[1,15]{1,0:T(1,128)} %pattern.1, s32[1,29]{1,0:T(1,128)} %filter_mask.1, bf16[15,128,128]{2,1,0:T(8,128)(2,1)} %bitcast.2), custom_call_target="tpu_custom_call" | custom-call | tf_op jit(solution)/shard_map/pallas_call | solution.py:274
  1.9 2.9 %collective-permute-start = (bf16[1936,128]{1,0:T(8,128)(2,1)}, bf16[1936,128]{1,0:T(8,128)(2,1)S(1)}, u32[]{:S(2)}, u32[]{:S(2)}) collective-permute-start(bf16[1936,128]{1,0:T(8,128)(2,1)} %shard_map.37.refs_0_), channel_id=1, source_target_pairs={{0,1},{1,0},{2,3},{3,2},{4,5},{5,4},{6,7},{7,6},{8,9},{9,8},{10,11... | collective-permute-start | bytes 1486856 | tf_op jit(solution)/shard_map/ppermute | solution.py:22
  4.9 1.5 %collective-permute-start.1 = (bf16[1936,128]{1,0:T(8,128)(2,1)}, bf16[1936,128]{1,0:T(8,128)(2,1)S(1)}, u32[]{:S(2)}, u32[]{:S(2)}) collective-permute-start(bf16[1936,128]{1,0:T(8,128)(2,1)} %shard_map.37.refs_0_), channel_id=1, source_target_pairs={{0,16},{1,17},{2,18},{3,19},{4,20},{5,21},{6,22},{7,23},{8,24},{9,... | collective-permute-start | bytes 1486856 | tf_op jit(solution)/shard_map/ppermute | solution.py:22
  6.4 3.6 %collective-permute-start.2 = (bf16[1936,128]{1,0:T(8,128)(2,1)}, bf16[1936,128]{1,0:T(8,128)(2,1)S(1)}, u32[]{:S(2)}, u32[]{:S(2)}) collective-permute-start(bf16[1936,128]{1,0:T(8,128)(2,1)} %shard_map.37.refs_0_), channel_id=1, source_target_pairs={{0,6},{1,7},{2,4},{3,5},{4,2},{5,3},{6,0},{7,1},{8,14},{9,15},{10,... | collective-permute-start | bytes 1486856 | tf_op jit(solution)/shard_map/ppermute | solution.py:22
  10.5 1.1 %constant_dynamic-update-slice_fusion.5 = bf16[11616,128]{1,0:T(8,128)(2,1)S(1)} fusion(bf16[1936,128]{1,0:T(8,128)(2,1)} %shard_map.37.refs_0_), kind=kLoop, calls=%fused_computation.7 | loop fusion | bytes 991232
  11.6 5.6 %collective-permute-done.refs_1_ = bf16[1936,128]{1,0:T(8,128)(2,1)S(1)} collective-permute-done((bf16[1936,128]{1,0:T(8,128)(2,1)}, bf16[1936,128]{1,0:T(8,128)(2,1)S(1)}, u32[]{:S(2)}, u32[]{:S(2)}) %collective-permute-start) | collective-permute-done | bytes 495648 | tf_op jit(solution)/shard_map/ppermute | solution.py:22
  17.3 11.2 %collective-permute-done.1.refs_2_ = bf16[1936,128]{1,0:T(8,128)(2,1)S(1)} collective-permute-done((bf16[1936,128]{1,0:T(8,128)(2,1)}, bf16[1936,128]{1,0:T(8,128)(2,1)S(1)}, u32[]{:S(2)}, u32[]{:S(2)}) %collective-permute-start.1) | collective-permute-done | bytes 495648 | tf_op jit(solution)/shard_map/ppermute | solution.py:22
  28.6 3.0 %collective-permute-done.3.refs_4_ = bf16[1936,128]{1,0:T(8,128)(2,1)S(1)} collective-permute-done((bf16[1936,128]{1,0:T(8,128)(2,1)}, bf16[1936,128]{1,0:T(8,128)(2,1)S(1)}, u32[]{:S(2)}, u32[]{:S(2)}) %collective-permute-start.3) | collective-permute-done | bytes 495648 | tf_op jit(solution)/shard_map/ppermute | solution.py:22
  32.0 0.6 collective-permute-start.6
  33.1 1.7 %collective-permute-start.8 = (bf16[1936,128]{1,0:T(8,128)(2,1)S(1)}, bf16[1936,128]{1,0:T(8,128)(2,1)S(1)}, u32[]{:S(2)}, u32[]{:S(2)}) collective-permute-start(bf16[1936,128]{1,0:T(8,128)(2,1)S(1)} %collective-permute-done.2.refs_3_), channel_id=1, source_target_pairs={{0,2},{1,3},{2,0},{3,1},{4,6},{5,7},{6,4},{7,5},{8,10},{9,11},{10,... | collective-permute-start | bytes 1486856 | tf_op jit(solution)/shard_map/ppermute | solution.py:22
  35.3 19.5 %collective-permute-done.8.refs_11_ = bf16[1936,128]{1,0:T(8,128)(2,1)S(1)} collective-permute-done((bf16[1936,128]{1,0:T(8,128)(2,1)S(1)}, bf16[1936,128]{1,0:T(8,128)(2,1)S(1)}, u32[]{:S(2)}, u32[]{:S(2)}) %collective-permute-start.8) | collective-permute-done | bytes 495648 | tf_op jit(solution)/shard_map/ppermute | solution.py:22
  54.8 1.6 %collective-permute-done.6.refs_9_ = bf16[3872,128]{1,0:T(8,128)(2,1)S(1)} collective-permute-done((bf16[3872,128]{1,0:T(8,128)(2,1)S(1)}, bf16[3872,128]{1,0:T(8,128)(2,1)S(1)}, u32[]{:S(2)}, u32[]{:S(2)}) %collective-permute-start.6) | collective-permute-done | bytes 991264 | tf_op jit(solution)/shard_map/ppermute | solution.py:22
  56.7 0.6 collective-permute-start.9
  57.3 0.6 collective-permute-start.12
  58.0 1.6 %collective-permute-start.13 = (bf16[2848,128]{1,0:T(8,128)(2,1)S(1)}, bf16[2848,128]{1,0:T(8,128)(2,1)S(1)}, u32[]{:S(2)}, u32[]{:S(2)}) collective-permute-start(bf16[2848,128]{1,0:T(8,128)(2,1)S(1)} %pad_maximum_fusion.1), channel_id=1, source_target_pairs={{0,16},{1,17},{2,18},{3,19},{4,20},{5,21},{6,22},{7,23},{8,24},{9,... | collective-permute-start | bytes 2187272 | tf_op jit(solution)/shard_map/ppermute | solution.py:22
  59.5 1.7 %collective-permute-start.14 = (bf16[1936,128]{1,0:T(8,128)(2,1)S(1)}, bf16[1936,128]{1,0:T(8,128)(2,1)S(1)}, u32[]{:S(2)}, u32[]{:S(2)}) collective-permute-start(bf16[1936,128]{1,0:T(8,128)(2,1)S(1)} %collective-permute-done.4.refs_5_), channel_id=1, source_target_pairs={{0,2},{1,3},{2,0},{3,1},{4,6},{5,7},{6,4},{7,5},{8,10},{9,11},{10,... | collective-permute-start | bytes 1486856 | tf_op jit(solution)/shard_map/ppermute | solution.py:22
  61.2 7.4 %shard_map.38.refs_3_ = bf16[56144,128]{1,0:T(8,128)(2,1)S(1)} custom-call(bf16[1936,128]{1,0:T(8,128)(2,1)S(1)} %copy-done, bf16[1936,128]{1,0:T(8,128)(2,1)S(1)} %collective-permute-done.refs_1_, bf16[1936,128]{1,0:T(8,128)(2,1)S(1)} %collective-permute-done.1.refs_2_, bf16[1936,128]{1,0:T(8,128)(2,1)S(1)} %collective-permute-done.2.refs_3_, ...), custom_call_target="tpu_custom_call" | custom-call | bytes 21807104 | tf_op jit(solution)/shard_map/pallas_call | solution.py:146
  68.6 3.6 %collective-permute-done.14.refs_2_ = bf16[1936,128]{1,0:T(8,128)(2,1)S(1)} collective-permute-done((bf16[1936,128]{1,0:T(8,128)(2,1)S(1)}, bf16[1936,128]{1,0:T(8,128)(2,1)S(1)}, u32[]{:S(2)}, u32[]{:S(2)}) %collective-permute-start.14) | collective-permute-done | bytes 495648 | tf_op jit(solution)/shard_map/ppermute | solution.py:22
  72.2 3.8 %collective-permute-done.13.refs_1_ = bf16[2848,128]{1,0:T(8,128)(2,1)S(1)} collective-permute-done((bf16[2848,128]{1,0:T(8,128)(2,1)S(1)}, bf16[2848,128]{1,0:T(8,128)(2,1)S(1)}, u32[]{:S(2)}, u32[]{:S(2)}) %collective-permute-start.13) | collective-permute-done | bytes 729120 | tf_op jit(solution)/shard_map/ppermute | solution.py:22
  77.2 1.3 %shard_map.39.refs_5_ = bf16[56144,128]{1,0:T(8,128)(2,1)S(1)} custom-call(bf16[2960,128]{1,0:T(8,128)(2,1)S(1)} %collective-permute-done.12.refs_0_, bf16[2848,128]{1,0:T(8,128)(2,1)S(1)} %collective-permute-done.13.refs_1_, bf16[1936,128]{1,0:T(8,128)(2,1)S(1)} %collective-permute-done.14.refs_2_, ...), custom_call_target="tpu_custom_call", output_to_operand_aliasing={{}: (3, {})} | custom-call | bytes 3964928 | tf_op jit(solution)/shard_map/pallas_call | solution.py:146
  78.6 1.6 %collective-permute-done.17.refs_2_ = bf16[1936,128]{1,0:T(8,128)(2,1)S(1)} collective-permute-done((bf16[1936,128]{1,0:T(8,128)(2,1)S(1)}, bf16[1936,128]{1,0:T(8,128)(2,1)S(1)}, u32[]{:S(2)}, u32[]{:S(2)}) %collective-permute-start.17) | collective-permute-done | bytes 495648 | tf_op jit(solution)/shard_map/ppermute | solution.py:22
  80.2 0.7 collective-permute-done.18.refs_3_
  80.9 0.7 collective-permute-done.19.refs_4_
  81.6 24.8 %shard_map.40 = (bf16[56144,128]{1,0:T(8,128)(2,1)S(1)}, bf16[29,128,128]{2,1,0:T(8,128)(2,1)}) custom-call(bf16[2960,128]{1,0:T(8,128)(2,1)S(1)} %collective-permute-done.15.refs_0_, bf16[2848,128]{1,0:T(8,128)(2,1)S(1)} %collective-permute-done.16.refs_1_, bf16[1936,128]{1,0:T(8,128)(2,1)S(1)} %collective-permute-done.17.refs_2_, ...), custom_call_target="tpu_custom_call", output_to_operand_aliasing={{0}: (5, {})} | custom-call | flops 16999999488 | bytes 15728640 | tf_op jit(solution)/shard_map/pallas_call | solution.py:284
  (32 shorter events, 3.8 us)
Async XLA Ops:
  1.9 15.3 %collective-permute-start = (bf16[1936,128]{1,0:T(8,128)(2,1)}, bf16[1936,128]{1,0:T(8,128)(2,1)S(1)}, u32[]{:S(2)}, u32[]{:S(2)}) collective-permute-start(bf16[1936,128]{1,0:T(8,128)(2,1)} %shard_map.37.refs_0_), channel_id=1, source_target_pairs={{0,1},{1,0},{2,3},{3,2},{4,5},{5,4},{6,7},{7,6},{8,9},{9,8},{10,11... | collective-permute-start | bytes 1486856 | tf_op jit(solution)/shard_map/ppermute | solution.py:22
  4.9 23.6 %collective-permute-start.1 = (bf16[1936,128]{1,0:T(8,128)(2,1)}, bf16[1936,128]{1,0:T(8,128)(2,1)S(1)}, u32[]{:S(2)}, u32[]{:S(2)}) collective-permute-start(bf16[1936,128]{1,0:T(8,128)(2,1)} %shard_map.37.refs_0_), channel_id=1, source_target_pairs={{0,16},{1,17},{2,18},{3,19},{4,20},{5,21},{6,22},{7,23},{8,24},{9,... | collective-permute-start | bytes 1486856 | tf_op jit(solution)/shard_map/ppermute | solution.py:22
  6.4 22.2 %collective-permute-start.2 = (bf16[1936,128]{1,0:T(8,128)(2,1)}, bf16[1936,128]{1,0:T(8,128)(2,1)S(1)}, u32[]{:S(2)}, u32[]{:S(2)}) collective-permute-start(bf16[1936,128]{1,0:T(8,128)(2,1)} %shard_map.37.refs_0_), channel_id=1, source_target_pairs={{0,6},{1,7},{2,4},{3,5},{4,2},{5,3},{6,0},{7,1},{8,14},{9,15},{10,... | collective-permute-start | bytes 1486856 | tf_op jit(solution)/shard_map/ppermute | solution.py:22
  10.0 21.7 %collective-permute-start.3 = (bf16[1936,128]{1,0:T(8,128)(2,1)}, bf16[1936,128]{1,0:T(8,128)(2,1)S(1)}, u32[]{:S(2)}, u32[]{:S(2)}) collective-permute-start(bf16[1936,128]{1,0:T(8,128)(2,1)} %shard_map.37.refs_0_), channel_id=1, source_target_pairs={{0,2},{1,3},{2,0},{3,1},{4,6},{5,7},{6,4},{7,5},{8,10},{9,11},{10,... | collective-permute-start | bytes 1486856 | tf_op jit(solution)/shard_map/ppermute | solution.py:22
  10.0 21.8 %collective-permute-start.4 = (bf16[1936,128]{1,0:T(8,128)(2,1)}, bf16[1936,128]{1,0:T(8,128)(2,1)S(1)}, u32[]{:S(2)}, u32[]{:S(2)}) collective-permute-start(bf16[1936,128]{1,0:T(8,128)(2,1)} %shard_map.37.refs_0_), channel_id=1, source_target_pairs={{0,17},{1,16},{2,19},{3,18},{4,21},{5,20},{6,23},{7,22},{8,25},{9,... | collective-permute-start | bytes 1486856 | tf_op jit(solution)/shard_map/ppermute | solution.py:22
  31.7 29.5 %copy-start = (bf16[1936,128]{1,0:T(8,128)(2,1)S(1)}, bf16[1936,128]{1,0:T(8,128)(2,1)}, u32[]{:S(2)}) copy-start(bf16[1936,128]{1,0:T(8,128)(2,1)} %shard_map.37.refs_0_) | copy-start | bytes 1486852
  31.9 24.7 %collective-permute-start.5 = (bf16[11616,128]{1,0:T(8,128)(2,1)S(1)}, bf16[11616,128]{1,0:T(8,128)(2,1)S(1)}, u32[]{:S(2)}, u32[]{:S(2)}) collective-permute-start(bf16[11616,128]{1,0:T(8,128)(2,1)S(1)} %constant_dynamic-update-slice_fusion), channel_id=1, source_target_pairs={{0,8},{1,9},{2,10},{3,11},{4,12},{5,13},{6,14},{7,15},{8,0},{9,1},... | collective-permute-start | bytes 8921096 | tf_op jit(solution)/shard_map/ppermute | solution.py:22
  32.0 24.3 %collective-permute-start.6 = (bf16[3872,128]{1,0:T(8,128)(2,1)S(1)}, bf16[3872,128]{1,0:T(8,128)(2,1)S(1)}, u32[]{:S(2)}, u32[]{:S(2)}) collective-permute-start(bf16[3872,128]{1,0:T(8,128)(2,1)S(1)} %get-tuple-element.29), channel_id=1, source_target_pairs={{0,16},{1,17},{2,18},{3,19},{4,20},{5,21},{6,22},{7,23},{8,24},{9,... | collective-permute-start | bytes 2973704 | tf_op jit(solution)/shard_map/ppermute | solution.py:22
  32.6 24.0 %collective-permute-start.7 = (bf16[3872,128]{1,0:T(8,128)(2,1)S(1)}, bf16[3872,128]{1,0:T(8,128)(2,1)S(1)}, u32[]{:S(2)}, u32[]{:S(2)}) collective-permute-start(bf16[3872,128]{1,0:T(8,128)(2,1)S(1)} %get-tuple-element.29), channel_id=1, source_target_pairs={{0,1},{1,0},{2,3},{3,2},{4,5},{5,4},{6,7},{7,6},{8,9},{9,8},{10,11... | collective-permute-start | bytes 2973704 | tf_op jit(solution)/shard_map/ppermute | solution.py:22
  33.1 21.7 %collective-permute-start.8 = (bf16[1936,128]{1,0:T(8,128)(2,1)S(1)}, bf16[1936,128]{1,0:T(8,128)(2,1)S(1)}, u32[]{:S(2)}, u32[]{:S(2)}) collective-permute-start(bf16[1936,128]{1,0:T(8,128)(2,1)S(1)} %collective-permute-done.2.refs_3_), channel_id=1, source_target_pairs={{0,2},{1,3},{2,0},{3,1},{4,6},{5,7},{6,4},{7,5},{8,10},{9,11},{10,... | collective-permute-start | bytes 1486856 | tf_op jit(solution)/shard_map/ppermute | solution.py:22
  34.8 24.8 %collective-permute-start.11 = (bf16[1936,128]{1,0:T(8,128)(2,1)S(1)}, bf16[1936,128]{1,0:T(8,128)(2,1)S(1)}, u32[]{:S(2)}, u32[]{:S(2)}) collective-permute-start(bf16[1936,128]{1,0:T(8,128)(2,1)S(1)} %collective-permute-done.4.refs_5_), channel_id=1, source_target_pairs={{0,4},{1,5},{2,6},{3,7},{4,0},{5,1},{6,2},{7,3},{8,12},{9,13},{10,... | collective-permute-start | bytes 1486856 | tf_op jit(solution)/shard_map/ppermute | solution.py:22
  56.6 4.6 %collective-permute-start.10 = (bf16[3872,128]{1,0:T(8,128)(2,1)S(1)}, bf16[3872,128]{1,0:T(8,128)(2,1)S(1)}, u32[]{:S(2)}, u32[]{:S(2)}) collective-permute-start(bf16[3872,128]{1,0:T(8,128)(2,1)S(1)} %collective-permute-done.6.refs_9_), channel_id=1, source_target_pairs={{0,8},{1,9},{2,10},{3,11},{4,12},{5,13},{6,14},{7,15},{8,0},{9,1},... | collective-permute-start | bytes 2973704 | tf_op jit(solution)/shard_map/ppermute | solution.py:22
  56.7 4.5 %collective-permute-start.9 = (bf16[3872,128]{1,0:T(8,128)(2,1)S(1)}, bf16[3872,128]{1,0:T(8,128)(2,1)S(1)}, u32[]{:S(2)}, u32[]{:S(2)}) collective-permute-start(bf16[3872,128]{1,0:T(8,128)(2,1)S(1)} %collective-permute-done.7.refs_7_), channel_id=1, source_target_pairs={{0,8},{1,9},{2,10},{3,11},{4,12},{5,13},{6,14},{7,15},{8,0},{9,1},... | collective-permute-start | bytes 2973704 | tf_op jit(solution)/shard_map/ppermute | solution.py:22
  57.3 18.9 %collective-permute-start.12 = (bf16[2960,128]{1,0:T(8,128)(2,1)S(1)}, bf16[2960,128]{1,0:T(8,128)(2,1)S(1)}, u32[]{:S(2)}, u32[]{:S(2)}) collective-permute-start(bf16[2960,128]{1,0:T(8,128)(2,1)S(1)} %pad_maximum_fusion), channel_id=1, source_target_pairs={{0,1},{1,0},{2,3},{3,2},{4,5},{5,4},{6,7},{7,6},{8,9},{9,8},{10,11... | collective-permute-start | bytes 2273288 | tf_op jit(solution)/shard_map/ppermute | solution.py:22
  58.0 18.0 %collective-permute-start.13 = (bf16[2848,128]{1,0:T(8,128)(2,1)S(1)}, bf16[2848,128]{1,0:T(8,128)(2,1)S(1)}, u32[]{:S(2)}, u32[]{:S(2)}) collective-permute-start(bf16[2848,128]{1,0:T(8,128)(2,1)S(1)} %pad_maximum_fusion.1), channel_id=1, source_target_pairs={{0,16},{1,17},{2,18},{3,19},{4,20},{5,21},{6,22},{7,23},{8,24},{9,... | collective-permute-start | bytes 2187272 | tf_op jit(solution)/shard_map/ppermute | solution.py:22
  59.5 12.7 %collective-permute-start.14 = (bf16[1936,128]{1,0:T(8,128)(2,1)S(1)}, bf16[1936,128]{1,0:T(8,128)(2,1)S(1)}, u32[]{:S(2)}, u32[]{:S(2)}) collective-permute-start(bf16[1936,128]{1,0:T(8,128)(2,1)S(1)} %collective-permute-done.4.refs_5_), channel_id=1, source_target_pairs={{0,2},{1,3},{2,0},{3,1},{4,6},{5,7},{6,4},{7,5},{8,10},{9,11},{10,... | collective-permute-start | bytes 1486856 | tf_op jit(solution)/shard_map/ppermute | solution.py:22
  76.2 5.4 %collective-permute-start.15 = (bf16[2960,128]{1,0:T(8,128)(2,1)S(1)}, bf16[2960,128]{1,0:T(8,128)(2,1)S(1)}, u32[]{:S(2)}, u32[]{:S(2)}) collective-permute-start(bf16[2960,128]{1,0:T(8,128)(2,1)S(1)} %collective-permute-done.12.refs_0_), channel_id=1, source_target_pairs={{0,8},{1,9},{2,10},{3,11},{4,12},{5,13},{6,14},{7,15},{8,0},{9,1},... | collective-permute-start | bytes 2273288 | tf_op jit(solution)/shard_map/ppermute | solution.py:22
  76.2 5.4 %collective-permute-start.16 = (bf16[2848,128]{1,0:T(8,128)(2,1)S(1)}, bf16[2848,128]{1,0:T(8,128)(2,1)S(1)}, u32[]{:S(2)}, u32[]{:S(2)}) collective-permute-start(bf16[2848,128]{1,0:T(8,128)(2,1)S(1)} %collective-permute-done.13.refs_1_), channel_id=1, source_target_pairs={{0,8},{1,9},{2,10},{3,11},{4,12},{5,13},{6,14},{7,15},{8,0},{9,1},... | collective-permute-start | bytes 2187272 | tf_op jit(solution)/shard_map/ppermute | solution.py:22
  76.7 3.5 %collective-permute-start.17 = (bf16[1936,128]{1,0:T(8,128)(2,1)S(1)}, bf16[1936,128]{1,0:T(8,128)(2,1)S(1)}, u32[]{:S(2)}, u32[]{:S(2)}) collective-permute-start(bf16[1936,128]{1,0:T(8,128)(2,1)S(1)} %collective-permute-done.8.refs_11_), channel_id=1, source_target_pairs={{0,8},{1,9},{2,10},{3,11},{4,12},{5,13},{6,14},{7,15},{8,0},{9,1},... | collective-permute-start | bytes 1486856 | tf_op jit(solution)/shard_map/ppermute | solution.py:22
  76.7 4.2 %collective-permute-start.18 = (bf16[1936,128]{1,0:T(8,128)(2,1)S(1)}, bf16[1936,128]{1,0:T(8,128)(2,1)S(1)}, u32[]{:S(2)}, u32[]{:S(2)}) collective-permute-start(bf16[1936,128]{1,0:T(8,128)(2,1)S(1)} %collective-permute-done.11.refs_12_), channel_id=1, source_target_pairs={{0,8},{1,9},{2,10},{3,11},{4,12},{5,13},{6,14},{7,15},{8,0},{9,1},... | collective-permute-start | bytes 1486856 | tf_op jit(solution)/shard_map/ppermute | solution.py:22
  77.2 4.4 %collective-permute-start.19 = (bf16[1936,128]{1,0:T(8,128)(2,1)S(1)}, bf16[1936,128]{1,0:T(8,128)(2,1)S(1)}, u32[]{:S(2)}, u32[]{:S(2)}) collective-permute-start(bf16[1936,128]{1,0:T(8,128)(2,1)S(1)} %collective-permute-done.14.refs_2_), channel_id=1, source_target_pairs={{0,8},{1,9},{2,10},{3,11},{4,12},{5,13},{6,14},{7,15},{8,0},{9,1},... | collective-permute-start | bytes 1486856 | tf_op jit(solution)/shard_map/ppermute | solution.py:22
